TPU v7x, 256 devices: a whole 4x4x8 slice. The times are simulated.
256 devices in a mesh: row: 64 (over x, z, core), col: 4 (over y).
Axes of the slice: x: 4, y: 4, z: 8, core: 2. Of those that a mesh axis runs over, the one named last changes fastest.
Arguments:
- blocks: bfloat16 [256, 28, 128, 128], P('row', 'col'), may hold values from -1.5 to 1.5
- nonzero: int32 [256, 28], P('row', 'col'), may hold values 0 or 1
- columns: int32 [256, 28], replicated, may hold values from 0 to 255, as said below
Outputs:
- square: bfloat16 [256, 28, 128, 128], P('row', 'col')
Inputs may be any that keep to these rules, and one draw needn't show every extreme that they name: The 28 columns of one block row are distinct. The rows of a slab of 4 consecutive block rows (slab s holds rows s * 4 to s * 4 + 3) all name every row of their own slab, and together name at most 1 distinct block rows of any other slab.
All inputs are finite; a program needn't handle non-finite values. No bound on the sum of `nonzero` on one device may be relied on, other than what follows from the above.
Results may differ from a plain program's by a relative error of at most 0.001.
Values may be sent and summed in bfloat16 or wider, within the bound.
No kernel may reach another device: no remote copies, remote signals or barrier semaphores. Data moves between devices by JAX's collectives and lax.ppermute only.
A program may use at most 192 MiB of HBM per device.

v0:
```python
import jax
import jax.numpy as jnp
from jax import lax
from jax.sharding import PartitionSpec as P


def shards(blocks, nonzero, columns):
    height = blocks.shape[0]
    quarter = blocks.shape[1]
    block_side = blocks.shape[2]
    slots_all = columns.shape[1]
    slab_count = lax.axis_size("row")
    my_slab = lax.axis_index("row")
    my_part = lax.axis_index("col")
    pooled = min(slots_all, (slab_count - 1) * height)
    capacity = (pooled + slab_count - 2) // (slab_count - 1)
    masked = blocks * nonzero[:, :, None, None].astype(jnp.bfloat16)
    levels = jnp.arange(capacity, dtype=jnp.int32)
    slab_ids = jnp.arange(slab_count, dtype=jnp.int32)
    local_rows = jnp.arange(height, dtype=jnp.int32)
    grouped = columns.reshape(slab_count, height * slots_all)
    targets = my_slab * height + local_rows
    wanted = jnp.any(grouped[:, :, None] == targets[None, None, :], axis=1)
    wanted = wanted & (slab_ids != my_slab)[:, None]
    ranking = jnp.cumsum(wanted.astype(jnp.int32), axis=1) - 1
    chosen = wanted[:, None, :] & (ranking[:, None, :] == levels[None, :, None])
    picked = jnp.sum(jnp.where(chosen, local_rows[None, None, :], 0), axis=2)
    filled = jnp.any(chosen, axis=2)
    outgoing = jnp.where(
        filled[:, :, None, None, None], masked[picked], jnp.zeros((), jnp.bfloat16)
    )
    incoming = lax.all_to_all(outgoing, "row", split_axis=0, concat_axis=0, tiled=True)
    row_table = jnp.concatenate(
        [incoming.reshape(slab_count * capacity, quarter, block_side, block_side), masked], axis=0
    )
    my_columns = lax.dynamic_slice_in_dim(columns, my_slab * height, height, 0)
    every_row = jnp.arange(slab_count * height, dtype=jnp.int32)
    requested = jnp.any(my_columns.reshape(-1)[:, None] == every_row[None, :], axis=0).reshape(
        slab_count, height
    )
    requested = requested & (slab_ids != my_slab)[:, None]
    request_rank = (jnp.cumsum(requested.astype(jnp.int32), axis=1) - 1).reshape(-1)
    source = my_columns // height
    within = my_columns % height
    slot_rank = jnp.sum(
        jnp.where(
            my_columns[:, :, None] == every_row[None, None, :], request_rank[None, None, :], 0
        ),
        axis=2,
    )
    row_index = jnp.where(
        source == my_slab, slab_count * capacity + within, source * capacity + slot_rank
    )
    far_cols = columns[my_columns]
    far_quarter = lax.dynamic_slice_in_dim(far_cols, my_part * quarter, quarter, 2)
    matches = (far_quarter[:, :, :, None] == my_columns[:, None, None, :]).astype(jnp.float32)
    whole = lax.all_gather(masked, "col", axis=1, tiled=True)
    extent = whole.shape[1]
    results = []
    for member in range(height):
        rows_used = row_index[member]
        gathered = row_table[rows_used]
        products = jnp.einsum(
            "tab,tubc->tuac", whole[member], gathered, preferred_element_type=jnp.float32
        )
        selector = matches[member].reshape(extent * quarter, slots_all)
        flattened = products.reshape(extent * quarter, block_side * block_side)
        dims = (((0,), (0,)), ((), ()))
        summed = lax.dot_general(
            selector,
            flattened,
            dims,
            precision=lax.Precision.HIGHEST,
            preferred_element_type=jnp.float32,
        )
        results.append(summed.reshape(slots_all, block_side, block_side))
    partial_value = jnp.stack(results, axis=0)
    square = lax.psum_scatter(partial_value, "col", scatter_dimension=1, tiled=True)
    return square.astype(jnp.bfloat16)


def solution(mesh):
    in_specs = (P("row", "col", None, None), P("row", "col"), P())
    out_specs = P("row", "col", None, None)
    return jax.shard_map(shards, mesh=mesh, in_specs=in_specs, out_specs=out_specs, check_vma=False)
```

profile of v0, /device:TPU:1, one launch (start us, length us, event | category | flops | bytes accessed | tf_op | source)
XLA Modules:
  0.0 714.9 jit_solution(17294167417742704943)
XLA Ops:
  6.5 0.7 convert_element_type.15
  7.2 0.9 copy.67
  8.1 0.8 add_select_fusion.2
  8.9 0.1 copy.70
  9.0 0.1 eq.91
  9.1 0.1 fusion.21
  9.2 0.1 reshape.244
  9.3 0.1 copy.74
  9.4 0.1 eq.80
  9.5 0.2 compare_reduce_fusion
  9.8 1.3 broadcast_multiply_fusion
  11.1 0.0 copy-start
  11.2 7.9 %gather_fusion.1 = bf16[64,7,128,128]{3,2,1,0:T(8,128)(2,1)} fusion(bf16[4,7,128,128]{3,2,1,0:T(8,128)(2,1)S(1)} %broadcast_multiply_fusion, s32[1024]{0:T(1024)S(1)} %pad_clamp_fusion.4), kind=kCustom, calls=%fused_computation.1 | custom fusion | bytes 29360384 | tf_op jit(solution)/shard_map/gather | solution.py:30
  19.1 13.4 %fusion = bf16[64,1,7,128,128]{4,3,2,1,0:T(8,128)(2,1)} fusion(bf16[64,7,128,128]{3,2,1,0:T(8,128)(2,1)} %gather_fusion.1, pred[64]{0:T(512)(128)(4,1)S(1)} %get-tuple-element.11), kind=kLoop, calls=%fused_computation.8 | loop fusion | flops 7340032 | bytes 29360192 | tf_op jit(solution)/shard_map/jit(_where)/select_n | solution.py:29
  32.5 13.2 %all-to-all-start = ((bf16[64,1,7,128,128]{4,3,2,1,0:T(8,128)(2,1)}), bf16[64,1,7,128,128]{4,3,2,1,0:T(8,128)(2,1)}, u32[]{:S(2)}, u32[]{:S(2)}) async-start(bf16[64,1,7,128,128]{4,3,2,1,0:T(8,128)(2,1)} %fusion), calls=%async_computation | async-start | bytes 29360128 | tf_op jit(solution)/shard_map/all_to_all | solution.py:32
  45.8 0.0 all-gather.2.cloned.1.call-start
  45.9 0.7 all-gather.2.cloned.1.call-update
  46.5 0.3 reduce-scatter.2.cloned.1.call-start
  46.9 0.1 copy.66
  47.0 0.1 reshape.251
  47.1 0.6 gather_fusion
  47.7 0.1 copy.68
  47.8 0.1 copy.75
  47.9 0.1 sub.17
  48.0 0.1 reshape.250
  48.2 0.1 copy.69
  48.3 0.2 broadcast_compare_fusion
  48.6 0.6 select_reduce_fusion
  49.3 0.2 slice_reduce_fusion.3
  49.6 316.8 %all-to-all-done = bf16[64,1,7,128,128]{4,3,2,1,0:T(8,128)(2,1)} async-done(((bf16[64,1,7,128,128]{4,3,2,1,0:T(8,128)(2,1)}), bf16[64,1,7,128,128]{4,3,2,1,0:T(8,128)(2,1)}, u32[]{:S(2)}, u32[]{:S(2)}) %all-to-all-start) | async-done | bytes 14680096 | tf_op jit(solution)/shard_map/all_to_all | solution.py:32
  366.4 13.3 %pad_maximum_fusion = bf16[68,7,128,128]{3,2,1,0:T(8,128)(2,1)} fusion(bf16[4,7,128,128]{3,2,1,0:T(8,128)(2,1)S(1)} %copy-done.1, bf16[64,7,128,128]{3,2,1,0:T(8,128)(2,1)} %bitcast.5), kind=kLoop, calls=%fused_computation.6 | loop fusion | flops 7798784 | bytes 31195136 | tf_op jit(solution)/shard_map/concatenate | solution.py:33
  379.7 9.5 %gather_fusion.5 = bf16[28,7,128,128]{3,2,1,0:T(8,128)(2,1)} fusion(bf16[68,7,128,128]{3,2,1,0:T(8,128)(2,1)} %pad_maximum_fusion, s32[1024]{0:T(1024)S(1)} %pad_clamp_fusion), kind=kCustom, calls=%fused_computation.5 | custom fusion | bytes 12845168 | tf_op jit(solution)/shard_map/gather | solution.py:62
  389.2 9.6 %gather_fusion.4 = bf16[28,7,128,128]{3,2,1,0:T(8,128)(2,1)} fusion(bf16[68,7,128,128]{3,2,1,0:T(8,128)(2,1)} %pad_maximum_fusion, s32[1024]{0:T(1024)S(1)} %pad_clamp_fusion.1), kind=kCustom, calls=%fused_computation.4 | custom fusion | bytes 12845168 | tf_op jit(solution)/shard_map/gather | solution.py:62
  398.8 9.6 %gather_fusion.3 = bf16[28,7,128,128]{3,2,1,0:T(8,128)(2,1)} fusion(bf16[68,7,128,128]{3,2,1,0:T(8,128)(2,1)} %pad_maximum_fusion, s32[1024]{0:T(1024)S(1)} %pad_clamp_fusion.2), kind=kCustom, calls=%fused_computation.3 | custom fusion | bytes 12845168 | tf_op jit(solution)/shard_map/gather | solution.py:62
  408.4 9.6 %gather_fusion.2 = bf16[28,7,128,128]{3,2,1,0:T(8,128)(2,1)} fusion(bf16[68,7,128,128]{3,2,1,0:T(8,128)(2,1)} %pad_maximum_fusion, s32[1024]{0:T(1024)S(1)} %pad_clamp_fusion.3), kind=kCustom, calls=%fused_computation.2 | custom fusion | bytes 12845168 | tf_op jit(solution)/shard_map/gather | solution.py:62
  417.9 9.5 %convolution_bitcast_fusion.3 = f32[28,7,128,128]{2,3,1,0:T(8,128)} fusion(bf16[28,7,128,128]{3,2,1,0:T(8,128)(2,1)} %gather_fusion.2, bf16[4,28,128,128]{3,2,1,0:T(8,128)(2,1)} %all-gather.2.cloned.1.call-done), kind=kOutput, calls=%fused_computation.24 | convolution fusion | flops 822083584 | bytes 20185088 | tf_op jit(solution)/shard_map/tab,tubc->tuac/dot_general | solution.py:63
  427.5 14.2 %copy.77 = f32[28,7,128,128]{3,2,1,0:T(8,128)} copy(f32[28,7,128,128]{2,3,1,0:T(8,128)} %convolution_bitcast_fusion.3) | data formatting | bytes 25690112 | tf_op jit(solution)/shard_map/tab,tubc->tuac/transpose | solution.py:63
  441.7 11.5 %slice_bitcast_fusion.3 = f32[128,128,196]{1,0,2:T(8,128)} fusion(f32[196,128,128]{2,1,0:T(8,128)} %bitcast.141), kind=kLoop, calls=%fused_computation.20 | loop fusion | bytes 25690112 | tf_op jit(solution)/shard_map/dot_general | solution.py:69
  453.2 9.5 %convolution_bitcast_fusion.2 = f32[28,7,128,128]{2,3,1,0:T(8,128)} fusion(bf16[28,7,128,128]{3,2,1,0:T(8,128)(2,1)} %gather_fusion.3, bf16[4,28,128,128]{3,2,1,0:T(8,128)(2,1)} %all-gather.2.cloned.1.call-done), kind=kOutput, calls=%fused_computation.23 | convolution fusion | flops 822083584 | bytes 20185088 | tf_op jit(solution)/shard_map/tab,tubc->tuac/dot_general | solution.py:63
  462.7 14.5 %copy.81 = f32[28,7,128,128]{3,2,1,0:T(8,128)} copy(f32[28,7,128,128]{2,3,1,0:T(8,128)} %convolution_bitcast_fusion.2) | data formatting | bytes 25690112 | tf_op jit(solution)/shard_map/tab,tubc->tuac/transpose | solution.py:63
  477.2 11.5 %slice_bitcast_fusion.2 = f32[128,128,196]{1,0,2:T(8,128)} fusion(f32[196,128,128]{2,1,0:T(8,128)} %bitcast.142), kind=kLoop, calls=%fused_computation.19 | loop fusion | bytes 25690112 | tf_op jit(solution)/shard_map/dot_general | solution.py:69
  488.7 9.6 %convolution_bitcast_fusion.1 = f32[28,7,128,128]{2,3,1,0:T(8,128)} fusion(bf16[28,7,128,128]{3,2,1,0:T(8,128)(2,1)} %gather_fusion.4, bf16[4,28,128,128]{3,2,1,0:T(8,128)(2,1)} %all-gather.2.cloned.1.call-done), kind=kOutput, calls=%fused_computation.22 | convolution fusion | flops 822083584 | bytes 20185088 | tf_op jit(solution)/shard_map/tab,tubc->tuac/dot_general | solution.py:63
  498.3 14.1 %copy.85 = f32[28,7,128,128]{3,2,1,0:T(8,128)} copy(f32[28,7,128,128]{2,3,1,0:T(8,128)} %convolution_bitcast_fusion.1) | data formatting | bytes 25690112 | tf_op jit(solution)/shard_map/tab,tubc->tuac/transpose | solution.py:63
  512.4 11.6 %slice_bitcast_fusion.1 = f32[128,128,196]{1,0,2:T(8,128)} fusion(f32[196,128,128]{2,1,0:T(8,128)} %bitcast.143), kind=kLoop, calls=%fused_computation.18 | loop fusion | bytes 25690112 | tf_op jit(solution)/shard_map/dot_general | solution.py:69
  524.0 9.6 %convolution_bitcast_fusion = f32[28,7,128,128]{2,3,1,0:T(8,128)} fusion(bf16[28,7,128,128]{3,2,1,0:T(8,128)(2,1)} %gather_fusion.5, bf16[4,28,128,128]{3,2,1,0:T(8,128)(2,1)} %all-gather.2.cloned.1.call-done), kind=kOutput, calls=%fused_computation.21 | convolution fusion | flops 822083584 | bytes 20185088 | tf_op jit(solution)/shard_map/tab,tubc->tuac/dot_general | solution.py:63
  533.5 14.2 %copy.89 = f32[28,7,128,128]{3,2,1,0:T(8,128)} copy(f32[28,7,128,128]{2,3,1,0:T(8,128)} %convolution_bitcast_fusion) | data formatting | bytes 25690112 | tf_op jit(solution)/shard_map/tab,tubc->tuac/transpose | solution.py:63
  547.7 11.5 %slice_bitcast_fusion = f32[128,128,196]{1,0,2:T(8,128)} fusion(f32[196,128,128]{2,1,0:T(8,128)} %bitcast.144), kind=kLoop, calls=%fused_computation.17 | loop fusion | bytes 25690112 | tf_op jit(solution)/shard_map/dot_general | solution.py:69
  559.2 17.5 %fusion.9 = f32[1,28,128,128]{3,1,2,0:T(8,128)S(1)} fusion(f32[128,128,196]{1,0,2:T(8,128)} %slice_bitcast_fusion.3, pred[196,28]{1,0:T(8,128)(4,1)S(1)} %reshape_squeeze.12), kind=kOutput, calls=%fused_computation.26 | convolution fusion | flops 1078984704 | bytes 14685552 | tf_op jit(solution)/shard_map/dot_general | solution.py:69
  576.7 0.0 slice-start.2
  576.7 0.0 slice-start.3
  576.7 0.0 slice-start.4
  576.7 0.0 slice-start.5
  576.7 18.1 %fusion.12 = f32[1,28,128,128]{3,1,2,0:T(8,128)} fusion(f32[128,128,196]{1,0,2:T(8,128)} %slice_bitcast_fusion.2, pred[196,28]{1,0:T(8,128)(4,1)S(1)} %reshape_squeeze.13), kind=kOutput, calls=%fused_computation.27 | convolution fusion | flops 1078984704 | bytes 14685552 | tf_op jit(solution)/shard_map/dot_general | solution.py:69
  594.8 0.0 slice-done
  594.9 0.0 slice-start.6
  594.9 0.0 slice-start.7
  594.9 14.2 %fusion.15 = f32[1,28,128,128]{3,1,2,0:T(8,128)} fusion(f32[128,128,196]{1,0,2:T(8,128)S(1)} %bitcast.138, pred[196,28]{1,0:T(8,128)(4,1)S(1)} %reshape_squeeze.14), kind=kOutput, calls=%fused_computation.28 | convolution fusion | flops 1078984704 | bytes 14685552 | tf_op jit(solution)/shard_map/dot_general | solution.py:69
  609.1 14.0 %fusion.18 = f32[1,28,128,128]{3,1,2,0:T(8,128)} fusion(f32[128,128,196]{1,0,2:T(8,128)S(1)} %bitcast.140, pred[196,28]{1,0:T(8,128)(4,1)S(1)} %reshape_squeeze.15), kind=kOutput, calls=%fused_computation.29 | convolution fusion | flops 1078984704 | bytes 14685552 | tf_op jit(solution)/shard_map/dot_general | solution.py:69
  623.1 2.7 pad_maximum_fusion.1
  625.9 7.2 %copy.92 = f32[4,28,128,128]{3,2,0,1:T(8,128)} copy(f32[4,28,128,128]{3,1,2,0:T(8,128)S(1)} %pad_maximum_fusion.1) | data formatting | bytes 14680064 | tf_op jit(solution)/shard_map/stack | solution.py:77
  633.1 0.0 reduce-scatter.2.cloned.1.call-update
  633.1 72.1 %reduce-scatter.2.cloned.1.call-done = f32[4,7,128,128]{3,2,0,1:T(8,128)} async-done(((f32[4,28,128,128]{3,2,0,1:T(8,128)}), f32[4,7,128,128]{3,2,0,1:T(8,128)}) %reduce-scatter.2.cloned.1.call-update) | async-done | bytes 1835024 | tf_op jit(solution)/shard_map/reduce_scatter | solution.py:78
  705.2 1.6 convert_element_type.17
  706.8 1.0 copy.93
  (41 shorter events, 0.4 us)
Async XLA Ops:
  11.1 8.0 %copy-start = (bf16[4,7,128,128]{3,2,1,0:T(8,128)(2,1)}, bf16[4,7,128,128]{3,2,1,0:T(8,128)(2,1)S(1)}, u32[]{:S(2)}) copy-start(bf16[4,7,128,128]{3,2,1,0:T(8,128)(2,1)S(1)} %broadcast_multiply_fusion) | copy-start | bytes 2752516
  32.5 333.9 %copy-start.1 = (bf16[4,7,128,128]{3,2,1,0:T(8,128)(2,1)S(1)}, bf16[4,7,128,128]{3,2,1,0:T(8,128)(2,1)}, u32[]{:S(2)}) copy-start(bf16[4,7,128,128]{3,2,1,0:T(8,128)(2,1)} %copy-done) | copy-start | bytes 2752516
  32.5 333.9 %all-to-all-start = ((bf16[64,1,7,128,128]{4,3,2,1,0:T(8,128)(2,1)}), bf16[64,1,7,128,128]{4,3,2,1,0:T(8,128)(2,1)}, u32[]{:S(2)}, u32[]{:S(2)}) async-start(bf16[64,1,7,128,128]{4,3,2,1,0:T(8,128)(2,1)} %fusion), calls=%async_computation | async-start | bytes 29360128 | tf_op jit(solution)/shard_map/all_to_all | solution.py:32
  45.8 372.1 %all-gather.2.cloned.1.call-start = ((), (), s32[]{:S(2)}) async-start(), calls=%async_computation.2 | async-start | bytes 4587520 | tf_op jit(solution)/shard_map/all_gather | solution.py:57
  46.5 658.6 %reduce-scatter.2.cloned.1.call-start = ((), (), s32[]{:S(2)}) async-start(), calls=%async_computation.3 | async-start | bytes 9175040 | tf_op jit(solution)/shard_map/reduce_scatter | solution.py:78
  559.2 35.6 %slice-start = ((s8[12845056]{0:T(1024)(128)(4,1)}), s8[4194304]{0:T(1024)(128)(4,1)S(1)}, s32[]{:S(2)}) async-start(s8[12845056]{0:T(1024)(128)(4,1)} %bitcast.137), calls=%async_computation.4 | async-start | bytes 8388608
  559.2 35.6 %slice-start.1 = ((s8[12845056]{0:T(1024)(128)(4,1)}), s8[4194304]{0:T(1024)(128)(4,1)S(1)}, s32[]{:S(2)}) async-start(s8[12845056]{0:T(1024)(128)(4,1)} %bitcast.137), calls=%async_computation.5 | async-start | bytes 8388608
  576.7 18.2 %slice-start.2 = ((s8[12845056]{0:T(1024)(128)(4,1)}), s8[4194304]{0:T(1024)(128)(4,1)S(1)}, s32[]{:S(2)}) async-start(s8[12845056]{0:T(1024)(128)(4,1)} %bitcast.137), calls=%async_computation.6 | async-start | bytes 8388608
  576.7 18.2 %slice-start.3 = ((s8[12845056]{0:T(1024)(128)(4,1)}), s8[262144]{0:T(1024)(128)(4,1)S(1)}, s32[]{:S(2)}) async-start(s8[12845056]{0:T(1024)(128)(4,1)} %bitcast.137), calls=%async_computation.7 | async-start | bytes 524288
  576.7 32.4 %slice-start.4 = ((s8[12845056]{0:T(1024)(128)(4,1)}), s8[4194304]{0:T(1024)(128)(4,1)S(1)}, s32[]{:S(2)}) async-start(s8[12845056]{0:T(1024)(128)(4,1)} %bitcast.139), calls=%async_computation.8 | async-start | bytes 8388608
  576.7 32.4 %slice-start.5 = ((s8[12845056]{0:T(1024)(128)(4,1)}), s8[4194304]{0:T(1024)(128)(4,1)S(1)}, s32[]{:S(2)}) async-start(s8[12845056]{0:T(1024)(128)(4,1)} %bitcast.139), calls=%async_computation.9 | async-start | bytes 8388608
  594.9 14.2 %slice-start.6 = ((s8[12845056]{0:T(1024)(128)(4,1)}), s8[4194304]{0:T(1024)(128)(4,1)S(1)}, s32[]{:S(2)}) async-start(s8[12845056]{0:T(1024)(128)(4,1)} %bitcast.139), calls=%async_computation.10 | async-start | bytes 8388608
  594.9 14.2 %slice-start.7 = ((s8[12845056]{0:T(1024)(128)(4,1)}), s8[262144]{0:T(1024)(128)(4,1)S(1)}, s32[]{:S(2)}) async-start(s8[12845056]{0:T(1024)(128)(4,1)} %bitcast.139), calls=%async_computation.11 | async-start | bytes 524288
  609.1 14.0 %copy-start.2 = (f32[1,28,128,128]{3,1,2,0:T(8,128)S(1)}, f32[1,28,128,128]{3,1,2,0:T(8,128)}, u32[]{:S(2)}) copy-start(f32[1,28,128,128]{3,1,2,0:T(8,128)} %fusion.12) | copy-start | bytes 5505028
Sparse Core Ops, SparseCore 0:
  48.4 47.5 all-gather.1
  633.2 71.8 reduce-scatter.1
where the time goes:
time: 720 us; the launch traced here: 715 us
  waiting for transfers between devices  390 us (54%)
  local copies, waits for them, and re-layouts  161 us (22%)
  matrix products  102 us (14%)
  other arithmetic  35.2 us (5%)
  between operations  13.9 us (2%)
  starting transfers between devices  13.6 us (2%)
    all_to_all x1, waiting for transfers between devices, shards(): lax.all_to_all(outgoing, 'row', split_axis=0, concat_axis=0, tiled=True)  317 us
    reduce_scatter x1, waiting for transfers between devices, shards(): lax.psum_scatter(partial_value, 'col', scatter_dimension=1, tiled=True)  72.1 us
    dot_general x4, matrix products, shards(): lax.dot_general(selector, flattened, dims, precision=lax.Precision.HIGHES...  63.7 us
    transpose x4, local copies, waits for them, and re-layouts, shards(): jnp.einsum('tab,tubc->tuac', whole[member], gathered, preferred_element_t...  56.9 us
    dot_general x4, local copies, waits for them, and re-layouts, shards(): lax.dot_general(selector, flattened, dims, precision=lax.Precision.HIGHES...  46.1 us
    dot_general x4, matrix products, shards(): jnp.einsum('tab,tubc->tuac', whole[member], gathered, preferred_element_t...  38.3 us
    gather x4, local copies, waits for them, and re-layouts, shards(): gathered = row_table[rows_used]  38.2 us
  transfers between devices with their start and end apart: 3, of which 2 were waited for; matrix products, arithmetic and copies ran while one was open for 8% of the time, Pallas kernels for 0%

commit v1 on v0

v1 whole, which is shorter than its diff:
```python
import functools

import jax
import jax.numpy as jnp
from jax import lax
from jax.experimental import pallas as pl
from jax.experimental.pallas import tpu as pltpu
from jax.sharding import Mesh
from jax.sharding import PartitionSpec as P

BF = jnp.bfloat16
F32 = jnp.float32
I32 = jnp.int32

NX, NZ, NC, NY = 4, 8, 2, 4
ROWS, SLOTS, SIDE = 256, 28, 128
HEIGHT, QUARTER = 4, 7
SLABS = ROWS // HEIGHT
CHIP_ENTRIES = NC * HEIGHT * SLOTS
CUT = SIDE // (NC * NY)
WIDE = SIDE // NY
CAP_Z = 44
CAP_X = 44
LISTED = 48
LIST_FAR = NX * CAP_X
GROUP = 8
FAR_GROUP = 4
ROWS_AT_ONCE = 4
HEIGHT_2 = NC * HEIGHT
OUT_COLS = 72
ZERO_BLOCK = NY * HEIGHT * QUARTER
VMEM_LIMIT = 48 * 1024 * 1024
ROW_AXES = ("x", "z", "core")


def vmem():
    return pl.BlockSpec(memory_space=pltpu.VMEM)


def smem():
    return pl.BlockSpec(memory_space=pltpu.SMEM)


def params():
    return pltpu.CompilerParams(vmem_limit_bytes=VMEM_LIMIT)


def cost(flops, moved):
    return pl.CostEstimate(flops=flops, bytes_accessed=moved, transcendentals=0)


def prepare_kernel(position_ref, keep_ref, blocks_ref, whole_ref, cuts_ref):
    part = position_ref[3]
    for row in range(HEIGHT):
        for slot in range(QUARTER):
            block = blocks_ref[row, slot]
            turned = jnp.where(keep_ref[row, slot] != 0, block, jnp.zeros_like(block)).T
            whole_ref[row, slot] = turned
            chip = (row + slot + part * QUARTER) & (NX - 1)
            for piece in range(NC * NY):
                cuts_ref[chip * (NC * NY) + piece, slot] = turned[piece * CUT : (piece + 1) * CUT]
    rows = iota((CUT, SIDE), 0) - position_ref[2] * HEIGHT
    lanes = iota((CUT, SIDE), 1) - position_ref[0] * SLOTS - part * QUARTER
    flags = jnp.zeros((CUT, SIDE), F32)
    for row in range(HEIGHT):
        for slot in range(QUARTER):
            here = (rows == row) & (lanes == slot)
            flags = jnp.where(here & (keep_ref[row, slot] != 0), 1.0, flags)
    for peer in range(NX * NC * NY):
        cuts_ref[peer, QUARTER] = flags.astype(BF)


def prepare(position, nonzero, blocks):
    return pl.pallas_call(
        prepare_kernel,
        out_shape=(
            jax.ShapeDtypeStruct((HEIGHT, QUARTER, SIDE, SIDE), BF),
            jax.ShapeDtypeStruct((NX * NC * NY, QUARTER + 1, CUT, SIDE), BF),
        ),
        in_specs=[smem(), smem(), vmem()],
        out_specs=(vmem(), vmem()),
        compiler_params=params(),
        name="prepare",
    )(position, nonzero, blocks)


def pack_kernel(unroll, index_ref, source_ref, *refs):
    out_ref = refs[-1]
    peers, count = out_ref.shape[0], out_ref.shape[1] // unroll * unroll
    for peer in range(peers):

        def step(i, carry):
            for j in range(unroll):
                at = i * unroll + j
                out_ref[peer, at] = source_ref[index_ref[0, peer * LISTED + at]]
            return carry

        lax.fori_loop(0, count // unroll, step, 0)
        if len(refs) > 1:
            out_ref[peer, count] = refs[0][peer]


def pack(index, source, peers, count, *notes):
    return pl.pallas_call(
        functools.partial(pack_kernel, 4),
        out_shape=jax.ShapeDtypeStruct((peers, count, CUT, SIDE), BF),
        in_specs=[smem(), vmem()] + [vmem()] * len(notes),
        out_specs=vmem(),
        compiler_params=params(),
        name="pack",
    )(index, source, *notes)


def own_block(whole_ref, place, rows):
    value = whole_ref[jnp.minimum(place, ZERO_BLOCK - 1), rows, :]
    return jnp.where(place < ZERO_BLOCK, value, jnp.zeros_like(value))


def out_place(place):
    return (place // QUARTER) % HEIGHT, place // (QUARTER * HEIGHT) * QUARTER + place % QUARTER


def own_kernel(
    plan_ref,
    whole_ref,
    out_ref,
    total,
    panel,
    near,
):
    first = pl.multiple_of(plan_ref[15, 0] * WIDE, WIDE)
    for inner in range(HEIGHT):
        for member in range(HEIGHT):
            panel[pl.ds(inner * SIDE, SIDE), pl.ds(member * SIDE, SIDE)] = own_block(
                whole_ref, plan_ref[9 + member, inner], pl.ds(0, SIDE)
            )

    def step(group, carry):
        for at in range(GROUP):
            for inner in range(HEIGHT):
                near[pl.ds(at * WIDE, WIDE), pl.ds(inner * SIDE, SIDE)] = own_block(
                    whole_ref, plan_ref[4 + inner, group * GROUP + at], pl.ds(first, WIDE)
                )
        value = jnp.dot(near[...], panel[...], preferred_element_type=F32)
        total[pl.ds(group * GROUP, GROUP)] = value.reshape(GROUP, WIDE, HEIGHT * SIDE)
        return carry

    lax.fori_loop(0, plan_ref[15, 1], step, 0)
    for place in range(ZERO_BLOCK):
        member, slot = out_place(place)
        column = plan_ref[8, member * (128 // HEIGHT) + slot]
        out_ref[place] = total[column, :, pl.ds(member * SIDE, SIDE)]


def own_sums(lists, whole):
    flops = 2 * 32 * WIDE * (HEIGHT * SIDE) ** 2
    return pl.pallas_call(
        own_kernel,
        out_shape=jax.ShapeDtypeStruct((ZERO_BLOCK, WIDE, SIDE), F32),
        in_specs=[smem(), vmem()],
        out_specs=vmem(),
        scratch_shapes=[
            pltpu.VMEM((OUT_COLS, WIDE, HEIGHT * SIDE), F32),
            pltpu.VMEM((HEIGHT * SIDE, HEIGHT * SIDE), BF),
            pltpu.VMEM((GROUP * WIDE, HEIGHT * SIDE), BF),
        ],
        compiler_params=params(),
        cost_estimate=cost(flops, 3 * ZERO_BLOCK * SIDE * SIDE),
        name="own_sums",
    )(lists, whole)


def far_kernel(
    own_ref,
    plan_ref,
    whole_ref,
    far_ref,
    near_ref,
    out_ref,
    total,
):
    def clear(group, carry):
        total[pl.ds(group * GROUP, GROUP)] = jnp.zeros((GROUP, WIDE, HEIGHT * SIDE), F32)
        return carry

    lax.fori_loop(0, own_ref[15, 1], clear, 0)

    def product(named, offset):
        begin = plan_ref[2, named]
        length = plan_ref[3, named]
        right = jnp.concatenate(
            [
                own_block(whole_ref, own_ref[member, named], pl.ds(0, SIDE))
                for member in range(HEIGHT)
            ],
            axis=1,
        )
        pieces, columns = [], []
        for at in range(FAR_GROUP):
            place = jnp.minimum(begin + offset + at, LIST_FAR - 1)
            index = plan_ref[0, place]
            for half in range(NC):
                pieces.append(far_ref[index + half * CAP_X])
            columns.append(jnp.where(offset + at < length, plan_ref[1, place], OUT_COLS))
        value = jnp.dot(jnp.concatenate(pieces, axis=0), right, preferred_element_type=F32)
        return value, columns

    def add(value, columns):
        for at, column in enumerate(columns):
            total[column] = total[column] + value[at * WIDE : (at + 1) * WIDE]

    def first_step(step, carry):
        done = [product(step * ROWS_AT_ONCE + at, 0) for at in range(ROWS_AT_ONCE)]
        for value, columns in done:
            add(value, columns)
        return carry

    named_rows = own_ref[15, 2]
    lax.fori_loop(0, (named_rows + ROWS_AT_ONCE - 1) // ROWS_AT_ONCE, first_step, 0)

    def rest(named, carry):
        def rest_step(step, inner_carry):
            add(*product(named, step * FAR_GROUP))
            return inner_carry

        lax.fori_loop(1, (plan_ref[3, named] + FAR_GROUP - 1) // FAR_GROUP, rest_step, 0)
        return carry

    lax.fori_loop(0, named_rows, rest, 0)

    for place in range(ZERO_BLOCK):
        member, slot = out_place(place)
        column = own_ref[8, member * (128 // HEIGHT) + slot]
        value = total[column, :, pl.ds(member * SIDE, SIDE)] + near_ref[place]
        out_ref[place] = value.astype(BF)


def far_sums(own_lists, far_lists, whole, far, near):
    return pl.pallas_call(
        far_kernel,
        out_shape=jax.ShapeDtypeStruct((ZERO_BLOCK, WIDE, SIDE), BF),
        in_specs=[smem(), smem(), vmem(), vmem(), vmem()],
        out_specs=vmem(),
        scratch_shapes=[pltpu.VMEM((OUT_COLS + 1, WIDE, HEIGHT * SIDE), F32)],
        compiler_params=params(),
        name="far_sums",
    )(own_lists, far_lists, whole, far, near)


def finish_kernel(cuts_ref, out_ref):
    for row in range(HEIGHT):
        for slot in range(QUARTER):
            turned = jnp.concatenate([cuts_ref[part, row, slot] for part in range(NY)], axis=0)
            out_ref[row, slot] = turned.T


def finish(cuts):
    return pl.pallas_call(
        finish_kernel,
        out_shape=jax.ShapeDtypeStruct((HEIGHT, QUARTER, SIDE, SIDE), BF),
        in_specs=[vmem()],
        out_specs=vmem(),
        compiler_params=params(),
        name="finish",
    )(cuts)


def iota(shape, axis):
    return lax.broadcasted_iota(I32, shape, axis)


def dot(a, b):
    return jnp.dot(a.astype(BF), b.astype(BF), preferred_element_type=F32)


def dot_rows(a, b):
    return lax.dot_general(
        a.astype(BF), b.astype(BF), (((1,), (1,)), ((), ())), preferred_element_type=F32
    )


def earlier(size, lower, group=None, key=None):
    row, column = iota((size, size), 0), iota((size, size), 1)
    first, second = (row, column) if key is None else (key(row), key(column))
    pairs = first > second if lower else first < second
    if group is not None:
        pairs = pairs & (group(row) == group(column))
    return pairs.astype(F32)


def places(need, order, group=None, key=None):
    lower = earlier(need.shape[0], True, group, key)
    return dot(need, order) + jnp.sum(dot(lower, need), axis=1, keepdims=True)


def select(need, groups, group, capacity, order):
    size, lanes = need.shape
    place = places(need, order, group)
    held = dot_rows(jnp.ones((8, lanes), F32), need)
    first = dot(held, earlier(size, False, group))[0:1]
    last = first + held[0:1]
    index = iota((groups * capacity, 1), 0)
    number = jnp.zeros_like(index)
    for boundary in range(1, groups):
        number = number + (index >= boundary * capacity).astype(I32)
    slot = (index - number * capacity).astype(F32)
    chosen = (first <= slot) & (slot < last)
    if group is not None:
        chosen = chosen & (number == group(iota((groups * capacity, size), 1)))
    chosen = chosen.astype(F32)
    code = jnp.where((need > 0) & (place < capacity), place, 250.0)
    return chosen, dot(chosen, code) == slot


def values_of(chosen, hit, value):
    value = jnp.where(hit, dot(chosen, value), 0.0)
    return dot_rows(jnp.ones((8, value.shape[1]), F32), value)


def quarter_of(slot):
    return sum((slot >= bound * QUARTER).astype(I32) for bound in range(1, NY))


def kept_blocks(slot, flags, begin):
    kept = jnp.zeros(slot.shape, F32)
    for number in range(SLOTS):
        at = begin + number
        kept = jnp.where(slot == number, flags[:, at : at + 1], kept)
    return kept


def plane_of(row):
    return (row // HEIGHT_2) % NZ


def pattern_kernel(columns_ref, slots_ref, union_ref, far_ref):
    step = 64
    for begin in range(0, ROWS, step):
        column = iota((step, ROWS), 1)
        found = jnp.full((step, ROWS), -1, I32)
        for slot in range(SLOTS):
            at = columns_ref[begin : begin + step, slot : slot + 1]
            found = jnp.where(at == column, slot, found)
        slots_ref[begin : begin + step, :] = found
    names = (slots_ref[...] >= 0).astype(F32)
    mine = iota((128, ROWS), 1) // HEIGHT == iota((128, ROWS), 0)
    union = (dot(mine.astype(F32), names) > 0).astype(F32)
    union_ref[...] = union
    far_ref[...] = jnp.where(mine, 0.0, union).T


def pattern(columns):
    return pl.pallas_call(
        pattern_kernel,
        out_shape=(
            jax.ShapeDtypeStruct((ROWS, ROWS), I32),
            jax.ShapeDtypeStruct((128, ROWS), F32),
            jax.ShapeDtypeStruct((ROWS, 128), F32),
        ),
        in_specs=[vmem()],
        out_specs=(vmem(), vmem(), vmem()),
        compiler_params=params(),
        cost_estimate=cost(2 * SLOTS * ROWS**3 // 4, 8 * ROWS**2),
        name="pattern",
    )(columns)


def send_kernel(position_ref, slots_ref, union_ref, far_ref, near_ref, send_ref, notes_ref):
    x, z = position_ref[0], position_ref[1]
    flags = functools.reduce(
        jnp.add,
        [near_ref[peer * (QUARTER + 1) + QUARTER].astype(F32) for peer in range(NX * NC * NY)],
    )[0:HEIGHT_2]
    plane = NX * HEIGHT_2
    slots, named_by, kept = [], [], []
    for number in range(NX):
        rows = pl.ds(pl.multiple_of((number * NZ + z) * HEIGHT_2, HEIGHT_2), HEIGHT_2)
        slots.append(slots_ref[rows, :])
        named_by.append(far_ref[rows, :])
        kept.append(kept_blocks(slots[-1], flags, number * SLOTS))
    slot = jnp.concatenate(slots, axis=0)
    row = iota(slot.shape, 0)
    mine = jnp.where(((row + slot) & (NX - 1)) == x, jnp.concatenate(kept, axis=0), 0.0)
    quarter = quarter_of(slot)
    held = ((row // HEIGHT_2 * NY + quarter) * NC + (row // HEIGHT) % NC) * (QUARTER + 1)
    held = (held + slot - quarter * QUARTER).astype(F32) * mine

    order = earlier(ROWS, False)
    union = union_ref[...]
    shape = (NZ * plane, 128)
    to = (iota(shape, 1) // NC) % NZ == iota(shape, 0) // plane
    named_by = jnp.concatenate(named_by * NZ, axis=0)
    wanted = dot(jnp.where(to, named_by, 0.0), union) > 0
    need = jnp.where(wanted, jnp.concatenate([mine] * NZ, axis=0), 0.0)
    chosen, hit = select(need, NZ, lambda index: index // plane, LISTED, order)
    held = jnp.concatenate([held] * NZ, axis=0)
    send_ref[...] = values_of(chosen, hit, held)[0:1].astype(I32)
    asked = dot(chosen, named_by) * dot_rows(hit.astype(F32), union)
    place = iota((8, LISTED), 1)
    for number in range(NZ):
        target = iota((NX * NC, 128), 0)
        slab = (target // NC * NZ + number) * NC + target % NC
        choice = (iota((NX * NC, 128), 1) == slab).astype(F32)
        part = dot_rows(choice, asked[number * LISTED : (number + 1) * LISTED])
        part = jnp.where(place < CAP_Z, part, 0.0)
        part = jnp.concatenate([part, jnp.zeros((8, SIDE - LISTED), F32)], axis=1)
        notes_ref[number] = jnp.concatenate([flags, part], axis=0).astype(BF)


def send_lists(position, slots, union, far, near):
    return pl.pallas_call(
        send_kernel,
        out_shape=(
            jax.ShapeDtypeStruct((1, NZ * LISTED), I32),
            jax.ShapeDtypeStruct((NZ, CUT, SIDE), BF),
        ),
        in_specs=[smem()] + [vmem()] * 4,
        out_specs=(vmem(), vmem()),
        compiler_params=params(),
        name="send_lists",
    )(position, slots, union, far, near)


def route_kernel(along_ref, out_ref):
    asked = jnp.concatenate(
        [along_ref[plane, CAP_Z].astype(F32)[CUT // 2 :] for plane in range(NZ)], axis=0
    )
    shape = asked.shape
    chosen, hit = select(asked, 8, lambda index: index & 7, LISTED, earlier(SIDE, False))
    source = values_of(chosen, hit, (iota(shape, 0) // 8).astype(F32))
    place = values_of(chosen, hit, iota(shape, 1).astype(F32))
    out_ref[...] = (source * (CAP_Z + 1) + place)[0:1].astype(I32)


def route(along):
    return pl.pallas_call(
        route_kernel,
        out_shape=jax.ShapeDtypeStruct((1, NX * NC * LISTED), I32),
        in_specs=[vmem()],
        out_specs=vmem(),
        compiler_params=params(),
        name="route",
    )(along)


def own_plan_kernel(position_ref, slots_ref, union_ref, out_ref):
    x, z, core, part = (position_ref[i] for i in range(4))
    chip = x * NZ + z
    slab = chip * NC + core
    order = earlier(ROWS, False)
    out_ref[...] = jnp.zeros_like(out_ref)
    mine = union_ref[pl.ds(slab, 1), :]
    rank = dot(jnp.broadcast_to(mine, (8, ROWS)), order)

    both = slots_ref[pl.ds(pl.multiple_of(chip * HEIGHT_2, HEIGHT_2), HEIGHT_2), :]
    swapped = jnp.concatenate([both[HEIGHT:], both[:HEIGHT]], axis=0)
    slot = jnp.where(core == 0, both, swapped)
    quarter = quarter_of(slot)
    held = (quarter * HEIGHT + iota(slot.shape, 0)) * QUARTER + slot - quarter * QUARTER
    held = jnp.where(slot >= 0, held - ZERO_BLOCK, 0).astype(F32)

    every = iota((1, ROWS), 1)
    named = jnp.where(every // HEIGHT == slab, 0.0, mine)
    position = dot(jnp.broadcast_to(named, (8, ROWS)), order)[0:1]
    number = iota((SLABS, ROWS), 0).astype(F32)
    chosen = ((position == number) & (named > 0)).astype(F32)
    out_ref[0:4, 0:SLABS] = dot_rows(held, chosen)[0:HEIGHT].astype(I32) + ZERO_BLOCK

    number = iota((OUT_COLS, ROWS), 0).astype(F32)
    chosen = ((rank[0:1] == number) & (mine > 0)).astype(F32)
    out_ref[4:8, 0:OUT_COLS] = dot_rows(held, chosen)[0:HEIGHT].astype(I32) + ZERO_BLOCK
    wide = 128 // HEIGHT
    chosen = jnp.concatenate(
        [slot[i : i + 1] == iota((wide, ROWS), 0) for i in range(HEIGHT)], axis=0
    )
    out_ref[8:9, 0:128] = dot_rows(rank, chosen.astype(F32))[0:1].astype(I32)
    chosen = (iota((8, ROWS), 1) == iota((8, ROWS), 0) + slab * HEIGHT).astype(F32)
    out_ref[9:13, 0:8] = dot_rows(held, chosen)[0:HEIGHT].astype(I32) + ZERO_BLOCK
    groups = ((jnp.sum(mine) + (GROUP - 1)) * (1.0 / GROUP)).astype(I32)
    lane = iota((1, 128), 1)
    scalars = jnp.where(lane == 0, part, 0)
    scalars = jnp.where(lane == 1, groups, scalars)
    out_ref[15:16, :] = jnp.where(lane == 2, jnp.sum(named).astype(I32), scalars)


def own_plan(position, slots, union):
    return pl.pallas_call(
        own_plan_kernel,
        out_shape=jax.ShapeDtypeStruct((16, 128), I32),
        in_specs=[smem(), vmem(), vmem()],
        out_specs=vmem(),
        compiler_params=params(),
        cost_estimate=cost(ROWS**3, 4 * ROWS**2),
        name="own_plan",
    )(position, slots, union)


def far_plan_kernel(position_ref, slots_ref, union_ref, far_ref, along_ref, out_ref, kept_ref):
    x, z, core = (position_ref[i] for i in range(3))
    slab = (x * NZ + z) * NC + core
    order = earlier(ROWS, False)
    out_ref[...] = jnp.zeros_like(out_ref)
    for plane in range(NZ):
        flags = along_ref[plane, CAP_Z].astype(F32)[0:HEIGHT_2]
        for number in range(NX):
            begin = (number * NZ + plane) * HEIGHT_2
            rows = slice(begin, begin + HEIGHT_2)
            kept_ref[rows, :] = kept_blocks(slots_ref[rows, :], flags, number * SLOTS)
    kept = kept_ref[...]
    far, union = far_ref[...], union_ref[...]
    dealt = (iota(kept.shape, 0) + slots_ref[...]) & (NX - 1)

    mine = union_ref[pl.ds(slab, 1), :]
    rank = dot(jnp.broadcast_to(mine, (8, ROWS)), order)[0:1]
    named = jnp.sum(jnp.where(iota(far.shape, 1) == slab, far, 0.0), axis=1, keepdims=True)
    need = kept * named * mine
    place = jnp.zeros((ROWS, ROWS), F32)
    for number in range(NX):
        inside = places(
            jnp.where(dealt == number, need, 0.0),
            order,
            key=lambda row: plane_of(row) * ROWS + row,
        )
        inside = jnp.minimum(inside, CAP_X - 1.0) + number * CAP_X
        place = jnp.where(dealt == number, inside, place)
    chosen, hit = select(need, 1, None, LIST_FAR, order)
    place = values_of(chosen, hit, place)[0:1].astype(I32)
    skipped = sum((place >= bound * CAP_X).astype(I32) for bound in range(1, NX))
    out_ref[0:1, 0:LIST_FAR] = place + skipped * ((NC - 1) * CAP_X)
    column = values_of(chosen, hit, jnp.broadcast_to(rank, (ROWS, ROWS)))
    out_ref[1:2, 0:LIST_FAR] = column[0:1].astype(I32)

    count = dot_rows(jnp.ones((8, ROWS), F32), need)
    start = jnp.minimum(dot(count, order), 250.0)
    row = jnp.where(iota((1, ROWS), 1) // HEIGHT == slab, 0.0, mine)
    position = dot(jnp.broadcast_to(row, (8, ROWS)), order)[0:1]
    number = iota((SLABS, ROWS), 0).astype(F32)
    chosen = ((position == number) & (row > 0)).astype(F32)
    out_ref[2:3, 0:SLABS] = dot_rows(start, chosen)[0:1].astype(I32)
    out_ref[3:4, 0:SLABS] = dot_rows(count, chosen)[0:1].astype(I32)

    in_plane = (plane_of(iota((8, ROWS), 1)) == iota((8, ROWS), 0)).astype(F32)
    sharing = [jnp.where(dealt == number, kept, 0.0) for number in range(NX)]
    most_x = jnp.float32(0)
    for names in sharing:
        most_x = jnp.maximum(most_x, jnp.max(jnp.sum(dot_rows(names, union) * far, axis=0)))
    most_z = jnp.float32(0)
    for to in range(NZ):
        part_of = (iota((ROWS, 128), 1) // NC) % NZ == to
        wanted = dot(jnp.where(part_of, far, 0.0), union) > 0
        for names in sharing:
            need = jnp.where(wanted, names, 0.0)
            most_z = jnp.maximum(most_z, jnp.max(jnp.sum(dot(in_plane, need), axis=1)))
    fits = (most_x <= CAP_X) & (most_z <= CAP_Z)
    out_ref[4:5, :] = jnp.zeros((1, 256), I32) + fits.astype(I32)


def far_plan(position, slots, union, far, along):
    return pl.pallas_call(
        far_plan_kernel,
        out_shape=jax.ShapeDtypeStruct((8, 256), I32),
        in_specs=[smem()] + [vmem()] * 4,
        out_specs=vmem(),
        scratch_shapes=[pltpu.VMEM((ROWS, ROWS), F32)],
        compiler_params=params(),
        cost_estimate=cost(2 * 60 * ROWS**3, 8 * ROWS**2),
        name="far_plan",
    )(position, slots, union, far, along)


def dense(blocks, nonzero, columns):
    slab = lax.axis_index(ROW_AXES)
    part = lax.axis_index("col")
    masked = blocks * nonzero[:, :, None, None].astype(BF)
    slab_ids = jnp.arange(SLABS, dtype=I32)
    local_rows = jnp.arange(HEIGHT, dtype=I32)
    grouped = columns.reshape(SLABS, HEIGHT * SLOTS)
    targets = slab * HEIGHT + local_rows
    wanted = jnp.any(grouped[:, :, None] == targets[None, None, :], axis=1)
    wanted = wanted & (slab_ids != slab)[:, None]
    picked = jnp.sum(jnp.where(wanted, local_rows, 0), axis=1)
    filled = jnp.any(wanted, axis=1)
    outgoing = jnp.where(filled[:, None, None, None], masked[picked], jnp.zeros((), BF))
    incoming = lax.all_to_all(outgoing, ROW_AXES, split_axis=0, concat_axis=0, tiled=True)
    row_table = jnp.concatenate([incoming, masked], axis=0)
    own_cols = lax.dynamic_slice_in_dim(columns, slab * HEIGHT, HEIGHT, 0)
    source = own_cols // HEIGHT
    row_index = jnp.where(source == slab, SLABS + own_cols % HEIGHT, source)
    far_cols = columns[own_cols]
    far_quarter = lax.dynamic_slice_in_dim(far_cols, part * QUARTER, QUARTER, 2)
    whole = lax.all_gather(masked, "col", axis=1, tiled=True)
    results = []
    for member in range(HEIGHT):
        match = far_quarter[member][:, :, None] == own_cols[member][None, None, :]
        products = jnp.einsum(
            "tab,tubc->tuac", whole[member], row_table[row_index[member]],
            preferred_element_type=F32,
        )
        summed = lax.dot_general(
            match.astype(F32).reshape(SLOTS * QUARTER, SLOTS),
            products.reshape(SLOTS * QUARTER, SIDE * SIDE),
            (((0,), (0,)), ((), ())),
            precision=lax.Precision.HIGHEST,
            preferred_element_type=F32,
        )
        results.append(summed.reshape(SLOTS, SIDE, SIDE))
    square = lax.psum_scatter(jnp.stack(results), "col", scatter_dimension=1, tiled=True)
    return square.astype(BF)


def shards(blocks, nonzero, columns):
    position = jnp.stack([lax.axis_index(name) for name in ROW_AXES + ("col",)])
    turned, cuts = prepare(position, nonzero, blocks)
    cuts, names = lax.optimization_barrier((cuts, columns))
    slots, union, named_by = pattern(names)
    near = lax.all_to_all(cuts, ("x", "col", "core"), split_axis=0, concat_axis=0, tiled=True)
    near, turned = lax.optimization_barrier((near, turned))
    whole = lax.all_gather(turned, "col", axis=0, tiled=False)
    whole = whole.reshape(ZERO_BLOCK, SIDE, SIDE)
    near = near.reshape(NX * NC * NY * (QUARTER + 1), CUT, SIDE)
    send, notes = send_lists(position, slots, union, named_by, near)
    packed = pack(send, near, NZ, CAP_Z + 1, notes)
    packed, slots = lax.optimization_barrier((packed, slots))
    along = lax.all_to_all(packed, "z", split_axis=0, concat_axis=0, tiled=True)
    own_lists = own_plan(position, slots, union)
    packed = pack(route(along), along.reshape(-1, CUT, SIDE), NX * NC, CAP_X)
    packed, notes = lax.optimization_barrier((packed, along))
    far = lax.all_to_all(packed, ("x", "core"), split_axis=0, concat_axis=0, tiled=True)
    far = far.reshape(NX * NC * CAP_X, CUT, SIDE)
    far_lists = far_plan(position, slots, union, named_by, notes)
    result = far_sums(own_lists, far_lists, whole, far, own_sums(own_lists, whole))
    result = result.reshape(NY, HEIGHT, QUARTER, WIDE, SIDE)
    result = lax.all_to_all(result, "col", split_axis=0, concat_axis=0, tiled=True)
    square = finish(result)
    return lax.cond(
        far_lists[4, 0] != 0,
        lambda value, *_: value,
        lambda _, *inputs: dense(*inputs),
        square,
        blocks,
        nonzero,
        columns,
    )


def solution(mesh):
    fine = Mesh(mesh.devices.reshape(NX, NZ, NC, NY), ROW_AXES + ("col",))
    spec = P(ROW_AXES, "col", None, None)
    return jax.shard_map(
        shards,
        mesh=fine,
        in_specs=(spec, P(ROW_AXES, "col"), P()),
        out_specs=spec,
        check_vma=False,
    )
```

time: 720 us -> 145 us (0.20)
  waiting for transfers between devices: 390 us -> 20.8 us
  local copies, waits for them, and re-layouts: 161 us -> 5.25 us
  matrix products: 102 us -> 0 us
  blocking collectives: 0 us -> 71.5 us
  other arithmetic: 35.2 us -> 0.08 us
  Pallas kernels: 0 us -> 24.4 us
    all_to_all x1 -> x2, waiting for transfers between devices: 317 us -> 20.7 us  [the longest x1 11.6 us: shards(): lax.all_to_all(result, 'col', split_axis=0, concat_axis=0, tiled=True)]
    dot_general x8 -> x0, matrix products: 102 us -> none  [the longest x4 63.7 us: shards(): lax.dot_general(selector, flattened, dims, precision=lax.Precision.HIGHES...]
    reduce_scatter x1 -> x0, waiting for transfers between devices: 72.1 us -> none  [shards(): lax.psum_scatter(partial_value, 'col', scatter_dimension=1, tiled=True)]
    all_to_all x0 -> x2, blocking collectives: none -> 71.5 us  [the longest x1 46.2 us: shards(): along = lax.all_to_all(packed, 'z', split_axis=0, concat_axis=0, tiled=True)]
    transpose x4 -> x0, local copies, waits for them, and re-layouts: 56.9 us -> none  [shards(): jnp.einsum('tab,tubc->tuac', whole[member], gathered, preferred_element_t...]
    gather x8 -> x0, local copies, waits for them, and re-layouts: 47 us -> none  [the longest x4 38.2 us: shards(): gathered = row_table[rows_used]]
    dot_general x4 -> x0, local copies, waits for them, and re-layouts: 46.1 us -> none  [shards(): lax.dot_general(selector, flattened, dims, precision=lax.Precision.HIGHES...]
    pallas_call x0 -> x11, Pallas kernels: none -> 24.4 us  [the longest x1 5.69 us: far_sums(): pl.pallas_call(far_kernel, out_shape=jax.ShapeDtypeStruct((ZERO_BLOCK, WI...]
  transfers between devices with their start and end apart: 3 -> 3, of which waited for: 2 -> 2; matrix products, arithmetic and copies ran while one was open for 8% -> 1% of each run, Pallas kernels for 0% -> 11%
where the time goes in v1:
time: 145 us; the launch traced here: 144 us
  blocking collectives  71.5 us (49%)
  Pallas kernels  24.4 us (17%)
  waiting for transfers between devices  20.8 us (14%)
  between operations  14.1 us (10%)
  starting transfers between devices  7.54 us (5%)
  local copies, waits for them, and re-layouts  5.25 us (4%)
    all_to_all x1, blocking collectives, shards(): along = lax.all_to_all(packed, 'z', split_axis=0, concat_axis=0, tiled=True)  46.2 us
    all_to_all x1, blocking collectives, shards(): lax.all_to_all(cuts, ('x', 'col', 'core'), split_axis=0, concat_axis=0, t...  25.3 us
    all_to_all x1, waiting for transfers between devices, shards(): lax.all_to_all(result, 'col', split_axis=0, concat_axis=0, tiled=True)  11.6 us
    all_to_all x1, waiting for transfers between devices, shards(): lax.all_to_all(packed, ('x', 'core'), split_axis=0, concat_axis=0, tiled=...  9.17 us
    pallas_call x1, Pallas kernels, far_sums(): pl.pallas_call(far_kernel, out_shape=jax.ShapeDtypeStruct((ZERO_BLOCK, WI...  5.69 us
    pallas_call x1, Pallas kernels, far_plan(): pl.pallas_call(far_plan_kernel, out_shape=jax.ShapeDtypeStruct((8, 256),...  5.02 us
    all_to_all x1, starting transfers between devices, shards(): lax.all_to_all(packed, ('x', 'core'), split_axis=0, concat_axis=0, tiled=...  4.03 us
    unnamed x10, local copies, waits for them, and re-layouts  3.87 us
  transfers between devices with their start and end apart: 3, of which 2 were waited for; matrix products, arithmetic and copies ran while one was open for 1% of the time, Pallas kernels for 11%

profile of v1, /device:TPU:1, one launch (start us, length us, event | category | flops | bytes accessed | tf_op | source)
XLA Modules:
  0.0 143.9 jit_solution(13833233857500330432)
XLA Ops:
  6.5 0.0 all-gather.6.cloned.1.call-start
  6.5 0.1 pad_add_fusion.position_ref
  6.6 2.5 %prepare.1 = (bf16[4,7,128,128]{3,2,1,0:T(8,128)(2,1)}, bf16[32,8,16,128]{3,2,1,0:T(8,128)(2,1)S(1)}) custom-call(s32[4]{0:T(128)S(1)} %pad_add_fusion.position_ref, s32[4,7]{1,0:T(4,128)} %keep_ref.1, bf16[4,7,128,128]{3,2,1,0:T(8,128)(2,1)} %blocks_ref.1), custom_call_target="tpu_custom_call" | custom-call | tf_op jit(solution)/shard_map/prepare/pallas_call | solution.py:74
  9.1 25.3 %all_to_all.24 = bf16[32,8,16,128]{3,2,1,0:T(8,128)(2,1)S(1)} all-to-all(bf16[32,8,16,128]{3,2,1,0:T(8,128)(2,1)S(1)} %get-tuple-element.38), channel_id=1, replica_groups=mesh['x'=4,'z'=8,'core'=2,'col'=4] {'x','col','core'}, dimensions={0} | all-to-all | bytes 2097152 | tf_op jit(solution)/shard_map/all_to_all | solution.py:616
  34.4 0.0 all-gather.6.cloned.1.call-update
  34.4 0.9 copy.75.columns_ref
  35.3 1.6 %pattern.1 = (s32[256,256]{1,0:T(8,128)S(1)}, f32[128,256]{1,0:T(8,128)S(1)}, f32[256,128]{1,0:T(8,128)S(1)}) custom-call(s32[256,28]{1,0:T(8,128)S(1)} %copy.75.columns_ref), custom_call_target="tpu_custom_call" | custom-call | flops 234881024 | bytes 524288 | tf_op jit(solution)/shard_map/pattern/pallas_call | solution.py:353
  36.9 1.8 %send_lists.1 = (s32[1,384]{1,0:T(1,128)S(1)}, bf16[8,16,128]{2,1,0:T(8,128)(2,1)S(1)}) custom-call(s32[4]{0:T(128)S(1)} %pad_add_fusion.position_ref, s32[256,256]{1,0:T(8,128)S(1)} %get-tuple-element.43.slots_ref, f32[128,256]{1,0:T(8,128)S(1)} %get-tuple-element.36.union_ref, f32[256,128]{1,0:T(8,128)S(1)} %get-tuple-element.37.far_ref, ...), custom_call_target="tpu_custom_call" | custom-call | tf_op jit(solution)/shard_map/send_lists/pallas_call | solution.py:411
  38.7 1.3 pack.2
  40.0 46.2 %all_to_all.25.along_ref = bf16[8,45,16,128]{3,2,1,0:T(8,128)(2,1)S(1)} all-to-all(bf16[8,45,16,128]{3,2,1,0:T(8,128)(2,1)S(1)} %pack.2), channel_id=1, replica_groups=mesh['x'=4,'z'=8,'core'=2,'col'=4] {'z'}, dimensions={0} | all-to-all | bytes 2949120 | tf_op jit(solution)/shard_map/all_to_all | solution.py:624
  86.3 0.7 route.1.index_ref
  87.0 2.5 %pack.3 = bf16[8,44,16,128]{3,2,1,0:T(8,128)(2,1)} custom-call(s32[1,384]{1,0:T(1,128)S(1)} %route.1.index_ref, bf16[360,16,128]{2,1,0:T(8,128)(2,1)S(1)} %bitcast.150), custom_call_target="tpu_custom_call" | custom-call | tf_op jit(solution)/shard_map/pack/pallas_call | solution.py:104
  89.4 4.0 %all-to-all-start.3 = ((bf16[8,44,16,128]{3,2,1,0:T(8,128)(2,1)}), bf16[8,44,16,128]{3,2,1,0:T(8,128)(2,1)S(1)}, u32[]{:S(2)}, u32[]{:S(2)}) async-start(bf16[8,44,16,128]{3,2,1,0:T(8,128)(2,1)} %pack.3), calls=%async_computation.4 | async-start | bytes 2883584 | tf_op jit(solution)/shard_map/all_to_all | solution.py:628
  93.5 0.8 own_plan.1.plan_ref.own_ref
  94.3 5.0 %far_plan.1.plan_ref = s32[8,256]{1,0:T(8,128)S(1)} custom-call(s32[4]{0:T(128)S(1)} %pad_add_fusion.position_ref, s32[256,256]{1,0:T(8,128)S(1)} %get-tuple-element.43.slots_ref, f32[128,256]{1,0:T(8,128)S(1)} %get-tuple-element.36.union_ref, f32[256,128]{1,0:T(8,128)S(1)} %get-tuple-element.37.far_ref, bf16[8,45,16,128]{3,2,1,0:T(8,128)(2,1)S(1)} %all_to_all.25.along_ref), custom_call_target="tpu_custom_call" | custom-call | flops 2013265920 | bytes 524288 | tf_op jit(solution)/shard_map/far_plan/pallas_call | solution.py:559
  99.3 0.0 all-gather.6.cloned.1.call-done
  99.4 0.0 copy-start
  99.4 2.0 %copy-done = bf16[16,7,128,128]{3,2,1,0:T(8,128)(2,1)S(1)} copy-done((bf16[16,7,128,128]{3,2,1,0:T(8,128)(2,1)S(1)}, bf16[16,7,128,128]{3,2,1,0:T(8,128)(2,1)}, u32[]{:S(2)}) %copy-start) | copy-done | bytes 3670040
  101.4 0.0 copy-start.6
  101.4 0.0 copy-start.7
  101.4 2.2 %own_sums.1.near_ref = f32[112,32,128]{2,1,0:T(8,128)S(1)} custom-call(s32[16,128]{1,0:T(8,128)S(1)} %own_plan.1.plan_ref.own_ref, bf16[112,128,128]{2,1,0:T(8,128)(2,1)S(1)} %bitcast.149), custom_call_target="tpu_custom_call" | custom-call | flops 536870912 | bytes 5505024 | tf_op jit(solution)/shard_map/own_sums/pallas_call | solution.py:157
  103.6 9.2 %all-to-all-done.3 = bf16[8,44,16,128]{3,2,1,0:T(8,128)(2,1)S(1)} async-done(((bf16[8,44,16,128]{3,2,1,0:T(8,128)(2,1)}), bf16[8,44,16,128]{3,2,1,0:T(8,128)(2,1)S(1)}, u32[]{:S(2)}, u32[]{:S(2)}) %all-to-all-start.3) | async-done | bytes 1441824 | tf_op jit(solution)/shard_map/all_to_all | solution.py:628
  112.8 5.7 %far_sums.1 = bf16[112,32,128]{2,1,0:T(8,128)(2,1)S(1)} custom-call(s32[16,128]{1,0:T(8,128)S(1)} %own_plan.1.plan_ref.own_ref, s32[8,256]{1,0:T(8,128)S(1)} %far_plan.1.plan_ref, bf16[112,128,128]{2,1,0:T(8,128)(2,1)} %bitcast.148, bf16[352,16,128]{2,1,0:T(8,128)(2,1)S(1)} %bitcast.153, f32[112,32,128]{2,1,0:T(8,128)S(1)} %own_sums.1.near_ref), custom_call_target="tpu_custom_call" | custom-call | tf_op jit(solution)/shard_map/far_sums/pallas_call | solution.py:239
  118.5 0.0 copy-start.1
  118.5 0.9 copy-done.1
  119.4 3.5 %all-to-all-start.4 = ((bf16[4,4,7,32,128]{4,3,2,1,0:T(8,128)(2,1)}), bf16[4,4,7,32,128]{4,3,2,1,0:T(8,128)(2,1)S(1)}, u32[]{:S(2)}, u32[]{:S(2)}) async-start(bf16[4,4,7,32,128]{4,3,2,1,0:T(8,128)(2,1)} %bitcast.154), calls=%async_computation.5 | async-start | bytes 1835008 | tf_op jit(solution)/shard_map/all_to_all | solution.py:633
  122.9 0.5 slice.68
  124.0 11.6 %all-to-all-done.4.cuts_ref = bf16[4,4,7,32,128]{4,3,2,1,0:T(8,128)(2,1)S(1)} async-done(((bf16[4,4,7,32,128]{4,3,2,1,0:T(8,128)(2,1)}), bf16[4,4,7,32,128]{4,3,2,1,0:T(8,128)(2,1)S(1)}, u32[]{:S(2)}, u32[]{:S(2)}) %all-to-all-start.4) | async-done | bytes 917536 | tf_op jit(solution)/shard_map/all_to_all | solution.py:633
  135.6 0.3 finish.1
  135.9 0.0 copy-done.6
  135.9 0.0 copy-done.7
  135.9 0.2 conditional.1
  136.1 0.0 copy-start.5
  136.1 0.9 copy-done.5
Async XLA Ops:
  6.5 92.8 %all-gather.6.cloned.1.call-start = ((), (), s32[]{:S(2)}) async-start(), calls=%async_computation.8 | async-start | bytes 4587520 | tf_op jit(solution)/shard_map/all_gather | solution.py:618
  89.4 23.4 %all-to-all-start.3 = ((bf16[8,44,16,128]{3,2,1,0:T(8,128)(2,1)}), bf16[8,44,16,128]{3,2,1,0:T(8,128)(2,1)S(1)}, u32[]{:S(2)}, u32[]{:S(2)}) async-start(bf16[8,44,16,128]{3,2,1,0:T(8,128)(2,1)} %pack.3), calls=%async_computation.4 | async-start | bytes 2883584 | tf_op jit(solution)/shard_map/all_to_all | solution.py:628
  99.4 2.0 %copy-start = (bf16[16,7,128,128]{3,2,1,0:T(8,128)(2,1)S(1)}, bf16[16,7,128,128]{3,2,1,0:T(8,128)(2,1)}, u32[]{:S(2)}) copy-start(bf16[16,7,128,128]{3,2,1,0:T(8,128)(2,1)} %all-gather.6.cloned.1.call-done) | copy-start | bytes 11010052
  101.4 34.4 %copy-start.6 = (s32[256,28]{0,1:T(8,128)S(1)}, s32[256,28]{0,1:T(8,128)}, u32[]{:S(2)}) copy-start(s32[256,28]{0,1:T(8,128)} %param.7) | copy-start | bytes 86020
  101.4 34.5 %copy-start.7 = (s32[4,7]{1,0:T(4,128)S(1)}, s32[4,7]{1,0:T(4,128)}, u32[]{:S(2)}) copy-start(s32[4,7]{1,0:T(4,128)} %keep_ref.1) | copy-start | bytes 340
  118.5 0.9 copy-start.1
  119.4 16.1 %all-to-all-start.4 = ((bf16[4,4,7,32,128]{4,3,2,1,0:T(8,128)(2,1)}), bf16[4,4,7,32,128]{4,3,2,1,0:T(8,128)(2,1)S(1)}, u32[]{:S(2)}, u32[]{:S(2)}) async-start(bf16[4,4,7,32,128]{4,3,2,1,0:T(8,128)(2,1)} %bitcast.154), calls=%async_computation.5 | async-start | bytes 1835008 | tf_op jit(solution)/shard_map/all_to_all | solution.py:633
  136.1 0.9 copy-start.5
Sparse Core Ops, SparseCore 0:
  34.5 45.6 all-gather.5

commit v2 on v1

v2 whole, which is shorter than its diff:
```python
import functools

import jax
import jax.numpy as jnp
from jax import lax
from jax.experimental import pallas as pl
from jax.experimental.pallas import tpu as pltpu
from jax.sharding import Mesh
from jax.sharding import PartitionSpec as P

BF = jnp.bfloat16
F32 = jnp.float32
I32 = jnp.int32

NX, NZ, NC, NY = 4, 8, 2, 4
ROWS, SLOTS, SIDE = 256, 28, 128
HEIGHT, QUARTER = 4, 7
SLABS = ROWS // HEIGHT
PEERS = NX * NC * NY
HELD = 32
ENTRIES = PEERS * HELD
PIECE = SIDE * SIDE // PEERS
WIDE = SIDE // NY
TARGETS = NX * NC
CAP_Z = 124
ROWS_Z = 128
CAP_X = 120
GROUP = 8
FAR_GROUP = 4
ROWS_AT_ONCE = 4
HEIGHT_2 = NC * HEIGHT
OUT_COLS = 72
ZERO_BLOCK = NY * HEIGHT * QUARTER
VMEM_LIMIT = 48 * 1024 * 1024
ROW_AXES = ("x", "z", "core")


def vmem():
    return pl.BlockSpec(memory_space=pltpu.VMEM)


def smem():
    return pl.BlockSpec(memory_space=pltpu.SMEM)


def params():
    return pltpu.CompilerParams(vmem_limit_bytes=VMEM_LIMIT)


def cost(flops, moved):
    return pl.CostEstimate(flops=flops, bytes_accessed=moved, transcendentals=0)


def prepare_kernel(position_ref, keep_ref, blocks_ref, whole_ref, cuts_ref, rows_ref):
    x, core, part = position_ref[0], position_ref[2], position_ref[3]
    lanes = iota((8, ENTRIES), 1) - ((part * NX + x) * NC + core) * HELD
    flags = jnp.zeros((8, ENTRIES), F32)
    for row in range(HEIGHT):
        for slot in range(QUARTER):
            number = row * QUARTER + slot
            keep = keep_ref[row, slot] != 0
            flags = jnp.where((lanes == number) & keep, 1.0, flags)
            block = blocks_ref[row, slot].astype(F32)
            turned = jnp.where(keep, block, jnp.zeros_like(block)).T
            whole_ref[row, slot] = turned.astype(BF)
            for quarter in range(NY):
                for part_of in range(NY):
                    begin = quarter * WIDE + part_of * TARGETS
                    rows = pl.ds(quarter * TARGETS * HELD + number, TARGETS, stride=HELD)
                    rows_ref[part_of, rows, :] = turned[begin : begin + TARGETS]
    for begin in range(0, PEERS, 8):
        for part_of in range(NY):
            for extra in range(HELD - SLOTS):
                rows = pl.ds(begin * HELD + SLOTS + extra, 8, stride=HELD)
                at = extra * PIECE + part_of * SIDE
                value = flags[:, at : at + SIDE] if extra < 2 else jnp.zeros((8, SIDE), F32)
                rows_ref[part_of, rows, :] = value
    for peer in range(PEERS):
        rows = pl.ds(peer * HELD, HELD)
        cuts_ref[peer] = jnp.concatenate(
            [rows_ref[part_of, rows, :] for part_of in range(NY)], axis=1
        ).astype(BF)


def prepare(position, nonzero, blocks):
    return pl.pallas_call(
        prepare_kernel,
        out_shape=(
            jax.ShapeDtypeStruct((HEIGHT, QUARTER, SIDE, SIDE), BF),
            jax.ShapeDtypeStruct((PEERS, HELD, PIECE), BF),
        ),
        in_specs=[smem(), smem(), vmem()],
        out_specs=(vmem(), vmem()),
        scratch_shapes=[pltpu.VMEM((NY, ENTRIES, SIDE), F32)],
        compiler_params=params(),
        name="prepare",
    )(position, nonzero, blocks)


def own_block(whole_ref, place, rows):
    value = whole_ref[jnp.minimum(place, ZERO_BLOCK - 1), rows, :]
    return jnp.where(place < ZERO_BLOCK, value, jnp.zeros_like(value))


def out_place(place):
    return (place // QUARTER) % HEIGHT, place // (QUARTER * HEIGHT) * QUARTER + place % QUARTER


def own_kernel(
    plan_ref,
    whole_ref,
    out_ref,
    total,
    panel,
    near,
):
    first = pl.multiple_of(plan_ref[15, 0] * WIDE, WIDE)
    for inner in range(HEIGHT):
        for member in range(HEIGHT):
            panel[pl.ds(inner * SIDE, SIDE), pl.ds(member * SIDE, SIDE)] = own_block(
                whole_ref, plan_ref[9 + member, inner], pl.ds(0, SIDE)
            )

    def step(group, carry):
        for at in range(GROUP):
            for inner in range(HEIGHT):
                near[pl.ds(at * WIDE, WIDE), pl.ds(inner * SIDE, SIDE)] = own_block(
                    whole_ref, plan_ref[4 + inner, group * GROUP + at], pl.ds(first, WIDE)
                )
        value = jnp.dot(near[...], panel[...], preferred_element_type=F32)
        total[pl.ds(group * GROUP, GROUP)] = value.reshape(GROUP, WIDE, HEIGHT * SIDE)
        return carry

    lax.fori_loop(0, plan_ref[15, 1], step, 0)
    for place in range(ZERO_BLOCK):
        member, slot = out_place(place)
        column = plan_ref[8, member * (128 // HEIGHT) + slot]
        out_ref[place] = total[column, :, pl.ds(member * SIDE, SIDE)]


def own_sums(lists, whole):
    flops = 2 * 32 * WIDE * (HEIGHT * SIDE) ** 2
    return pl.pallas_call(
        own_kernel,
        out_shape=jax.ShapeDtypeStruct((ZERO_BLOCK, WIDE, SIDE), F32),
        in_specs=[smem(), vmem()],
        out_specs=vmem(),
        scratch_shapes=[
            pltpu.VMEM((OUT_COLS, WIDE, HEIGHT * SIDE), F32),
            pltpu.VMEM((HEIGHT * SIDE, HEIGHT * SIDE), BF),
            pltpu.VMEM((GROUP * WIDE, HEIGHT * SIDE), BF),
        ],
        compiler_params=params(),
        cost_estimate=cost(flops, 3 * ZERO_BLOCK * SIDE * SIDE),
        name="own_sums",
    )(lists, whole)


def far_kernel(
    own_ref,
    plan_ref,
    whole_ref,
    far_ref,
    near_ref,
    out_ref,
    total,
    pieces_ref,
):
    for sender in range(TARGETS):
        rows = pl.ds(sender * CAP_X, CAP_X)
        for part in range(NY):
            lanes = slice(part * SIDE, (part + 1) * SIDE)
            pieces_ref[part, rows, :] = far_ref[rows, lanes].astype(F32)

    def clear(group, carry):
        total[pl.ds(group * GROUP, GROUP)] = jnp.zeros((GROUP, WIDE, HEIGHT * SIDE), F32)
        return carry

    lax.fori_loop(0, own_ref[15, 1], clear, 0)

    def product(named, offset):
        begin = plan_ref[2, named]
        length = plan_ref[3, named]
        right = jnp.concatenate(
            [
                own_block(whole_ref, own_ref[member, named], pl.ds(0, SIDE))
                for member in range(HEIGHT)
            ],
            axis=1,
        )
        pieces, columns = [], []
        for at in range(FAR_GROUP):
            place = jnp.minimum(begin + offset + at, CAP_X - 1)
            rows = pl.ds(plan_ref[0, place], TARGETS, stride=CAP_X)
            for part in range(NY):
                pieces.append(pieces_ref[part, rows, :])
            columns.append(jnp.where(offset + at < length, plan_ref[1, place], OUT_COLS))
        left = jnp.concatenate(pieces, axis=0).astype(BF)
        return jnp.dot(left, right, preferred_element_type=F32), columns

    def add(value, columns):
        for at, column in enumerate(columns):
            total[column] = total[column] + value[at * WIDE : (at + 1) * WIDE]

    def first_step(step, carry):
        done = [product(step * ROWS_AT_ONCE + at, 0) for at in range(ROWS_AT_ONCE)]
        for value, columns in done:
            add(value, columns)
        return carry

    named_rows = own_ref[15, 2]
    lax.fori_loop(0, (named_rows + ROWS_AT_ONCE - 1) // ROWS_AT_ONCE, first_step, 0)

    def rest(named, carry):
        def rest_step(step, inner_carry):
            add(*product(named, step * FAR_GROUP))
            return inner_carry

        lax.fori_loop(1, (plan_ref[3, named] + FAR_GROUP - 1) // FAR_GROUP, rest_step, 0)
        return carry

    lax.fori_loop(0, named_rows, rest, 0)

    for place in range(ZERO_BLOCK):
        member, slot = out_place(place)
        column = own_ref[8, member * (128 // HEIGHT) + slot]
        value = total[column, :, pl.ds(member * SIDE, SIDE)] + near_ref[place]
        out_ref[place] = value.astype(BF)


def far_sums(own_lists, far_lists, whole, far, near):
    return pl.pallas_call(
        far_kernel,
        out_shape=jax.ShapeDtypeStruct((ZERO_BLOCK, WIDE, SIDE), BF),
        in_specs=[smem(), smem(), vmem(), vmem(), vmem()],
        out_specs=vmem(),
        scratch_shapes=[
            pltpu.VMEM((OUT_COLS + 1, WIDE, HEIGHT * SIDE), F32),
            pltpu.VMEM((NY, TARGETS * CAP_X, SIDE), F32),
        ],
        compiler_params=params(),
        name="far_sums",
    )(own_lists, far_lists, whole, far, near)


def finish_kernel(cuts_ref, out_ref):
    for row in range(HEIGHT):
        for slot in range(QUARTER):
            turned = jnp.concatenate([cuts_ref[part, row, slot] for part in range(NY)], axis=0)
            out_ref[row, slot] = turned.T


def finish(cuts):
    return pl.pallas_call(
        finish_kernel,
        out_shape=jax.ShapeDtypeStruct((HEIGHT, QUARTER, SIDE, SIDE), BF),
        in_specs=[vmem()],
        out_specs=vmem(),
        compiler_params=params(),
        name="finish",
    )(cuts)


def iota(shape, axis):
    return lax.broadcasted_iota(I32, shape, axis)


def dot(a, b):
    return jnp.dot(a.astype(BF), b.astype(BF), preferred_element_type=F32)


def dot_rows(a, b):
    return lax.dot_general(
        a.astype(BF), b.astype(BF), (((1,), (1,)), ((), ())), preferred_element_type=F32
    )


def earlier(size):
    return (iota((size, size), 0) < iota((size, size), 1)).astype(F32)


def places(need):
    order = earlier(SIDE)
    parts = []
    before = jnp.zeros((need.shape[0], 1), F32)
    for begin in range(0, need.shape[1], SIDE):
        part = need[:, begin : begin + SIDE]
        parts.append(dot(part, order) + before)
        before = before + jnp.sum(part, axis=1, keepdims=True)
    return jnp.concatenate(parts, axis=1)


def codes(need, capacity):
    place = places(need)
    return jnp.where((need > 0) & (place < capacity), place, -1.0)


def one_hot(code, rows):
    return (iota((rows, code.shape[1]), 0).astype(F32) == code).astype(F32)


def quarter_of(slot):
    return sum((slot >= bound * QUARTER).astype(I32) for bound in range(1, NY))


def pattern_kernel(position_ref, columns_ref, entries_ref, slots_ref, union_ref, need_ref, kq_ref):
    step = 64
    for begin in range(0, ROWS, step):
        column = iota((step, ROWS), 1)
        found = jnp.full((step, ROWS), -1, I32)
        for slot in range(SLOTS):
            at = columns_ref[begin : begin + step, slot : slot + 1]
            found = jnp.where(at == column, slot, found)
        slots_ref[begin : begin + step, :] = found
    names = (slots_ref[...] >= 0).astype(F32)
    mine = iota((128, ROWS), 1) // HEIGHT == iota((128, ROWS), 0)
    union = (dot(mine.astype(F32), names) > 0).astype(F32)
    union_ref[...] = union

    entry = iota((1, ENTRIES), 1)
    peer, number = entry // HELD, entry % HELD
    x, core = (peer // NC) % NX, peer % NC
    row = ((x * NZ + position_ref[1]) * NC + core) * HEIGHT + quarter_of(number)
    column = entries_ref[...]
    every = iota((ROWS, ENTRIES), 0)
    named = dot(jnp.where(mine, 0.0, union), (every == row).astype(F32))
    need_ref[...] = named * dot(union, (every == column).astype(F32))
    kind = iota((8, ENTRIES), 0)
    both = jnp.where(kind == 1, jnp.maximum(column, 0), 0)
    kq_ref[...] = jnp.where(kind == 0, row, both).astype(F32)


def pattern(position, columns, entries):
    return pl.pallas_call(
        pattern_kernel,
        out_shape=(
            jax.ShapeDtypeStruct((ROWS, ROWS), I32),
            jax.ShapeDtypeStruct((128, ROWS), F32),
            jax.ShapeDtypeStruct((128, ENTRIES), F32),
            jax.ShapeDtypeStruct((8, ENTRIES), F32),
        ),
        in_specs=[smem(), vmem(), vmem()],
        out_specs=(vmem(), vmem(), vmem(), vmem()),
        compiler_params=params(),
        cost_estimate=cost(2 * SLOTS * ROWS**3 // 4, 8 * ROWS**2),
        name="pattern",
    )(position, columns, entries)


def send_kernel(need_ref, kq_ref, near_ref, out_ref, chosen_ref):
    near = near_ref[...]
    kind = iota((8, ENTRIES), 0)
    pick = (iota((8, ENTRIES), 1) % HELD == SLOTS + kind) & (kind < 2)
    flags = dot(pick.astype(F32), near)
    flags = jnp.concatenate([flags[0:1], flags[1:2]], axis=1)
    need = need_ref[...] * flags
    slab = iota((8, 128), 1)
    plane = (slab // NC) % NZ == iota((8, 128), 0)
    wanted = (dot(plane.astype(F32), need) > 0).astype(F32)
    code = codes(wanted, CAP_Z)
    most = jnp.max(jnp.sum(wanted, axis=1, keepdims=True), axis=0, keepdims=True)
    most = jnp.broadcast_to(jnp.minimum(most, 250.0), (1, 128))
    totals = jnp.minimum(dot_rows(jnp.ones((8, ENTRIES), F32), need)[0:1], 250.0)
    for to in range(NZ):
        chosen_ref[to * ROWS_Z : (to + 1) * ROWS_Z, :] = one_hot(code[to : to + 1], ROWS_Z).astype(BF)
    packed = jnp.dot(chosen_ref[...], near, preferred_element_type=F32)
    tail = iota((16, PIECE), 0)
    kq = kq_ref[...]
    for to in range(NZ):
        target = iota((8, 128), 0)
        choice = slab == (target // NC * NZ + to) * NC + target % NC
        asked = jnp.concatenate([dot(choice.astype(F32), need), kq], axis=0)
        notes = dot_rows(asked, chosen_ref[to * ROWS_Z : (to + 1) * ROWS_Z, :])
        first = jnp.concatenate([notes[i : i + 1] for i in range(4)], axis=1)
        second = jnp.concatenate([notes[i : i + 1] for i in range(4, 8)], axis=1)
        third = jnp.concatenate([notes[8:9], notes[9:10], totals, most], axis=1)
        begin = to * ROWS_Z
        out_ref[to, 0 : ROWS_Z - 16] = packed[begin : begin + ROWS_Z - 16].astype(BF)
        value = packed[begin + ROWS_Z - 16 : begin + ROWS_Z]
        value = jnp.where(tail == 12, first, value)
        value = jnp.where(tail == 13, second, value)
        value = jnp.where(tail == 14, third, value)
        out_ref[to, ROWS_Z - 16 : ROWS_Z] = value.astype(BF)


def send(need, kq, near):
    return pl.pallas_call(
        send_kernel,
        out_shape=jax.ShapeDtypeStruct((NZ, ROWS_Z, PIECE), BF),
        in_specs=[vmem()] * 3,
        out_specs=vmem(),
        scratch_shapes=[pltpu.VMEM((NZ * ROWS_Z, ENTRIES), BF)],
        compiler_params=params(),
        name="send",
    )(need, kq, near)


def notes_of(along_ref):
    asked, third = [], []
    for plane in range(NZ):
        rows = pl.ds(plane * ROWS_Z + ROWS_Z - 16, 16)
        notes = along_ref[rows, :].astype(F32)
        asked.append(
            jnp.concatenate(
                [
                    notes[12 + i // 4 : 13 + i // 4, i % 4 * SIDE : (i % 4 + 1) * SIDE]
                    for i in range(TARGETS)
                ],
                axis=0,
            )
        )
        third.append(notes[14:15])
    return jnp.concatenate(asked, axis=1), third


def route_kernel(along_ref, out_ref, chosen_ref):
    asked, _ = notes_of(along_ref)
    code = codes(asked, CAP_X)
    for to in range(TARGETS):
        chosen_ref[to * SIDE : (to + 1) * SIDE, :] = one_hot(code[to : to + 1], SIDE).astype(BF)
    packed = jnp.dot(chosen_ref[...], along_ref[...], preferred_element_type=F32)
    for to in range(TARGETS):
        out_ref[to] = packed[to * SIDE : to * SIDE + CAP_X].astype(BF)


def route(along):
    return pl.pallas_call(
        route_kernel,
        out_shape=jax.ShapeDtypeStruct((TARGETS, CAP_X, PIECE), BF),
        in_specs=[vmem()],
        out_specs=vmem(),
        scratch_shapes=[pltpu.VMEM((TARGETS * SIDE, NZ * ROWS_Z), BF)],
        compiler_params=params(),
        name="route",
    )(along)


def own_plan_kernel(position_ref, slots_ref, union_ref, out_ref):
    x, z, core, part = (position_ref[i] for i in range(4))
    chip = x * NZ + z
    slab = chip * NC + core
    order = earlier(ROWS)
    out_ref[...] = jnp.zeros_like(out_ref)
    mine = union_ref[pl.ds(slab, 1), :]
    rank = dot(jnp.broadcast_to(mine, (8, ROWS)), order)

    both = slots_ref[pl.ds(pl.multiple_of(chip * HEIGHT_2, HEIGHT_2), HEIGHT_2), :]
    swapped = jnp.concatenate([both[HEIGHT:], both[:HEIGHT]], axis=0)
    slot = jnp.where(core == 0, both, swapped)
    quarter = quarter_of(slot)
    held = (quarter * HEIGHT + iota(slot.shape, 0)) * QUARTER + slot - quarter * QUARTER
    held = jnp.where(slot >= 0, held - ZERO_BLOCK, 0).astype(F32)

    every = iota((1, ROWS), 1)
    named = jnp.where(every // HEIGHT == slab, 0.0, mine)
    position = dot(jnp.broadcast_to(named, (8, ROWS)), order)[0:1]
    number = iota((SLABS, ROWS), 0).astype(F32)
    chosen = ((position == number) & (named > 0)).astype(F32)
    out_ref[0:4, 0:SLABS] = dot_rows(held, chosen)[0:HEIGHT].astype(I32) + ZERO_BLOCK

    number = iota((OUT_COLS, ROWS), 0).astype(F32)
    chosen = ((rank[0:1] == number) & (mine > 0)).astype(F32)
    out_ref[4:8, 0:OUT_COLS] = dot_rows(held, chosen)[0:HEIGHT].astype(I32) + ZERO_BLOCK
    wide = 128 // HEIGHT
    chosen = jnp.concatenate(
        [slot[i : i + 1] == iota((wide, ROWS), 0) for i in range(HEIGHT)], axis=0
    )
    out_ref[8:9, 0:128] = dot_rows(rank, chosen.astype(F32))[0:1].astype(I32)
    chosen = (iota((8, ROWS), 1) == iota((8, ROWS), 0) + slab * HEIGHT).astype(F32)
    out_ref[9:13, 0:8] = dot_rows(held, chosen)[0:HEIGHT].astype(I32) + ZERO_BLOCK
    groups = ((jnp.sum(mine) + (GROUP - 1)) * (1.0 / GROUP)).astype(I32)
    lane = iota((1, 128), 1)
    scalars = jnp.where(lane == 0, part, 0)
    scalars = jnp.where(lane == 1, groups, scalars)
    out_ref[15:16, :] = jnp.where(lane == 2, jnp.sum(named).astype(I32), scalars)


def own_plan(position, slots, union):
    return pl.pallas_call(
        own_plan_kernel,
        out_shape=jax.ShapeDtypeStruct((16, 128), I32),
        in_specs=[smem(), vmem(), vmem()],
        out_specs=vmem(),
        compiler_params=params(),
        cost_estimate=cost(ROWS**3, 4 * ROWS**2),
        name="own_plan",
    )(position, slots, union)


def far_plan_kernel(position_ref, union_ref, along_ref, out_ref):
    x, z, core = (position_ref[i] for i in range(3))
    slab = (x * NZ + z) * NC + core
    out_ref[...] = jnp.zeros_like(out_ref)
    asked, third = notes_of(along_ref)
    mine = iota(asked.shape, 0) == x * NC + core
    asked = jnp.sum(jnp.where(mine, asked, 0.0), axis=0, keepdims=True)
    number = jnp.sum(asked).astype(I32)
    code = codes(jnp.broadcast_to(asked, (8, asked.shape[1])), CAP_X)[0:1]
    chosen = one_hot(code, SIDE)
    row = jnp.concatenate([part[:, :SIDE] for part in third], axis=1)
    column = jnp.concatenate([part[:, SIDE : 2 * SIDE] for part in third], axis=1)
    row_down = jnp.sum(chosen * row, axis=1, keepdims=True).astype(I32)
    column_down = jnp.sum(chosen * column, axis=1, keepdims=True).astype(I32)
    row_along = dot_rows(jnp.broadcast_to(row, (8, row.shape[1])), chosen)[0:1].astype(I32)

    down, along = iota((SIDE, SIDE), 0), iota((SIDE, SIDE), 1)
    less = (row_down < row_along) | ((row_down == row_along) & (down < along))
    order = jnp.sum((less & (down < number)).astype(F32), axis=0, keepdims=True)
    ordered = ((order == down.astype(F32)) & (along < number)).astype(F32)
    position = iota((8, SIDE), 1).astype(F32)
    out_ref[0:1, 0:SIDE] = dot_rows(position, ordered)[0:1].astype(I32)
    names = union_ref[pl.ds(slab, 1), :]
    order = earlier(ROWS)
    rank = dot(jnp.broadcast_to(names, (8, ROWS)), order)
    every = iota((SIDE, ROWS), 1)
    rank = dot_rows(rank, (every == column_down).astype(F32))
    out_ref[1:2, 0:SIDE] = dot_rows(rank, ordered)[0:1].astype(I32)

    valid = iota((SIDE, ROWS), 0) < number
    count = dot(jnp.ones((8, SIDE), F32), ((every == row_down) & valid).astype(F32))
    start = jnp.minimum(dot(count, order), 250.0)
    row = jnp.where(iota((1, ROWS), 1) // HEIGHT == slab, 0.0, names)
    position = dot(jnp.broadcast_to(row, (8, ROWS)), order)[0:1]
    chosen = ((position == iota((SLABS, ROWS), 0).astype(F32)) & (row > 0)).astype(F32)
    out_ref[2:3, 0:SLABS] = dot_rows(start, chosen)[0:1].astype(I32)
    out_ref[3:4, 0:SLABS] = dot_rows(count, chosen)[0:1].astype(I32)

    third = functools.reduce(jnp.maximum, third), functools.reduce(jnp.add, third)
    most_z = jnp.max(third[0][:, 3 * SIDE :])
    most_x = jnp.max(third[1][:, 2 * SIDE : 3 * SIDE])
    fits = (most_x <= CAP_X) & (most_z <= CAP_Z)
    out_ref[4:5, :] = jnp.zeros((1, SIDE), I32) + fits.astype(I32)


def far_plan(position, union, along):
    return pl.pallas_call(
        far_plan_kernel,
        out_shape=jax.ShapeDtypeStruct((8, 128), I32),
        in_specs=[smem(), vmem(), vmem()],
        out_specs=vmem(),
        compiler_params=params(),
        cost_estimate=cost(2 * 20 * ROWS**3, 8 * ROWS**2),
        name="far_plan",
    )(position, union, along)


def dense(blocks, nonzero, columns):
    slab = lax.axis_index(ROW_AXES)
    part = lax.axis_index("col")
    masked = blocks * nonzero[:, :, None, None].astype(BF)
    slab_ids = jnp.arange(SLABS, dtype=I32)
    local_rows = jnp.arange(HEIGHT, dtype=I32)
    grouped = columns.reshape(SLABS, HEIGHT * SLOTS)
    targets = slab * HEIGHT + local_rows
    wanted = jnp.any(grouped[:, :, None] == targets[None, None, :], axis=1)
    wanted = wanted & (slab_ids != slab)[:, None]
    picked = jnp.sum(jnp.where(wanted, local_rows, 0), axis=1)
    filled = jnp.any(wanted, axis=1)
    outgoing = jnp.where(filled[:, None, None, None], masked[picked], jnp.zeros((), BF))
    incoming = lax.all_to_all(outgoing, ROW_AXES, split_axis=0, concat_axis=0, tiled=True)
    row_table = jnp.concatenate([incoming, masked], axis=0)
    own_cols = lax.dynamic_slice_in_dim(columns, slab * HEIGHT, HEIGHT, 0)
    source = own_cols // HEIGHT
    row_index = jnp.where(source == slab, SLABS + own_cols % HEIGHT, source)
    far_cols = columns[own_cols]
    far_quarter = lax.dynamic_slice_in_dim(far_cols, part * QUARTER, QUARTER, 2)
    whole = lax.all_gather(masked, "col", axis=1, tiled=True)
    results = []
    for member in range(HEIGHT):
        match = far_quarter[member][:, :, None] == own_cols[member][None, None, :]
        products = jnp.einsum(
            "tab,tubc->tuac", whole[member], row_table[row_index[member]],
            preferred_element_type=F32,
        )
        summed = lax.dot_general(
            match.astype(F32).reshape(SLOTS * QUARTER, SLOTS),
            products.reshape(SLOTS * QUARTER, SIDE * SIDE),
            (((0,), (0,)), ((), ())),
            precision=lax.Precision.HIGHEST,
            preferred_element_type=F32,
        )
        results.append(summed.reshape(SLOTS, SIDE, SIDE))
    square = lax.psum_scatter(jnp.stack(results), "col", scatter_dimension=1, tiled=True)
    return square.astype(BF)


def plane_columns(columns):
    split = columns.reshape(NX, NZ, NC, HEIGHT, NY, QUARTER)
    mine = lax.dynamic_index_in_dim(split, lax.axis_index("z"), 1, keepdims=False)
    mine = mine.transpose(3, 0, 1, 2, 4).reshape(PEERS, SLOTS)
    return jnp.pad(mine, ((0, 0), (0, HELD - SLOTS)), constant_values=-1).reshape(1, ENTRIES)


def shards(blocks, nonzero, columns):
    position = jnp.stack([lax.axis_index(name) for name in ROW_AXES + ("col",)])
    turned, cuts = prepare(position, nonzero, blocks)
    cuts, names = lax.optimization_barrier((cuts, columns))
    slots, union, need, kq = pattern(position, names, plane_columns(columns))
    near = lax.all_to_all(cuts, ("col", "x", "core"), split_axis=0, concat_axis=0, tiled=True)
    near, turned, need = lax.optimization_barrier((near, turned, need))
    whole = lax.all_gather(turned, "col", axis=0, tiled=False)
    whole = whole.reshape(ZERO_BLOCK, SIDE, SIDE)
    packed = send(need, kq, near.reshape(ENTRIES, PIECE))
    packed, slots = lax.optimization_barrier((packed, slots))
    along = lax.all_to_all(packed, "z", split_axis=0, concat_axis=0, tiled=True)
    along = along.reshape(NZ * ROWS_Z, PIECE)
    own_lists = own_plan(position, slots, union)
    packed, notes = lax.optimization_barrier((route(along), along))
    far = lax.all_to_all(packed, ("x", "core"), split_axis=0, concat_axis=0, tiled=True)
    far_lists = far_plan(position, union, notes)
    far = far.reshape(TARGETS * CAP_X, PIECE)
    far, fits = lax.optimization_barrier((far, far_lists[4, 0] != 0))
    result = far_sums(own_lists, far_lists, whole, far, own_sums(own_lists, whole))
    result = result.reshape(NY, HEIGHT, QUARTER, WIDE, SIDE)
    result = lax.all_to_all(result, "col", split_axis=0, concat_axis=0, tiled=True)
    square = finish(result)
    return lax.cond(
        fits,
        lambda value, *_: value,
        lambda _, *inputs: dense(*inputs),
        square,
        blocks,
        nonzero,
        columns,
    )


def solution(mesh):
    fine = Mesh(mesh.devices.reshape(NX, NZ, NC, NY), ROW_AXES + ("col",))
    spec = P(ROW_AXES, "col", None, None)
    return jax.shard_map(
        shards,
        mesh=fine,
        in_specs=(spec, P(ROW_AXES, "col"), P()),
        out_specs=spec,
        check_vma=False,
    )
```

time: 145 us -> 134 us (0.924)
  blocking collectives: 71.5 us -> 35.8 us
  waiting for transfers between devices: 20.8 us -> 36.5 us
  starting transfers between devices: 7.54 us -> 17.5 us
    all_to_all x1 -> x0, blocking collectives: 25.3 us -> none  [shards(): lax.all_to_all(cuts, ('x', 'col', 'core'), split_axis=0, concat_axis=0, t...]
    all_to_all x0 -> x1, waiting for transfers between devices: none -> 12.4 us  [shards(): lax.all_to_all(cuts, ('col', 'x', 'core'), split_axis=0, concat_axis=0, t...]
    all_to_all x1, blocking collectives: 46.2 us -> 35.8 us  [shards(): along = lax.all_to_all(packed, 'z', split_axis=0, concat_axis=0, tiled=True)]
    all_to_all x0 -> x1, starting transfers between devices: none -> 8.59 us  [shards(): lax.all_to_all(cuts, ('col', 'x', 'core'), split_axis=0, concat_axis=0, t...]
    pallas_call x5 -> x3, Pallas kernels: 11.3 us -> 6.55 us  [the longest x1 2.68 us: send(): pl.pallas_call(send_kernel, out_shape=jax.ShapeDtypeStruct((NZ, ROWS_Z, P...]
    all_to_all x1, waiting for transfers between devices: 11.6 us -> 13.3 us  [shards(): lax.all_to_all(result, 'col', split_axis=0, concat_axis=0, tiled=True)]
    all_to_all x1, waiting for transfers between devices: 9.17 us -> 10.9 us  [shards(): lax.all_to_all(packed, ('x', 'core'), split_axis=0, concat_axis=0, tiled=...]
    pallas_call x1, Pallas kernels: 2.48 us -> 4.06 us  [prepare(): pl.pallas_call(prepare_kernel, out_shape=(jax.ShapeDtypeStruct((HEIGHT, Q...]
  transfers between devices with their start and end apart: 3 -> 4, of which waited for: 2 -> 3; matrix products, arithmetic and copies ran while one was open for 1% -> 2% of each run, Pallas kernels for 11% -> 5%
where the time goes in v2:
time: 134 us; the launch traced here: 133 us
  waiting for transfers between devices  36.5 us (27%)
  blocking collectives  35.8 us (27%)
  Pallas kernels  24.5 us (18%)
  starting transfers between devices  17.5 us (13%)
  between operations  14.1 us (11%)
  local copies, waits for them, and re-layouts  4.81 us (4%)
    all_to_all x1, blocking collectives, shards(): along = lax.all_to_all(packed, 'z', split_axis=0, concat_axis=0, tiled=True)  35.8 us
    all_to_all x1, waiting for transfers between devices, shards(): lax.all_to_all(result, 'col', split_axis=0, concat_axis=0, tiled=True)  13.3 us
    all_to_all x1, waiting for transfers between devices, shards(): lax.all_to_all(cuts, ('col', 'x', 'core'), split_axis=0, concat_axis=0, t...  12.4 us
    all_to_all x1, waiting for transfers between devices, shards(): lax.all_to_all(packed, ('x', 'core'), split_axis=0, concat_axis=0, tiled=...  10.9 us
    all_to_all x1, starting transfers between devices, shards(): lax.all_to_all(cuts, ('col', 'x', 'core'), split_axis=0, concat_axis=0, t...  8.59 us
    pallas_call x1, Pallas kernels, far_sums(): pl.pallas_call(far_kernel, out_shape=jax.ShapeDtypeStruct((ZERO_BLOCK, WI...  7.08 us
    all_to_all x1, starting transfers between devices, shards(): lax.all_to_all(packed, ('x', 'core'), split_axis=0, concat_axis=0, tiled=...  5.33 us
    pallas_call x1, Pallas kernels, prepare(): pl.pallas_call(prepare_kernel, out_shape=(jax.ShapeDtypeStruct((HEIGHT, Q...  4.06 us
  transfers between devices with their start and end apart: 4, of which 3 were waited for; matrix products, arithmetic and copies ran while one was open for 2% of the time, Pallas kernels for 5%

profile of v2, /device:TPU:1, one launch (start us, length us, event | category | flops | bytes accessed | tf_op | source)
XLA Modules:
  0.0 133.2 jit_solution(3168105377138120507)
XLA Ops:
  6.5 0.1 pad_add_fusion.position_ref
  6.6 4.1 %prepare.1 = (bf16[4,7,128,128]{3,2,1,0:T(8,128)(2,1)}, bf16[32,32,512]{2,1,0:T(8,128)(2,1)}) custom-call(s32[4]{0:T(128)S(1)} %pad_add_fusion.position_ref, s32[4,7]{1,0:T(4,128)} %keep_ref.1, bf16[4,7,128,128]{3,2,1,0:T(8,128)(2,1)} %blocks_ref.1), custom_call_target="tpu_custom_call" | custom-call | tf_op jit(solution)/shard_map/prepare/pallas_call | solution.py:86
  10.7 8.6 %all-to-all-start.1 = ((bf16[32,32,512]{2,1,0:T(8,128)(2,1)}), bf16[32,32,512]{2,1,0:T(8,128)(2,1)S(1)}, u32[]{:S(2)}, u32[]{:S(2)}) async-start(bf16[32,32,512]{2,1,0:T(8,128)(2,1)} %get-tuple-element.36), calls=%async_computation.2 | async-start | bytes 2097152 | tf_op jit(solution)/shard_map/all_to_all | solution.py:599
  19.3 0.0 all-gather.6.cloned.1.call-start
  19.3 0.9 copy.101
  20.2 0.3 reshape.220
  20.5 0.1 reshape.221
  20.6 0.1 reshape.222.entries_ref
  20.7 0.9 copy.103.columns_ref
  21.6 2.5 %pattern.1 = (s32[256,256]{1,0:T(8,128)S(1)}, f32[128,256]{1,0:T(8,128)S(1)}, f32[128,1024]{1,0:T(8,128)S(1)}, f32[8,1024]{1,0:T(8,128)S(1)}) custom-call(s32[4]{0:T(128)S(1)} %pad_add_fusion.position_ref, s32[256,28]{1,0:T(8,128)S(1)} %copy.103.columns_ref, s32[1,1024]{1,0:T(1,128)S(1)} %reshape.222.entries_ref), custom_call_target="tpu_custom_call" | custom-call | flops 234881024 | bytes 524288 | tf_op jit(solution)/shard_map/pattern/pallas_call | solution.py:334
  24.1 12.4 %all-to-all-done.1 = bf16[32,32,512]{2,1,0:T(8,128)(2,1)S(1)} async-done(((bf16[32,32,512]{2,1,0:T(8,128)(2,1)}), bf16[32,32,512]{2,1,0:T(8,128)(2,1)S(1)}, u32[]{:S(2)}, u32[]{:S(2)}) %all-to-all-start.1) | async-done | bytes 1048608 | tf_op jit(solution)/shard_map/all_to_all | solution.py:599
  36.4 0.0 all-gather.6.cloned.1.call-update
  36.5 0.0 copy-start.4
  36.5 0.0 copy-start.5
  36.5 0.0 copy-start.6
  36.5 2.7 %send.1 = bf16[8,128,512]{2,1,0:T(8,128)(2,1)S(1)} custom-call(f32[128,1024]{1,0:T(8,128)S(1)} %get-tuple-element.40.need_ref, f32[8,1024]{1,0:T(8,128)S(1)} %get-tuple-element.41.kq_ref, bf16[1024,512]{1,0:T(8,128)(2,1)S(1)} %bitcast.156), custom_call_target="tpu_custom_call" | custom-call | tf_op jit(solution)/shard_map/send/pallas_call | solution.py:387
  39.2 35.8 %all_to_all.24 = bf16[8,128,512]{2,1,0:T(8,128)(2,1)S(1)} all-to-all(bf16[8,128,512]{2,1,0:T(8,128)(2,1)S(1)} %send.1), channel_id=1, replica_groups=mesh['x'=4,'z'=8,'core'=2,'col'=4] {'z'}, dimensions={0} | all-to-all | bytes 2097152 | tf_op jit(solution)/shard_map/all_to_all | solution.py:605
  75.0 2.3 %route.1 = bf16[8,120,512]{2,1,0:T(8,128)(2,1)} custom-call(bf16[1024,512]{1,0:T(8,128)(2,1)S(1)} %bitcast.154), custom_call_target="tpu_custom_call" | custom-call | tf_op jit(solution)/shard_map/route/pallas_call | solution.py:427
  77.3 5.3 %all-to-all-start.3 = ((bf16[8,120,512]{2,1,0:T(8,128)(2,1)}), bf16[8,120,512]{2,1,0:T(8,128)(2,1)S(1)}, u32[]{:S(2)}, u32[]{:S(2)}) async-start(bf16[8,120,512]{2,1,0:T(8,128)(2,1)} %route.1), calls=%async_computation.4 | async-start | bytes 1966080 | tf_op jit(solution)/shard_map/all_to_all | solution.py:609
  82.6 0.8 own_plan.1.plan_ref.own_ref
  83.5 1.6 %far_plan.1.plan_ref = s32[8,128]{1,0:T(8,128)S(1)} custom-call(s32[4]{0:T(128)S(1)} %pad_add_fusion.position_ref, f32[128,256]{1,0:T(8,128)S(1)} %get-tuple-element.46.union_ref, bf16[1024,512]{1,0:T(8,128)(2,1)S(1)} %bitcast.155), custom_call_target="tpu_custom_call" | custom-call | flops 671088640 | bytes 524288 | tf_op jit(solution)/shard_map/far_plan/pallas_call | solution.py:536
  85.0 0.5 slice.51
  86.2 10.9 %all-to-all-done.3 = bf16[8,120,512]{2,1,0:T(8,128)(2,1)S(1)} async-done(((bf16[8,120,512]{2,1,0:T(8,128)(2,1)}), bf16[8,120,512]{2,1,0:T(8,128)(2,1)S(1)}, u32[]{:S(2)}, u32[]{:S(2)}) %all-to-all-start.3) | async-done | bytes 983072 | tf_op jit(solution)/shard_map/all_to_all | solution.py:609
  97.1 0.0 all-gather.6.cloned.1.call-done
  97.1 0.0 copy-start
  97.1 2.0 %copy-done = bf16[16,7,128,128]{3,2,1,0:T(8,128)(2,1)S(1)} copy-done((bf16[16,7,128,128]{3,2,1,0:T(8,128)(2,1)S(1)}, bf16[16,7,128,128]{3,2,1,0:T(8,128)(2,1)}, u32[]{:S(2)}) %copy-start) | copy-done | bytes 3670040
  99.1 2.2 %own_sums.1.near_ref = f32[112,32,128]{2,1,0:T(8,128)S(1)} custom-call(s32[16,128]{1,0:T(8,128)S(1)} %own_plan.1.plan_ref.own_ref, bf16[112,128,128]{2,1,0:T(8,128)(2,1)S(1)} %bitcast.153), custom_call_target="tpu_custom_call" | custom-call | flops 536870912 | bytes 5505024 | tf_op jit(solution)/shard_map/own_sums/pallas_call | solution.py:143
  101.3 7.1 %far_sums.1 = bf16[112,32,128]{2,1,0:T(8,128)(2,1)} custom-call(s32[16,128]{1,0:T(8,128)S(1)} %own_plan.1.plan_ref.own_ref, s32[8,128]{1,0:T(8,128)S(1)} %far_plan.1.plan_ref, bf16[112,128,128]{2,1,0:T(8,128)(2,1)} %bitcast.152, bf16[960,512]{1,0:T(8,128)(2,1)S(1)} %bitcast.157, f32[112,32,128]{2,1,0:T(8,128)S(1)} %own_sums.1.near_ref), custom_call_target="tpu_custom_call" | custom-call | tf_op jit(solution)/shard_map/far_sums/pallas_call | solution.py:232
  108.4 3.5 %all-to-all-start.4 = ((bf16[4,4,7,32,128]{4,3,2,1,0:T(8,128)(2,1)}), bf16[4,4,7,32,128]{4,3,2,1,0:T(8,128)(2,1)S(1)}, u32[]{:S(2)}, u32[]{:S(2)}) async-start(bf16[4,4,7,32,128]{4,3,2,1,0:T(8,128)(2,1)} %bitcast.53), calls=%async_computation.5 | async-start | bytes 1835008 | tf_op jit(solution)/shard_map/all_to_all | solution.py:615
  111.9 13.3 %all-to-all-done.4.cuts_ref = bf16[4,4,7,32,128]{4,3,2,1,0:T(8,128)(2,1)S(1)} async-done(((bf16[4,4,7,32,128]{4,3,2,1,0:T(8,128)(2,1)}), bf16[4,4,7,32,128]{4,3,2,1,0:T(8,128)(2,1)S(1)}, u32[]{:S(2)}, u32[]{:S(2)}) %all-to-all-start.4) | async-done | bytes 917536 | tf_op jit(solution)/shard_map/all_to_all | solution.py:615
  125.2 0.0 copy-done.4
  125.2 0.0 copy-done.5
  125.2 0.0 copy-done.6
  125.2 1.2 finish.1
  (4 shorter events, 0.0 us)
Async XLA Ops:
  10.7 25.8 %all-to-all-start.1 = ((bf16[32,32,512]{2,1,0:T(8,128)(2,1)}), bf16[32,32,512]{2,1,0:T(8,128)(2,1)S(1)}, u32[]{:S(2)}, u32[]{:S(2)}) async-start(bf16[32,32,512]{2,1,0:T(8,128)(2,1)} %get-tuple-element.36), calls=%async_computation.2 | async-start | bytes 2097152 | tf_op jit(solution)/shard_map/all_to_all | solution.py:599
  19.3 77.8 %all-gather.6.cloned.1.call-start = ((), (), s32[]{:S(2)}) async-start(), calls=%async_computation.8 | async-start | bytes 4587520 | tf_op jit(solution)/shard_map/all_gather | solution.py:601
  36.5 88.7 %copy-start.4 = (bf16[4,7,128,128]{3,2,1,0:T(8,128)(2,1)S(1)}, bf16[4,7,128,128]{3,2,1,0:T(8,128)(2,1)}, u32[]{:S(2)}) copy-start(bf16[4,7,128,128]{3,2,1,0:T(8,128)(2,1)} %blocks_ref.1) | copy-start | bytes 2752516
  36.5 88.7 %copy-start.5 = (s32[256,28]{0,1:T(8,128)S(1)}, s32[256,28]{0,1:T(8,128)}, u32[]{:S(2)}) copy-start(s32[256,28]{0,1:T(8,128)} %param.7) | copy-start | bytes 86020
  36.5 88.7 %copy-start.6 = (s32[4,7]{1,0:T(4,128)S(1)}, s32[4,7]{1,0:T(4,128)}, u32[]{:S(2)}) copy-start(s32[4,7]{1,0:T(4,128)} %keep_ref.1) | copy-start | bytes 340
  77.3 19.7 %all-to-all-start.3 = ((bf16[8,120,512]{2,1,0:T(8,128)(2,1)}), bf16[8,120,512]{2,1,0:T(8,128)(2,1)S(1)}, u32[]{:S(2)}, u32[]{:S(2)}) async-start(bf16[8,120,512]{2,1,0:T(8,128)(2,1)} %route.1), calls=%async_computation.4 | async-start | bytes 1966080 | tf_op jit(solution)/shard_map/all_to_all | solution.py:609
  97.1 2.0 %copy-start = (bf16[16,7,128,128]{3,2,1,0:T(8,128)(2,1)S(1)}, bf16[16,7,128,128]{3,2,1,0:T(8,128)(2,1)}, u32[]{:S(2)}) copy-start(bf16[16,7,128,128]{3,2,1,0:T(8,128)(2,1)} %all-gather.6.cloned.1.call-done) | copy-start | bytes 11010052
  108.4 16.8 %all-to-all-start.4 = ((bf16[4,4,7,32,128]{4,3,2,1,0:T(8,128)(2,1)}), bf16[4,4,7,32,128]{4,3,2,1,0:T(8,128)(2,1)S(1)}, u32[]{:S(2)}, u32[]{:S(2)}) async-start(bf16[4,4,7,32,128]{4,3,2,1,0:T(8,128)(2,1)} %bitcast.53), calls=%async_computation.5 | async-start | bytes 1835008 | tf_op jit(solution)/shard_map/all_to_all | solution.py:615
Sparse Core Ops, SparseCore 0:
  36.6 45.4 all-gather.5

commit v3 on v2

--- a/solution.py
+++ b/solution.py
@@ -51,7 +51,7 @@
     return pl.CostEstimate(flops=flops, bytes_accessed=moved, transcendentals=0)
 
 
-def prepare_kernel(position_ref, keep_ref, blocks_ref, whole_ref, cuts_ref, rows_ref):
+def prepare_kernel(position_ref, keep_ref, blocks_ref, cuts_ref, rows_ref):
     x, core, part = position_ref[0], position_ref[2], position_ref[3]
     lanes = iota((8, ENTRIES), 1) - ((part * NX + x) * NC + core) * HELD
     flags = jnp.zeros((8, ENTRIES), F32)
@@ -62,7 +62,6 @@
             flags = jnp.where((lanes == number) & keep, 1.0, flags)
             block = blocks_ref[row, slot].astype(F32)
             turned = jnp.where(keep, block, jnp.zeros_like(block)).T
-            whole_ref[row, slot] = turned.astype(BF)
             for quarter in range(NY):
                 for part_of in range(NY):
                     begin = quarter * WIDE + part_of * TARGETS
@@ -85,16 +84,34 @@
 def prepare(position, nonzero, blocks):
     return pl.pallas_call(
         prepare_kernel,
-        out_shape=(
-            jax.ShapeDtypeStruct((HEIGHT, QUARTER, SIDE, SIDE), BF),
-            jax.ShapeDtypeStruct((PEERS, HELD, PIECE), BF),
-        ),
+        out_shape=jax.ShapeDtypeStruct((PEERS, HELD, PIECE), BF),
         in_specs=[smem(), smem(), vmem()],
-        out_specs=(vmem(), vmem()),
+        out_specs=vmem(),
         scratch_shapes=[pltpu.VMEM((NY, ENTRIES, SIDE), F32)],
         compiler_params=params(),
         name="prepare",
     )(position, nonzero, blocks)
+
+
+def turn_kernel(keep_ref, blocks_ref, out_ref):
+    for row in range(HEIGHT):
+        for slot in range(QUARTER):
+            block = blocks_ref[row, slot]
+            out_ref[row, slot] = jnp.where(
+                keep_ref[row, slot] != 0, block, jnp.zeros_like(block)
+            ).T
+
+
+def turn(nonzero, blocks):
+    return pl.pallas_call(
+        turn_kernel,
+        out_shape=jax.ShapeDtypeStruct((HEIGHT, QUARTER, SIDE, SIDE), BF),
+        in_specs=[smem(), vmem()],
+        out_specs=vmem(),
+        compiler_params=params(),
+        cost_estimate=cost(2 * SLOTS * SIDE**3, 4 * SLOTS * SIDE**2),
+        name="turn",
+    )(nonzero, blocks)
 
 
 def own_block(whole_ref, place, rows):
@@ -593,8 +610,9 @@
 
 def shards(blocks, nonzero, columns):
     position = jnp.stack([lax.axis_index(name) for name in ROW_AXES + ("col",)])
-    turned, cuts = prepare(position, nonzero, blocks)
-    cuts, names = lax.optimization_barrier((cuts, columns))
+    cuts = prepare(position, nonzero, blocks)
+    cuts, names, same = lax.optimization_barrier((cuts, columns, blocks))
+    turned = turn(nonzero, same)
     slots, union, need, kq = pattern(position, names, plane_columns(columns))
     near = lax.all_to_all(cuts, ("col", "x", "core"), split_axis=0, concat_axis=0, tiled=True)
     near, turned, need = lax.optimization_barrier((near, turned, need))
@@ -609,8 +627,9 @@
     far = lax.all_to_all(packed, ("x", "core"), split_axis=0, concat_axis=0, tiled=True)
     far_lists = far_plan(position, union, notes)
     far = far.reshape(TARGETS * CAP_X, PIECE)
-    far, fits = lax.optimization_barrier((far, far_lists[4, 0] != 0))
-    result = far_sums(own_lists, far_lists, whole, far, own_sums(own_lists, whole))
+    own = own_sums(own_lists, whole)
+    far, fits, own = lax.optimization_barrier((far, far_lists[4, 0] != 0, own))
+    result = far_sums(own_lists, far_lists, whole, far, own)
     result = result.reshape(NY, HEIGHT, QUARTER, WIDE, SIDE)
     result = lax.all_to_all(result, "col", split_axis=0, concat_axis=0, tiled=True)
     square = finish(result)

time: 134 us -> 130 us (0.970)
  waiting for transfers between devices: 36.5 us -> 29.3 us
  local copies, waits for them, and re-layouts: 4.81 us -> 6.63 us
    all_to_all x1, waiting for transfers between devices: 10.9 us -> 6.57 us  [shards(): lax.all_to_all(packed, ('x', 'core'), split_axis=0, concat_axis=0, tiled=...]
    all_to_all x1, waiting for transfers between devices: 12.4 us -> 9.97 us  [shards(): lax.all_to_all(cuts, ('col', 'x', 'core'), split_axis=0, concat_axis=0, t...]
    pallas_call x1 -> x2, Pallas kernels: 4.06 us -> 6.18 us  [the longest x1 3.77 us: prepare(): pl.pallas_call(prepare_kernel, out_shape=jax.ShapeDtypeStruct((PEERS, HEL...]
    unnamed x9 -> x11, local copies, waits for them, and re-layouts: 2.92 us -> 4.75 us
  transfers between devices with their start and end apart: 4 -> 4, of which waited for: 3 -> 3; matrix products, arithmetic and copies ran while one was open for 2% -> 2% of each run, Pallas kernels for 5% -> 9%
where the time goes in v3:
time: 130 us; the launch traced here: 129 us
  blocking collectives  35.8 us (28%)
  waiting for transfers between devices  29.3 us (23%)
  Pallas kernels  24.9 us (19%)
  starting transfers between devices  17.5 us (13%)
  between operations  14.2 us (11%)
  local copies, waits for them, and re-layouts  6.63 us (5%)
    all_to_all x1, blocking collectives, shards(): along = lax.all_to_all(packed, 'z', split_axis=0, concat_axis=0, tiled=True)  35.8 us
    all_to_all x1, waiting for transfers between devices, shards(): lax.all_to_all(result, 'col', split_axis=0, concat_axis=0, tiled=True)  12.7 us
    all_to_all x1, waiting for transfers between devices, shards(): lax.all_to_all(cuts, ('col', 'x', 'core'), split_axis=0, concat_axis=0, t...  9.97 us
    all_to_all x1, starting transfers between devices, shards(): lax.all_to_all(cuts, ('col', 'x', 'core'), split_axis=0, concat_axis=0, t...  8.59 us
    all_to_all x1, waiting for transfers between devices, shards(): lax.all_to_all(packed, ('x', 'core'), split_axis=0, concat_axis=0, tiled=...  6.57 us
    pallas_call x1, Pallas kernels, far_sums(): pl.pallas_call(far_kernel, out_shape=jax.ShapeDtypeStruct((ZERO_BLOCK, WI...  6.35 us
    all_to_all x1, starting transfers between devices, shards(): lax.all_to_all(packed, ('x', 'core'), split_axis=0, concat_axis=0, tiled=...  5.33 us
    unnamed x11, local copies, waits for them, and re-layouts  4.75 us
  transfers between devices with their start and end apart: 4, of which 3 were waited for; matrix products, arithmetic and copies ran while one was open for 2% of the time, Pallas kernels for 9%

profile of v3, /device:TPU:1, one launch (start us, length us, event | category | flops | bytes accessed | tf_op | source)
XLA Modules:
  0.0 128.5 jit_solution(4454265481548954603)
XLA Ops:
  6.5 0.1 pad_add_fusion.position_ref
  6.6 3.8 %prepare.1 = bf16[32,32,512]{2,1,0:T(8,128)(2,1)} custom-call(s32[4]{0:T(128)S(1)} %pad_add_fusion.position_ref, s32[4,7]{1,0:T(4,128)} %keep_ref.3, bf16[4,7,128,128]{3,2,1,0:T(8,128)(2,1)} %blocks_ref.2), custom_call_target="tpu_custom_call" | custom-call | tf_op jit(solution)/shard_map/prepare/pallas_call | solution.py:85
  10.4 8.6 %all-to-all-start.1 = ((bf16[32,32,512]{2,1,0:T(8,128)(2,1)}), bf16[32,32,512]{2,1,0:T(8,128)(2,1)S(1)}, u32[]{:S(2)}, u32[]{:S(2)}) async-start(bf16[32,32,512]{2,1,0:T(8,128)(2,1)} %prepare.1), calls=%async_computation.2 | async-start | bytes 2097152 | tf_op jit(solution)/shard_map/all_to_all | solution.py:617
  19.0 0.0 all-gather.6.cloned.1.call-start
  19.0 0.9 copy.101
  19.9 0.3 reshape.220
  20.2 0.1 reshape.221
  20.3 0.1 reshape.222.entries_ref
  20.4 0.9 copy.103.columns_ref
  21.3 2.4 %turn.1 = bf16[4,7,128,128]{3,2,1,0:T(8,128)(2,1)} custom-call(s32[4,7]{1,0:T(4,128)} %keep_ref.3, bf16[4,7,128,128]{3,2,1,0:T(8,128)(2,1)} %blocks_ref.2), custom_call_target="tpu_custom_call" | custom-call | flops 117440512 | bytes 1835008 | tf_op jit(solution)/shard_map/turn/pallas_call | solution.py:106
  23.7 2.5 %pattern.1 = (s32[256,256]{1,0:T(8,128)S(1)}, f32[128,256]{1,0:T(8,128)S(1)}, f32[128,1024]{1,0:T(8,128)S(1)}, f32[8,1024]{1,0:T(8,128)S(1)}) custom-call(s32[4]{0:T(128)S(1)} %pad_add_fusion.position_ref, s32[256,28]{1,0:T(8,128)S(1)} %copy.103.columns_ref, s32[1,1024]{1,0:T(1,128)S(1)} %reshape.222.entries_ref), custom_call_target="tpu_custom_call" | custom-call | flops 234881024 | bytes 524288 | tf_op jit(solution)/shard_map/pattern/pallas_call | solution.py:351
  26.2 10.0 %all-to-all-done.1 = bf16[32,32,512]{2,1,0:T(8,128)(2,1)S(1)} async-done(((bf16[32,32,512]{2,1,0:T(8,128)(2,1)}), bf16[32,32,512]{2,1,0:T(8,128)(2,1)S(1)}, u32[]{:S(2)}, u32[]{:S(2)}) %all-to-all-start.1) | async-done | bytes 1048608 | tf_op jit(solution)/shard_map/all_to_all | solution.py:617
  36.2 0.0 all-gather.6.cloned.1.call-update
  36.2 0.0 copy-start.6
  36.2 0.0 copy-start.7
  36.2 2.7 %send.1 = bf16[8,128,512]{2,1,0:T(8,128)(2,1)S(1)} custom-call(f32[128,1024]{1,0:T(8,128)S(1)} %get-tuple-element.39.need_ref, f32[8,1024]{1,0:T(8,128)S(1)} %get-tuple-element.40.kq_ref, bf16[1024,512]{1,0:T(8,128)(2,1)S(1)} %bitcast.156), custom_call_target="tpu_custom_call" | custom-call | tf_op jit(solution)/shard_map/send/pallas_call | solution.py:404
  38.9 35.8 %all_to_all.24 = bf16[8,128,512]{2,1,0:T(8,128)(2,1)S(1)} all-to-all(bf16[8,128,512]{2,1,0:T(8,128)(2,1)S(1)} %send.1), channel_id=1, replica_groups=mesh['x'=4,'z'=8,'core'=2,'col'=4] {'z'}, dimensions={0} | all-to-all | bytes 2097152 | tf_op jit(solution)/shard_map/all_to_all | solution.py:623
  74.7 2.3 %route.1 = bf16[8,120,512]{2,1,0:T(8,128)(2,1)} custom-call(bf16[1024,512]{1,0:T(8,128)(2,1)S(1)} %bitcast.154), custom_call_target="tpu_custom_call" | custom-call | tf_op jit(solution)/shard_map/route/pallas_call | solution.py:444
  77.0 5.3 %all-to-all-start.3 = ((bf16[8,120,512]{2,1,0:T(8,128)(2,1)}), bf16[8,120,512]{2,1,0:T(8,128)(2,1)S(1)}, u32[]{:S(2)}, u32[]{:S(2)}) async-start(bf16[8,120,512]{2,1,0:T(8,128)(2,1)} %route.1), calls=%async_computation.4 | async-start | bytes 1966080 | tf_op jit(solution)/shard_map/all_to_all | solution.py:627
  82.3 0.8 own_plan.1.plan_ref.own_ref
  83.2 1.6 %far_plan.1.plan_ref = s32[8,128]{1,0:T(8,128)S(1)} custom-call(s32[4]{0:T(128)S(1)} %pad_add_fusion.position_ref, f32[128,256]{1,0:T(8,128)S(1)} %get-tuple-element.45.union_ref, bf16[1024,512]{1,0:T(8,128)(2,1)S(1)} %bitcast.155), custom_call_target="tpu_custom_call" | custom-call | flops 671088640 | bytes 524288 | tf_op jit(solution)/shard_map/far_plan/pallas_call | solution.py:553
  84.7 0.5 slice.51
  85.9 0.0 all-gather.6.cloned.1.call-done
  85.9 0.0 copy-start
  85.9 2.0 %copy-done = bf16[16,7,128,128]{3,2,1,0:T(8,128)(2,1)S(1)} copy-done((bf16[16,7,128,128]{3,2,1,0:T(8,128)(2,1)S(1)}, bf16[16,7,128,128]{3,2,1,0:T(8,128)(2,1)}, u32[]{:S(2)}) %copy-start) | copy-done | bytes 3670040
  88.0 2.2 %own_sums.1.near_ref = f32[112,32,128]{2,1,0:T(8,128)S(1)} custom-call(s32[16,128]{1,0:T(8,128)S(1)} %own_plan.1.plan_ref.own_ref, bf16[112,128,128]{2,1,0:T(8,128)(2,1)S(1)} %bitcast.153), custom_call_target="tpu_custom_call" | custom-call | flops 536870912 | bytes 5505024 | tf_op jit(solution)/shard_map/own_sums/pallas_call | solution.py:160
  90.2 6.6 %all-to-all-done.3 = bf16[8,120,512]{2,1,0:T(8,128)(2,1)S(1)} async-done(((bf16[8,120,512]{2,1,0:T(8,128)(2,1)}), bf16[8,120,512]{2,1,0:T(8,128)(2,1)S(1)}, u32[]{:S(2)}, u32[]{:S(2)}) %all-to-all-start.3) | async-done | bytes 983072 | tf_op jit(solution)/shard_map/all_to_all | solution.py:627
  96.8 6.4 %far_sums.1 = bf16[112,32,128]{2,1,0:T(8,128)(2,1)S(1)} custom-call(s32[16,128]{1,0:T(8,128)S(1)} %own_plan.1.plan_ref.own_ref, s32[8,128]{1,0:T(8,128)S(1)} %far_plan.1.plan_ref, bf16[112,128,128]{2,1,0:T(8,128)(2,1)} %bitcast.152, bf16[960,512]{1,0:T(8,128)(2,1)S(1)} %bitcast.157, f32[112,32,128]{2,1,0:T(8,128)S(1)} %own_sums.1.near_ref), custom_call_target="tpu_custom_call" | custom-call | tf_op jit(solution)/shard_map/far_sums/pallas_call | solution.py:249
  103.1 0.0 copy-start.1
  103.1 0.9 copy-done.1
  104.0 3.5 %all-to-all-start.4 = ((bf16[4,4,7,32,128]{4,3,2,1,0:T(8,128)(2,1)}), bf16[4,4,7,32,128]{4,3,2,1,0:T(8,128)(2,1)S(1)}, u32[]{:S(2)}, u32[]{:S(2)}) async-start(bf16[4,4,7,32,128]{4,3,2,1,0:T(8,128)(2,1)} %bitcast.158), calls=%async_computation.5 | async-start | bytes 1835008 | tf_op jit(solution)/shard_map/all_to_all | solution.py:634
  107.6 12.7 %all-to-all-done.4.cuts_ref = bf16[4,4,7,32,128]{4,3,2,1,0:T(8,128)(2,1)S(1)} async-done(((bf16[4,4,7,32,128]{4,3,2,1,0:T(8,128)(2,1)}), bf16[4,4,7,32,128]{4,3,2,1,0:T(8,128)(2,1)S(1)}, u32[]{:S(2)}, u32[]{:S(2)}) %all-to-all-start.4) | async-done | bytes 917536 | tf_op jit(solution)/shard_map/all_to_all | solution.py:634
  120.2 0.0 copy-done.6
  120.2 0.0 copy-done.7
  120.2 0.3 finish.1
  120.5 0.2 conditional.1
  120.8 0.0 copy-start.5
  120.8 0.9 copy-done.5
  (3 shorter events, 0.0 us)
Async XLA Ops:
  10.4 25.8 %all-to-all-start.1 = ((bf16[32,32,512]{2,1,0:T(8,128)(2,1)}), bf16[32,32,512]{2,1,0:T(8,128)(2,1)S(1)}, u32[]{:S(2)}, u32[]{:S(2)}) async-start(bf16[32,32,512]{2,1,0:T(8,128)(2,1)} %prepare.1), calls=%async_computation.2 | async-start | bytes 2097152 | tf_op jit(solution)/shard_map/all_to_all | solution.py:617
  19.0 66.9 %all-gather.6.cloned.1.call-start = ((), (), s32[]{:S(2)}) async-start(), calls=%async_computation.8 | async-start | bytes 4587520 | tf_op jit(solution)/shard_map/all_gather | solution.py:619
  36.2 84.0 %copy-start.6 = (s32[256,28]{0,1:T(8,128)S(1)}, s32[256,28]{0,1:T(8,128)}, u32[]{:S(2)}) copy-start(s32[256,28]{0,1:T(8,128)} %param.7) | copy-start | bytes 86020
  36.2 84.0 %copy-start.7 = (s32[4,7]{1,0:T(4,128)S(1)}, s32[4,7]{1,0:T(4,128)}, u32[]{:S(2)}) copy-start(s32[4,7]{1,0:T(4,128)} %keep_ref.3) | copy-start | bytes 340
  77.0 19.7 %all-to-all-start.3 = ((bf16[8,120,512]{2,1,0:T(8,128)(2,1)}), bf16[8,120,512]{2,1,0:T(8,128)(2,1)S(1)}, u32[]{:S(2)}, u32[]{:S(2)}) async-start(bf16[8,120,512]{2,1,0:T(8,128)(2,1)} %route.1), calls=%async_computation.4 | async-start | bytes 1966080 | tf_op jit(solution)/shard_map/all_to_all | solution.py:627
  85.9 2.0 %copy-start = (bf16[16,7,128,128]{3,2,1,0:T(8,128)(2,1)S(1)}, bf16[16,7,128,128]{3,2,1,0:T(8,128)(2,1)}, u32[]{:S(2)}) copy-start(bf16[16,7,128,128]{3,2,1,0:T(8,128)(2,1)} %all-gather.6.cloned.1.call-done) | copy-start | bytes 11010052
  103.1 0.9 copy-start.1
  104.0 16.2 %all-to-all-start.4 = ((bf16[4,4,7,32,128]{4,3,2,1,0:T(8,128)(2,1)}), bf16[4,4,7,32,128]{4,3,2,1,0:T(8,128)(2,1)S(1)}, u32[]{:S(2)}, u32[]{:S(2)}) async-start(bf16[4,4,7,32,128]{4,3,2,1,0:T(8,128)(2,1)} %bitcast.158), calls=%async_computation.5 | async-start | bytes 1835008 | tf_op jit(solution)/shard_map/all_to_all | solution.py:634
  120.8 0.9 copy-start.5
Sparse Core Ops, SparseCore 0:
  36.3 45.4 all-gather.5

commit v4 on v3

--- a/solution.py
+++ b/solution.py
@@ -364,7 +364,9 @@
     )(position, columns, entries)
 
 
-def send_kernel(need_ref, kq_ref, near_ref, out_ref, chosen_ref):
+def send_kernel(position_ref, need_ref, kq_ref, near_ref, *refs):
+    *out_refs, chosen_ref = refs
+    z = position_ref[1]
     near = near_ref[...]
     kind = iota((8, ENTRIES), 0)
     pick = (iota((8, ENTRIES), 1) % HELD == SLOTS + kind) & (kind < 2)
@@ -372,7 +374,7 @@
     flags = jnp.concatenate([flags[0:1], flags[1:2]], axis=1)
     need = need_ref[...] * flags
     slab = iota((8, 128), 1)
-    plane = (slab // NC) % NZ == iota((8, 128), 0)
+    plane = (slab // NC) % NZ == (iota((8, 128), 0) + z) & (NZ - 1)
     wanted = (dot(plane.astype(F32), need) > 0).astype(F32)
     code = codes(wanted, CAP_Z)
     most = jnp.max(jnp.sum(wanted, axis=1, keepdims=True), axis=0, keepdims=True)
@@ -385,38 +387,37 @@
     kq = kq_ref[...]
     for to in range(NZ):
         target = iota((8, 128), 0)
-        choice = slab == (target // NC * NZ + to) * NC + target % NC
+        choice = slab == (target // NC * NZ + ((z + to) & (NZ - 1))) * NC + target % NC
         asked = jnp.concatenate([dot(choice.astype(F32), need), kq], axis=0)
         notes = dot_rows(asked, chosen_ref[to * ROWS_Z : (to + 1) * ROWS_Z, :])
         first = jnp.concatenate([notes[i : i + 1] for i in range(4)], axis=1)
         second = jnp.concatenate([notes[i : i + 1] for i in range(4, 8)], axis=1)
         third = jnp.concatenate([notes[8:9], notes[9:10], totals, most], axis=1)
         begin = to * ROWS_Z
-        out_ref[to, 0 : ROWS_Z - 16] = packed[begin : begin + ROWS_Z - 16].astype(BF)
+        out_refs[to][0 : ROWS_Z - 16] = packed[begin : begin + ROWS_Z - 16].astype(BF)
         value = packed[begin + ROWS_Z - 16 : begin + ROWS_Z]
         value = jnp.where(tail == 12, first, value)
         value = jnp.where(tail == 13, second, value)
         value = jnp.where(tail == 14, third, value)
-        out_ref[to, ROWS_Z - 16 : ROWS_Z] = value.astype(BF)
-
-
-def send(need, kq, near):
+        out_refs[to][ROWS_Z - 16 : ROWS_Z] = value.astype(BF)
+
+
+def send(position, need, kq, near):
     return pl.pallas_call(
         send_kernel,
-        out_shape=jax.ShapeDtypeStruct((NZ, ROWS_Z, PIECE), BF),
-        in_specs=[vmem()] * 3,
-        out_specs=vmem(),
+        out_shape=[jax.ShapeDtypeStruct((ROWS_Z, PIECE), BF)] * NZ,
+        in_specs=[smem()] + [vmem()] * 3,
+        out_specs=[vmem()] * NZ,
         scratch_shapes=[pltpu.VMEM((NZ * ROWS_Z, ENTRIES), BF)],
         compiler_params=params(),
         name="send",
-    )(need, kq, near)
-
-
-def notes_of(along_ref):
+    )(position, need, kq, near)
+
+
+def notes_of(along_refs):
     asked, third = [], []
-    for plane in range(NZ):
-        rows = pl.ds(plane * ROWS_Z + ROWS_Z - 16, 16)
-        notes = along_ref[rows, :].astype(F32)
+    for along_ref in along_refs:
+        notes = along_ref[ROWS_Z - 16 : ROWS_Z].astype(F32)
         asked.append(
             jnp.concatenate(
                 [
@@ -430,8 +431,11 @@
     return jnp.concatenate(asked, axis=1), third
 
 
-def route_kernel(along_ref, out_ref, chosen_ref):
-    asked, _ = notes_of(along_ref)
+def route_kernel(*refs):
+    *along_refs, out_ref, chosen_ref, along_ref = refs
+    asked, _ = notes_of(along_refs)
+    for number, ref in enumerate(along_refs):
+        along_ref[number * ROWS_Z : (number + 1) * ROWS_Z] = ref[...]
     code = codes(asked, CAP_X)
     for to in range(TARGETS):
         chosen_ref[to * SIDE : (to + 1) * SIDE, :] = one_hot(code[to : to + 1], SIDE).astype(BF)
@@ -444,12 +448,15 @@
     return pl.pallas_call(
         route_kernel,
         out_shape=jax.ShapeDtypeStruct((TARGETS, CAP_X, PIECE), BF),
-        in_specs=[vmem()],
-        out_specs=vmem(),
-        scratch_shapes=[pltpu.VMEM((TARGETS * SIDE, NZ * ROWS_Z), BF)],
+        in_specs=[vmem()] * NZ,
+        out_specs=vmem(),
+        scratch_shapes=[
+            pltpu.VMEM((TARGETS * SIDE, NZ * ROWS_Z), BF),
+            pltpu.VMEM((NZ * ROWS_Z, PIECE), BF),
+        ],
         compiler_params=params(),
         name="route",
-    )(along)
+    )(*along)
 
 
 def own_plan_kernel(position_ref, slots_ref, union_ref, out_ref):
@@ -504,11 +511,12 @@
     )(position, slots, union)
 
 
-def far_plan_kernel(position_ref, union_ref, along_ref, out_ref):
+def far_plan_kernel(position_ref, union_ref, *refs):
+    *along_refs, out_ref = refs
     x, z, core = (position_ref[i] for i in range(3))
     slab = (x * NZ + z) * NC + core
     out_ref[...] = jnp.zeros_like(out_ref)
-    asked, third = notes_of(along_ref)
+    asked, third = notes_of(along_refs)
     mine = iota(asked.shape, 0) == x * NC + core
     asked = jnp.sum(jnp.where(mine, asked, 0.0), axis=0, keepdims=True)
     number = jnp.sum(asked).astype(I32)
@@ -553,12 +561,12 @@
     return pl.pallas_call(
         far_plan_kernel,
         out_shape=jax.ShapeDtypeStruct((8, 128), I32),
-        in_specs=[smem(), vmem(), vmem()],
+        in_specs=[smem()] + [vmem()] * (1 + NZ),
         out_specs=vmem(),
         compiler_params=params(),
         cost_estimate=cost(2 * 20 * ROWS**3, 8 * ROWS**2),
         name="far_plan",
-    )(position, union, along)
+    )(position, union, *along)
 
 
 def dense(blocks, nonzero, columns):
@@ -618,10 +626,12 @@
     near, turned, need = lax.optimization_barrier((near, turned, need))
     whole = lax.all_gather(turned, "col", axis=0, tiled=False)
     whole = whole.reshape(ZERO_BLOCK, SIDE, SIDE)
-    packed = send(need, kq, near.reshape(ENTRIES, PIECE))
+    packed = send(position, need, kq, near.reshape(ENTRIES, PIECE))
     packed, slots = lax.optimization_barrier((packed, slots))
-    along = lax.all_to_all(packed, "z", split_axis=0, concat_axis=0, tiled=True)
-    along = along.reshape(NZ * ROWS_Z, PIECE)
+    along = [packed[0]] + [
+        lax.ppermute(packed[step], "z", [(i, (i + step) % NZ) for i in range(NZ)])
+        for step in range(1, NZ)
+    ]
     own_lists = own_plan(position, slots, union)
     packed, notes = lax.optimization_barrier((route(along), along))
     far = lax.all_to_all(packed, ("x", "core"), split_axis=0, concat_axis=0, tiled=True)

time: 130 us -> 128 us (0.985)
  blocking collectives: 35.8 us -> 0 us
  waiting for transfers between devices: 29.3 us -> 46.3 us
  starting transfers between devices: 17.5 us -> 33.1 us
    all_to_all x1 -> x0, blocking collectives: 35.8 us -> none  [shards(): along = lax.all_to_all(packed, 'z', split_axis=0, concat_axis=0, tiled=True)]
    ppermute x0 -> x7, starting transfers between devices: none -> 17.2 us  [shards(): lax.ppermute(packed[step], 'z', [(i, (i + step) % NZ) for i in range(NZ)])]
    ppermute x0 -> x7, waiting for transfers between devices: none -> 17.2 us  [shards(): lax.ppermute(packed[step], 'z', [(i, (i + step) % NZ) for i in range(NZ)])]
    all_to_all x1, starting transfers between devices: 5.33 us -> 3.8 us  [shards(): lax.all_to_all(packed, ('x', 'core'), split_axis=0, concat_axis=0, tiled=...]
  transfers between devices with their start and end apart: 4 -> 11, of which waited for: 3 -> 7; matrix products, arithmetic and copies ran while one was open for 2% -> 2% of each run, Pallas kernels for 9% -> 9%
where the time goes in v4:
time: 128 us; the launch traced here: 126 us
  waiting for transfers between devices  46.3 us (36%)
  starting transfers between devices  33.1 us (26%)
  Pallas kernels  25.3 us (20%)
  between operations  14.2 us (11%)
  local copies, waits for them, and re-layouts  6.66 us (5%)
    ppermute x7, starting transfers between devices, shards(): lax.ppermute(packed[step], 'z', [(i, (i + step) % NZ) for i in range(NZ)])  17.2 us
    ppermute x7, waiting for transfers between devices, shards(): lax.ppermute(packed[step], 'z', [(i, (i + step) % NZ) for i in range(NZ)])  17.2 us
    all_to_all x1, waiting for transfers between devices, shards(): lax.all_to_all(result, 'col', split_axis=0, concat_axis=0, tiled=True)  12.6 us
    all_to_all x1, waiting for transfers between devices, shards(): lax.all_to_all(cuts, ('col', 'x', 'core'), split_axis=0, concat_axis=0, t...  9.97 us
    all_to_all x1, starting transfers between devices, shards(): lax.all_to_all(cuts, ('col', 'x', 'core'), split_axis=0, concat_axis=0, t...  8.59 us
    all_to_all x1, waiting for transfers between devices, shards(): lax.all_to_all(packed, ('x', 'core'), split_axis=0, concat_axis=0, tiled=...  6.51 us
    pallas_call x1, Pallas kernels, far_sums(): pl.pallas_call(far_kernel, out_shape=jax.ShapeDtypeStruct((ZERO_BLOCK, WI...  6.16 us
    unnamed x11, local copies, waits for them, and re-layouts  4.74 us
  transfers between devices with their start and end apart: 11, of which 7 were waited for; matrix products, arithmetic and copies ran while one was open for 2% of the time, Pallas kernels for 9%

profile of v4, /device:TPU:1, one launch (start us, length us, event | category | flops | bytes accessed | tf_op | source)
XLA Modules:
  0.0 126.0 jit_solution(466143488958105896)
XLA Ops:
  6.5 0.1 pad_add_fusion.position_ref
  6.6 3.8 %prepare.1 = bf16[32,32,512]{2,1,0:T(8,128)(2,1)} custom-call(s32[4]{0:T(128)S(1)} %pad_add_fusion.position_ref, s32[4,7]{1,0:T(4,128)} %keep_ref.3, bf16[4,7,128,128]{3,2,1,0:T(8,128)(2,1)} %blocks_ref.2), custom_call_target="tpu_custom_call" | custom-call | tf_op jit(solution)/shard_map/prepare/pallas_call | solution.py:85
  10.4 8.6 %all-to-all-start.1 = ((bf16[32,32,512]{2,1,0:T(8,128)(2,1)}), bf16[32,32,512]{2,1,0:T(8,128)(2,1)S(1)}, u32[]{:S(2)}, u32[]{:S(2)}) async-start(bf16[32,32,512]{2,1,0:T(8,128)(2,1)} %prepare.1), calls=%async_computation.2 | async-start | bytes 2097152 | tf_op jit(solution)/shard_map/all_to_all | solution.py:625
  19.0 0.0 all-gather.6.cloned.1.call-start
  19.1 0.9 copy.101
  19.9 0.3 reshape.217
  20.3 0.1 reshape.218
  20.4 0.1 reshape.219.entries_ref
  20.4 0.9 copy.103.columns_ref
  21.3 2.4 %turn.1 = bf16[4,7,128,128]{3,2,1,0:T(8,128)(2,1)} custom-call(s32[4,7]{1,0:T(4,128)} %keep_ref.3, bf16[4,7,128,128]{3,2,1,0:T(8,128)(2,1)} %blocks_ref.2), custom_call_target="tpu_custom_call" | custom-call | flops 117440512 | bytes 1835008 | tf_op jit(solution)/shard_map/turn/pallas_call | solution.py:106
  23.7 0.0 copy-start.6
  23.7 0.0 copy-start.7
  23.7 2.5 %pattern.1 = (s32[256,256]{1,0:T(8,128)S(1)}, f32[128,256]{1,0:T(8,128)S(1)}, f32[128,1024]{1,0:T(8,128)S(1)}, f32[8,1024]{1,0:T(8,128)S(1)}) custom-call(s32[4]{0:T(128)S(1)} %pad_add_fusion.position_ref, s32[256,28]{1,0:T(8,128)S(1)} %copy.103.columns_ref, s32[1,1024]{1,0:T(1,128)S(1)} %reshape.219.entries_ref), custom_call_target="tpu_custom_call" | custom-call | flops 234881024 | bytes 524288 | tf_op jit(solution)/shard_map/pattern/pallas_call | solution.py:351
  26.2 10.0 %all-to-all-done.1 = bf16[32,32,512]{2,1,0:T(8,128)(2,1)S(1)} async-done(((bf16[32,32,512]{2,1,0:T(8,128)(2,1)}), bf16[32,32,512]{2,1,0:T(8,128)(2,1)S(1)}, u32[]{:S(2)}, u32[]{:S(2)}) %all-to-all-start.1) | async-done | bytes 1048608 | tf_op jit(solution)/shard_map/all_to_all | solution.py:625
  36.2 0.0 all-gather.6.cloned.1.call-update
  36.2 3.2 %send.1 = (bf16[128,512]{1,0:T(8,128)(2,1)S(1)}, bf16[128,512]{1,0:T(8,128)(2,1)S(1)}, bf16[128,512]{1,0:T(8,128)(2,1)S(1)}, bf16[128,512]{1,0:T(8,128)(2,1)S(1)...) custom-call(s32[4]{0:T(128)S(1)} %pad_add_fusion.position_ref, ...), custom_call_target="tpu_custom_call" | custom-call | tf_op jit(solution)/shard_map/send/pallas_call | solution.py:406
  39.4 1.7 %collective-permute-start = (bf16[128,512]{1,0:T(8,128)(2,1)S(1)}, bf16[128,512]{1,0:T(8,128)(2,1)S(1)}, u32[]{:S(2)}, u32[]{:S(2)}) collective-permute-start(bf16[128,512]{1,0:T(8,128)(2,1)S(1)} %get-tuple-element.74), channel_id=1, source_target_pairs={{0,8},{8,16},{16,24},{24,32},{32,40},{40,48},{48,56},{56,0},{1,9},... | collective-permute-start | bytes 393224 | tf_op jit(solution)/shard_map/ppermute | solution.py:632
  41.2 3.0 %collective-permute-start.1 = (bf16[128,512]{1,0:T(8,128)(2,1)S(1)}, bf16[128,512]{1,0:T(8,128)(2,1)S(1)}, u32[]{:S(2)}, u32[]{:S(2)}) collective-permute-start(bf16[128,512]{1,0:T(8,128)(2,1)S(1)} %get-tuple-element.75), channel_id=1, source_target_pairs={{0,16},{8,24},{16,32},{24,40},{32,48},{40,56},{48,0},{56,8},{1,17}... | collective-permute-start | bytes 393224 | tf_op jit(solution)/shard_map/ppermute | solution.py:632
  44.2 3.8 %collective-permute-start.2 = (bf16[128,512]{1,0:T(8,128)(2,1)S(1)}, bf16[128,512]{1,0:T(8,128)(2,1)S(1)}, u32[]{:S(2)}, u32[]{:S(2)}) collective-permute-start(bf16[128,512]{1,0:T(8,128)(2,1)S(1)} %get-tuple-element.76), channel_id=1, source_target_pairs={{0,24},{8,32},{16,40},{24,48},{32,56},{40,0},{48,8},{56,16},{1,25}... | collective-permute-start | bytes 393224 | tf_op jit(solution)/shard_map/ppermute | solution.py:632
  47.9 0.5 collective-permute-start.3
  48.4 4.5 %collective-permute-start.4 = (bf16[128,512]{1,0:T(8,128)(2,1)S(1)}, bf16[128,512]{1,0:T(8,128)(2,1)S(1)}, u32[]{:S(2)}, u32[]{:S(2)}) collective-permute-start(bf16[128,512]{1,0:T(8,128)(2,1)S(1)} %get-tuple-element.78), channel_id=1, source_target_pairs={{0,40},{8,48},{16,56},{24,0},{32,8},{40,16},{48,24},{56,32},{1,41}... | collective-permute-start | bytes 393224 | tf_op jit(solution)/shard_map/ppermute | solution.py:632
  52.8 0.0 collective-permute-done.refs_1_
  52.8 2.4 %collective-permute-start.5 = (bf16[128,512]{1,0:T(8,128)(2,1)S(1)}, bf16[128,512]{1,0:T(8,128)(2,1)S(1)}, u32[]{:S(2)}, u32[]{:S(2)}) collective-permute-start(bf16[128,512]{1,0:T(8,128)(2,1)S(1)} %get-tuple-element.79), channel_id=1, source_target_pairs={{0,48},{8,56},{16,0},{24,8},{32,16},{40,24},{48,32},{56,40},{1,49}... | collective-permute-start | bytes 393224 | tf_op jit(solution)/shard_map/ppermute | solution.py:632
  55.2 0.0 collective-permute-done.1.refs_2_
  55.2 1.4 %collective-permute-start.6 = (bf16[128,512]{1,0:T(8,128)(2,1)S(1)}, bf16[128,512]{1,0:T(8,128)(2,1)S(1)}, u32[]{:S(2)}, u32[]{:S(2)}) collective-permute-start(bf16[128,512]{1,0:T(8,128)(2,1)S(1)} %get-tuple-element.80), channel_id=1, source_target_pairs={{0,56},{8,0},{16,8},{24,16},{32,24},{40,32},{48,40},{56,48},{1,57}... | collective-permute-start | bytes 393224 | tf_op jit(solution)/shard_map/ppermute | solution.py:632
  56.7 7.8 %collective-permute-done.2.refs_3_ = bf16[128,512]{1,0:T(8,128)(2,1)S(1)} collective-permute-done((bf16[128,512]{1,0:T(8,128)(2,1)S(1)}, bf16[128,512]{1,0:T(8,128)(2,1)S(1)}, u32[]{:S(2)}, u32[]{:S(2)}) %collective-permute-start.2) | collective-permute-done | bytes 131104 | tf_op jit(solution)/shard_map/ppermute | solution.py:632
  64.4 0.8 collective-permute-done.3.refs_4_
  65.2 0.0 collective-permute-done.4.refs_5_
  65.2 7.8 %collective-permute-done.5.refs_6_ = bf16[128,512]{1,0:T(8,128)(2,1)S(1)} collective-permute-done((bf16[128,512]{1,0:T(8,128)(2,1)S(1)}, bf16[128,512]{1,0:T(8,128)(2,1)S(1)}, u32[]{:S(2)}, u32[]{:S(2)}) %collective-permute-start.5) | collective-permute-done | bytes 131104 | tf_op jit(solution)/shard_map/ppermute | solution.py:632
  73.0 0.9 collective-permute-done.6.refs_7_
  73.9 2.3 %route.1 = bf16[8,120,512]{2,1,0:T(8,128)(2,1)} custom-call(bf16[128,512]{1,0:T(8,128)(2,1)S(1)} %get-tuple-element.83.refs_0_, bf16[128,512]{1,0:T(8,128)(2,1)S(1)} %collective-permute-done.refs_1_, bf16[128,512]{1,0:T(8,128)(2,1)S(1)} %collective-permute-done.1.refs_2_, bf16[128,512]{1,0:T(8,128)(2,1)S(1)} %collective-permute-done.2.refs_3_, ...), custom_call_target="tpu_custom_call" | custom-call | tf_op jit(solution)/shard_map/route/pallas_call | solution.py:448
  76.2 3.8 %all-to-all-start.2 = ((bf16[8,120,512]{2,1,0:T(8,128)(2,1)}), bf16[8,120,512]{2,1,0:T(8,128)(2,1)S(1)}, u32[]{:S(2)}, u32[]{:S(2)}) async-start(bf16[8,120,512]{2,1,0:T(8,128)(2,1)} %route.1), calls=%async_computation.3 | async-start | bytes 1966080 | tf_op jit(solution)/shard_map/all_to_all | solution.py:637
  80.0 0.8 own_plan.1.plan_ref.own_ref
  80.8 1.6 %far_plan.1.plan_ref = s32[8,128]{1,0:T(8,128)S(1)} custom-call(s32[4]{0:T(128)S(1)} %pad_add_fusion.position_ref, f32[128,256]{1,0:T(8,128)S(1)} %get-tuple-element.82.union_ref, bf16[128,512]{1,0:T(8,128)(2,1)S(1)} %get-tuple-element.83.refs_0_, bf16[128,512]{1,0:T(8,128)(2,1)S(1)} %collective-permute-done.refs_1_, ...), custom_call_target="tpu_custom_call" | custom-call | flops 671088640 | bytes 524288 | tf_op jit(solution)/shard_map/far_plan/pallas_call | solution.py:561
  82.4 0.6 slice.51
  83.6 0.0 all-gather.6.cloned.1.call-done
  83.6 0.0 copy-start
  83.6 2.0 %copy-done = bf16[16,7,128,128]{3,2,1,0:T(8,128)(2,1)S(1)} copy-done((bf16[16,7,128,128]{3,2,1,0:T(8,128)(2,1)S(1)}, bf16[16,7,128,128]{3,2,1,0:T(8,128)(2,1)}, u32[]{:S(2)}) %copy-start) | copy-done | bytes 3670040
  85.7 2.2 %own_sums.1.near_ref = f32[112,32,128]{2,1,0:T(8,128)S(1)} custom-call(s32[16,128]{1,0:T(8,128)S(1)} %own_plan.1.plan_ref.own_ref, bf16[112,128,128]{2,1,0:T(8,128)(2,1)S(1)} %bitcast.152), custom_call_target="tpu_custom_call" | custom-call | flops 536870912 | bytes 5505024 | tf_op jit(solution)/shard_map/own_sums/pallas_call | solution.py:160
  87.9 6.5 %all-to-all-done.2 = bf16[8,120,512]{2,1,0:T(8,128)(2,1)S(1)} async-done(((bf16[8,120,512]{2,1,0:T(8,128)(2,1)}), bf16[8,120,512]{2,1,0:T(8,128)(2,1)S(1)}, u32[]{:S(2)}, u32[]{:S(2)}) %all-to-all-start.2) | async-done | bytes 983072 | tf_op jit(solution)/shard_map/all_to_all | solution.py:637
  94.4 6.2 %far_sums.1 = bf16[112,32,128]{2,1,0:T(8,128)(2,1)S(1)} custom-call(s32[16,128]{1,0:T(8,128)S(1)} %own_plan.1.plan_ref.own_ref, s32[8,128]{1,0:T(8,128)S(1)} %far_plan.1.plan_ref, bf16[112,128,128]{2,1,0:T(8,128)(2,1)} %bitcast.151, bf16[960,512]{1,0:T(8,128)(2,1)S(1)} %bitcast.154, f32[112,32,128]{2,1,0:T(8,128)S(1)} %own_sums.1.near_ref), custom_call_target="tpu_custom_call" | custom-call | tf_op jit(solution)/shard_map/far_sums/pallas_call | solution.py:249
  100.5 0.0 copy-start.1
  100.6 0.9 copy-done.1
  101.5 3.5 %all-to-all-start.3 = ((bf16[4,4,7,32,128]{4,3,2,1,0:T(8,128)(2,1)}), bf16[4,4,7,32,128]{4,3,2,1,0:T(8,128)(2,1)S(1)}, u32[]{:S(2)}, u32[]{:S(2)}) async-start(bf16[4,4,7,32,128]{4,3,2,1,0:T(8,128)(2,1)} %bitcast.155), calls=%async_computation.4 | async-start | bytes 1835008 | tf_op jit(solution)/shard_map/all_to_all | solution.py:644
  105.0 12.6 %all-to-all-done.3.cuts_ref = bf16[4,4,7,32,128]{4,3,2,1,0:T(8,128)(2,1)S(1)} async-done(((bf16[4,4,7,32,128]{4,3,2,1,0:T(8,128)(2,1)}), bf16[4,4,7,32,128]{4,3,2,1,0:T(8,128)(2,1)S(1)}, u32[]{:S(2)}, u32[]{:S(2)}) %all-to-all-start.3) | async-done | bytes 917536 | tf_op jit(solution)/shard_map/all_to_all | solution.py:644
  117.6 0.0 copy-done.6
  117.6 0.0 copy-done.7
  117.6 0.3 finish.1
  117.9 0.3 conditional.1
  118.2 0.0 copy-start.5
  118.2 0.9 copy-done.5
  (3 shorter events, 0.0 us)
Async XLA Ops:
  10.4 25.8 %all-to-all-start.1 = ((bf16[32,32,512]{2,1,0:T(8,128)(2,1)}), bf16[32,32,512]{2,1,0:T(8,128)(2,1)S(1)}, u32[]{:S(2)}, u32[]{:S(2)}) async-start(bf16[32,32,512]{2,1,0:T(8,128)(2,1)} %prepare.1), calls=%async_computation.2 | async-start | bytes 2097152 | tf_op jit(solution)/shard_map/all_to_all | solution.py:625
  19.0 64.6 %all-gather.6.cloned.1.call-start = ((), (), s32[]{:S(2)}) async-start(), calls=%async_computation.7 | async-start | bytes 4587520 | tf_op jit(solution)/shard_map/all_gather | solution.py:627
  23.7 93.9 %copy-start.6 = (s32[256,28]{0,1:T(8,128)S(1)}, s32[256,28]{0,1:T(8,128)}, u32[]{:S(2)}) copy-start(s32[256,28]{0,1:T(8,128)} %param.7) | copy-start | bytes 86020
  23.7 93.9 %copy-start.7 = (s32[4,7]{1,0:T(4,128)S(1)}, s32[4,7]{1,0:T(4,128)}, u32[]{:S(2)}) copy-start(s32[4,7]{1,0:T(4,128)} %keep_ref.3) | copy-start | bytes 340
  39.4 13.4 %collective-permute-start = (bf16[128,512]{1,0:T(8,128)(2,1)S(1)}, bf16[128,512]{1,0:T(8,128)(2,1)S(1)}, u32[]{:S(2)}, u32[]{:S(2)}) collective-permute-start(bf16[128,512]{1,0:T(8,128)(2,1)S(1)} %get-tuple-element.74), channel_id=1, source_target_pairs={{0,8},{8,16},{16,24},{24,32},{32,40},{40,48},{48,56},{56,0},{1,9},... | collective-permute-start | bytes 393224 | tf_op jit(solution)/shard_map/ppermute | solution.py:632
  41.2 14.1 %collective-permute-start.1 = (bf16[128,512]{1,0:T(8,128)(2,1)S(1)}, bf16[128,512]{1,0:T(8,128)(2,1)S(1)}, u32[]{:S(2)}, u32[]{:S(2)}) collective-permute-start(bf16[128,512]{1,0:T(8,128)(2,1)S(1)} %get-tuple-element.75), channel_id=1, source_target_pairs={{0,16},{8,24},{16,32},{24,40},{32,48},{40,56},{48,0},{56,8},{1,17}... | collective-permute-start | bytes 393224 | tf_op jit(solution)/shard_map/ppermute | solution.py:632
  44.2 20.3 %collective-permute-start.2 = (bf16[128,512]{1,0:T(8,128)(2,1)S(1)}, bf16[128,512]{1,0:T(8,128)(2,1)S(1)}, u32[]{:S(2)}, u32[]{:S(2)}) collective-permute-start(bf16[128,512]{1,0:T(8,128)(2,1)S(1)} %get-tuple-element.76), channel_id=1, source_target_pairs={{0,24},{8,32},{16,40},{24,48},{32,56},{40,0},{48,8},{56,16},{1,25}... | collective-permute-start | bytes 393224 | tf_op jit(solution)/shard_map/ppermute | solution.py:632
  47.9 17.3 %collective-permute-start.3 = (bf16[128,512]{1,0:T(8,128)(2,1)S(1)}, bf16[128,512]{1,0:T(8,128)(2,1)S(1)}, u32[]{:S(2)}, u32[]{:S(2)}) collective-permute-start(bf16[128,512]{1,0:T(8,128)(2,1)S(1)} %get-tuple-element.77), channel_id=1, source_target_pairs={{0,32},{8,40},{16,48},{24,56},{32,0},{40,8},{48,16},{56,24},{1,33}... | collective-permute-start | bytes 393224 | tf_op jit(solution)/shard_map/ppermute | solution.py:632
  48.4 16.8 %collective-permute-start.4 = (bf16[128,512]{1,0:T(8,128)(2,1)S(1)}, bf16[128,512]{1,0:T(8,128)(2,1)S(1)}, u32[]{:S(2)}, u32[]{:S(2)}) collective-permute-start(bf16[128,512]{1,0:T(8,128)(2,1)S(1)} %get-tuple-element.78), channel_id=1, source_target_pairs={{0,40},{8,48},{16,56},{24,0},{32,8},{40,16},{48,24},{56,32},{1,41}... | collective-permute-start | bytes 393224 | tf_op jit(solution)/shard_map/ppermute | solution.py:632
  52.8 20.1 %collective-permute-start.5 = (bf16[128,512]{1,0:T(8,128)(2,1)S(1)}, bf16[128,512]{1,0:T(8,128)(2,1)S(1)}, u32[]{:S(2)}, u32[]{:S(2)}) collective-permute-start(bf16[128,512]{1,0:T(8,128)(2,1)S(1)} %get-tuple-element.79), channel_id=1, source_target_pairs={{0,48},{8,56},{16,0},{24,8},{32,16},{40,24},{48,32},{56,40},{1,49}... | collective-permute-start | bytes 393224 | tf_op jit(solution)/shard_map/ppermute | solution.py:632
  55.2 18.6 %collective-permute-start.6 = (bf16[128,512]{1,0:T(8,128)(2,1)S(1)}, bf16[128,512]{1,0:T(8,128)(2,1)S(1)}, u32[]{:S(2)}, u32[]{:S(2)}) collective-permute-start(bf16[128,512]{1,0:T(8,128)(2,1)S(1)} %get-tuple-element.80), channel_id=1, source_target_pairs={{0,56},{8,0},{16,8},{24,16},{32,24},{40,32},{48,40},{56,48},{1,57}... | collective-permute-start | bytes 393224 | tf_op jit(solution)/shard_map/ppermute | solution.py:632
  76.2 18.2 %all-to-all-start.2 = ((bf16[8,120,512]{2,1,0:T(8,128)(2,1)}), bf16[8,120,512]{2,1,0:T(8,128)(2,1)S(1)}, u32[]{:S(2)}, u32[]{:S(2)}) async-start(bf16[8,120,512]{2,1,0:T(8,128)(2,1)} %route.1), calls=%async_computation.3 | async-start | bytes 1966080 | tf_op jit(solution)/shard_map/all_to_all | solution.py:637
  83.6 2.0 %copy-start = (bf16[16,7,128,128]{3,2,1,0:T(8,128)(2,1)S(1)}, bf16[16,7,128,128]{3,2,1,0:T(8,128)(2,1)}, u32[]{:S(2)}) copy-start(bf16[16,7,128,128]{3,2,1,0:T(8,128)(2,1)} %all-gather.6.cloned.1.call-done) | copy-start | bytes 11010052
  100.5 0.9 copy-start.1
  101.5 16.1 %all-to-all-start.3 = ((bf16[4,4,7,32,128]{4,3,2,1,0:T(8,128)(2,1)}), bf16[4,4,7,32,128]{4,3,2,1,0:T(8,128)(2,1)S(1)}, u32[]{:S(2)}, u32[]{:S(2)}) async-start(bf16[4,4,7,32,128]{4,3,2,1,0:T(8,128)(2,1)} %bitcast.155), calls=%async_computation.4 | async-start | bytes 1835008 | tf_op jit(solution)/shard_map/all_to_all | solution.py:644
  118.2 0.9 copy-start.5
Sparse Core Ops, SparseCore 0:
  36.3 45.5 all-gather.5

commit v5 on v4

--- a/solution.py
+++ b/solution.py
@@ -25,6 +25,8 @@
 CAP_Z = 124
 ROWS_Z = 128
 CAP_X = 120
+ORDER_Z = (3, 5, 4, 2, 6, 1, 7)
+ORDER_Y = (1, 3, 2)
 GROUP = 8
 FAR_GROUP = 4
 ROWS_AT_ONCE = 4
@@ -60,8 +62,8 @@
             number = row * QUARTER + slot
             keep = keep_ref[row, slot] != 0
             flags = jnp.where((lanes == number) & keep, 1.0, flags)
-            block = blocks_ref[row, slot].astype(F32)
-            turned = jnp.where(keep, block, jnp.zeros_like(block)).T
+            block = blocks_ref[row, slot]
+            turned = jnp.where(keep, block, jnp.zeros_like(block)).T.astype(F32)
             for quarter in range(NY):
                 for part_of in range(NY):
                     begin = quarter * WIDE + part_of * TARGETS
@@ -179,10 +181,9 @@
     whole_ref,
     far_ref,
     near_ref,
-    out_ref,
-    total,
-    pieces_ref,
+    *refs,
 ):
+    *out_refs, total, pieces_ref = refs
     for sender in range(TARGETS):
         rows = pl.ds(sender * CAP_X, CAP_X)
         for part in range(NY):
@@ -238,19 +239,22 @@
 
     lax.fori_loop(0, named_rows, rest, 0)
 
-    for place in range(ZERO_BLOCK):
-        member, slot = out_place(place)
-        column = own_ref[8, member * (128 // HEIGHT) + slot]
-        value = total[column, :, pl.ds(member * SIDE, SIDE)] + near_ref[place]
-        out_ref[place] = value.astype(BF)
+    for step, out_ref in enumerate(out_refs):
+        part = (own_ref[15, 0] + step) & (NY - 1)
+        for place in range(HEIGHT * QUARTER):
+            member, slot = place // QUARTER, part * QUARTER + place % QUARTER
+            column = own_ref[8, member * (128 // HEIGHT) + slot]
+            value = total[column, :, pl.ds(member * SIDE, SIDE)]
+            value = value + near_ref[part * (HEIGHT * QUARTER) + place]
+            out_ref[place] = value.astype(BF)
 
 
 def far_sums(own_lists, far_lists, whole, far, near):
     return pl.pallas_call(
         far_kernel,
-        out_shape=jax.ShapeDtypeStruct((ZERO_BLOCK, WIDE, SIDE), BF),
+        out_shape=[jax.ShapeDtypeStruct((HEIGHT * QUARTER, WIDE, SIDE), BF)] * NY,
         in_specs=[smem(), smem(), vmem(), vmem(), vmem()],
-        out_specs=vmem(),
+        out_specs=[vmem()] * NY,
         scratch_shapes=[
             pltpu.VMEM((OUT_COLS + 1, WIDE, HEIGHT * SIDE), F32),
             pltpu.VMEM((NY, TARGETS * CAP_X, SIDE), F32),
@@ -260,22 +264,28 @@
     )(own_lists, far_lists, whole, far, near)
 
 
-def finish_kernel(cuts_ref, out_ref):
+def finish_kernel(position_ref, *refs):
+    *cut_refs, out_ref, turned_ref = refs
+    for step, cut_ref in zip((0,) + ORDER_Y, cut_refs):
+        part = (position_ref[3] - step) & (NY - 1)
+        rows = pl.ds(pl.multiple_of(part * WIDE, WIDE), WIDE)
+        for place in range(HEIGHT * QUARTER):
+            turned_ref[place, rows, :] = cut_ref[place]
     for row in range(HEIGHT):
         for slot in range(QUARTER):
-            turned = jnp.concatenate([cuts_ref[part, row, slot] for part in range(NY)], axis=0)
-            out_ref[row, slot] = turned.T
-
-
-def finish(cuts):
+            out_ref[row, slot] = turned_ref[row * QUARTER + slot].T
+
+
+def finish(position, cuts):
     return pl.pallas_call(
         finish_kernel,
         out_shape=jax.ShapeDtypeStruct((HEIGHT, QUARTER, SIDE, SIDE), BF),
-        in_specs=[vmem()],
+        in_specs=[smem()] + [vmem()] * NY,
         out_specs=vmem(),
+        scratch_shapes=[pltpu.VMEM((HEIGHT * QUARTER, SIDE, SIDE), BF)],
         compiler_params=params(),
         name="finish",
-    )(cuts)
+    )(position, *cuts)
 
 
 def iota(shape, axis):
@@ -630,7 +640,7 @@
     packed, slots = lax.optimization_barrier((packed, slots))
     along = [packed[0]] + [
         lax.ppermute(packed[step], "z", [(i, (i + step) % NZ) for i in range(NZ)])
-        for step in range(1, NZ)
+        for step in ORDER_Z
     ]
     own_lists = own_plan(position, slots, union)
     packed, notes = lax.optimization_barrier((route(along), along))
@@ -640,9 +650,11 @@
     own = own_sums(own_lists, whole)
     far, fits, own = lax.optimization_barrier((far, far_lists[4, 0] != 0, own))
     result = far_sums(own_lists, far_lists, whole, far, own)
-    result = result.reshape(NY, HEIGHT, QUARTER, WIDE, SIDE)
-    result = lax.all_to_all(result, "col", split_axis=0, concat_axis=0, tiled=True)
-    square = finish(result)
+    cuts = [result[0]]
+    for step in ORDER_Y:
+        pairs = [(i, (i + step) % NY) for i in range(NY)]
+        cuts.append(lax.ppermute(result[step], "col", pairs))
+    square = finish(position, cuts)
     return lax.cond(
         fits,
         lambda value, *_: value,

time: 128 us -> 121 us (0.945)
  the two profiles are of different devices: /device:TPU:1 before, /device:TPU:96 now
where the time goes in v5:
time: 121 us; the launch traced here: 120 us
  waiting for transfers between devices  42 us (35%)
  starting transfers between devices  29.9 us (25%)
  Pallas kernels  29.1 us (24%)
  between operations  14.1 us (12%)
  local copies, waits for them, and re-layouts  4.77 us (4%)
    ppermute x7, starting transfers between devices, shards(): lax.ppermute(packed[step], 'z', [(i, (i + step) % NZ) for i in range(NZ)])  15.7 us
    ppermute x7, waiting for transfers between devices, shards(): lax.ppermute(packed[step], 'z', [(i, (i + step) % NZ) for i in range(NZ)])  15.4 us
    all_to_all x1, waiting for transfers between devices, shards(): lax.all_to_all(cuts, ('col', 'x', 'core'), split_axis=0, concat_axis=0, t...  10.1 us
    ppermute x3, waiting for transfers between devices, shards(): cuts.append(lax.ppermute(result[step], 'col', pairs))  9.03 us
    pallas_call x1, Pallas kernels, far_sums(): pl.pallas_call(far_kernel, out_shape=[jax.ShapeDtypeStruct((HEIGHT * QUAR...  8.04 us
    all_to_all x1, starting transfers between devices, shards(): lax.all_to_all(cuts, ('col', 'x', 'core'), split_axis=0, concat_axis=0, t...  7.32 us
    all_to_all x1, waiting for transfers between devices, shards(): lax.all_to_all(packed, ('x', 'core'), split_axis=0, concat_axis=0, tiled=...  6.29 us
    pallas_call x1, Pallas kernels, prepare(): pl.pallas_call(prepare_kernel, out_shape=jax.ShapeDtypeStruct((PEERS, HEL...  4.21 us
  transfers between devices with their start and end apart: 13, of which 10 were waited for; matrix products, arithmetic and copies ran while one was open for 2% of the time, Pallas kernels for 10%

profile of v5, /device:TPU:96, one launch (start us, length us, event | category | flops | bytes accessed | tf_op | source)
XLA Modules:
  0.0 120.0 jit_solution(12780888120811308501)
XLA Ops:
  6.5 0.1 pad_add_fusion.position_ref
  6.6 4.2 %prepare.1 = bf16[32,32,512]{2,1,0:T(8,128)(2,1)} custom-call(s32[4]{0:T(128)S(1)} %pad_add_fusion.position_ref, s32[4,7]{1,0:T(4,128)} %keep_ref.3, bf16[4,7,128,128]{3,2,1,0:T(8,128)(2,1)} %blocks_ref.2), custom_call_target="tpu_custom_call" | custom-call | tf_op jit(solution)/shard_map/prepare/pallas_call | solution.py:87
  10.8 7.3 %all-to-all-start.1 = ((bf16[32,32,512]{2,1,0:T(8,128)(2,1)}), bf16[32,32,512]{2,1,0:T(8,128)(2,1)S(1)}, u32[]{:S(2)}, u32[]{:S(2)}) async-start(bf16[32,32,512]{2,1,0:T(8,128)(2,1)} %prepare.1), calls=%async_computation.2 | async-start | bytes 2097152 | tf_op jit(solution)/shard_map/all_to_all | solution.py:635
  18.1 0.0 all-gather.6.cloned.1.call-start
  18.2 0.9 copy.101
  19.1 0.3 reshape.214
  19.4 0.1 reshape.215
  19.5 0.1 reshape.216.entries_ref
  19.6 0.9 copy.103.columns_ref
  20.4 2.4 %turn.1 = bf16[4,7,128,128]{3,2,1,0:T(8,128)(2,1)} custom-call(s32[4,7]{1,0:T(4,128)} %keep_ref.3, bf16[4,7,128,128]{3,2,1,0:T(8,128)(2,1)} %blocks_ref.2), custom_call_target="tpu_custom_call" | custom-call | flops 117440512 | bytes 1835008 | tf_op jit(solution)/shard_map/turn/pallas_call | solution.py:108
  22.8 2.5 %pattern.1 = (s32[256,256]{1,0:T(8,128)S(1)}, f32[128,256]{1,0:T(8,128)S(1)}, f32[128,1024]{1,0:T(8,128)S(1)}, f32[8,1024]{1,0:T(8,128)S(1)}) custom-call(s32[4]{0:T(128)S(1)} %pad_add_fusion.position_ref, s32[256,28]{1,0:T(8,128)S(1)} %copy.103.columns_ref, s32[1,1024]{1,0:T(1,128)S(1)} %reshape.216.entries_ref), custom_call_target="tpu_custom_call" | custom-call | flops 234881024 | bytes 524288 | tf_op jit(solution)/shard_map/pattern/pallas_call | solution.py:361
  25.3 10.1 %all-to-all-done.1 = bf16[32,32,512]{2,1,0:T(8,128)(2,1)S(1)} async-done(((bf16[32,32,512]{2,1,0:T(8,128)(2,1)}), bf16[32,32,512]{2,1,0:T(8,128)(2,1)S(1)}, u32[]{:S(2)}, u32[]{:S(2)}) %all-to-all-start.1) | async-done | bytes 1048608 | tf_op jit(solution)/shard_map/all_to_all | solution.py:635
  35.5 0.0 all-gather.6.cloned.1.call-update
  35.5 3.2 %send.1 = (bf16[128,512]{1,0:T(8,128)(2,1)S(1)}, bf16[128,512]{1,0:T(8,128)(2,1)S(1)}, bf16[128,512]{1,0:T(8,128)(2,1)S(1)}, bf16[128,512]{1,0:T(8,128)(2,1)S(1)...) custom-call(s32[4]{0:T(128)S(1)} %pad_add_fusion.position_ref, ...), custom_call_target="tpu_custom_call" | custom-call | tf_op jit(solution)/shard_map/send/pallas_call | solution.py:416
  38.7 4.1 %collective-permute-start = (bf16[128,512]{1,0:T(8,128)(2,1)S(1)}, bf16[128,512]{1,0:T(8,128)(2,1)S(1)}, u32[]{:S(2)}, u32[]{:S(2)}) collective-permute-start(bf16[128,512]{1,0:T(8,128)(2,1)S(1)} %get-tuple-element.78), channel_id=1, source_target_pairs={{0,24},{8,32},{16,40},{24,48},{32,56},{40,0},{48,8},{56,16},{1,25}... | collective-permute-start | bytes 393224 | tf_op jit(solution)/shard_map/ppermute | solution.py:642
  42.8 0.0 collective-permute-start.1
  42.8 4.3 %collective-permute-start.2 = (bf16[128,512]{1,0:T(8,128)(2,1)S(1)}, bf16[128,512]{1,0:T(8,128)(2,1)S(1)}, u32[]{:S(2)}, u32[]{:S(2)}) collective-permute-start(bf16[128,512]{1,0:T(8,128)(2,1)S(1)} %get-tuple-element.80), channel_id=1, source_target_pairs={{0,32},{8,40},{16,48},{24,56},{32,0},{40,8},{48,16},{56,24},{1,33}... | collective-permute-start | bytes 393224 | tf_op jit(solution)/shard_map/ppermute | solution.py:642
  47.1 0.8 collective-permute-start.3
  48.0 2.1 %collective-permute-start.4 = (bf16[128,512]{1,0:T(8,128)(2,1)S(1)}, bf16[128,512]{1,0:T(8,128)(2,1)S(1)}, u32[]{:S(2)}, u32[]{:S(2)}) collective-permute-start(bf16[128,512]{1,0:T(8,128)(2,1)S(1)} %get-tuple-element.82), channel_id=1, source_target_pairs={{0,48},{8,56},{16,0},{24,8},{32,16},{40,24},{48,32},{56,40},{1,49}... | collective-permute-start | bytes 393224 | tf_op jit(solution)/shard_map/ppermute | solution.py:642
  50.0 2.5 %collective-permute-done.refs_1_ = bf16[128,512]{1,0:T(8,128)(2,1)S(1)} collective-permute-done((bf16[128,512]{1,0:T(8,128)(2,1)S(1)}, bf16[128,512]{1,0:T(8,128)(2,1)S(1)}, u32[]{:S(2)}, u32[]{:S(2)}) %collective-permute-start) | collective-permute-done | bytes 131104 | tf_op jit(solution)/shard_map/ppermute | solution.py:642
  52.5 3.5 %collective-permute-start.5 = (bf16[128,512]{1,0:T(8,128)(2,1)S(1)}, bf16[128,512]{1,0:T(8,128)(2,1)S(1)}, u32[]{:S(2)}, u32[]{:S(2)}) collective-permute-start(bf16[128,512]{1,0:T(8,128)(2,1)S(1)} %get-tuple-element.83), channel_id=1, source_target_pairs={{0,8},{8,16},{16,24},{24,32},{32,40},{40,48},{48,56},{56,0},{1,9},... | collective-permute-start | bytes 393224 | tf_op jit(solution)/shard_map/ppermute | solution.py:642
  56.0 3.5 %collective-permute-done.1.refs_2_ = bf16[128,512]{1,0:T(8,128)(2,1)S(1)} collective-permute-done((bf16[128,512]{1,0:T(8,128)(2,1)S(1)}, bf16[128,512]{1,0:T(8,128)(2,1)S(1)}, u32[]{:S(2)}, u32[]{:S(2)}) %collective-permute-start.1) | collective-permute-done | bytes 131104 | tf_op jit(solution)/shard_map/ppermute | solution.py:642
  59.5 0.9 collective-permute-start.6
  60.4 0.3 collective-permute-done.2.refs_3_
  60.7 3.1 %collective-permute-done.3.refs_4_ = bf16[128,512]{1,0:T(8,128)(2,1)S(1)} collective-permute-done((bf16[128,512]{1,0:T(8,128)(2,1)S(1)}, bf16[128,512]{1,0:T(8,128)(2,1)S(1)}, u32[]{:S(2)}, u32[]{:S(2)}) %collective-permute-start.3) | collective-permute-done | bytes 131104 | tf_op jit(solution)/shard_map/ppermute | solution.py:642
  63.7 4.1 %collective-permute-done.4.refs_5_ = bf16[128,512]{1,0:T(8,128)(2,1)S(1)} collective-permute-done((bf16[128,512]{1,0:T(8,128)(2,1)S(1)}, bf16[128,512]{1,0:T(8,128)(2,1)S(1)}, u32[]{:S(2)}, u32[]{:S(2)}) %collective-permute-start.4) | collective-permute-done | bytes 131104 | tf_op jit(solution)/shard_map/ppermute | solution.py:642
  67.8 0.0 collective-permute-done.5.refs_6_
  67.8 2.1 %collective-permute-done.6.refs_7_ = bf16[128,512]{1,0:T(8,128)(2,1)S(1)} collective-permute-done((bf16[128,512]{1,0:T(8,128)(2,1)S(1)}, bf16[128,512]{1,0:T(8,128)(2,1)S(1)}, u32[]{:S(2)}, u32[]{:S(2)}) %collective-permute-start.6) | collective-permute-done | bytes 131104 | tf_op jit(solution)/shard_map/ppermute | solution.py:642
  69.8 2.3 %route.1 = bf16[8,120,512]{2,1,0:T(8,128)(2,1)} custom-call(bf16[128,512]{1,0:T(8,128)(2,1)S(1)} %get-tuple-element.87.refs_0_, bf16[128,512]{1,0:T(8,128)(2,1)S(1)} %collective-permute-done.refs_1_, bf16[128,512]{1,0:T(8,128)(2,1)S(1)} %collective-permute-done.1.refs_2_, bf16[128,512]{1,0:T(8,128)(2,1)S(1)} %collective-permute-done.2.refs_3_, ...), custom_call_target="tpu_custom_call" | custom-call | tf_op jit(solution)/shard_map/route/pallas_call | solution.py:458
  72.1 3.6 %all-to-all-start.2 = ((bf16[8,120,512]{2,1,0:T(8,128)(2,1)}), bf16[8,120,512]{2,1,0:T(8,128)(2,1)S(1)}, u32[]{:S(2)}, u32[]{:S(2)}) async-start(bf16[8,120,512]{2,1,0:T(8,128)(2,1)} %route.1), calls=%async_computation.3 | async-start | bytes 1966080 | tf_op jit(solution)/shard_map/all_to_all | solution.py:647
  75.7 0.8 own_plan.1.plan_ref.own_ref
  76.6 1.6 %far_plan.1.plan_ref = s32[8,128]{1,0:T(8,128)S(1)} custom-call(s32[4]{0:T(128)S(1)} %pad_add_fusion.position_ref, f32[128,256]{1,0:T(8,128)S(1)} %get-tuple-element.86.union_ref, bf16[128,512]{1,0:T(8,128)(2,1)S(1)} %get-tuple-element.87.refs_0_, bf16[128,512]{1,0:T(8,128)(2,1)S(1)} %collective-permute-done.refs_1_, ...), custom_call_target="tpu_custom_call" | custom-call | flops 671088640 | bytes 524288 | tf_op jit(solution)/shard_map/far_plan/pallas_call | solution.py:571
  78.1 0.5 slice.51
  79.2 1.1 all-gather.6.cloned.1.call-done
  80.3 0.0 copy-start
  80.3 2.0 %copy-done = bf16[16,7,128,128]{3,2,1,0:T(8,128)(2,1)S(1)} copy-done((bf16[16,7,128,128]{3,2,1,0:T(8,128)(2,1)S(1)}, bf16[16,7,128,128]{3,2,1,0:T(8,128)(2,1)}, u32[]{:S(2)}) %copy-start) | copy-done | bytes 3670040
  82.4 2.2 %own_sums.1.near_ref = f32[112,32,128]{2,1,0:T(8,128)S(1)} custom-call(s32[16,128]{1,0:T(8,128)S(1)} %own_plan.1.plan_ref.own_ref, bf16[112,128,128]{2,1,0:T(8,128)(2,1)S(1)} %bitcast.151), custom_call_target="tpu_custom_call" | custom-call | flops 536870912 | bytes 5505024 | tf_op jit(solution)/shard_map/own_sums/pallas_call | solution.py:162
  84.6 6.3 %all-to-all-done.2 = bf16[8,120,512]{2,1,0:T(8,128)(2,1)S(1)} async-done(((bf16[8,120,512]{2,1,0:T(8,128)(2,1)}), bf16[8,120,512]{2,1,0:T(8,128)(2,1)S(1)}, u32[]{:S(2)}, u32[]{:S(2)}) %all-to-all-start.2) | async-done | bytes 983072 | tf_op jit(solution)/shard_map/all_to_all | solution.py:647
  90.9 8.0 %far_sums.1 = (bf16[28,32,128]{2,1,0:T(8,128)(2,1)S(1)}, bf16[28,32,128]{2,1,0:T(8,128)(2,1)}, bf16[28,32,128]{2,1,0:T(8,128)(2,1)S(1)}, bf16[28,32,128]{2,1,0:T(8,128)(2,1)S(1)}) custom-call(s32[16,128]{1,0:T(8,128)S(1)} %own_plan.1.plan_ref.own_ref, s32[8,128]{1,0:T(8,128)S(1)} %far_plan.1.plan_ref, bf16[112,128,128]{2,1,0:T(8,128)(2,1)} %bitcast.150, ...), custom_call_target="tpu_custom_call" | custom-call | tf_op jit(solution)/shard_map/far_sums/pallas_call | solution.py:253
  98.9 0.1 collective-permute-start.7
  99.0 3.2 %collective-permute-start.8 = (bf16[28,32,128]{2,1,0:T(8,128)(2,1)S(1)}, bf16[28,32,128]{2,1,0:T(8,128)(2,1)S(1)}, u32[]{:S(2)}, u32[]{:S(2)}) collective-permute-start(bf16[28,32,128]{2,1,0:T(8,128)(2,1)S(1)} %get-tuple-element.102), channel_id=1, source_target_pairs={{0,3},{1,0},{2,1},{3,2},{4,7},{5,4},{6,5},{7,6},{8,11},{9,8},{10,9... | collective-permute-start | bytes 688136 | tf_op jit(solution)/shard_map/ppermute | solution.py:656
  102.2 0.1 collective-permute-start.9
  102.2 9.0 %collective-permute-done.7.refs_1_ = bf16[28,32,128]{2,1,0:T(8,128)(2,1)S(1)} collective-permute-done((bf16[28,32,128]{2,1,0:T(8,128)(2,1)}, bf16[28,32,128]{2,1,0:T(8,128)(2,1)S(1)}, u32[]{:S(2)}, u32[]{:S(2)}) %collective-permute-start.7) | collective-permute-done | bytes 229408 | tf_op jit(solution)/shard_map/ppermute | solution.py:656
  111.3 0.0 collective-permute-done.8.refs_2_
  111.3 0.0 collective-permute-done.9.refs_3_
  111.3 1.9 %finish.1 = bf16[4,7,128,128]{3,2,1,0:T(8,128)(2,1)} custom-call(s32[4]{0:T(128)S(1)} %pad_add_fusion.position_ref, bf16[28,32,128]{2,1,0:T(8,128)(2,1)S(1)} %get-tuple-element.100.refs_0_, bf16[28,32,128]{2,1,0:T(8,128)(2,1)S(1)} %collective-permute-done.7.refs_1_, bf16[28,32,128]{2,1,0:T(8,128)(2,1)S(1)} %collective-permute-done.8.refs_2_, ...), custom_call_target="tpu_custom_call" | custom-call | tf_op jit(solution)/shard_map/finish/pallas_call | solution.py:280
  (4 shorter events, 0.0 us)
Async XLA Ops:
  10.8 24.7 %all-to-all-start.1 = ((bf16[32,32,512]{2,1,0:T(8,128)(2,1)}), bf16[32,32,512]{2,1,0:T(8,128)(2,1)S(1)}, u32[]{:S(2)}, u32[]{:S(2)}) async-start(bf16[32,32,512]{2,1,0:T(8,128)(2,1)} %prepare.1), calls=%async_computation.2 | async-start | bytes 2097152 | tf_op jit(solution)/shard_map/all_to_all | solution.py:635
  18.1 62.2 %all-gather.6.cloned.1.call-start = ((), (), s32[]{:S(2)}) async-start(), calls=%async_computation.6 | async-start | bytes 4587520 | tf_op jit(solution)/shard_map/all_gather | solution.py:637
  38.7 13.8 %collective-permute-start = (bf16[128,512]{1,0:T(8,128)(2,1)S(1)}, bf16[128,512]{1,0:T(8,128)(2,1)S(1)}, u32[]{:S(2)}, u32[]{:S(2)}) collective-permute-start(bf16[128,512]{1,0:T(8,128)(2,1)S(1)} %get-tuple-element.78), channel_id=1, source_target_pairs={{0,24},{8,32},{16,40},{24,48},{32,56},{40,0},{48,8},{56,16},{1,25}... | collective-permute-start | bytes 393224 | tf_op jit(solution)/shard_map/ppermute | solution.py:642
  42.8 16.7 %collective-permute-start.1 = (bf16[128,512]{1,0:T(8,128)(2,1)S(1)}, bf16[128,512]{1,0:T(8,128)(2,1)S(1)}, u32[]{:S(2)}, u32[]{:S(2)}) collective-permute-start(bf16[128,512]{1,0:T(8,128)(2,1)S(1)} %get-tuple-element.79), channel_id=1, source_target_pairs={{0,40},{8,48},{16,56},{24,0},{32,8},{40,16},{48,24},{56,32},{1,41}... | collective-permute-start | bytes 393224 | tf_op jit(solution)/shard_map/ppermute | solution.py:642
  42.8 17.8 %collective-permute-start.2 = (bf16[128,512]{1,0:T(8,128)(2,1)S(1)}, bf16[128,512]{1,0:T(8,128)(2,1)S(1)}, u32[]{:S(2)}, u32[]{:S(2)}) collective-permute-start(bf16[128,512]{1,0:T(8,128)(2,1)S(1)} %get-tuple-element.80), channel_id=1, source_target_pairs={{0,32},{8,40},{16,48},{24,56},{32,0},{40,8},{48,16},{56,24},{1,33}... | collective-permute-start | bytes 393224 | tf_op jit(solution)/shard_map/ppermute | solution.py:642
  47.1 16.6 %collective-permute-start.3 = (bf16[128,512]{1,0:T(8,128)(2,1)S(1)}, bf16[128,512]{1,0:T(8,128)(2,1)S(1)}, u32[]{:S(2)}, u32[]{:S(2)}) collective-permute-start(bf16[128,512]{1,0:T(8,128)(2,1)S(1)} %get-tuple-element.81), channel_id=1, source_target_pairs={{0,16},{8,24},{16,32},{24,40},{32,48},{40,56},{48,0},{56,8},{1,17}... | collective-permute-start | bytes 393224 | tf_op jit(solution)/shard_map/ppermute | solution.py:642
  48.0 19.8 %collective-permute-start.4 = (bf16[128,512]{1,0:T(8,128)(2,1)S(1)}, bf16[128,512]{1,0:T(8,128)(2,1)S(1)}, u32[]{:S(2)}, u32[]{:S(2)}) collective-permute-start(bf16[128,512]{1,0:T(8,128)(2,1)S(1)} %get-tuple-element.82), channel_id=1, source_target_pairs={{0,48},{8,56},{16,0},{24,8},{32,16},{40,24},{48,32},{56,40},{1,49}... | collective-permute-start | bytes 393224 | tf_op jit(solution)/shard_map/ppermute | solution.py:642
  52.5 15.2 %collective-permute-start.5 = (bf16[128,512]{1,0:T(8,128)(2,1)S(1)}, bf16[128,512]{1,0:T(8,128)(2,1)S(1)}, u32[]{:S(2)}, u32[]{:S(2)}) collective-permute-start(bf16[128,512]{1,0:T(8,128)(2,1)S(1)} %get-tuple-element.83), channel_id=1, source_target_pairs={{0,8},{8,16},{16,24},{24,32},{32,40},{40,48},{48,56},{56,0},{1,9},... | collective-permute-start | bytes 393224 | tf_op jit(solution)/shard_map/ppermute | solution.py:642
  59.5 10.3 %collective-permute-start.6 = (bf16[128,512]{1,0:T(8,128)(2,1)S(1)}, bf16[128,512]{1,0:T(8,128)(2,1)S(1)}, u32[]{:S(2)}, u32[]{:S(2)}) collective-permute-start(bf16[128,512]{1,0:T(8,128)(2,1)S(1)} %get-tuple-element.84), channel_id=1, source_target_pairs={{0,56},{8,0},{16,8},{24,16},{32,24},{40,32},{48,40},{56,48},{1,57}... | collective-permute-start | bytes 393224 | tf_op jit(solution)/shard_map/ppermute | solution.py:642
  72.1 18.7 %all-to-all-start.2 = ((bf16[8,120,512]{2,1,0:T(8,128)(2,1)}), bf16[8,120,512]{2,1,0:T(8,128)(2,1)S(1)}, u32[]{:S(2)}, u32[]{:S(2)}) async-start(bf16[8,120,512]{2,1,0:T(8,128)(2,1)} %route.1), calls=%async_computation.3 | async-start | bytes 1966080 | tf_op jit(solution)/shard_map/all_to_all | solution.py:647
  80.3 2.0 %copy-start = (bf16[16,7,128,128]{3,2,1,0:T(8,128)(2,1)S(1)}, bf16[16,7,128,128]{3,2,1,0:T(8,128)(2,1)}, u32[]{:S(2)}) copy-start(bf16[16,7,128,128]{3,2,1,0:T(8,128)(2,1)} %all-gather.6.cloned.1.call-done) | copy-start | bytes 11010052
  98.9 12.3 %collective-permute-start.7 = (bf16[28,32,128]{2,1,0:T(8,128)(2,1)}, bf16[28,32,128]{2,1,0:T(8,128)(2,1)S(1)}, u32[]{:S(2)}, u32[]{:S(2)}) collective-permute-start(bf16[28,32,128]{2,1,0:T(8,128)(2,1)} %get-tuple-element.101), channel_id=1, source_target_pairs={{0,1},{1,2},{2,3},{3,0},{4,5},{5,6},{6,7},{7,4},{8,9},{9,10},{10,1... | collective-permute-start | bytes 688136 | tf_op jit(solution)/shard_map/ppermute | solution.py:656
  99.0 12.3 %collective-permute-start.8 = (bf16[28,32,128]{2,1,0:T(8,128)(2,1)S(1)}, bf16[28,32,128]{2,1,0:T(8,128)(2,1)S(1)}, u32[]{:S(2)}, u32[]{:S(2)}) collective-permute-start(bf16[28,32,128]{2,1,0:T(8,128)(2,1)S(1)} %get-tuple-element.102), channel_id=1, source_target_pairs={{0,3},{1,0},{2,1},{3,2},{4,7},{5,4},{6,5},{7,6},{8,11},{9,8},{10,9... | collective-permute-start | bytes 688136 | tf_op jit(solution)/shard_map/ppermute | solution.py:656
  102.2 9.1 %collective-permute-start.9 = (bf16[28,32,128]{2,1,0:T(8,128)(2,1)S(1)}, bf16[28,32,128]{2,1,0:T(8,128)(2,1)S(1)}, u32[]{:S(2)}, u32[]{:S(2)}) collective-permute-start(bf16[28,32,128]{2,1,0:T(8,128)(2,1)S(1)} %get-tuple-element.103), channel_id=1, source_target_pairs={{0,2},{1,3},{2,0},{3,1},{4,6},{5,7},{6,4},{7,5},{8,10},{9,11},{10,... | collective-permute-start | bytes 688136 | tf_op jit(solution)/shard_map/ppermute | solution.py:656
Sparse Core Ops, SparseCore 0:
  35.6 44.6 all-gather.5

commit v6 on v5

--- a/solution.py
+++ b/solution.py
@@ -62,25 +62,24 @@
             number = row * QUARTER + slot
             keep = keep_ref[row, slot] != 0
             flags = jnp.where((lanes == number) & keep, 1.0, flags)
-            block = blocks_ref[row, slot]
-            turned = jnp.where(keep, block, jnp.zeros_like(block)).T.astype(F32)
+            block = blocks_ref[row, slot].astype(F32)
+            rows_ref[number] = jnp.where(keep, block, jnp.zeros_like(block)).T
+    for part_of in range(NY):
+        for extra in range(HELD - SLOTS):
+            at = extra * PIECE + part_of * SIDE
+            value = flags[:, at : at + SIDE] if extra < 2 else jnp.zeros((8, SIDE), F32)
             for quarter in range(NY):
-                for part_of in range(NY):
-                    begin = quarter * WIDE + part_of * TARGETS
-                    rows = pl.ds(quarter * TARGETS * HELD + number, TARGETS, stride=HELD)
-                    rows_ref[part_of, rows, :] = turned[begin : begin + TARGETS]
-    for begin in range(0, PEERS, 8):
+                begin = quarter * WIDE + part_of * TARGETS
+                rows_ref[SLOTS + extra, begin : begin + TARGETS] = value
+    for quarter in range(NY):
+        peers = slice(quarter * TARGETS, (quarter + 1) * TARGETS)
         for part_of in range(NY):
-            for extra in range(HELD - SLOTS):
-                rows = pl.ds(begin * HELD + SLOTS + extra, 8, stride=HELD)
-                at = extra * PIECE + part_of * SIDE
-                value = flags[:, at : at + SIDE] if extra < 2 else jnp.zeros((8, SIDE), F32)
-                rows_ref[part_of, rows, :] = value
-    for peer in range(PEERS):
-        rows = pl.ds(peer * HELD, HELD)
-        cuts_ref[peer] = jnp.concatenate(
-            [rows_ref[part_of, rows, :] for part_of in range(NY)], axis=1
-        ).astype(BF)
+            begin = quarter * WIDE + part_of * TARGETS
+            for half in range(0, HELD, 16):
+                rows = rows_ref[half : half + 16, begin : begin + TARGETS]
+                cuts_ref[peers, half : half + 16, part_of * SIDE : (part_of + 1) * SIDE] = (
+                    jnp.swapaxes(rows, 0, 1).astype(BF)
+                )
 
 
 def prepare(position, nonzero, blocks):
@@ -89,7 +88,7 @@
         out_shape=jax.ShapeDtypeStruct((PEERS, HELD, PIECE), BF),
         in_specs=[smem(), smem(), vmem()],
         out_specs=vmem(),
-        scratch_shapes=[pltpu.VMEM((NY, ENTRIES, SIDE), F32)],
+        scratch_shapes=[pltpu.VMEM((HELD, SIDE, SIDE), F32)],
         compiler_params=params(),
         name="prepare",
     )(position, nonzero, blocks)
@@ -196,23 +195,23 @@
 
     lax.fori_loop(0, own_ref[15, 1], clear, 0)
 
-    def product(named, offset):
-        begin = plan_ref[2, named]
-        length = plan_ref[3, named]
+    def product(step):
+        begin = plan_ref[2, step]
+        length = plan_ref[3, step]
         right = jnp.concatenate(
             [
-                own_block(whole_ref, own_ref[member, named], pl.ds(0, SIDE))
+                own_block(whole_ref, plan_ref[4 + member, step], pl.ds(0, SIDE))
                 for member in range(HEIGHT)
             ],
             axis=1,
         )
         pieces, columns = [], []
         for at in range(FAR_GROUP):
-            place = jnp.minimum(begin + offset + at, CAP_X - 1)
+            place = jnp.minimum(begin + at, CAP_X - 1)
             rows = pl.ds(plan_ref[0, place], TARGETS, stride=CAP_X)
             for part in range(NY):
                 pieces.append(pieces_ref[part, rows, :])
-            columns.append(jnp.where(offset + at < length, plan_ref[1, place], OUT_COLS))
+            columns.append(jnp.where(at < length, plan_ref[1, place], OUT_COLS))
         left = jnp.concatenate(pieces, axis=0).astype(BF)
         return jnp.dot(left, right, preferred_element_type=F32), columns
 
@@ -220,24 +219,13 @@
         for at, column in enumerate(columns):
             total[column] = total[column] + value[at * WIDE : (at + 1) * WIDE]
 
-    def first_step(step, carry):
-        done = [product(step * ROWS_AT_ONCE + at, 0) for at in range(ROWS_AT_ONCE)]
+    def steps(number, carry):
+        done = [product(number * ROWS_AT_ONCE + at) for at in range(ROWS_AT_ONCE)]
         for value, columns in done:
             add(value, columns)
         return carry
 
-    named_rows = own_ref[15, 2]
-    lax.fori_loop(0, (named_rows + ROWS_AT_ONCE - 1) // ROWS_AT_ONCE, first_step, 0)
-
-    def rest(named, carry):
-        def rest_step(step, inner_carry):
-            add(*product(named, step * FAR_GROUP))
-            return inner_carry
-
-        lax.fori_loop(1, (plan_ref[3, named] + FAR_GROUP - 1) // FAR_GROUP, rest_step, 0)
-        return carry
-
-    lax.fori_loop(0, named_rows, rest, 0)
+    lax.fori_loop(0, (plan_ref[8, 0] + ROWS_AT_ONCE - 1) // ROWS_AT_ONCE, steps, 0)
 
     for step, out_ref in enumerate(out_refs):
         part = (own_ref[15, 0] + step) & (NY - 1)
@@ -469,29 +457,25 @@
     )(*along)
 
 
+def own_places(position_ref, slots_ref):
+    chip = position_ref[0] * NZ + position_ref[1]
+    both = slots_ref[pl.ds(pl.multiple_of(chip * HEIGHT_2, HEIGHT_2), HEIGHT_2), :]
+    swapped = jnp.concatenate([both[HEIGHT:], both[:HEIGHT]], axis=0)
+    slot = jnp.where(position_ref[2] == 0, both, swapped)
+    quarter = quarter_of(slot)
+    held = (quarter * HEIGHT + iota(slot.shape, 0)) * QUARTER + slot - quarter * QUARTER
+    return slot, jnp.where(slot >= 0, held - ZERO_BLOCK, 0).astype(F32)
+
+
 def own_plan_kernel(position_ref, slots_ref, union_ref, out_ref):
     x, z, core, part = (position_ref[i] for i in range(4))
-    chip = x * NZ + z
-    slab = chip * NC + core
+    slab = (x * NZ + z) * NC + core
     order = earlier(ROWS)
     out_ref[...] = jnp.zeros_like(out_ref)
     mine = union_ref[pl.ds(slab, 1), :]
     rank = dot(jnp.broadcast_to(mine, (8, ROWS)), order)
 
-    both = slots_ref[pl.ds(pl.multiple_of(chip * HEIGHT_2, HEIGHT_2), HEIGHT_2), :]
-    swapped = jnp.concatenate([both[HEIGHT:], both[:HEIGHT]], axis=0)
-    slot = jnp.where(core == 0, both, swapped)
-    quarter = quarter_of(slot)
-    held = (quarter * HEIGHT + iota(slot.shape, 0)) * QUARTER + slot - quarter * QUARTER
-    held = jnp.where(slot >= 0, held - ZERO_BLOCK, 0).astype(F32)
-
-    every = iota((1, ROWS), 1)
-    named = jnp.where(every // HEIGHT == slab, 0.0, mine)
-    position = dot(jnp.broadcast_to(named, (8, ROWS)), order)[0:1]
-    number = iota((SLABS, ROWS), 0).astype(F32)
-    chosen = ((position == number) & (named > 0)).astype(F32)
-    out_ref[0:4, 0:SLABS] = dot_rows(held, chosen)[0:HEIGHT].astype(I32) + ZERO_BLOCK
-
+    slot, held = own_places(position_ref, slots_ref)
     number = iota((OUT_COLS, ROWS), 0).astype(F32)
     chosen = ((rank[0:1] == number) & (mine > 0)).astype(F32)
     out_ref[4:8, 0:OUT_COLS] = dot_rows(held, chosen)[0:HEIGHT].astype(I32) + ZERO_BLOCK
@@ -505,8 +489,7 @@
     groups = ((jnp.sum(mine) + (GROUP - 1)) * (1.0 / GROUP)).astype(I32)
     lane = iota((1, 128), 1)
     scalars = jnp.where(lane == 0, part, 0)
-    scalars = jnp.where(lane == 1, groups, scalars)
-    out_ref[15:16, :] = jnp.where(lane == 2, jnp.sum(named).astype(I32), scalars)
+    out_ref[15:16, :] = jnp.where(lane == 1, groups, scalars)
 
 
 def own_plan(position, slots, union):
@@ -521,7 +504,7 @@
     )(position, slots, union)
 
 
-def far_plan_kernel(position_ref, union_ref, *refs):
+def far_plan_kernel(position_ref, slots_ref, union_ref, *refs):
     *along_refs, out_ref = refs
     x, z, core = (position_ref[i] for i in range(3))
     slab = (x * NZ + z) * NC + core
@@ -553,30 +536,40 @@
 
     valid = iota((SIDE, ROWS), 0) < number
     count = dot(jnp.ones((8, SIDE), F32), ((every == row_down) & valid).astype(F32))
-    start = jnp.minimum(dot(count, order), 250.0)
-    row = jnp.where(iota((1, ROWS), 1) // HEIGHT == slab, 0.0, names)
-    position = dot(jnp.broadcast_to(row, (8, ROWS)), order)[0:1]
-    chosen = ((position == iota((SLABS, ROWS), 0).astype(F32)) & (row > 0)).astype(F32)
-    out_ref[2:3, 0:SLABS] = dot_rows(start, chosen)[0:1].astype(I32)
-    out_ref[3:4, 0:SLABS] = dot_rows(count, chosen)[0:1].astype(I32)
+    start = jnp.minimum(dot(count, order), 250.0)[0:1]
+    _, held = own_places(position_ref, slots_ref)
+    needed = ((count + (FAR_GROUP - 1)) * (1.0 / FAR_GROUP)).astype(I32).astype(F32)
+    first = dot(needed, order)[0:1]
+    number = iota((SIDE, ROWS), 0).astype(F32)
+    chosen = ((first <= number) & (number < first + needed[0:1])).astype(F32)
+    kind = iota((8, ROWS), 0)
+    values = jnp.where(kind == 0, start, jnp.where(kind == 1, first, count))
+    values = dot_rows(values, chosen).astype(I32)
+    done = (iota((1, SIDE), 1) - values[1:2]) * FAR_GROUP
+    steps = jnp.sum(needed[0:1]).astype(I32)
+    valid = iota((1, SIDE), 1) < steps
+    out_ref[2:3, :] = jnp.where(valid, values[0:1] + done, 0)
+    out_ref[3:4, :] = jnp.where(valid, values[2:3] - done, 0)
+    out_ref[4:8, :] = dot_rows(held, chosen)[0:HEIGHT].astype(I32) + ZERO_BLOCK
+    out_ref[8:9, :] = jnp.zeros((1, SIDE), I32) + jnp.minimum(steps, SIDE)
 
     third = functools.reduce(jnp.maximum, third), functools.reduce(jnp.add, third)
     most_z = jnp.max(third[0][:, 3 * SIDE :])
     most_x = jnp.max(third[1][:, 2 * SIDE : 3 * SIDE])
     fits = (most_x <= CAP_X) & (most_z <= CAP_Z)
-    out_ref[4:5, :] = jnp.zeros((1, SIDE), I32) + fits.astype(I32)
-
-
-def far_plan(position, union, along):
+    out_ref[9:10, :] = jnp.zeros((1, SIDE), I32) + fits.astype(I32)
+
+
+def far_plan(position, slots, union, along):
     return pl.pallas_call(
         far_plan_kernel,
-        out_shape=jax.ShapeDtypeStruct((8, 128), I32),
-        in_specs=[smem()] + [vmem()] * (1 + NZ),
+        out_shape=jax.ShapeDtypeStruct((16, 128), I32),
+        in_specs=[smem()] + [vmem()] * (2 + NZ),
         out_specs=vmem(),
         compiler_params=params(),
         cost_estimate=cost(2 * 20 * ROWS**3, 8 * ROWS**2),
         name="far_plan",
-    )(position, union, *along)
+    )(position, slots, union, *along)
 
 
 def dense(blocks, nonzero, columns):
@@ -633,7 +626,6 @@
     turned = turn(nonzero, same)
     slots, union, need, kq = pattern(position, names, plane_columns(columns))
     near = lax.all_to_all(cuts, ("col", "x", "core"), split_axis=0, concat_axis=0, tiled=True)
-    near, turned, need = lax.optimization_barrier((near, turned, need))
     whole = lax.all_gather(turned, "col", axis=0, tiled=False)
     whole = whole.reshape(ZERO_BLOCK, SIDE, SIDE)
     packed = send(position, need, kq, near.reshape(ENTRIES, PIECE))
@@ -645,10 +637,10 @@
     own_lists = own_plan(position, slots, union)
     packed, notes = lax.optimization_barrier((route(along), along))
     far = lax.all_to_all(packed, ("x", "core"), split_axis=0, concat_axis=0, tiled=True)
-    far_lists = far_plan(position, union, notes)
+    far_lists = far_plan(position, slots, union, notes)
     far = far.reshape(TARGETS * CAP_X, PIECE)
     own = own_sums(own_lists, whole)
-    far, fits, own = lax.optimization_barrier((far, far_lists[4, 0] != 0, own))
+    far, fits, own = lax.optimization_barrier((far, far_lists[9, 0] != 0, own))
     result = far_sums(own_lists, far_lists, whole, far, own)
     cuts = [result[0]]
     for step in ORDER_Y:

time: 121 us -> 121 us (level)
  the two profiles are of different devices: /device:TPU:96 before, /device:TPU:1 now
where the time goes in v6:
time: 121 us; the launch traced here: 120 us
  waiting for transfers between devices  40.5 us (33%)
  starting transfers between devices  34.2 us (28%)
  Pallas kernels  25.9 us (21%)
  between operations  14.1 us (12%)
  local copies, waits for them, and re-layouts  4.83 us (4%)
    ppermute x7, starting transfers between devices, shards(): lax.ppermute(packed[step], 'z', [(i, (i + step) % NZ) for i in range(NZ)])  18.3 us
    all_to_all x1, waiting for transfers between devices, shards(): lax.all_to_all(cuts, ('col', 'x', 'core'), split_axis=0, concat_axis=0, t...  12.4 us
    ppermute x7, waiting for transfers between devices, shards(): lax.ppermute(packed[step], 'z', [(i, (i + step) % NZ) for i in range(NZ)])  12.3 us
    ppermute x3, waiting for transfers between devices, shards(): cuts.append(lax.ppermute(result[step], 'col', pairs))  9.23 us
    all_to_all x1, starting transfers between devices, shards(): lax.all_to_all(cuts, ('col', 'x', 'core'), split_axis=0, concat_axis=0, t...  8.6 us
    all_to_all x1, waiting for transfers between devices, shards(): lax.all_to_all(packed, ('x', 'core'), split_axis=0, concat_axis=0, tiled=...  6.46 us
    pallas_call x1, Pallas kernels, far_sums(): pl.pallas_call(far_kernel, out_shape=[jax.ShapeDtypeStruct((HEIGHT * QUAR...  6.13 us
    all_to_all x1, starting transfers between devices, shards(): lax.all_to_all(packed, ('x', 'core'), split_axis=0, concat_axis=0, tiled=...  4.62 us
  transfers between devices with their start and end apart: 13, of which 9 were waited for; matrix products, arithmetic and copies ran while one was open for 2% of the time, Pallas kernels for 8%

profile of v6, /device:TPU:1, one launch (start us, length us, event | category | flops | bytes accessed | tf_op | source)
XLA Modules:
  0.0 119.6 jit_solution(738141586909367202)
XLA Ops:
  6.5 0.0 all-gather.6.cloned.1.call-start
  6.5 0.1 pad_add_fusion.position_ref
  6.6 2.9 %prepare.1 = bf16[32,32,512]{2,1,0:T(8,128)(2,1)} custom-call(s32[4]{0:T(128)S(1)} %pad_add_fusion.position_ref, s32[4,7]{1,0:T(4,128)} %keep_ref.3, bf16[4,7,128,128]{3,2,1,0:T(8,128)(2,1)} %blocks_ref.2), custom_call_target="tpu_custom_call" | custom-call | tf_op jit(solution)/shard_map/prepare/pallas_call | solution.py:86
  9.5 2.4 %turn.1 = bf16[4,7,128,128]{3,2,1,0:T(8,128)(2,1)} custom-call(s32[4,7]{1,0:T(4,128)} %keep_ref.3, bf16[4,7,128,128]{3,2,1,0:T(8,128)(2,1)} %blocks_ref.2), custom_call_target="tpu_custom_call" | custom-call | flops 117440512 | bytes 1835008 | tf_op jit(solution)/shard_map/turn/pallas_call | solution.py:107
  11.9 0.0 copy-start.4
  11.9 0.0 copy-start.5
  11.9 0.0 all-gather.6.cloned.1.call-update
  11.9 8.6 %all-to-all-start.1 = ((bf16[32,32,512]{2,1,0:T(8,128)(2,1)}), bf16[32,32,512]{2,1,0:T(8,128)(2,1)S(1)}, u32[]{:S(2)}, u32[]{:S(2)}) async-start(bf16[32,32,512]{2,1,0:T(8,128)(2,1)} %prepare.1), calls=%async_computation.2 | async-start | bytes 2097152 | tf_op jit(solution)/shard_map/all_to_all | solution.py:628
  20.6 0.9 copy.101
  21.4 0.3 reshape.214
  21.7 0.1 reshape.215
  21.8 0.1 reshape.216.entries_ref
  21.9 0.9 copy.103.columns_ref
  22.8 2.5 %pattern.1 = (s32[256,256]{1,0:T(8,128)S(1)}, f32[128,256]{1,0:T(8,128)S(1)}, f32[128,1024]{1,0:T(8,128)S(1)}, f32[8,1024]{1,0:T(8,128)S(1)}) custom-call(s32[4]{0:T(128)S(1)} %pad_add_fusion.position_ref, s32[256,28]{1,0:T(8,128)S(1)} %copy.103.columns_ref, s32[1,1024]{1,0:T(1,128)S(1)} %reshape.216.entries_ref), custom_call_target="tpu_custom_call" | custom-call | flops 234881024 | bytes 524288 | tf_op jit(solution)/shard_map/pattern/pallas_call | solution.py:349
  25.3 12.4 %all-to-all-done.1 = bf16[32,32,512]{2,1,0:T(8,128)(2,1)S(1)} async-done(((bf16[32,32,512]{2,1,0:T(8,128)(2,1)}), bf16[32,32,512]{2,1,0:T(8,128)(2,1)S(1)}, u32[]{:S(2)}, u32[]{:S(2)}) %all-to-all-start.1) | async-done | bytes 1048608 | tf_op jit(solution)/shard_map/all_to_all | solution.py:628
  37.7 3.2 %send.1 = (bf16[128,512]{1,0:T(8,128)(2,1)S(1)}, bf16[128,512]{1,0:T(8,128)(2,1)S(1)}, bf16[128,512]{1,0:T(8,128)(2,1)S(1)}, bf16[128,512]{1,0:T(8,128)(2,1)S(1)...) custom-call(s32[4]{0:T(128)S(1)} %pad_add_fusion.position_ref, ...), custom_call_target="tpu_custom_call" | custom-call | tf_op jit(solution)/shard_map/send/pallas_call | solution.py:404
  41.0 4.4 %collective-permute-start = (bf16[128,512]{1,0:T(8,128)(2,1)S(1)}, bf16[128,512]{1,0:T(8,128)(2,1)S(1)}, u32[]{:S(2)}, u32[]{:S(2)}) collective-permute-start(bf16[128,512]{1,0:T(8,128)(2,1)S(1)} %get-tuple-element.72), channel_id=1, source_target_pairs={{0,24},{8,32},{16,40},{24,48},{32,56},{40,0},{48,8},{56,16},{1,25}... | collective-permute-start | bytes 393224 | tf_op jit(solution)/shard_map/ppermute | solution.py:634
  45.4 2.2 %collective-permute-start.1 = (bf16[128,512]{1,0:T(8,128)(2,1)S(1)}, bf16[128,512]{1,0:T(8,128)(2,1)S(1)}, u32[]{:S(2)}, u32[]{:S(2)}) collective-permute-start(bf16[128,512]{1,0:T(8,128)(2,1)S(1)} %get-tuple-element.73), channel_id=1, source_target_pairs={{0,40},{8,48},{16,56},{24,0},{32,8},{40,16},{48,24},{56,32},{1,41}... | collective-permute-start | bytes 393224 | tf_op jit(solution)/shard_map/ppermute | solution.py:634
  47.6 4.8 %collective-permute-start.2 = (bf16[128,512]{1,0:T(8,128)(2,1)S(1)}, bf16[128,512]{1,0:T(8,128)(2,1)S(1)}, u32[]{:S(2)}, u32[]{:S(2)}) collective-permute-start(bf16[128,512]{1,0:T(8,128)(2,1)S(1)} %get-tuple-element.74), channel_id=1, source_target_pairs={{0,32},{8,40},{16,48},{24,56},{32,0},{40,8},{48,16},{56,24},{1,33}... | collective-permute-start | bytes 393224 | tf_op jit(solution)/shard_map/ppermute | solution.py:634
  52.4 1.2 collective-permute-start.3
  53.6 2.4 %collective-permute-start.4 = (bf16[128,512]{1,0:T(8,128)(2,1)S(1)}, bf16[128,512]{1,0:T(8,128)(2,1)S(1)}, u32[]{:S(2)}, u32[]{:S(2)}) collective-permute-start(bf16[128,512]{1,0:T(8,128)(2,1)S(1)} %get-tuple-element.76), channel_id=1, source_target_pairs={{0,48},{8,56},{16,0},{24,8},{32,16},{40,24},{48,32},{56,40},{1,49}... | collective-permute-start | bytes 393224 | tf_op jit(solution)/shard_map/ppermute | solution.py:634
  56.0 0.0 collective-permute-done.refs_1_
  56.0 1.0 collective-permute-start.5
  57.0 0.0 collective-permute-done.1.refs_2_
  57.0 2.3 %collective-permute-start.6 = (bf16[128,512]{1,0:T(8,128)(2,1)S(1)}, bf16[128,512]{1,0:T(8,128)(2,1)S(1)}, u32[]{:S(2)}, u32[]{:S(2)}) collective-permute-start(bf16[128,512]{1,0:T(8,128)(2,1)S(1)} %get-tuple-element.78), channel_id=1, source_target_pairs={{0,56},{8,0},{16,8},{24,16},{32,24},{40,32},{48,40},{56,48},{1,57}... | collective-permute-start | bytes 393224 | tf_op jit(solution)/shard_map/ppermute | solution.py:634
  59.2 3.8 %collective-permute-done.2.refs_3_ = bf16[128,512]{1,0:T(8,128)(2,1)S(1)} collective-permute-done((bf16[128,512]{1,0:T(8,128)(2,1)S(1)}, bf16[128,512]{1,0:T(8,128)(2,1)S(1)}, u32[]{:S(2)}, u32[]{:S(2)}) %collective-permute-start.2) | collective-permute-done | bytes 131104 | tf_op jit(solution)/shard_map/ppermute | solution.py:634
  63.1 4.5 %collective-permute-done.3.refs_4_ = bf16[128,512]{1,0:T(8,128)(2,1)S(1)} collective-permute-done((bf16[128,512]{1,0:T(8,128)(2,1)S(1)}, bf16[128,512]{1,0:T(8,128)(2,1)S(1)}, u32[]{:S(2)}, u32[]{:S(2)}) %collective-permute-start.3) | collective-permute-done | bytes 131104 | tf_op jit(solution)/shard_map/ppermute | solution.py:634
  67.6 0.9 collective-permute-done.4.refs_5_
  68.5 1.4 %collective-permute-done.5.refs_6_ = bf16[128,512]{1,0:T(8,128)(2,1)S(1)} collective-permute-done((bf16[128,512]{1,0:T(8,128)(2,1)S(1)}, bf16[128,512]{1,0:T(8,128)(2,1)S(1)}, u32[]{:S(2)}, u32[]{:S(2)}) %collective-permute-start.5) | collective-permute-done | bytes 131104 | tf_op jit(solution)/shard_map/ppermute | solution.py:634
  69.8 1.7 %collective-permute-done.6.refs_7_ = bf16[128,512]{1,0:T(8,128)(2,1)S(1)} collective-permute-done((bf16[128,512]{1,0:T(8,128)(2,1)S(1)}, bf16[128,512]{1,0:T(8,128)(2,1)S(1)}, u32[]{:S(2)}, u32[]{:S(2)}) %collective-permute-start.6) | collective-permute-done | bytes 131104 | tf_op jit(solution)/shard_map/ppermute | solution.py:634
  71.5 2.3 %route.1 = bf16[8,120,512]{2,1,0:T(8,128)(2,1)} custom-call(bf16[128,512]{1,0:T(8,128)(2,1)S(1)} %get-tuple-element.82.refs_0_, bf16[128,512]{1,0:T(8,128)(2,1)S(1)} %collective-permute-done.refs_1_, bf16[128,512]{1,0:T(8,128)(2,1)S(1)} %collective-permute-done.1.refs_2_, bf16[128,512]{1,0:T(8,128)(2,1)S(1)} %collective-permute-done.2.refs_3_, ...), custom_call_target="tpu_custom_call" | custom-call | tf_op jit(solution)/shard_map/route/pallas_call | solution.py:446
  73.8 4.6 %all-to-all-start.2 = ((bf16[8,120,512]{2,1,0:T(8,128)(2,1)}), bf16[8,120,512]{2,1,0:T(8,128)(2,1)S(1)}, u32[]{:S(2)}, u32[]{:S(2)}) async-start(bf16[8,120,512]{2,1,0:T(8,128)(2,1)} %route.1), calls=%async_computation.3 | async-start | bytes 1966080 | tf_op jit(solution)/shard_map/all_to_all | solution.py:639
  78.5 0.8 own_plan.1.plan_ref.own_ref
  79.3 1.6 %far_plan.1.plan_ref = s32[16,128]{1,0:T(8,128)S(1)} custom-call(s32[4]{0:T(128)S(1)} %pad_add_fusion.position_ref, s32[256,256]{1,0:T(8,128)S(1)} %get-tuple-element.80.slots_ref, f32[128,256]{1,0:T(8,128)S(1)} %get-tuple-element.81.union_ref, bf16[128,512]{1,0:T(8,128)(2,1)S(1)} %get-tuple-element.82.refs_0_, ...), custom_call_target="tpu_custom_call" | custom-call | flops 671088640 | bytes 524288 | tf_op jit(solution)/shard_map/far_plan/pallas_call | solution.py:564
  80.9 0.6 slice.68
  82.1 0.0 all-gather.6.cloned.1.call-done
  82.1 0.0 copy-start
  82.2 2.0 %copy-done = bf16[16,7,128,128]{3,2,1,0:T(8,128)(2,1)S(1)} copy-done((bf16[16,7,128,128]{3,2,1,0:T(8,128)(2,1)S(1)}, bf16[16,7,128,128]{3,2,1,0:T(8,128)(2,1)}, u32[]{:S(2)}) %copy-start) | copy-done | bytes 3670040
  84.2 2.2 %own_sums.1.near_ref = f32[112,32,128]{2,1,0:T(8,128)S(1)} custom-call(s32[16,128]{1,0:T(8,128)S(1)} %own_plan.1.plan_ref.own_ref, bf16[112,128,128]{2,1,0:T(8,128)(2,1)S(1)} %bitcast.151), custom_call_target="tpu_custom_call" | custom-call | flops 536870912 | bytes 5505024 | tf_op jit(solution)/shard_map/own_sums/pallas_call | solution.py:161
  86.4 6.5 %all-to-all-done.2 = bf16[8,120,512]{2,1,0:T(8,128)(2,1)S(1)} async-done(((bf16[8,120,512]{2,1,0:T(8,128)(2,1)}), bf16[8,120,512]{2,1,0:T(8,128)(2,1)S(1)}, u32[]{:S(2)}, u32[]{:S(2)}) %all-to-all-start.2) | async-done | bytes 983072 | tf_op jit(solution)/shard_map/all_to_all | solution.py:639
  92.9 6.1 %far_sums.1 = (bf16[28,32,128]{2,1,0:T(8,128)(2,1)S(1)}, bf16[28,32,128]{2,1,0:T(8,128)(2,1)}, bf16[28,32,128]{2,1,0:T(8,128)(2,1)S(1)}, bf16[28,32,128]{2,1,0:T(8,128)(2,1)}) custom-call(s32[16,128]{1,0:T(8,128)S(1)} %own_plan.1.plan_ref.own_ref, s32[16,128]{1,0:T(8,128)S(1)} %far_plan.1.plan_ref, bf16[112,128,128]{2,1,0:T(8,128)(2,1)} %bitcast.150, ...), custom_call_target="tpu_custom_call" | custom-call | tf_op jit(solution)/shard_map/far_sums/pallas_call | solution.py:241
  99.0 0.0 collective-permute-start.7
  99.0 2.7 %collective-permute-start.8 = (bf16[28,32,128]{2,1,0:T(8,128)(2,1)}, bf16[28,32,128]{2,1,0:T(8,128)(2,1)S(1)}, u32[]{:S(2)}, u32[]{:S(2)}) collective-permute-start(bf16[28,32,128]{2,1,0:T(8,128)(2,1)} %get-tuple-element.96), channel_id=1, source_target_pairs={{0,3},{1,0},{2,1},{3,2},{4,7},{5,4},{6,5},{7,6},{8,11},{9,8},{10,9... | collective-permute-start | bytes 688136 | tf_op jit(solution)/shard_map/ppermute | solution.py:648
  101.7 0.0 collective-permute-start.9
  101.7 5.7 %collective-permute-done.7.refs_1_ = bf16[28,32,128]{2,1,0:T(8,128)(2,1)S(1)} collective-permute-done((bf16[28,32,128]{2,1,0:T(8,128)(2,1)}, bf16[28,32,128]{2,1,0:T(8,128)(2,1)S(1)}, u32[]{:S(2)}, u32[]{:S(2)}) %collective-permute-start.7) | collective-permute-done | bytes 229408 | tf_op jit(solution)/shard_map/ppermute | solution.py:648
  107.3 0.0 collective-permute-done.8.refs_2_
  107.3 3.6 %collective-permute-done.9.refs_3_ = bf16[28,32,128]{2,1,0:T(8,128)(2,1)S(1)} collective-permute-done((bf16[28,32,128]{2,1,0:T(8,128)(2,1)S(1)}, bf16[28,32,128]{2,1,0:T(8,128)(2,1)S(1)}, u32[]{:S(2)}, u32[]{:S(2)}) %collective-permute-start.9) | collective-permute-done | bytes 229408 | tf_op jit(solution)/shard_map/ppermute | solution.py:648
  110.9 0.0 copy-done.4
  110.9 0.0 copy-done.5
  110.9 1.9 %finish.1 = bf16[4,7,128,128]{3,2,1,0:T(8,128)(2,1)} custom-call(s32[4]{0:T(128)S(1)} %pad_add_fusion.position_ref, bf16[28,32,128]{2,1,0:T(8,128)(2,1)S(1)} %get-tuple-element.94.refs_0_, bf16[28,32,128]{2,1,0:T(8,128)(2,1)S(1)} %collective-permute-done.7.refs_1_, bf16[28,32,128]{2,1,0:T(8,128)(2,1)S(1)} %collective-permute-done.8.refs_2_, ...), custom_call_target="tpu_custom_call" | custom-call | tf_op jit(solution)/shard_map/finish/pallas_call | solution.py:268
  (4 shorter events, 0.0 us)
Async XLA Ops:
  6.5 75.6 %all-gather.6.cloned.1.call-start = ((), (), s32[]{:S(2)}) async-start(), calls=%async_computation.6 | async-start | bytes 4587520 | tf_op jit(solution)/shard_map/all_gather | solution.py:629
  11.9 99.0 %copy-start.4 = (s32[256,28]{0,1:T(8,128)S(1)}, s32[256,28]{0,1:T(8,128)}, u32[]{:S(2)}) copy-start(s32[256,28]{0,1:T(8,128)} %param.7) | copy-start | bytes 86020
  11.9 99.0 %copy-start.5 = (s32[4,7]{1,0:T(4,128)S(1)}, s32[4,7]{1,0:T(4,128)}, u32[]{:S(2)}) copy-start(s32[4,7]{1,0:T(4,128)} %keep_ref.3) | copy-start | bytes 340
  11.9 25.8 %all-to-all-start.1 = ((bf16[32,32,512]{2,1,0:T(8,128)(2,1)}), bf16[32,32,512]{2,1,0:T(8,128)(2,1)S(1)}, u32[]{:S(2)}, u32[]{:S(2)}) async-start(bf16[32,32,512]{2,1,0:T(8,128)(2,1)} %prepare.1), calls=%async_computation.2 | async-start | bytes 2097152 | tf_op jit(solution)/shard_map/all_to_all | solution.py:628
  41.0 15.0 %collective-permute-start = (bf16[128,512]{1,0:T(8,128)(2,1)S(1)}, bf16[128,512]{1,0:T(8,128)(2,1)S(1)}, u32[]{:S(2)}, u32[]{:S(2)}) collective-permute-start(bf16[128,512]{1,0:T(8,128)(2,1)S(1)} %get-tuple-element.72), channel_id=1, source_target_pairs={{0,24},{8,32},{16,40},{24,48},{32,56},{40,0},{48,8},{56,16},{1,25}... | collective-permute-start | bytes 393224 | tf_op jit(solution)/shard_map/ppermute | solution.py:634
  45.4 11.6 %collective-permute-start.1 = (bf16[128,512]{1,0:T(8,128)(2,1)S(1)}, bf16[128,512]{1,0:T(8,128)(2,1)S(1)}, u32[]{:S(2)}, u32[]{:S(2)}) collective-permute-start(bf16[128,512]{1,0:T(8,128)(2,1)S(1)} %get-tuple-element.73), channel_id=1, source_target_pairs={{0,40},{8,48},{16,56},{24,0},{32,8},{40,16},{48,24},{56,32},{1,41}... | collective-permute-start | bytes 393224 | tf_op jit(solution)/shard_map/ppermute | solution.py:634
  47.6 15.5 %collective-permute-start.2 = (bf16[128,512]{1,0:T(8,128)(2,1)S(1)}, bf16[128,512]{1,0:T(8,128)(2,1)S(1)}, u32[]{:S(2)}, u32[]{:S(2)}) collective-permute-start(bf16[128,512]{1,0:T(8,128)(2,1)S(1)} %get-tuple-element.74), channel_id=1, source_target_pairs={{0,32},{8,40},{16,48},{24,56},{32,0},{40,8},{48,16},{56,24},{1,33}... | collective-permute-start | bytes 393224 | tf_op jit(solution)/shard_map/ppermute | solution.py:634
  52.4 15.2 %collective-permute-start.3 = (bf16[128,512]{1,0:T(8,128)(2,1)S(1)}, bf16[128,512]{1,0:T(8,128)(2,1)S(1)}, u32[]{:S(2)}, u32[]{:S(2)}) collective-permute-start(bf16[128,512]{1,0:T(8,128)(2,1)S(1)} %get-tuple-element.75), channel_id=1, source_target_pairs={{0,16},{8,24},{16,32},{24,40},{32,48},{40,56},{48,0},{56,8},{1,17}... | collective-permute-start | bytes 393224 | tf_op jit(solution)/shard_map/ppermute | solution.py:634
  53.6 14.8 %collective-permute-start.4 = (bf16[128,512]{1,0:T(8,128)(2,1)S(1)}, bf16[128,512]{1,0:T(8,128)(2,1)S(1)}, u32[]{:S(2)}, u32[]{:S(2)}) collective-permute-start(bf16[128,512]{1,0:T(8,128)(2,1)S(1)} %get-tuple-element.76), channel_id=1, source_target_pairs={{0,48},{8,56},{16,0},{24,8},{32,16},{40,24},{48,32},{56,40},{1,49}... | collective-permute-start | bytes 393224 | tf_op jit(solution)/shard_map/ppermute | solution.py:634
  56.0 13.9 %collective-permute-start.5 = (bf16[128,512]{1,0:T(8,128)(2,1)S(1)}, bf16[128,512]{1,0:T(8,128)(2,1)S(1)}, u32[]{:S(2)}, u32[]{:S(2)}) collective-permute-start(bf16[128,512]{1,0:T(8,128)(2,1)S(1)} %get-tuple-element.77), channel_id=1, source_target_pairs={{0,8},{8,16},{16,24},{24,32},{32,40},{40,48},{48,56},{56,0},{1,9},... | collective-permute-start | bytes 393224 | tf_op jit(solution)/shard_map/ppermute | solution.py:634
  57.0 14.6 %collective-permute-start.6 = (bf16[128,512]{1,0:T(8,128)(2,1)S(1)}, bf16[128,512]{1,0:T(8,128)(2,1)S(1)}, u32[]{:S(2)}, u32[]{:S(2)}) collective-permute-start(bf16[128,512]{1,0:T(8,128)(2,1)S(1)} %get-tuple-element.78), channel_id=1, source_target_pairs={{0,56},{8,0},{16,8},{24,16},{32,24},{40,32},{48,40},{56,48},{1,57}... | collective-permute-start | bytes 393224 | tf_op jit(solution)/shard_map/ppermute | solution.py:634
  73.8 19.0 %all-to-all-start.2 = ((bf16[8,120,512]{2,1,0:T(8,128)(2,1)}), bf16[8,120,512]{2,1,0:T(8,128)(2,1)S(1)}, u32[]{:S(2)}, u32[]{:S(2)}) async-start(bf16[8,120,512]{2,1,0:T(8,128)(2,1)} %route.1), calls=%async_computation.3 | async-start | bytes 1966080 | tf_op jit(solution)/shard_map/all_to_all | solution.py:639
  82.1 2.0 %copy-start = (bf16[16,7,128,128]{3,2,1,0:T(8,128)(2,1)S(1)}, bf16[16,7,128,128]{3,2,1,0:T(8,128)(2,1)}, u32[]{:S(2)}) copy-start(bf16[16,7,128,128]{3,2,1,0:T(8,128)(2,1)} %all-gather.6.cloned.1.call-done) | copy-start | bytes 11010052
  99.0 8.4 %collective-permute-start.7 = (bf16[28,32,128]{2,1,0:T(8,128)(2,1)}, bf16[28,32,128]{2,1,0:T(8,128)(2,1)S(1)}, u32[]{:S(2)}, u32[]{:S(2)}) collective-permute-start(bf16[28,32,128]{2,1,0:T(8,128)(2,1)} %get-tuple-element.95), channel_id=1, source_target_pairs={{0,1},{1,2},{2,3},{3,0},{4,5},{5,6},{6,7},{7,4},{8,9},{9,10},{10,1... | collective-permute-start | bytes 688136 | tf_op jit(solution)/shard_map/ppermute | solution.py:648
  99.0 8.4 %collective-permute-start.8 = (bf16[28,32,128]{2,1,0:T(8,128)(2,1)}, bf16[28,32,128]{2,1,0:T(8,128)(2,1)S(1)}, u32[]{:S(2)}, u32[]{:S(2)}) collective-permute-start(bf16[28,32,128]{2,1,0:T(8,128)(2,1)} %get-tuple-element.96), channel_id=1, source_target_pairs={{0,3},{1,0},{2,1},{3,2},{4,7},{5,4},{6,5},{7,6},{8,11},{9,8},{10,9... | collective-permute-start | bytes 688136 | tf_op jit(solution)/shard_map/ppermute | solution.py:648
  101.7 9.2 %collective-permute-start.9 = (bf16[28,32,128]{2,1,0:T(8,128)(2,1)S(1)}, bf16[28,32,128]{2,1,0:T(8,128)(2,1)S(1)}, u32[]{:S(2)}, u32[]{:S(2)}) collective-permute-start(bf16[28,32,128]{2,1,0:T(8,128)(2,1)S(1)} %get-tuple-element.97), channel_id=1, source_target_pairs={{0,2},{1,3},{2,0},{3,1},{4,6},{5,7},{6,4},{7,5},{8,10},{9,11},{10,... | collective-permute-start | bytes 688136 | tf_op jit(solution)/shard_map/ppermute | solution.py:648
Sparse Core Ops, SparseCore 0:
  12.1 53.8 all-gather.5

commit v7 on v6

--- a/solution.py
+++ b/solution.py
@@ -28,7 +28,7 @@
 ORDER_Z = (3, 5, 4, 2, 6, 1, 7)
 ORDER_Y = (1, 3, 2)
 GROUP = 8
-FAR_GROUP = 4
+FAR_GROUP = 3
 ROWS_AT_ONCE = 4
 HEIGHT_2 = NC * HEIGHT
 OUT_COLS = 72
@@ -253,15 +253,17 @@
 
 
 def finish_kernel(position_ref, *refs):
-    *cut_refs, out_ref, turned_ref = refs
-    for step, cut_ref in zip((0,) + ORDER_Y, cut_refs):
-        part = (position_ref[3] - step) & (NY - 1)
-        rows = pl.ds(pl.multiple_of(part * WIDE, WIDE), WIDE)
-        for place in range(HEIGHT * QUARTER):
-            turned_ref[place, rows, :] = cut_ref[place]
-    for row in range(HEIGHT):
-        for slot in range(QUARTER):
-            out_ref[row, slot] = turned_ref[row * QUARTER + slot].T
+    *cut_refs, out_ref = refs
+    at = dict(zip((0,) + ORDER_Y, cut_refs))
+    for part in range(NY):
+
+        @pl.when(position_ref[3] == part)
+        def _():
+            order = [at[(part - sender) % NY] for sender in range(NY)]
+            for row in range(HEIGHT):
+                for slot in range(QUARTER):
+                    cuts = [ref[row * QUARTER + slot] for ref in order]
+                    out_ref[row, slot] = jnp.concatenate(cuts, axis=0).T
 
 
 def finish(position, cuts):
@@ -270,7 +272,6 @@
         out_shape=jax.ShapeDtypeStruct((HEIGHT, QUARTER, SIDE, SIDE), BF),
         in_specs=[smem()] + [vmem()] * NY,
         out_specs=vmem(),
-        scratch_shapes=[pltpu.VMEM((HEIGHT * QUARTER, SIDE, SIDE), BF)],
         compiler_params=params(),
         name="finish",
     )(position, *cuts)
@@ -311,7 +312,8 @@
 
 
 def one_hot(code, rows):
-    return (iota((rows, code.shape[1]), 0).astype(F32) == code).astype(F32)
+    number = iota((rows, code.shape[1]), 0).astype(F32).astype(BF)
+    return jnp.where(number == code.astype(BF), jnp.ones((), BF), jnp.zeros((), BF))
 
 
 def quarter_of(slot):
@@ -379,7 +381,7 @@
     most = jnp.broadcast_to(jnp.minimum(most, 250.0), (1, 128))
     totals = jnp.minimum(dot_rows(jnp.ones((8, ENTRIES), F32), need)[0:1], 250.0)
     for to in range(NZ):
-        chosen_ref[to * ROWS_Z : (to + 1) * ROWS_Z, :] = one_hot(code[to : to + 1], ROWS_Z).astype(BF)
+        chosen_ref[to * ROWS_Z : (to + 1) * ROWS_Z, :] = one_hot(code[to : to + 1], ROWS_Z)
     packed = jnp.dot(chosen_ref[...], near, preferred_element_type=F32)
     tail = iota((16, PIECE), 0)
     kq = kq_ref[...]
@@ -436,7 +438,7 @@
         along_ref[number * ROWS_Z : (number + 1) * ROWS_Z] = ref[...]
     code = codes(asked, CAP_X)
     for to in range(TARGETS):
-        chosen_ref[to * SIDE : (to + 1) * SIDE, :] = one_hot(code[to : to + 1], SIDE).astype(BF)
+        chosen_ref[to * SIDE : (to + 1) * SIDE, :] = one_hot(code[to : to + 1], SIDE)
     packed = jnp.dot(chosen_ref[...], along_ref[...], preferred_element_type=F32)
     for to in range(TARGETS):
         out_ref[to] = packed[to * SIDE : to * SIDE + CAP_X].astype(BF)
@@ -514,7 +516,7 @@
     asked = jnp.sum(jnp.where(mine, asked, 0.0), axis=0, keepdims=True)
     number = jnp.sum(asked).astype(I32)
     code = codes(jnp.broadcast_to(asked, (8, asked.shape[1])), CAP_X)[0:1]
-    chosen = one_hot(code, SIDE)
+    chosen = one_hot(code, SIDE).astype(F32)
     row = jnp.concatenate([part[:, :SIDE] for part in third], axis=1)
     column = jnp.concatenate([part[:, SIDE : 2 * SIDE] for part in third], axis=1)
     row_down = jnp.sum(chosen * row, axis=1, keepdims=True).astype(I32)
@@ -626,6 +628,7 @@
     turned = turn(nonzero, same)
     slots, union, need, kq = pattern(position, names, plane_columns(columns))
     near = lax.all_to_all(cuts, ("col", "x", "core"), split_axis=0, concat_axis=0, tiled=True)
+    near, turned, need = lax.optimization_barrier((near, turned, need))
     whole = lax.all_gather(turned, "col", axis=0, tiled=False)
     whole = whole.reshape(ZERO_BLOCK, SIDE, SIDE)
     packed = send(position, need, kq, near.reshape(ENTRIES, PIECE))

time: 121 us -> 119 us (0.983)
  waiting for transfers between devices: 40.5 us -> 37.9 us
    all_to_all x1, waiting for transfers between devices: 12.4 us -> 9.95 us  [shards(): lax.all_to_all(cuts, ('col', 'x', 'core'), split_axis=0, concat_axis=0, t...]
    all_gather x1, waiting for transfers between devices: 0.02 us -> 1.51 us  [shards(): whole = lax.all_gather(turned, 'col', axis=0, tiled=False)]
    all_to_all x1, waiting for transfers between devices: 6.46 us -> 5 us  [shards(): lax.all_to_all(packed, ('x', 'core'), split_axis=0, concat_axis=0, tiled=...]
  transfers between devices with their start and end apart: 13 -> 13, of which waited for: 9 -> 11; matrix products, arithmetic and copies ran while one was open for 2% -> 2% of each run, Pallas kernels for 8% -> 10%
where the time goes in v7:
time: 119 us; the launch traced here: 117 us
  waiting for transfers between devices  37.9 us (32%)
  starting transfers between devices  33.9 us (28%)
  Pallas kernels  26 us (22%)
  between operations  14.1 us (12%)
  local copies, waits for them, and re-layouts  4.84 us (4%)
    ppermute x7, starting transfers between devices, shards(): lax.ppermute(packed[step], 'z', [(i, (i + step) % NZ) for i in range(NZ)])  18.3 us
    ppermute x7, waiting for transfers between devices, shards(): lax.ppermute(packed[step], 'z', [(i, (i + step) % NZ) for i in range(NZ)])  12.4 us
    all_to_all x1, waiting for transfers between devices, shards(): lax.all_to_all(cuts, ('col', 'x', 'core'), split_axis=0, concat_axis=0, t...  9.95 us
    ppermute x3, waiting for transfers between devices, shards(): cuts.append(lax.ppermute(result[step], 'col', pairs))  8.97 us
    all_to_all x1, starting transfers between devices, shards(): lax.all_to_all(cuts, ('col', 'x', 'core'), split_axis=0, concat_axis=0, t...  8.59 us
    pallas_call x1, Pallas kernels, far_sums(): pl.pallas_call(far_kernel, out_shape=[jax.ShapeDtypeStruct((HEIGHT * QUAR...  6.28 us
    all_to_all x1, waiting for transfers between devices, shards(): lax.all_to_all(packed, ('x', 'core'), split_axis=0, concat_axis=0, tiled=...  5 us
    all_to_all x1, starting transfers between devices, shards(): lax.all_to_all(packed, ('x', 'core'), split_axis=0, concat_axis=0, tiled=...  4.27 us
  transfers between devices with their start and end apart: 13, of which 11 were waited for; matrix products, arithmetic and copies ran while one was open for 2% of the time, Pallas kernels for 10%

profile of v7, /device:TPU:1, one launch (start us, length us, event | category | flops | bytes accessed | tf_op | source)
XLA Modules:
  0.0 116.8 jit_solution(841009892832646895)
XLA Ops:
  6.5 0.1 pad_add_fusion.position_ref
  6.6 2.9 %prepare.1 = bf16[32,32,512]{2,1,0:T(8,128)(2,1)} custom-call(s32[4]{0:T(128)S(1)} %pad_add_fusion.position_ref, s32[4,7]{1,0:T(4,128)} %keep_ref.3, bf16[4,7,128,128]{3,2,1,0:T(8,128)(2,1)} %blocks_ref.2), custom_call_target="tpu_custom_call" | custom-call | tf_op jit(solution)/shard_map/prepare/pallas_call | solution.py:86
  9.5 8.6 %all-to-all-start.1 = ((bf16[32,32,512]{2,1,0:T(8,128)(2,1)}), bf16[32,32,512]{2,1,0:T(8,128)(2,1)S(1)}, u32[]{:S(2)}, u32[]{:S(2)}) async-start(bf16[32,32,512]{2,1,0:T(8,128)(2,1)} %prepare.1), calls=%async_computation.2 | async-start | bytes 2097152 | tf_op jit(solution)/shard_map/all_to_all | solution.py:630
  18.1 0.0 copy-start.4
  18.1 0.0 copy-start.5
  18.2 0.0 all-gather.6.cloned.1.call-start
  18.2 0.9 copy.101
  19.1 0.3 reshape.214
  19.4 0.1 reshape.215
  19.5 0.1 reshape.216.entries_ref
  19.6 0.9 copy.103.columns_ref
  20.5 2.4 %turn.1 = bf16[4,7,128,128]{3,2,1,0:T(8,128)(2,1)} custom-call(s32[4,7]{1,0:T(4,128)} %keep_ref.3, bf16[4,7,128,128]{3,2,1,0:T(8,128)(2,1)} %blocks_ref.2), custom_call_target="tpu_custom_call" | custom-call | flops 117440512 | bytes 1835008 | tf_op jit(solution)/shard_map/turn/pallas_call | solution.py:107
  22.9 2.5 %pattern.1 = (s32[256,256]{1,0:T(8,128)S(1)}, f32[128,256]{1,0:T(8,128)S(1)}, f32[128,1024]{1,0:T(8,128)S(1)}, f32[8,1024]{1,0:T(8,128)S(1)}) custom-call(s32[4]{0:T(128)S(1)} %pad_add_fusion.position_ref, s32[256,28]{1,0:T(8,128)S(1)} %copy.103.columns_ref, s32[1,1024]{1,0:T(1,128)S(1)} %reshape.216.entries_ref), custom_call_target="tpu_custom_call" | custom-call | flops 234881024 | bytes 524288 | tf_op jit(solution)/shard_map/pattern/pallas_call | solution.py:351
  25.4 10.0 %all-to-all-done.1 = bf16[32,32,512]{2,1,0:T(8,128)(2,1)S(1)} async-done(((bf16[32,32,512]{2,1,0:T(8,128)(2,1)}), bf16[32,32,512]{2,1,0:T(8,128)(2,1)S(1)}, u32[]{:S(2)}, u32[]{:S(2)}) %all-to-all-start.1) | async-done | bytes 1048608 | tf_op jit(solution)/shard_map/all_to_all | solution.py:630
  35.3 0.0 all-gather.6.cloned.1.call-update
  35.3 3.2 %send.1 = (bf16[128,512]{1,0:T(8,128)(2,1)S(1)}, bf16[128,512]{1,0:T(8,128)(2,1)S(1)}, bf16[128,512]{1,0:T(8,128)(2,1)S(1)}, bf16[128,512]{1,0:T(8,128)(2,1)S(1)...) custom-call(s32[4]{0:T(128)S(1)} %pad_add_fusion.position_ref, ...), custom_call_target="tpu_custom_call" | custom-call | tf_op jit(solution)/shard_map/send/pallas_call | solution.py:406
  38.6 4.4 %collective-permute-start = (bf16[128,512]{1,0:T(8,128)(2,1)S(1)}, bf16[128,512]{1,0:T(8,128)(2,1)S(1)}, u32[]{:S(2)}, u32[]{:S(2)}) collective-permute-start(bf16[128,512]{1,0:T(8,128)(2,1)S(1)} %get-tuple-element.78), channel_id=1, source_target_pairs={{0,24},{8,32},{16,40},{24,48},{32,56},{40,0},{48,8},{56,16},{1,25}... | collective-permute-start | bytes 393224 | tf_op jit(solution)/shard_map/ppermute | solution.py:637
  43.0 2.2 %collective-permute-start.1 = (bf16[128,512]{1,0:T(8,128)(2,1)S(1)}, bf16[128,512]{1,0:T(8,128)(2,1)S(1)}, u32[]{:S(2)}, u32[]{:S(2)}) collective-permute-start(bf16[128,512]{1,0:T(8,128)(2,1)S(1)} %get-tuple-element.79), channel_id=1, source_target_pairs={{0,40},{8,48},{16,56},{24,0},{32,8},{40,16},{48,24},{56,32},{1,41}... | collective-permute-start | bytes 393224 | tf_op jit(solution)/shard_map/ppermute | solution.py:637
  45.2 4.8 %collective-permute-start.2 = (bf16[128,512]{1,0:T(8,128)(2,1)S(1)}, bf16[128,512]{1,0:T(8,128)(2,1)S(1)}, u32[]{:S(2)}, u32[]{:S(2)}) collective-permute-start(bf16[128,512]{1,0:T(8,128)(2,1)S(1)} %get-tuple-element.80), channel_id=1, source_target_pairs={{0,32},{8,40},{16,48},{24,56},{32,0},{40,8},{48,16},{56,24},{1,33}... | collective-permute-start | bytes 393224 | tf_op jit(solution)/shard_map/ppermute | solution.py:637
  50.0 1.2 %collective-permute-start.3 = (bf16[128,512]{1,0:T(8,128)(2,1)S(1)}, bf16[128,512]{1,0:T(8,128)(2,1)S(1)}, u32[]{:S(2)}, u32[]{:S(2)}) collective-permute-start(bf16[128,512]{1,0:T(8,128)(2,1)S(1)} %get-tuple-element.81), channel_id=1, source_target_pairs={{0,16},{8,24},{16,32},{24,40},{32,48},{40,56},{48,0},{56,8},{1,17}... | collective-permute-start | bytes 393224 | tf_op jit(solution)/shard_map/ppermute | solution.py:637
  51.2 2.4 %collective-permute-start.4 = (bf16[128,512]{1,0:T(8,128)(2,1)S(1)}, bf16[128,512]{1,0:T(8,128)(2,1)S(1)}, u32[]{:S(2)}, u32[]{:S(2)}) collective-permute-start(bf16[128,512]{1,0:T(8,128)(2,1)S(1)} %get-tuple-element.82), channel_id=1, source_target_pairs={{0,48},{8,56},{16,0},{24,8},{32,16},{40,24},{48,32},{56,40},{1,49}... | collective-permute-start | bytes 393224 | tf_op jit(solution)/shard_map/ppermute | solution.py:637
  53.6 0.0 collective-permute-done.refs_1_
  53.6 1.0 collective-permute-start.5
  54.6 0.0 collective-permute-done.1.refs_2_
  54.6 2.3 %collective-permute-start.6 = (bf16[128,512]{1,0:T(8,128)(2,1)S(1)}, bf16[128,512]{1,0:T(8,128)(2,1)S(1)}, u32[]{:S(2)}, u32[]{:S(2)}) collective-permute-start(bf16[128,512]{1,0:T(8,128)(2,1)S(1)} %get-tuple-element.84), channel_id=1, source_target_pairs={{0,56},{8,0},{16,8},{24,16},{32,24},{40,32},{48,40},{56,48},{1,57}... | collective-permute-start | bytes 393224 | tf_op jit(solution)/shard_map/ppermute | solution.py:637
  56.8 3.9 %collective-permute-done.2.refs_3_ = bf16[128,512]{1,0:T(8,128)(2,1)S(1)} collective-permute-done((bf16[128,512]{1,0:T(8,128)(2,1)S(1)}, bf16[128,512]{1,0:T(8,128)(2,1)S(1)}, u32[]{:S(2)}, u32[]{:S(2)}) %collective-permute-start.2) | collective-permute-done | bytes 131104 | tf_op jit(solution)/shard_map/ppermute | solution.py:637
  60.8 4.4 %collective-permute-done.3.refs_4_ = bf16[128,512]{1,0:T(8,128)(2,1)S(1)} collective-permute-done((bf16[128,512]{1,0:T(8,128)(2,1)S(1)}, bf16[128,512]{1,0:T(8,128)(2,1)S(1)}, u32[]{:S(2)}, u32[]{:S(2)}) %collective-permute-start.3) | collective-permute-done | bytes 131104 | tf_op jit(solution)/shard_map/ppermute | solution.py:637
  65.2 1.0 collective-permute-done.4.refs_5_
  66.2 1.4 %collective-permute-done.5.refs_6_ = bf16[128,512]{1,0:T(8,128)(2,1)S(1)} collective-permute-done((bf16[128,512]{1,0:T(8,128)(2,1)S(1)}, bf16[128,512]{1,0:T(8,128)(2,1)S(1)}, u32[]{:S(2)}, u32[]{:S(2)}) %collective-permute-start.5) | collective-permute-done | bytes 131104 | tf_op jit(solution)/shard_map/ppermute | solution.py:637
  67.6 1.7 %collective-permute-done.6.refs_7_ = bf16[128,512]{1,0:T(8,128)(2,1)S(1)} collective-permute-done((bf16[128,512]{1,0:T(8,128)(2,1)S(1)}, bf16[128,512]{1,0:T(8,128)(2,1)S(1)}, u32[]{:S(2)}, u32[]{:S(2)}) %collective-permute-start.6) | collective-permute-done | bytes 131104 | tf_op jit(solution)/shard_map/ppermute | solution.py:637
  69.3 2.3 %route.1 = bf16[8,120,512]{2,1,0:T(8,128)(2,1)} custom-call(bf16[128,512]{1,0:T(8,128)(2,1)S(1)} %get-tuple-element.88.refs_0_, bf16[128,512]{1,0:T(8,128)(2,1)S(1)} %collective-permute-done.refs_1_, bf16[128,512]{1,0:T(8,128)(2,1)S(1)} %collective-permute-done.1.refs_2_, bf16[128,512]{1,0:T(8,128)(2,1)S(1)} %collective-permute-done.2.refs_3_, ...), custom_call_target="tpu_custom_call" | custom-call | tf_op jit(solution)/shard_map/route/pallas_call | solution.py:448
  71.6 4.3 %all-to-all-start.2 = ((bf16[8,120,512]{2,1,0:T(8,128)(2,1)}), bf16[8,120,512]{2,1,0:T(8,128)(2,1)S(1)}, u32[]{:S(2)}, u32[]{:S(2)}) async-start(bf16[8,120,512]{2,1,0:T(8,128)(2,1)} %route.1), calls=%async_computation.3 | async-start | bytes 1966080 | tf_op jit(solution)/shard_map/all_to_all | solution.py:642
  75.8 0.8 own_plan.1.plan_ref.own_ref
  76.7 1.6 %far_plan.1.plan_ref = s32[16,128]{1,0:T(8,128)S(1)} custom-call(s32[4]{0:T(128)S(1)} %pad_add_fusion.position_ref, s32[256,256]{1,0:T(8,128)S(1)} %get-tuple-element.86.slots_ref, f32[128,256]{1,0:T(8,128)S(1)} %get-tuple-element.87.union_ref, bf16[128,512]{1,0:T(8,128)(2,1)S(1)} %get-tuple-element.88.refs_0_, ...), custom_call_target="tpu_custom_call" | custom-call | flops 671088640 | bytes 524288 | tf_op jit(solution)/shard_map/far_plan/pallas_call | solution.py:566
  78.3 0.6 slice.68
  79.5 1.5 %all-gather.6.cloned.1.call-done = bf16[16,7,128,128]{3,2,1,0:T(8,128)(2,1)} async-done(((bf16[4,7,128,128]{3,2,1,0:T(8,128)(2,1)}), bf16[16,7,128,128]{3,2,1,0:T(8,128)(2,1)}) %all-gather.6.cloned.1.call-update) | async-done | bytes 3670032 | tf_op jit(solution)/shard_map/all_gather | solution.py:632
  81.0 0.0 copy-start
  81.0 2.0 %copy-done = bf16[16,7,128,128]{3,2,1,0:T(8,128)(2,1)S(1)} copy-done((bf16[16,7,128,128]{3,2,1,0:T(8,128)(2,1)S(1)}, bf16[16,7,128,128]{3,2,1,0:T(8,128)(2,1)}, u32[]{:S(2)}) %copy-start) | copy-done | bytes 3670040
  83.0 2.2 %own_sums.1.near_ref = f32[112,32,128]{2,1,0:T(8,128)S(1)} custom-call(s32[16,128]{1,0:T(8,128)S(1)} %own_plan.1.plan_ref.own_ref, bf16[112,128,128]{2,1,0:T(8,128)(2,1)S(1)} %bitcast.151), custom_call_target="tpu_custom_call" | custom-call | flops 536870912 | bytes 5505024 | tf_op jit(solution)/shard_map/own_sums/pallas_call | solution.py:161
  85.2 5.0 %all-to-all-done.2 = bf16[8,120,512]{2,1,0:T(8,128)(2,1)S(1)} async-done(((bf16[8,120,512]{2,1,0:T(8,128)(2,1)}), bf16[8,120,512]{2,1,0:T(8,128)(2,1)S(1)}, u32[]{:S(2)}, u32[]{:S(2)}) %all-to-all-start.2) | async-done | bytes 983072 | tf_op jit(solution)/shard_map/all_to_all | solution.py:642
  90.2 6.3 %far_sums.1 = (bf16[28,32,128]{2,1,0:T(8,128)(2,1)S(1)}, bf16[28,32,128]{2,1,0:T(8,128)(2,1)}, bf16[28,32,128]{2,1,0:T(8,128)(2,1)S(1)}, bf16[28,32,128]{2,1,0:T(8,128)(2,1)}) custom-call(s32[16,128]{1,0:T(8,128)S(1)} %own_plan.1.plan_ref.own_ref, s32[16,128]{1,0:T(8,128)S(1)} %far_plan.1.plan_ref, bf16[112,128,128]{2,1,0:T(8,128)(2,1)} %bitcast.150, ...), custom_call_target="tpu_custom_call" | custom-call | tf_op jit(solution)/shard_map/far_sums/pallas_call | solution.py:241
  96.5 0.0 collective-permute-start.7
  96.5 2.7 %collective-permute-start.8 = (bf16[28,32,128]{2,1,0:T(8,128)(2,1)}, bf16[28,32,128]{2,1,0:T(8,128)(2,1)S(1)}, u32[]{:S(2)}, u32[]{:S(2)}) collective-permute-start(bf16[28,32,128]{2,1,0:T(8,128)(2,1)} %get-tuple-element.102), channel_id=1, source_target_pairs={{0,3},{1,0},{2,1},{3,2},{4,7},{5,4},{6,5},{7,6},{8,11},{9,8},{10,9... | collective-permute-start | bytes 688136 | tf_op jit(solution)/shard_map/ppermute | solution.py:651
  99.2 0.0 collective-permute-start.9
  99.2 4.3 %collective-permute-done.7.refs_1_ = bf16[28,32,128]{2,1,0:T(8,128)(2,1)S(1)} collective-permute-done((bf16[28,32,128]{2,1,0:T(8,128)(2,1)}, bf16[28,32,128]{2,1,0:T(8,128)(2,1)S(1)}, u32[]{:S(2)}, u32[]{:S(2)}) %collective-permute-start.7) | collective-permute-done | bytes 229408 | tf_op jit(solution)/shard_map/ppermute | solution.py:651
  103.5 0.8 collective-permute-done.8.refs_2_
  104.3 3.8 %collective-permute-done.9.refs_3_ = bf16[28,32,128]{2,1,0:T(8,128)(2,1)S(1)} collective-permute-done((bf16[28,32,128]{2,1,0:T(8,128)(2,1)S(1)}, bf16[28,32,128]{2,1,0:T(8,128)(2,1)S(1)}, u32[]{:S(2)}, u32[]{:S(2)}) %collective-permute-start.9) | collective-permute-done | bytes 229408 | tf_op jit(solution)/shard_map/ppermute | solution.py:651
  108.2 0.0 copy-done.4
  108.2 0.0 copy-done.5
  108.2 1.8 %finish.1 = bf16[4,7,128,128]{3,2,1,0:T(8,128)(2,1)} custom-call(s32[4]{0:T(128)S(1)} %pad_add_fusion.position_ref, bf16[28,32,128]{2,1,0:T(8,128)(2,1)S(1)} %get-tuple-element.100.refs_0_, bf16[28,32,128]{2,1,0:T(8,128)(2,1)S(1)} %collective-permute-done.7.refs_1_, bf16[28,32,128]{2,1,0:T(8,128)(2,1)S(1)} %collective-permute-done.8.refs_2_, ...), custom_call_target="tpu_custom_call" | custom-call | tf_op jit(solution)/shard_map/finish/pallas_call | solution.py:270
  (4 shorter events, 0.0 us)
Async XLA Ops:
  9.5 25.8 %all-to-all-start.1 = ((bf16[32,32,512]{2,1,0:T(8,128)(2,1)}), bf16[32,32,512]{2,1,0:T(8,128)(2,1)S(1)}, u32[]{:S(2)}, u32[]{:S(2)}) async-start(bf16[32,32,512]{2,1,0:T(8,128)(2,1)} %prepare.1), calls=%async_computation.2 | async-start | bytes 2097152 | tf_op jit(solution)/shard_map/all_to_all | solution.py:630
  18.1 90.0 %copy-start.4 = (s32[256,28]{0,1:T(8,128)S(1)}, s32[256,28]{0,1:T(8,128)}, u32[]{:S(2)}) copy-start(s32[256,28]{0,1:T(8,128)} %param.7) | copy-start | bytes 86020
  18.1 90.0 %copy-start.5 = (s32[4,7]{1,0:T(4,128)S(1)}, s32[4,7]{1,0:T(4,128)}, u32[]{:S(2)}) copy-start(s32[4,7]{1,0:T(4,128)} %keep_ref.3) | copy-start | bytes 340
  18.2 62.8 %all-gather.6.cloned.1.call-start = ((), (), s32[]{:S(2)}) async-start(), calls=%async_computation.6 | async-start | bytes 4587520 | tf_op jit(solution)/shard_map/all_gather | solution.py:632
  38.6 15.0 %collective-permute-start = (bf16[128,512]{1,0:T(8,128)(2,1)S(1)}, bf16[128,512]{1,0:T(8,128)(2,1)S(1)}, u32[]{:S(2)}, u32[]{:S(2)}) collective-permute-start(bf16[128,512]{1,0:T(8,128)(2,1)S(1)} %get-tuple-element.78), channel_id=1, source_target_pairs={{0,24},{8,32},{16,40},{24,48},{32,56},{40,0},{48,8},{56,16},{1,25}... | collective-permute-start | bytes 393224 | tf_op jit(solution)/shard_map/ppermute | solution.py:637
  43.0 11.6 %collective-permute-start.1 = (bf16[128,512]{1,0:T(8,128)(2,1)S(1)}, bf16[128,512]{1,0:T(8,128)(2,1)S(1)}, u32[]{:S(2)}, u32[]{:S(2)}) collective-permute-start(bf16[128,512]{1,0:T(8,128)(2,1)S(1)} %get-tuple-element.79), channel_id=1, source_target_pairs={{0,40},{8,48},{16,56},{24,0},{32,8},{40,16},{48,24},{56,32},{1,41}... | collective-permute-start | bytes 393224 | tf_op jit(solution)/shard_map/ppermute | solution.py:637
  45.2 15.6 %collective-permute-start.2 = (bf16[128,512]{1,0:T(8,128)(2,1)S(1)}, bf16[128,512]{1,0:T(8,128)(2,1)S(1)}, u32[]{:S(2)}, u32[]{:S(2)}) collective-permute-start(bf16[128,512]{1,0:T(8,128)(2,1)S(1)} %get-tuple-element.80), channel_id=1, source_target_pairs={{0,32},{8,40},{16,48},{24,56},{32,0},{40,8},{48,16},{56,24},{1,33}... | collective-permute-start | bytes 393224 | tf_op jit(solution)/shard_map/ppermute | solution.py:637
  50.0 15.2 %collective-permute-start.3 = (bf16[128,512]{1,0:T(8,128)(2,1)S(1)}, bf16[128,512]{1,0:T(8,128)(2,1)S(1)}, u32[]{:S(2)}, u32[]{:S(2)}) collective-permute-start(bf16[128,512]{1,0:T(8,128)(2,1)S(1)} %get-tuple-element.81), channel_id=1, source_target_pairs={{0,16},{8,24},{16,32},{24,40},{32,48},{40,56},{48,0},{56,8},{1,17}... | collective-permute-start | bytes 393224 | tf_op jit(solution)/shard_map/ppermute | solution.py:637
  51.2 15.0 %collective-permute-start.4 = (bf16[128,512]{1,0:T(8,128)(2,1)S(1)}, bf16[128,512]{1,0:T(8,128)(2,1)S(1)}, u32[]{:S(2)}, u32[]{:S(2)}) collective-permute-start(bf16[128,512]{1,0:T(8,128)(2,1)S(1)} %get-tuple-element.82), channel_id=1, source_target_pairs={{0,48},{8,56},{16,0},{24,8},{32,16},{40,24},{48,32},{56,40},{1,49}... | collective-permute-start | bytes 393224 | tf_op jit(solution)/shard_map/ppermute | solution.py:637
  53.6 14.0 %collective-permute-start.5 = (bf16[128,512]{1,0:T(8,128)(2,1)S(1)}, bf16[128,512]{1,0:T(8,128)(2,1)S(1)}, u32[]{:S(2)}, u32[]{:S(2)}) collective-permute-start(bf16[128,512]{1,0:T(8,128)(2,1)S(1)} %get-tuple-element.83), channel_id=1, source_target_pairs={{0,8},{8,16},{16,24},{24,32},{32,40},{40,48},{48,56},{56,0},{1,9},... | collective-permute-start | bytes 393224 | tf_op jit(solution)/shard_map/ppermute | solution.py:637
  54.6 14.7 %collective-permute-start.6 = (bf16[128,512]{1,0:T(8,128)(2,1)S(1)}, bf16[128,512]{1,0:T(8,128)(2,1)S(1)}, u32[]{:S(2)}, u32[]{:S(2)}) collective-permute-start(bf16[128,512]{1,0:T(8,128)(2,1)S(1)} %get-tuple-element.84), channel_id=1, source_target_pairs={{0,56},{8,0},{16,8},{24,16},{32,24},{40,32},{48,40},{56,48},{1,57}... | collective-permute-start | bytes 393224 | tf_op jit(solution)/shard_map/ppermute | solution.py:637
  71.6 18.7 %all-to-all-start.2 = ((bf16[8,120,512]{2,1,0:T(8,128)(2,1)}), bf16[8,120,512]{2,1,0:T(8,128)(2,1)S(1)}, u32[]{:S(2)}, u32[]{:S(2)}) async-start(bf16[8,120,512]{2,1,0:T(8,128)(2,1)} %route.1), calls=%async_computation.3 | async-start | bytes 1966080 | tf_op jit(solution)/shard_map/all_to_all | solution.py:642
  81.0 2.0 %copy-start = (bf16[16,7,128,128]{3,2,1,0:T(8,128)(2,1)S(1)}, bf16[16,7,128,128]{3,2,1,0:T(8,128)(2,1)}, u32[]{:S(2)}) copy-start(bf16[16,7,128,128]{3,2,1,0:T(8,128)(2,1)} %all-gather.6.cloned.1.call-done) | copy-start | bytes 11010052
  96.5 7.0 %collective-permute-start.7 = (bf16[28,32,128]{2,1,0:T(8,128)(2,1)}, bf16[28,32,128]{2,1,0:T(8,128)(2,1)S(1)}, u32[]{:S(2)}, u32[]{:S(2)}) collective-permute-start(bf16[28,32,128]{2,1,0:T(8,128)(2,1)} %get-tuple-element.101), channel_id=1, source_target_pairs={{0,1},{1,2},{2,3},{3,0},{4,5},{5,6},{6,7},{7,4},{8,9},{9,10},{10,1... | collective-permute-start | bytes 688136 | tf_op jit(solution)/shard_map/ppermute | solution.py:651
  96.5 7.8 %collective-permute-start.8 = (bf16[28,32,128]{2,1,0:T(8,128)(2,1)}, bf16[28,32,128]{2,1,0:T(8,128)(2,1)S(1)}, u32[]{:S(2)}, u32[]{:S(2)}) collective-permute-start(bf16[28,32,128]{2,1,0:T(8,128)(2,1)} %get-tuple-element.102), channel_id=1, source_target_pairs={{0,3},{1,0},{2,1},{3,2},{4,7},{5,4},{6,5},{7,6},{8,11},{9,8},{10,9... | collective-permute-start | bytes 688136 | tf_op jit(solution)/shard_map/ppermute | solution.py:651
  99.2 9.0 %collective-permute-start.9 = (bf16[28,32,128]{2,1,0:T(8,128)(2,1)S(1)}, bf16[28,32,128]{2,1,0:T(8,128)(2,1)S(1)}, u32[]{:S(2)}, u32[]{:S(2)}) collective-permute-start(bf16[28,32,128]{2,1,0:T(8,128)(2,1)S(1)} %get-tuple-element.103), channel_id=1, source_target_pairs={{0,2},{1,3},{2,0},{3,1},{4,6},{5,7},{6,4},{7,5},{8,10},{9,11},{10,... | collective-permute-start | bytes 688136 | tf_op jit(solution)/shard_map/ppermute | solution.py:651
Sparse Core Ops, SparseCore 0:
  35.5 45.4 all-gather.5

commit v8 on v7

--- a/solution.py
+++ b/solution.py
@@ -25,11 +25,11 @@
 CAP_Z = 124
 ROWS_Z = 128
 CAP_X = 120
-ORDER_Z = (3, 5, 4, 2, 6, 1, 7)
-ORDER_Y = (1, 3, 2)
+ORDER_Z = (4, 3, 5, 2, 6, 1, 7)
+ORDER_Y = (2, 1, 3)
 GROUP = 8
 FAR_GROUP = 3
-ROWS_AT_ONCE = 4
+STEPS_AT_ONCE = 8
 HEIGHT_2 = NC * HEIGHT
 OUT_COLS = 72
 ZERO_BLOCK = NY * HEIGHT * QUARTER
@@ -195,16 +195,9 @@
 
     lax.fori_loop(0, own_ref[15, 1], clear, 0)
 
-    def product(step):
+    def add_product(step):
         begin = plan_ref[2, step]
         length = plan_ref[3, step]
-        right = jnp.concatenate(
-            [
-                own_block(whole_ref, plan_ref[4 + member, step], pl.ds(0, SIDE))
-                for member in range(HEIGHT)
-            ],
-            axis=1,
-        )
         pieces, columns = [], []
         for at in range(FAR_GROUP):
             place = jnp.minimum(begin + at, CAP_X - 1)
@@ -213,19 +206,26 @@
                 pieces.append(pieces_ref[part, rows, :])
             columns.append(jnp.where(at < length, plan_ref[1, place], OUT_COLS))
         left = jnp.concatenate(pieces, axis=0).astype(BF)
-        return jnp.dot(left, right, preferred_element_type=F32), columns
-
-    def add(value, columns):
-        for at, column in enumerate(columns):
-            total[column] = total[column] + value[at * WIDE : (at + 1) * WIDE]
+        for member in range(0, HEIGHT, 2):
+            right = jnp.concatenate(
+                [
+                    own_block(whole_ref, plan_ref[4 + member + at, step], pl.ds(0, SIDE))
+                    for at in range(2)
+                ],
+                axis=1,
+            )
+            value = jnp.dot(left, right, preferred_element_type=F32)
+            lanes = pl.ds(member * SIDE, 2 * SIDE)
+            for at, column in enumerate(columns):
+                rows = slice(at * WIDE, (at + 1) * WIDE)
+                total[column, :, lanes] = total[column, :, lanes] + value[rows]
 
     def steps(number, carry):
-        done = [product(number * ROWS_AT_ONCE + at) for at in range(ROWS_AT_ONCE)]
-        for value, columns in done:
-            add(value, columns)
+        for at in range(STEPS_AT_ONCE):
+            add_product(number * STEPS_AT_ONCE + at)
         return carry
 
-    lax.fori_loop(0, (plan_ref[8, 0] + ROWS_AT_ONCE - 1) // ROWS_AT_ONCE, steps, 0)
+    lax.fori_loop(0, (plan_ref[8, 0] + STEPS_AT_ONCE - 1) // STEPS_AT_ONCE, steps, 0)
 
     for step, out_ref in enumerate(out_refs):
         part = (own_ref[15, 0] + step) & (NY - 1)

time: 119 us -> 120 us (level); the launches traced: 117 us -> 120 us
  waiting for transfers between devices: 37.9 us -> 42.2 us
  starting transfers between devices: 33.9 us -> 32.4 us
    ppermute x7, waiting for transfers between devices: 12.4 us -> 15.3 us  [shards(): lax.ppermute(packed[step], 'z', [(i, (i + step) % NZ) for i in range(NZ)])]
    ppermute x7, starting transfers between devices: 18.3 us -> 15.8 us  [shards(): lax.ppermute(packed[step], 'z', [(i, (i + step) % NZ) for i in range(NZ)])]
    ppermute x3, waiting for transfers between devices: 8.97 us -> 10.5 us  [shards(): cuts.append(lax.ppermute(result[step], 'col', pairs))]
  transfers between devices with their start and end apart: 13 -> 13, of which waited for: 11 -> 10; matrix products, arithmetic and copies ran while one was open for 2% -> 2% of each run, Pallas kernels for 10% -> 10%
where the time goes in v8:
time: 120 us
  waiting for transfers between devices  42.2 us (35%)
  starting transfers between devices  32.4 us (27%)
  Pallas kernels  25.8 us (22%)
  between operations  14.1 us (12%)
  local copies, waits for them, and re-layouts  4.84 us (4%)
    ppermute x7, starting transfers between devices, shards(): lax.ppermute(packed[step], 'z', [(i, (i + step) % NZ) for i in range(NZ)])  15.8 us
    ppermute x7, waiting for transfers between devices, shards(): lax.ppermute(packed[step], 'z', [(i, (i + step) % NZ) for i in range(NZ)])  15.3 us
    ppermute x3, waiting for transfers between devices, shards(): cuts.append(lax.ppermute(result[step], 'col', pairs))  10.5 us
    all_to_all x1, waiting for transfers between devices, shards(): lax.all_to_all(cuts, ('col', 'x', 'core'), split_axis=0, concat_axis=0, t...  9.95 us
    all_to_all x1, starting transfers between devices, shards(): lax.all_to_all(cuts, ('col', 'x', 'core'), split_axis=0, concat_axis=0, t...  8.59 us
    pallas_call x1, Pallas kernels, far_sums(): pl.pallas_call(far_kernel, out_shape=[jax.ShapeDtypeStruct((HEIGHT * QUAR...  6.1 us
    all_to_all x1, waiting for transfers between devices, shards(): lax.all_to_all(packed, ('x', 'core'), split_axis=0, concat_axis=0, tiled=...  5.37 us
    all_to_all x1, starting transfers between devices, shards(): lax.all_to_all(packed, ('x', 'core'), split_axis=0, concat_axis=0, tiled=...  4.3 us
  transfers between devices with their start and end apart: 13, of which 10 were waited for; matrix products, arithmetic and copies ran while one was open for 2% of the time, Pallas kernels for 10%

profile of v8, /device:TPU:1, one launch (start us, length us, event | category | flops | bytes accessed | tf_op | source)
XLA Modules:
  0.0 119.5 jit_solution(6760022928182452969)
XLA Ops:
  6.5 0.1 pad_add_fusion.position_ref
  6.6 2.9 %prepare.1 = bf16[32,32,512]{2,1,0:T(8,128)(2,1)} custom-call(s32[4]{0:T(128)S(1)} %pad_add_fusion.position_ref, s32[4,7]{1,0:T(4,128)} %keep_ref.3, bf16[4,7,128,128]{3,2,1,0:T(8,128)(2,1)} %blocks_ref.2), custom_call_target="tpu_custom_call" | custom-call | tf_op jit(solution)/shard_map/prepare/pallas_call | solution.py:86
  9.5 8.6 %all-to-all-start.1 = ((bf16[32,32,512]{2,1,0:T(8,128)(2,1)}), bf16[32,32,512]{2,1,0:T(8,128)(2,1)S(1)}, u32[]{:S(2)}, u32[]{:S(2)}) async-start(bf16[32,32,512]{2,1,0:T(8,128)(2,1)} %prepare.1), calls=%async_computation.2 | async-start | bytes 2097152 | tf_op jit(solution)/shard_map/all_to_all | solution.py:630
  18.1 0.0 copy-start.4
  18.1 0.0 copy-start.5
  18.2 0.0 all-gather.6.cloned.1.call-start
  18.2 0.9 copy.101
  19.1 0.3 reshape.214
  19.4 0.1 reshape.215
  19.5 0.1 reshape.216.entries_ref
  19.6 0.9 copy.103.columns_ref
  20.5 2.4 %turn.1 = bf16[4,7,128,128]{3,2,1,0:T(8,128)(2,1)} custom-call(s32[4,7]{1,0:T(4,128)} %keep_ref.3, bf16[4,7,128,128]{3,2,1,0:T(8,128)(2,1)} %blocks_ref.2), custom_call_target="tpu_custom_call" | custom-call | flops 117440512 | bytes 1835008 | tf_op jit(solution)/shard_map/turn/pallas_call | solution.py:107
  22.9 2.5 %pattern.1 = (s32[256,256]{1,0:T(8,128)S(1)}, f32[128,256]{1,0:T(8,128)S(1)}, f32[128,1024]{1,0:T(8,128)S(1)}, f32[8,1024]{1,0:T(8,128)S(1)}) custom-call(s32[4]{0:T(128)S(1)} %pad_add_fusion.position_ref, s32[256,28]{1,0:T(8,128)S(1)} %copy.103.columns_ref, s32[1,1024]{1,0:T(1,128)S(1)} %reshape.216.entries_ref), custom_call_target="tpu_custom_call" | custom-call | flops 234881024 | bytes 524288 | tf_op jit(solution)/shard_map/pattern/pallas_call | solution.py:351
  25.4 10.0 %all-to-all-done.1 = bf16[32,32,512]{2,1,0:T(8,128)(2,1)S(1)} async-done(((bf16[32,32,512]{2,1,0:T(8,128)(2,1)}), bf16[32,32,512]{2,1,0:T(8,128)(2,1)S(1)}, u32[]{:S(2)}, u32[]{:S(2)}) %all-to-all-start.1) | async-done | bytes 1048608 | tf_op jit(solution)/shard_map/all_to_all | solution.py:630
  35.3 0.0 all-gather.6.cloned.1.call-update
  35.3 3.2 %send.1 = (bf16[128,512]{1,0:T(8,128)(2,1)S(1)}, bf16[128,512]{1,0:T(8,128)(2,1)S(1)}, bf16[128,512]{1,0:T(8,128)(2,1)S(1)}, bf16[128,512]{1,0:T(8,128)(2,1)S(1)...) custom-call(s32[4]{0:T(128)S(1)} %pad_add_fusion.position_ref, ...), custom_call_target="tpu_custom_call" | custom-call | tf_op jit(solution)/shard_map/send/pallas_call | solution.py:406
  38.6 7.0 %collective-permute-start = (bf16[128,512]{1,0:T(8,128)(2,1)S(1)}, bf16[128,512]{1,0:T(8,128)(2,1)S(1)}, u32[]{:S(2)}, u32[]{:S(2)}) collective-permute-start(bf16[128,512]{1,0:T(8,128)(2,1)S(1)} %get-tuple-element.78), channel_id=1, source_target_pairs={{0,32},{8,40},{16,48},{24,56},{32,0},{40,8},{48,16},{56,24},{1,33}... | collective-permute-start | bytes 393224 | tf_op jit(solution)/shard_map/ppermute | solution.py:637
  45.6 1.6 %collective-permute-start.1 = (bf16[128,512]{1,0:T(8,128)(2,1)S(1)}, bf16[128,512]{1,0:T(8,128)(2,1)S(1)}, u32[]{:S(2)}, u32[]{:S(2)}) collective-permute-start(bf16[128,512]{1,0:T(8,128)(2,1)S(1)} %get-tuple-element.79), channel_id=1, source_target_pairs={{0,24},{8,32},{16,40},{24,48},{32,56},{40,0},{48,8},{56,16},{1,25}... | collective-permute-start | bytes 393224 | tf_op jit(solution)/shard_map/ppermute | solution.py:637
  47.2 2.8 %collective-permute-start.2 = (bf16[128,512]{1,0:T(8,128)(2,1)S(1)}, bf16[128,512]{1,0:T(8,128)(2,1)S(1)}, u32[]{:S(2)}, u32[]{:S(2)}) collective-permute-start(bf16[128,512]{1,0:T(8,128)(2,1)S(1)} %get-tuple-element.80), channel_id=1, source_target_pairs={{0,40},{8,48},{16,56},{24,0},{32,8},{40,16},{48,24},{56,32},{1,41}... | collective-permute-start | bytes 393224 | tf_op jit(solution)/shard_map/ppermute | solution.py:637
  50.0 1.2 collective-permute-start.3
  51.2 2.4 %collective-permute-start.4 = (bf16[128,512]{1,0:T(8,128)(2,1)S(1)}, bf16[128,512]{1,0:T(8,128)(2,1)S(1)}, u32[]{:S(2)}, u32[]{:S(2)}) collective-permute-start(bf16[128,512]{1,0:T(8,128)(2,1)S(1)} %get-tuple-element.82), channel_id=1, source_target_pairs={{0,48},{8,56},{16,0},{24,8},{32,16},{40,24},{48,32},{56,40},{1,49}... | collective-permute-start | bytes 393224 | tf_op jit(solution)/shard_map/ppermute | solution.py:637
  53.6 0.0 collective-permute-done.refs_1_
  53.6 0.7 collective-permute-start.5
  54.3 7.4 %collective-permute-done.1.refs_2_ = bf16[128,512]{1,0:T(8,128)(2,1)S(1)} collective-permute-done((bf16[128,512]{1,0:T(8,128)(2,1)S(1)}, bf16[128,512]{1,0:T(8,128)(2,1)S(1)}, u32[]{:S(2)}, u32[]{:S(2)}) %collective-permute-start.1) | collective-permute-done | bytes 131104 | tf_op jit(solution)/shard_map/ppermute | solution.py:637
  61.7 0.0 collective-permute-start.6
  61.7 0.0 collective-permute-done.2.refs_3_
  61.7 0.7 collective-permute-done.3.refs_4_
  62.4 3.4 %collective-permute-done.4.refs_5_ = bf16[128,512]{1,0:T(8,128)(2,1)S(1)} collective-permute-done((bf16[128,512]{1,0:T(8,128)(2,1)S(1)}, bf16[128,512]{1,0:T(8,128)(2,1)S(1)}, u32[]{:S(2)}, u32[]{:S(2)}) %collective-permute-start.4) | collective-permute-done | bytes 131104 | tf_op jit(solution)/shard_map/ppermute | solution.py:637
  65.9 3.1 %collective-permute-done.5.refs_6_ = bf16[128,512]{1,0:T(8,128)(2,1)S(1)} collective-permute-done((bf16[128,512]{1,0:T(8,128)(2,1)S(1)}, bf16[128,512]{1,0:T(8,128)(2,1)S(1)}, u32[]{:S(2)}, u32[]{:S(2)}) %collective-permute-start.5) | collective-permute-done | bytes 131104 | tf_op jit(solution)/shard_map/ppermute | solution.py:637
  68.9 0.7 collective-permute-done.6.refs_7_
  69.6 2.3 %route.1 = bf16[8,120,512]{2,1,0:T(8,128)(2,1)} custom-call(bf16[128,512]{1,0:T(8,128)(2,1)S(1)} %get-tuple-element.88.refs_0_, bf16[128,512]{1,0:T(8,128)(2,1)S(1)} %collective-permute-done.refs_1_, bf16[128,512]{1,0:T(8,128)(2,1)S(1)} %collective-permute-done.1.refs_2_, bf16[128,512]{1,0:T(8,128)(2,1)S(1)} %collective-permute-done.2.refs_3_, ...), custom_call_target="tpu_custom_call" | custom-call | tf_op jit(solution)/shard_map/route/pallas_call | solution.py:448
  71.9 4.3 %all-to-all-start.2 = ((bf16[8,120,512]{2,1,0:T(8,128)(2,1)}), bf16[8,120,512]{2,1,0:T(8,128)(2,1)S(1)}, u32[]{:S(2)}, u32[]{:S(2)}) async-start(bf16[8,120,512]{2,1,0:T(8,128)(2,1)} %route.1), calls=%async_computation.3 | async-start | bytes 1966080 | tf_op jit(solution)/shard_map/all_to_all | solution.py:642
  76.2 0.8 own_plan.1.plan_ref.own_ref
  77.0 1.6 %far_plan.1.plan_ref = s32[16,128]{1,0:T(8,128)S(1)} custom-call(s32[4]{0:T(128)S(1)} %pad_add_fusion.position_ref, s32[256,256]{1,0:T(8,128)S(1)} %get-tuple-element.86.slots_ref, f32[128,256]{1,0:T(8,128)S(1)} %get-tuple-element.87.union_ref, bf16[128,512]{1,0:T(8,128)(2,1)S(1)} %get-tuple-element.88.refs_0_, ...), custom_call_target="tpu_custom_call" | custom-call | flops 671088640 | bytes 524288 | tf_op jit(solution)/shard_map/far_plan/pallas_call | solution.py:566
  78.6 0.6 slice.68
  79.9 1.1 all-gather.6.cloned.1.call-done
  81.0 0.0 copy-start
  81.0 2.0 %copy-done = bf16[16,7,128,128]{3,2,1,0:T(8,128)(2,1)S(1)} copy-done((bf16[16,7,128,128]{3,2,1,0:T(8,128)(2,1)S(1)}, bf16[16,7,128,128]{3,2,1,0:T(8,128)(2,1)}, u32[]{:S(2)}) %copy-start) | copy-done | bytes 3670040
  83.0 2.2 %own_sums.1.near_ref = f32[112,32,128]{2,1,0:T(8,128)S(1)} custom-call(s32[16,128]{1,0:T(8,128)S(1)} %own_plan.1.plan_ref.own_ref, bf16[112,128,128]{2,1,0:T(8,128)(2,1)S(1)} %bitcast.151), custom_call_target="tpu_custom_call" | custom-call | flops 536870912 | bytes 5505024 | tf_op jit(solution)/shard_map/own_sums/pallas_call | solution.py:161
  85.2 5.4 %all-to-all-done.2 = bf16[8,120,512]{2,1,0:T(8,128)(2,1)S(1)} async-done(((bf16[8,120,512]{2,1,0:T(8,128)(2,1)}), bf16[8,120,512]{2,1,0:T(8,128)(2,1)S(1)}, u32[]{:S(2)}, u32[]{:S(2)}) %all-to-all-start.2) | async-done | bytes 983072 | tf_op jit(solution)/shard_map/all_to_all | solution.py:642
  90.6 6.1 %far_sums.1 = (bf16[28,32,128]{2,1,0:T(8,128)(2,1)S(1)}, bf16[28,32,128]{2,1,0:T(8,128)(2,1)}, bf16[28,32,128]{2,1,0:T(8,128)(2,1)}, bf16[28,32,128]{2,1,0:T(8,128)(2,1)S(1)}) custom-call(s32[16,128]{1,0:T(8,128)S(1)} %own_plan.1.plan_ref.own_ref, s32[16,128]{1,0:T(8,128)S(1)} %far_plan.1.plan_ref, bf16[112,128,128]{2,1,0:T(8,128)(2,1)} %bitcast.150, ...), custom_call_target="tpu_custom_call" | custom-call | tf_op jit(solution)/shard_map/far_sums/pallas_call | solution.py:241
  96.7 1.0 collective-permute-start.7
  97.7 0.1 collective-permute-start.8
  97.8 2.6 %collective-permute-start.9 = (bf16[28,32,128]{2,1,0:T(8,128)(2,1)S(1)}, bf16[28,32,128]{2,1,0:T(8,128)(2,1)S(1)}, u32[]{:S(2)}, u32[]{:S(2)}) collective-permute-start(bf16[28,32,128]{2,1,0:T(8,128)(2,1)S(1)} %get-tuple-element.103), channel_id=1, source_target_pairs={{0,3},{1,0},{2,1},{3,2},{4,7},{5,4},{6,5},{7,6},{8,11},{9,8},{10,9... | collective-permute-start | bytes 688136 | tf_op jit(solution)/shard_map/ppermute | solution.py:651
  100.4 4.3 %collective-permute-done.7.refs_1_ = bf16[28,32,128]{2,1,0:T(8,128)(2,1)S(1)} collective-permute-done((bf16[28,32,128]{2,1,0:T(8,128)(2,1)}, bf16[28,32,128]{2,1,0:T(8,128)(2,1)S(1)}, u32[]{:S(2)}, u32[]{:S(2)}) %collective-permute-start.7) | collective-permute-done | bytes 229408 | tf_op jit(solution)/shard_map/ppermute | solution.py:651
  104.7 6.1 %collective-permute-done.8.refs_2_ = bf16[28,32,128]{2,1,0:T(8,128)(2,1)S(1)} collective-permute-done((bf16[28,32,128]{2,1,0:T(8,128)(2,1)}, bf16[28,32,128]{2,1,0:T(8,128)(2,1)S(1)}, u32[]{:S(2)}, u32[]{:S(2)}) %collective-permute-start.8) | collective-permute-done | bytes 229408 | tf_op jit(solution)/shard_map/ppermute | solution.py:651
  110.9 0.0 collective-permute-done.9.refs_3_
  110.9 0.0 copy-done.4
  110.9 0.0 copy-done.5
  110.9 1.8 %finish.1 = bf16[4,7,128,128]{3,2,1,0:T(8,128)(2,1)} custom-call(s32[4]{0:T(128)S(1)} %pad_add_fusion.position_ref, bf16[28,32,128]{2,1,0:T(8,128)(2,1)S(1)} %get-tuple-element.100.refs_0_, bf16[28,32,128]{2,1,0:T(8,128)(2,1)S(1)} %collective-permute-done.7.refs_1_, bf16[28,32,128]{2,1,0:T(8,128)(2,1)S(1)} %collective-permute-done.8.refs_2_, ...), custom_call_target="tpu_custom_call" | custom-call | tf_op jit(solution)/shard_map/finish/pallas_call | solution.py:270
  (4 shorter events, 0.0 us)
Async XLA Ops:
  9.5 25.8 %all-to-all-start.1 = ((bf16[32,32,512]{2,1,0:T(8,128)(2,1)}), bf16[32,32,512]{2,1,0:T(8,128)(2,1)S(1)}, u32[]{:S(2)}, u32[]{:S(2)}) async-start(bf16[32,32,512]{2,1,0:T(8,128)(2,1)} %prepare.1), calls=%async_computation.2 | async-start | bytes 2097152 | tf_op jit(solution)/shard_map/all_to_all | solution.py:630
  18.1 92.7 %copy-start.4 = (s32[256,28]{0,1:T(8,128)S(1)}, s32[256,28]{0,1:T(8,128)}, u32[]{:S(2)}) copy-start(s32[256,28]{0,1:T(8,128)} %param.7) | copy-start | bytes 86020
  18.1 92.7 %copy-start.5 = (s32[4,7]{1,0:T(4,128)S(1)}, s32[4,7]{1,0:T(4,128)}, u32[]{:S(2)}) copy-start(s32[4,7]{1,0:T(4,128)} %keep_ref.3) | copy-start | bytes 340
  18.2 62.8 %all-gather.6.cloned.1.call-start = ((), (), s32[]{:S(2)}) async-start(), calls=%async_computation.6 | async-start | bytes 4587520 | tf_op jit(solution)/shard_map/all_gather | solution.py:632
  38.6 15.1 %collective-permute-start = (bf16[128,512]{1,0:T(8,128)(2,1)S(1)}, bf16[128,512]{1,0:T(8,128)(2,1)S(1)}, u32[]{:S(2)}, u32[]{:S(2)}) collective-permute-start(bf16[128,512]{1,0:T(8,128)(2,1)S(1)} %get-tuple-element.78), channel_id=1, source_target_pairs={{0,32},{8,40},{16,48},{24,56},{32,0},{40,8},{48,16},{56,24},{1,33}... | collective-permute-start | bytes 393224 | tf_op jit(solution)/shard_map/ppermute | solution.py:637
  45.6 16.2 %collective-permute-start.1 = (bf16[128,512]{1,0:T(8,128)(2,1)S(1)}, bf16[128,512]{1,0:T(8,128)(2,1)S(1)}, u32[]{:S(2)}, u32[]{:S(2)}) collective-permute-start(bf16[128,512]{1,0:T(8,128)(2,1)S(1)} %get-tuple-element.79), channel_id=1, source_target_pairs={{0,24},{8,32},{16,40},{24,48},{32,56},{40,0},{48,8},{56,16},{1,25}... | collective-permute-start | bytes 393224 | tf_op jit(solution)/shard_map/ppermute | solution.py:637
  47.2 14.5 %collective-permute-start.2 = (bf16[128,512]{1,0:T(8,128)(2,1)S(1)}, bf16[128,512]{1,0:T(8,128)(2,1)S(1)}, u32[]{:S(2)}, u32[]{:S(2)}) collective-permute-start(bf16[128,512]{1,0:T(8,128)(2,1)S(1)} %get-tuple-element.80), channel_id=1, source_target_pairs={{0,40},{8,48},{16,56},{24,0},{32,8},{40,16},{48,24},{56,32},{1,41}... | collective-permute-start | bytes 393224 | tf_op jit(solution)/shard_map/ppermute | solution.py:637
  50.0 12.4 %collective-permute-start.3 = (bf16[128,512]{1,0:T(8,128)(2,1)S(1)}, bf16[128,512]{1,0:T(8,128)(2,1)S(1)}, u32[]{:S(2)}, u32[]{:S(2)}) collective-permute-start(bf16[128,512]{1,0:T(8,128)(2,1)S(1)} %get-tuple-element.81), channel_id=1, source_target_pairs={{0,16},{8,24},{16,32},{24,40},{32,48},{40,56},{48,0},{56,8},{1,17}... | collective-permute-start | bytes 393224 | tf_op jit(solution)/shard_map/ppermute | solution.py:637
  51.2 14.6 %collective-permute-start.4 = (bf16[128,512]{1,0:T(8,128)(2,1)S(1)}, bf16[128,512]{1,0:T(8,128)(2,1)S(1)}, u32[]{:S(2)}, u32[]{:S(2)}) collective-permute-start(bf16[128,512]{1,0:T(8,128)(2,1)S(1)} %get-tuple-element.82), channel_id=1, source_target_pairs={{0,48},{8,56},{16,0},{24,8},{32,16},{40,24},{48,32},{56,40},{1,49}... | collective-permute-start | bytes 393224 | tf_op jit(solution)/shard_map/ppermute | solution.py:637
  53.6 15.3 %collective-permute-start.5 = (bf16[128,512]{1,0:T(8,128)(2,1)S(1)}, bf16[128,512]{1,0:T(8,128)(2,1)S(1)}, u32[]{:S(2)}, u32[]{:S(2)}) collective-permute-start(bf16[128,512]{1,0:T(8,128)(2,1)S(1)} %get-tuple-element.83), channel_id=1, source_target_pairs={{0,8},{8,16},{16,24},{24,32},{32,40},{40,48},{48,56},{56,0},{1,9},... | collective-permute-start | bytes 393224 | tf_op jit(solution)/shard_map/ppermute | solution.py:637
  61.7 7.9 %collective-permute-start.6 = (bf16[128,512]{1,0:T(8,128)(2,1)S(1)}, bf16[128,512]{1,0:T(8,128)(2,1)S(1)}, u32[]{:S(2)}, u32[]{:S(2)}) collective-permute-start(bf16[128,512]{1,0:T(8,128)(2,1)S(1)} %get-tuple-element.84), channel_id=1, source_target_pairs={{0,56},{8,0},{16,8},{24,16},{32,24},{40,32},{48,40},{56,48},{1,57}... | collective-permute-start | bytes 393224 | tf_op jit(solution)/shard_map/ppermute | solution.py:637
  71.9 18.7 %all-to-all-start.2 = ((bf16[8,120,512]{2,1,0:T(8,128)(2,1)}), bf16[8,120,512]{2,1,0:T(8,128)(2,1)S(1)}, u32[]{:S(2)}, u32[]{:S(2)}) async-start(bf16[8,120,512]{2,1,0:T(8,128)(2,1)} %route.1), calls=%async_computation.3 | async-start | bytes 1966080 | tf_op jit(solution)/shard_map/all_to_all | solution.py:642
  81.0 2.0 %copy-start = (bf16[16,7,128,128]{3,2,1,0:T(8,128)(2,1)S(1)}, bf16[16,7,128,128]{3,2,1,0:T(8,128)(2,1)}, u32[]{:S(2)}) copy-start(bf16[16,7,128,128]{3,2,1,0:T(8,128)(2,1)} %all-gather.6.cloned.1.call-done) | copy-start | bytes 11010052
  96.7 8.0 %collective-permute-start.7 = (bf16[28,32,128]{2,1,0:T(8,128)(2,1)}, bf16[28,32,128]{2,1,0:T(8,128)(2,1)S(1)}, u32[]{:S(2)}, u32[]{:S(2)}) collective-permute-start(bf16[28,32,128]{2,1,0:T(8,128)(2,1)} %get-tuple-element.101), channel_id=1, source_target_pairs={{0,2},{1,3},{2,0},{3,1},{4,6},{5,7},{6,4},{7,5},{8,10},{9,11},{10,... | collective-permute-start | bytes 688136 | tf_op jit(solution)/shard_map/ppermute | solution.py:651
  97.7 13.1 %collective-permute-start.8 = (bf16[28,32,128]{2,1,0:T(8,128)(2,1)}, bf16[28,32,128]{2,1,0:T(8,128)(2,1)S(1)}, u32[]{:S(2)}, u32[]{:S(2)}) collective-permute-start(bf16[28,32,128]{2,1,0:T(8,128)(2,1)} %get-tuple-element.102), channel_id=1, source_target_pairs={{0,1},{1,2},{2,3},{3,0},{4,5},{5,6},{6,7},{7,4},{8,9},{9,10},{10,1... | collective-permute-start | bytes 688136 | tf_op jit(solution)/shard_map/ppermute | solution.py:651
  97.8 13.0 %collective-permute-start.9 = (bf16[28,32,128]{2,1,0:T(8,128)(2,1)S(1)}, bf16[28,32,128]{2,1,0:T(8,128)(2,1)S(1)}, u32[]{:S(2)}, u32[]{:S(2)}) collective-permute-start(bf16[28,32,128]{2,1,0:T(8,128)(2,1)S(1)} %get-tuple-element.103), channel_id=1, source_target_pairs={{0,3},{1,0},{2,1},{3,2},{4,7},{5,4},{6,5},{7,6},{8,11},{9,8},{10,9... | collective-permute-start | bytes 688136 | tf_op jit(solution)/shard_map/ppermute | solution.py:651
Sparse Core Ops, SparseCore 0:
  35.5 45.4 all-gather.5

commit v9 on v8

--- a/solution.py
+++ b/solution.py
@@ -182,7 +182,8 @@
     near_ref,
     *refs,
 ):
-    *out_refs, total, pieces_ref = refs
+    *out_refs, low, high, pieces_ref = refs
+    halves = (low, high)
     for sender in range(TARGETS):
         rows = pl.ds(sender * CAP_X, CAP_X)
         for part in range(NY):
@@ -190,7 +191,8 @@
             pieces_ref[part, rows, :] = far_ref[rows, lanes].astype(F32)
 
     def clear(group, carry):
-        total[pl.ds(group * GROUP, GROUP)] = jnp.zeros((GROUP, WIDE, HEIGHT * SIDE), F32)
+        for total in halves:
+            total[pl.ds(group * GROUP, GROUP)] = jnp.zeros((GROUP, WIDE, 2 * SIDE), F32)
         return carry
 
     lax.fori_loop(0, own_ref[15, 1], clear, 0)
@@ -206,19 +208,18 @@
                 pieces.append(pieces_ref[part, rows, :])
             columns.append(jnp.where(at < length, plan_ref[1, place], OUT_COLS))
         left = jnp.concatenate(pieces, axis=0).astype(BF)
-        for member in range(0, HEIGHT, 2):
+        for half, total in enumerate(halves):
             right = jnp.concatenate(
                 [
-                    own_block(whole_ref, plan_ref[4 + member + at, step], pl.ds(0, SIDE))
+                    own_block(whole_ref, plan_ref[4 + 2 * half + at, step], pl.ds(0, SIDE))
                     for at in range(2)
                 ],
                 axis=1,
             )
             value = jnp.dot(left, right, preferred_element_type=F32)
-            lanes = pl.ds(member * SIDE, 2 * SIDE)
+            before = [total[column] for column in columns]
             for at, column in enumerate(columns):
-                rows = slice(at * WIDE, (at + 1) * WIDE)
-                total[column, :, lanes] = total[column, :, lanes] + value[rows]
+                total[column] = before[at] + value[at * WIDE : (at + 1) * WIDE]
 
     def steps(number, carry):
         for at in range(STEPS_AT_ONCE):
@@ -232,7 +233,7 @@
         for place in range(HEIGHT * QUARTER):
             member, slot = place // QUARTER, part * QUARTER + place % QUARTER
             column = own_ref[8, member * (128 // HEIGHT) + slot]
-            value = total[column, :, pl.ds(member * SIDE, SIDE)]
+            value = halves[member // 2][column, :, pl.ds(member % 2 * SIDE, SIDE)]
             value = value + near_ref[part * (HEIGHT * QUARTER) + place]
             out_ref[place] = value.astype(BF)
 
@@ -244,7 +245,8 @@
         in_specs=[smem(), smem(), vmem(), vmem(), vmem()],
         out_specs=[vmem()] * NY,
         scratch_shapes=[
-            pltpu.VMEM((OUT_COLS + 1, WIDE, HEIGHT * SIDE), F32),
+            pltpu.VMEM((OUT_COLS + 1, WIDE, 2 * SIDE), F32),
+            pltpu.VMEM((OUT_COLS + 1, WIDE, 2 * SIDE), F32),
             pltpu.VMEM((NY, TARGETS * CAP_X, SIDE), F32),
         ],
         compiler_params=params(),
@@ -383,13 +385,17 @@
     for to in range(NZ):
         chosen_ref[to * ROWS_Z : (to + 1) * ROWS_Z, :] = one_hot(code[to : to + 1], ROWS_Z)
     packed = jnp.dot(chosen_ref[...], near, preferred_element_type=F32)
+    kq = kq_ref[...]
+    line = iota((128, ENTRIES), 0)
+    facts = jnp.where(line == SLABS, kq[0:1], jnp.where(line == SLABS + 1, kq[1:2], need))
+    facts = jnp.dot(chosen_ref[...], facts.T.astype(BF), preferred_element_type=F32)
     tail = iota((16, PIECE), 0)
-    kq = kq_ref[...]
+    slab = iota((16, 128), 1)
+    target = iota((16, 128), 0)
     for to in range(NZ):
-        target = iota((8, 128), 0)
-        choice = slab == (target // NC * NZ + ((z + to) & (NZ - 1))) * NC + target % NC
-        asked = jnp.concatenate([dot(choice.astype(F32), need), kq], axis=0)
-        notes = dot_rows(asked, chosen_ref[to * ROWS_Z : (to + 1) * ROWS_Z, :])
+        choice = (target // NC * NZ + ((z + to) & (NZ - 1))) * NC + target % NC
+        choice = slab == jnp.where(target < TARGETS, choice, SLABS - TARGETS + target)
+        notes = dot_rows(choice, facts[to * ROWS_Z : (to + 1) * ROWS_Z])
         first = jnp.concatenate([notes[i : i + 1] for i in range(4)], axis=1)
         second = jnp.concatenate([notes[i : i + 1] for i in range(4, 8)], axis=1)
         third = jnp.concatenate([notes[8:9], notes[9:10], totals, most], axis=1)

time: 120 us -> 120 us (level)
  no operation moved by 1% of the time
where the time goes in v9:
time: 120 us; the launch traced here: 119 us
  waiting for transfers between devices  42.2 us (35%)
  starting transfers between devices  32.4 us (27%)
  Pallas kernels  25.7 us (21%)
  between operations  14.1 us (12%)
  local copies, waits for them, and re-layouts  4.84 us (4%)
    ppermute x7, starting transfers between devices, shards(): lax.ppermute(packed[step], 'z', [(i, (i + step) % NZ) for i in range(NZ)])  15.8 us
    ppermute x7, waiting for transfers between devices, shards(): lax.ppermute(packed[step], 'z', [(i, (i + step) % NZ) for i in range(NZ)])  15.3 us
    ppermute x3, waiting for transfers between devices, shards(): cuts.append(lax.ppermute(result[step], 'col', pairs))  10.5 us
    all_to_all x1, waiting for transfers between devices, shards(): lax.all_to_all(cuts, ('col', 'x', 'core'), split_axis=0, concat_axis=0, t...  9.95 us
    all_to_all x1, starting transfers between devices, shards(): lax.all_to_all(cuts, ('col', 'x', 'core'), split_axis=0, concat_axis=0, t...  8.59 us
    pallas_call x1, Pallas kernels, far_sums(): pl.pallas_call(far_kernel, out_shape=[jax.ShapeDtypeStruct((HEIGHT * QUAR...  6.08 us
    all_to_all x1, waiting for transfers between devices, shards(): lax.all_to_all(packed, ('x', 'core'), split_axis=0, concat_axis=0, tiled=...  5.26 us
    all_to_all x1, starting transfers between devices, shards(): lax.all_to_all(packed, ('x', 'core'), split_axis=0, concat_axis=0, tiled=...  4.3 us
  transfers between devices with their start and end apart: 13, of which 10 were waited for; matrix products, arithmetic and copies ran while one was open for 2% of the time, Pallas kernels for 10%

profile of v9, /device:TPU:1, one launch (start us, length us, event | category | flops | bytes accessed | tf_op | source)
XLA Modules:
  0.0 119.4 jit_solution(16529436716796255773)
XLA Ops:
  6.5 0.1 pad_add_fusion.position_ref
  6.6 2.9 %prepare.1 = bf16[32,32,512]{2,1,0:T(8,128)(2,1)} custom-call(s32[4]{0:T(128)S(1)} %pad_add_fusion.position_ref, s32[4,7]{1,0:T(4,128)} %keep_ref.3, bf16[4,7,128,128]{3,2,1,0:T(8,128)(2,1)} %blocks_ref.2), custom_call_target="tpu_custom_call" | custom-call | tf_op jit(solution)/shard_map/prepare/pallas_call | solution.py:86
  9.5 8.6 %all-to-all-start.1 = ((bf16[32,32,512]{2,1,0:T(8,128)(2,1)}), bf16[32,32,512]{2,1,0:T(8,128)(2,1)S(1)}, u32[]{:S(2)}, u32[]{:S(2)}) async-start(bf16[32,32,512]{2,1,0:T(8,128)(2,1)} %prepare.1), calls=%async_computation.2 | async-start | bytes 2097152 | tf_op jit(solution)/shard_map/all_to_all | solution.py:636
  18.1 0.0 copy-start.4
  18.1 0.0 copy-start.5
  18.2 0.0 all-gather.6.cloned.1.call-start
  18.2 0.9 copy.101
  19.1 0.3 reshape.214
  19.4 0.1 reshape.215
  19.5 0.1 reshape.216.entries_ref
  19.6 0.9 copy.103.columns_ref
  20.5 2.4 %turn.1 = bf16[4,7,128,128]{3,2,1,0:T(8,128)(2,1)} custom-call(s32[4,7]{1,0:T(4,128)} %keep_ref.3, bf16[4,7,128,128]{3,2,1,0:T(8,128)(2,1)} %blocks_ref.2), custom_call_target="tpu_custom_call" | custom-call | flops 117440512 | bytes 1835008 | tf_op jit(solution)/shard_map/turn/pallas_call | solution.py:107
  22.9 2.5 %pattern.1 = (s32[256,256]{1,0:T(8,128)S(1)}, f32[128,256]{1,0:T(8,128)S(1)}, f32[128,1024]{1,0:T(8,128)S(1)}, f32[8,1024]{1,0:T(8,128)S(1)}) custom-call(s32[4]{0:T(128)S(1)} %pad_add_fusion.position_ref, s32[256,28]{1,0:T(8,128)S(1)} %copy.103.columns_ref, s32[1,1024]{1,0:T(1,128)S(1)} %reshape.216.entries_ref), custom_call_target="tpu_custom_call" | custom-call | flops 234881024 | bytes 524288 | tf_op jit(solution)/shard_map/pattern/pallas_call | solution.py:353
  25.4 10.0 %all-to-all-done.1 = bf16[32,32,512]{2,1,0:T(8,128)(2,1)S(1)} async-done(((bf16[32,32,512]{2,1,0:T(8,128)(2,1)}), bf16[32,32,512]{2,1,0:T(8,128)(2,1)S(1)}, u32[]{:S(2)}, u32[]{:S(2)}) %all-to-all-start.1) | async-done | bytes 1048608 | tf_op jit(solution)/shard_map/all_to_all | solution.py:636
  35.3 0.0 all-gather.6.cloned.1.call-update
  35.3 3.1 %send.1 = (bf16[128,512]{1,0:T(8,128)(2,1)S(1)}, bf16[128,512]{1,0:T(8,128)(2,1)S(1)}, bf16[128,512]{1,0:T(8,128)(2,1)S(1)}, bf16[128,512]{1,0:T(8,128)(2,1)S(1)...) custom-call(s32[4]{0:T(128)S(1)} %pad_add_fusion.position_ref, ...), custom_call_target="tpu_custom_call" | custom-call | tf_op jit(solution)/shard_map/send/pallas_call | solution.py:412
  38.5 7.0 %collective-permute-start = (bf16[128,512]{1,0:T(8,128)(2,1)S(1)}, bf16[128,512]{1,0:T(8,128)(2,1)S(1)}, u32[]{:S(2)}, u32[]{:S(2)}) collective-permute-start(bf16[128,512]{1,0:T(8,128)(2,1)S(1)} %get-tuple-element.78), channel_id=1, source_target_pairs={{0,32},{8,40},{16,48},{24,56},{32,0},{40,8},{48,16},{56,24},{1,33}... | collective-permute-start | bytes 393224 | tf_op jit(solution)/shard_map/ppermute | solution.py:643
  45.4 1.6 %collective-permute-start.1 = (bf16[128,512]{1,0:T(8,128)(2,1)S(1)}, bf16[128,512]{1,0:T(8,128)(2,1)S(1)}, u32[]{:S(2)}, u32[]{:S(2)}) collective-permute-start(bf16[128,512]{1,0:T(8,128)(2,1)S(1)} %get-tuple-element.79), channel_id=1, source_target_pairs={{0,24},{8,32},{16,40},{24,48},{32,56},{40,0},{48,8},{56,16},{1,25}... | collective-permute-start | bytes 393224 | tf_op jit(solution)/shard_map/ppermute | solution.py:643
  47.1 2.8 %collective-permute-start.2 = (bf16[128,512]{1,0:T(8,128)(2,1)S(1)}, bf16[128,512]{1,0:T(8,128)(2,1)S(1)}, u32[]{:S(2)}, u32[]{:S(2)}) collective-permute-start(bf16[128,512]{1,0:T(8,128)(2,1)S(1)} %get-tuple-element.80), channel_id=1, source_target_pairs={{0,40},{8,48},{16,56},{24,0},{32,8},{40,16},{48,24},{56,32},{1,41}... | collective-permute-start | bytes 393224 | tf_op jit(solution)/shard_map/ppermute | solution.py:643
  49.9 1.2 collective-permute-start.3
  51.1 2.4 %collective-permute-start.4 = (bf16[128,512]{1,0:T(8,128)(2,1)S(1)}, bf16[128,512]{1,0:T(8,128)(2,1)S(1)}, u32[]{:S(2)}, u32[]{:S(2)}) collective-permute-start(bf16[128,512]{1,0:T(8,128)(2,1)S(1)} %get-tuple-element.82), channel_id=1, source_target_pairs={{0,48},{8,56},{16,0},{24,8},{32,16},{40,24},{48,32},{56,40},{1,49}... | collective-permute-start | bytes 393224 | tf_op jit(solution)/shard_map/ppermute | solution.py:643
  53.5 0.0 collective-permute-done.refs_1_
  53.5 0.7 collective-permute-start.5
  54.2 7.4 %collective-permute-done.1.refs_2_ = bf16[128,512]{1,0:T(8,128)(2,1)S(1)} collective-permute-done((bf16[128,512]{1,0:T(8,128)(2,1)S(1)}, bf16[128,512]{1,0:T(8,128)(2,1)S(1)}, u32[]{:S(2)}, u32[]{:S(2)}) %collective-permute-start.1) | collective-permute-done | bytes 131104 | tf_op jit(solution)/shard_map/ppermute | solution.py:643
  61.6 0.0 collective-permute-start.6
  61.6 0.0 collective-permute-done.2.refs_3_
  61.6 0.7 collective-permute-done.3.refs_4_
  62.3 3.4 %collective-permute-done.4.refs_5_ = bf16[128,512]{1,0:T(8,128)(2,1)S(1)} collective-permute-done((bf16[128,512]{1,0:T(8,128)(2,1)S(1)}, bf16[128,512]{1,0:T(8,128)(2,1)S(1)}, u32[]{:S(2)}, u32[]{:S(2)}) %collective-permute-start.4) | collective-permute-done | bytes 131104 | tf_op jit(solution)/shard_map/ppermute | solution.py:643
  65.8 3.1 %collective-permute-done.5.refs_6_ = bf16[128,512]{1,0:T(8,128)(2,1)S(1)} collective-permute-done((bf16[128,512]{1,0:T(8,128)(2,1)S(1)}, bf16[128,512]{1,0:T(8,128)(2,1)S(1)}, u32[]{:S(2)}, u32[]{:S(2)}) %collective-permute-start.5) | collective-permute-done | bytes 131104 | tf_op jit(solution)/shard_map/ppermute | solution.py:643
  68.8 0.7 collective-permute-done.6.refs_7_
  69.5 2.3 %route.1 = bf16[8,120,512]{2,1,0:T(8,128)(2,1)} custom-call(bf16[128,512]{1,0:T(8,128)(2,1)S(1)} %get-tuple-element.88.refs_0_, bf16[128,512]{1,0:T(8,128)(2,1)S(1)} %collective-permute-done.refs_1_, bf16[128,512]{1,0:T(8,128)(2,1)S(1)} %collective-permute-done.1.refs_2_, bf16[128,512]{1,0:T(8,128)(2,1)S(1)} %collective-permute-done.2.refs_3_, ...), custom_call_target="tpu_custom_call" | custom-call | tf_op jit(solution)/shard_map/route/pallas_call | solution.py:454
  71.8 4.3 %all-to-all-start.2 = ((bf16[8,120,512]{2,1,0:T(8,128)(2,1)}), bf16[8,120,512]{2,1,0:T(8,128)(2,1)S(1)}, u32[]{:S(2)}, u32[]{:S(2)}) async-start(bf16[8,120,512]{2,1,0:T(8,128)(2,1)} %route.1), calls=%async_computation.3 | async-start | bytes 1966080 | tf_op jit(solution)/shard_map/all_to_all | solution.py:648
  76.1 0.8 own_plan.1.plan_ref.own_ref
  76.9 1.6 %far_plan.1.plan_ref = s32[16,128]{1,0:T(8,128)S(1)} custom-call(s32[4]{0:T(128)S(1)} %pad_add_fusion.position_ref, s32[256,256]{1,0:T(8,128)S(1)} %get-tuple-element.86.slots_ref, f32[128,256]{1,0:T(8,128)S(1)} %get-tuple-element.87.union_ref, bf16[128,512]{1,0:T(8,128)(2,1)S(1)} %get-tuple-element.88.refs_0_, ...), custom_call_target="tpu_custom_call" | custom-call | flops 671088640 | bytes 524288 | tf_op jit(solution)/shard_map/far_plan/pallas_call | solution.py:572
  78.5 0.6 slice.68
  79.7 1.3 %all-gather.6.cloned.1.call-done = bf16[16,7,128,128]{3,2,1,0:T(8,128)(2,1)} async-done(((bf16[4,7,128,128]{3,2,1,0:T(8,128)(2,1)}), bf16[16,7,128,128]{3,2,1,0:T(8,128)(2,1)}) %all-gather.6.cloned.1.call-update) | async-done | bytes 3670032 | tf_op jit(solution)/shard_map/all_gather | solution.py:638
  81.0 0.0 copy-start
  81.0 2.0 %copy-done = bf16[16,7,128,128]{3,2,1,0:T(8,128)(2,1)S(1)} copy-done((bf16[16,7,128,128]{3,2,1,0:T(8,128)(2,1)S(1)}, bf16[16,7,128,128]{3,2,1,0:T(8,128)(2,1)}, u32[]{:S(2)}) %copy-start) | copy-done | bytes 3670040
  83.0 2.2 %own_sums.1.near_ref = f32[112,32,128]{2,1,0:T(8,128)S(1)} custom-call(s32[16,128]{1,0:T(8,128)S(1)} %own_plan.1.plan_ref.own_ref, bf16[112,128,128]{2,1,0:T(8,128)(2,1)S(1)} %bitcast.151), custom_call_target="tpu_custom_call" | custom-call | flops 536870912 | bytes 5505024 | tf_op jit(solution)/shard_map/own_sums/pallas_call | solution.py:161
  85.2 5.3 %all-to-all-done.2 = bf16[8,120,512]{2,1,0:T(8,128)(2,1)S(1)} async-done(((bf16[8,120,512]{2,1,0:T(8,128)(2,1)}), bf16[8,120,512]{2,1,0:T(8,128)(2,1)S(1)}, u32[]{:S(2)}, u32[]{:S(2)}) %all-to-all-start.2) | async-done | bytes 983072 | tf_op jit(solution)/shard_map/all_to_all | solution.py:648
  90.5 6.1 %far_sums.1 = (bf16[28,32,128]{2,1,0:T(8,128)(2,1)S(1)}, bf16[28,32,128]{2,1,0:T(8,128)(2,1)}, bf16[28,32,128]{2,1,0:T(8,128)(2,1)}, bf16[28,32,128]{2,1,0:T(8,128)(2,1)S(1)}) custom-call(s32[16,128]{1,0:T(8,128)S(1)} %own_plan.1.plan_ref.own_ref, s32[16,128]{1,0:T(8,128)S(1)} %far_plan.1.plan_ref, bf16[112,128,128]{2,1,0:T(8,128)(2,1)} %bitcast.150, ...), custom_call_target="tpu_custom_call" | custom-call | tf_op jit(solution)/shard_map/far_sums/pallas_call | solution.py:242
  96.6 1.0 collective-permute-start.7
  97.6 0.1 collective-permute-start.8
  97.7 2.6 %collective-permute-start.9 = (bf16[28,32,128]{2,1,0:T(8,128)(2,1)S(1)}, bf16[28,32,128]{2,1,0:T(8,128)(2,1)S(1)}, u32[]{:S(2)}, u32[]{:S(2)}) collective-permute-start(bf16[28,32,128]{2,1,0:T(8,128)(2,1)S(1)} %get-tuple-element.103), channel_id=1, source_target_pairs={{0,3},{1,0},{2,1},{3,2},{4,7},{5,4},{6,5},{7,6},{8,11},{9,8},{10,9... | collective-permute-start | bytes 688136 | tf_op jit(solution)/shard_map/ppermute | solution.py:657
  100.3 4.3 %collective-permute-done.7.refs_1_ = bf16[28,32,128]{2,1,0:T(8,128)(2,1)S(1)} collective-permute-done((bf16[28,32,128]{2,1,0:T(8,128)(2,1)}, bf16[28,32,128]{2,1,0:T(8,128)(2,1)S(1)}, u32[]{:S(2)}, u32[]{:S(2)}) %collective-permute-start.7) | collective-permute-done | bytes 229408 | tf_op jit(solution)/shard_map/ppermute | solution.py:657
  104.6 6.1 %collective-permute-done.8.refs_2_ = bf16[28,32,128]{2,1,0:T(8,128)(2,1)S(1)} collective-permute-done((bf16[28,32,128]{2,1,0:T(8,128)(2,1)}, bf16[28,32,128]{2,1,0:T(8,128)(2,1)S(1)}, u32[]{:S(2)}, u32[]{:S(2)}) %collective-permute-start.8) | collective-permute-done | bytes 229408 | tf_op jit(solution)/shard_map/ppermute | solution.py:657
  110.7 0.0 collective-permute-done.9.refs_3_
  110.7 0.0 copy-done.4
  110.7 0.0 copy-done.5
  110.8 1.8 %finish.1 = bf16[4,7,128,128]{3,2,1,0:T(8,128)(2,1)} custom-call(s32[4]{0:T(128)S(1)} %pad_add_fusion.position_ref, bf16[28,32,128]{2,1,0:T(8,128)(2,1)S(1)} %get-tuple-element.100.refs_0_, bf16[28,32,128]{2,1,0:T(8,128)(2,1)S(1)} %collective-permute-done.7.refs_1_, bf16[28,32,128]{2,1,0:T(8,128)(2,1)S(1)} %collective-permute-done.8.refs_2_, ...), custom_call_target="tpu_custom_call" | custom-call | tf_op jit(solution)/shard_map/finish/pallas_call | solution.py:272
  (4 shorter events, 0.0 us)
Async XLA Ops:
  9.5 25.8 %all-to-all-start.1 = ((bf16[32,32,512]{2,1,0:T(8,128)(2,1)}), bf16[32,32,512]{2,1,0:T(8,128)(2,1)S(1)}, u32[]{:S(2)}, u32[]{:S(2)}) async-start(bf16[32,32,512]{2,1,0:T(8,128)(2,1)} %prepare.1), calls=%async_computation.2 | async-start | bytes 2097152 | tf_op jit(solution)/shard_map/all_to_all | solution.py:636
  18.1 92.6 %copy-start.4 = (s32[256,28]{0,1:T(8,128)S(1)}, s32[256,28]{0,1:T(8,128)}, u32[]{:S(2)}) copy-start(s32[256,28]{0,1:T(8,128)} %param.7) | copy-start | bytes 86020
  18.1 92.6 %copy-start.5 = (s32[4,7]{1,0:T(4,128)S(1)}, s32[4,7]{1,0:T(4,128)}, u32[]{:S(2)}) copy-start(s32[4,7]{1,0:T(4,128)} %keep_ref.3) | copy-start | bytes 340
  18.2 62.8 %all-gather.6.cloned.1.call-start = ((), (), s32[]{:S(2)}) async-start(), calls=%async_computation.6 | async-start | bytes 4587520 | tf_op jit(solution)/shard_map/all_gather | solution.py:638
  38.5 15.0 %collective-permute-start = (bf16[128,512]{1,0:T(8,128)(2,1)S(1)}, bf16[128,512]{1,0:T(8,128)(2,1)S(1)}, u32[]{:S(2)}, u32[]{:S(2)}) collective-permute-start(bf16[128,512]{1,0:T(8,128)(2,1)S(1)} %get-tuple-element.78), channel_id=1, source_target_pairs={{0,32},{8,40},{16,48},{24,56},{32,0},{40,8},{48,16},{56,24},{1,33}... | collective-permute-start | bytes 393224 | tf_op jit(solution)/shard_map/ppermute | solution.py:643
  45.4 16.2 %collective-permute-start.1 = (bf16[128,512]{1,0:T(8,128)(2,1)S(1)}, bf16[128,512]{1,0:T(8,128)(2,1)S(1)}, u32[]{:S(2)}, u32[]{:S(2)}) collective-permute-start(bf16[128,512]{1,0:T(8,128)(2,1)S(1)} %get-tuple-element.79), channel_id=1, source_target_pairs={{0,24},{8,32},{16,40},{24,48},{32,56},{40,0},{48,8},{56,16},{1,25}... | collective-permute-start | bytes 393224 | tf_op jit(solution)/shard_map/ppermute | solution.py:643
  47.1 14.5 %collective-permute-start.2 = (bf16[128,512]{1,0:T(8,128)(2,1)S(1)}, bf16[128,512]{1,0:T(8,128)(2,1)S(1)}, u32[]{:S(2)}, u32[]{:S(2)}) collective-permute-start(bf16[128,512]{1,0:T(8,128)(2,1)S(1)} %get-tuple-element.80), channel_id=1, source_target_pairs={{0,40},{8,48},{16,56},{24,0},{32,8},{40,16},{48,24},{56,32},{1,41}... | collective-permute-start | bytes 393224 | tf_op jit(solution)/shard_map/ppermute | solution.py:643
  49.9 12.4 %collective-permute-start.3 = (bf16[128,512]{1,0:T(8,128)(2,1)S(1)}, bf16[128,512]{1,0:T(8,128)(2,1)S(1)}, u32[]{:S(2)}, u32[]{:S(2)}) collective-permute-start(bf16[128,512]{1,0:T(8,128)(2,1)S(1)} %get-tuple-element.81), channel_id=1, source_target_pairs={{0,16},{8,24},{16,32},{24,40},{32,48},{40,56},{48,0},{56,8},{1,17}... | collective-permute-start | bytes 393224 | tf_op jit(solution)/shard_map/ppermute | solution.py:643
  51.1 14.6 %collective-permute-start.4 = (bf16[128,512]{1,0:T(8,128)(2,1)S(1)}, bf16[128,512]{1,0:T(8,128)(2,1)S(1)}, u32[]{:S(2)}, u32[]{:S(2)}) collective-permute-start(bf16[128,512]{1,0:T(8,128)(2,1)S(1)} %get-tuple-element.82), channel_id=1, source_target_pairs={{0,48},{8,56},{16,0},{24,8},{32,16},{40,24},{48,32},{56,40},{1,49}... | collective-permute-start | bytes 393224 | tf_op jit(solution)/shard_map/ppermute | solution.py:643
  53.5 15.3 %collective-permute-start.5 = (bf16[128,512]{1,0:T(8,128)(2,1)S(1)}, bf16[128,512]{1,0:T(8,128)(2,1)S(1)}, u32[]{:S(2)}, u32[]{:S(2)}) collective-permute-start(bf16[128,512]{1,0:T(8,128)(2,1)S(1)} %get-tuple-element.83), channel_id=1, source_target_pairs={{0,8},{8,16},{16,24},{24,32},{32,40},{40,48},{48,56},{56,0},{1,9},... | collective-permute-start | bytes 393224 | tf_op jit(solution)/shard_map/ppermute | solution.py:643
  61.6 7.9 %collective-permute-start.6 = (bf16[128,512]{1,0:T(8,128)(2,1)S(1)}, bf16[128,512]{1,0:T(8,128)(2,1)S(1)}, u32[]{:S(2)}, u32[]{:S(2)}) collective-permute-start(bf16[128,512]{1,0:T(8,128)(2,1)S(1)} %get-tuple-element.84), channel_id=1, source_target_pairs={{0,56},{8,0},{16,8},{24,16},{32,24},{40,32},{48,40},{56,48},{1,57}... | collective-permute-start | bytes 393224 | tf_op jit(solution)/shard_map/ppermute | solution.py:643
  71.8 18.7 %all-to-all-start.2 = ((bf16[8,120,512]{2,1,0:T(8,128)(2,1)}), bf16[8,120,512]{2,1,0:T(8,128)(2,1)S(1)}, u32[]{:S(2)}, u32[]{:S(2)}) async-start(bf16[8,120,512]{2,1,0:T(8,128)(2,1)} %route.1), calls=%async_computation.3 | async-start | bytes 1966080 | tf_op jit(solution)/shard_map/all_to_all | solution.py:648
  81.0 2.0 %copy-start = (bf16[16,7,128,128]{3,2,1,0:T(8,128)(2,1)S(1)}, bf16[16,7,128,128]{3,2,1,0:T(8,128)(2,1)}, u32[]{:S(2)}) copy-start(bf16[16,7,128,128]{3,2,1,0:T(8,128)(2,1)} %all-gather.6.cloned.1.call-done) | copy-start | bytes 11010052
  96.6 8.0 %collective-permute-start.7 = (bf16[28,32,128]{2,1,0:T(8,128)(2,1)}, bf16[28,32,128]{2,1,0:T(8,128)(2,1)S(1)}, u32[]{:S(2)}, u32[]{:S(2)}) collective-permute-start(bf16[28,32,128]{2,1,0:T(8,128)(2,1)} %get-tuple-element.101), channel_id=1, source_target_pairs={{0,2},{1,3},{2,0},{3,1},{4,6},{5,7},{6,4},{7,5},{8,10},{9,11},{10,... | collective-permute-start | bytes 688136 | tf_op jit(solution)/shard_map/ppermute | solution.py:657
  97.6 13.1 %collective-permute-start.8 = (bf16[28,32,128]{2,1,0:T(8,128)(2,1)}, bf16[28,32,128]{2,1,0:T(8,128)(2,1)S(1)}, u32[]{:S(2)}, u32[]{:S(2)}) collective-permute-start(bf16[28,32,128]{2,1,0:T(8,128)(2,1)} %get-tuple-element.102), channel_id=1, source_target_pairs={{0,1},{1,2},{2,3},{3,0},{4,5},{5,6},{6,7},{7,4},{8,9},{9,10},{10,1... | collective-permute-start | bytes 688136 | tf_op jit(solution)/shard_map/ppermute | solution.py:657
  97.7 13.0 %collective-permute-start.9 = (bf16[28,32,128]{2,1,0:T(8,128)(2,1)S(1)}, bf16[28,32,128]{2,1,0:T(8,128)(2,1)S(1)}, u32[]{:S(2)}, u32[]{:S(2)}) collective-permute-start(bf16[28,32,128]{2,1,0:T(8,128)(2,1)S(1)} %get-tuple-element.103), channel_id=1, source_target_pairs={{0,3},{1,0},{2,1},{3,2},{4,7},{5,4},{6,5},{7,6},{8,11},{9,8},{10,9... | collective-permute-start | bytes 688136 | tf_op jit(solution)/shard_map/ppermute | solution.py:657
Sparse Core Ops, SparseCore 0:
  35.5 45.4 all-gather.5

commit v10 on v9

--- a/solution.py
+++ b/solution.py
@@ -27,6 +27,7 @@
 CAP_X = 120
 ORDER_Z = (4, 3, 5, 2, 6, 1, 7)
 ORDER_Y = (2, 1, 3)
+ORDER_X = ((2, 0), (2, 1), (1, 0), (3, 0), (1, 1), (3, 1), (0, 1))
 GROUP = 8
 FAR_GROUP = 3
 STEPS_AT_ONCE = 8
@@ -178,17 +179,18 @@
     own_ref,
     plan_ref,
     whole_ref,
-    far_ref,
     near_ref,
+    position_ref,
     *refs,
 ):
-    *out_refs, low, high, pieces_ref = refs
+    *out_refs, low, high, pieces_ref = refs[TARGETS:]
     halves = (low, high)
-    for sender in range(TARGETS):
-        rows = pl.ds(sender * CAP_X, CAP_X)
+    for (along_x, across), far_ref in zip(((0, 0),) + ORDER_X, refs):
+        sender = ((position_ref[0] - along_x) & (NX - 1)) * NC + ((position_ref[2] + across) & 1)
+        rows = pl.ds(pl.multiple_of(sender * CAP_X, 8), CAP_X)
         for part in range(NY):
             lanes = slice(part * SIDE, (part + 1) * SIDE)
-            pieces_ref[part, rows, :] = far_ref[rows, lanes].astype(F32)
+            pieces_ref[part, rows, :] = far_ref[:, lanes].astype(F32)
 
     def clear(group, carry):
         for total in halves:
@@ -238,11 +240,11 @@
             out_ref[place] = value.astype(BF)
 
 
-def far_sums(own_lists, far_lists, whole, far, near):
+def far_sums(own_lists, far_lists, whole, near, position, far):
     return pl.pallas_call(
         far_kernel,
         out_shape=[jax.ShapeDtypeStruct((HEIGHT * QUARTER, WIDE, SIDE), BF)] * NY,
-        in_specs=[smem(), smem(), vmem(), vmem(), vmem()],
+        in_specs=[smem(), smem(), vmem(), vmem(), smem()] + [vmem()] * TARGETS,
         out_specs=[vmem()] * NY,
         scratch_shapes=[
             pltpu.VMEM((OUT_COLS + 1, WIDE, 2 * SIDE), F32),
@@ -251,7 +253,7 @@
         ],
         compiler_params=params(),
         name="far_sums",
-    )(own_lists, far_lists, whole, far, near)
+    )(own_lists, far_lists, whole, near, position, *far)
 
 
 def finish_kernel(position_ref, *refs):
@@ -437,9 +439,16 @@
     return jnp.concatenate(asked, axis=1), third
 
 
-def route_kernel(*refs):
-    *along_refs, out_ref, chosen_ref, along_ref = refs
+def route_kernel(position_ref, *refs):
+    along_refs, out_refs = refs[:NZ], refs[NZ : NZ + TARGETS]
+    chosen_ref, along_ref = refs[NZ + TARGETS :]
     asked, _ = notes_of(along_refs)
+    line = iota(asked.shape, 0)
+    ordered = []
+    for along_x, across in ((0, 0),) + ORDER_X:
+        to = ((position_ref[0] + along_x) & (NX - 1)) * NC + ((position_ref[2] + across) & 1)
+        ordered.append(jnp.sum(jnp.where(line == to, asked, 0.0), axis=0, keepdims=True))
+    asked = jnp.concatenate(ordered, axis=0)
     for number, ref in enumerate(along_refs):
         along_ref[number * ROWS_Z : (number + 1) * ROWS_Z] = ref[...]
     code = codes(asked, CAP_X)
@@ -447,22 +456,22 @@
         chosen_ref[to * SIDE : (to + 1) * SIDE, :] = one_hot(code[to : to + 1], SIDE)
     packed = jnp.dot(chosen_ref[...], along_ref[...], preferred_element_type=F32)
     for to in range(TARGETS):
-        out_ref[to] = packed[to * SIDE : to * SIDE + CAP_X].astype(BF)
-
-
-def route(along):
+        out_refs[to][...] = packed[to * SIDE : to * SIDE + CAP_X].astype(BF)
+
+
+def route(position, along):
     return pl.pallas_call(
         route_kernel,
-        out_shape=jax.ShapeDtypeStruct((TARGETS, CAP_X, PIECE), BF),
-        in_specs=[vmem()] * NZ,
-        out_specs=vmem(),
+        out_shape=[jax.ShapeDtypeStruct((CAP_X, PIECE), BF)] * TARGETS,
+        in_specs=[smem()] + [vmem()] * NZ,
+        out_specs=[vmem()] * TARGETS,
         scratch_shapes=[
             pltpu.VMEM((TARGETS * SIDE, NZ * ROWS_Z), BF),
             pltpu.VMEM((NZ * ROWS_Z, PIECE), BF),
         ],
         compiler_params=params(),
         name="route",
-    )(*along)
+    )(position, *along)
 
 
 def own_places(position_ref, slots_ref):
@@ -644,13 +653,18 @@
         for step in ORDER_Z
     ]
     own_lists = own_plan(position, slots, union)
-    packed, notes = lax.optimization_barrier((route(along), along))
-    far = lax.all_to_all(packed, ("x", "core"), split_axis=0, concat_axis=0, tiled=True)
+    along, own_lists = lax.optimization_barrier((along, own_lists))
+    packed, notes = lax.optimization_barrier((route(position, along), along))
+    far = [packed[0]]
+    for number, (along_x, across) in enumerate(ORDER_X):
+        pairs = [
+            (i, ((i // NC + along_x) % NX) * NC + (i + across) % NC) for i in range(TARGETS)
+        ]
+        far.append(lax.ppermute(packed[1 + number], ("x", "core"), pairs))
     far_lists = far_plan(position, slots, union, notes)
-    far = far.reshape(TARGETS * CAP_X, PIECE)
     own = own_sums(own_lists, whole)
     far, fits, own = lax.optimization_barrier((far, far_lists[9, 0] != 0, own))
-    result = far_sums(own_lists, far_lists, whole, far, own)
+    result = far_sums(own_lists, far_lists, whole, own, position, far)
     cuts = [result[0]]
     for step in ORDER_Y:
         pairs = [(i, (i + step) % NY) for i in range(NY)]

time: 120 us -> 117 us (0.975)
  waiting for transfers between devices: 42.2 us -> 34.4 us
  starting transfers between devices: 32.4 us -> 38.8 us
    ppermute x0 -> x7, starting transfers between devices: none -> 9.88 us  [shards(): far.append(lax.ppermute(packed[1 + number], ('x', 'core'), pairs))]
    all_to_all x1 -> x0, waiting for transfers between devices: 5.26 us -> none  [shards(): lax.all_to_all(packed, ('x', 'core'), split_axis=0, concat_axis=0, tiled=...]
    all_to_all x1 -> x0, starting transfers between devices: 4.3 us -> none  [shards(): lax.all_to_all(packed, ('x', 'core'), split_axis=0, concat_axis=0, tiled=...]
    all_gather x1, waiting for transfers between devices: 1.26 us -> 0.02 us  [shards(): whole = lax.all_gather(turned, 'col', axis=0, tiled=False)]
    unnamed x7 -> x9, local copies, waits for them, and re-layouts: 2.92 us -> 2.91 us
  transfers between devices with their start and end apart: 13 -> 19, of which waited for: 10 -> 8; matrix products, arithmetic and copies ran while one was open for 2% -> 2% of each run, Pallas kernels for 10% -> 10%
where the time goes in v10:
time: 117 us
  starting transfers between devices  38.8 us (33%)
  waiting for transfers between devices  34.4 us (29%)
  Pallas kernels  24.5 us (21%)
  between operations  14.3 us (12%)
  local copies, waits for them, and re-layouts  4.85 us (4%)
    ppermute x7, starting transfers between devices, shards(): lax.ppermute(packed[step], 'z', [(i, (i + step) % NZ) for i in range(NZ)])  15.8 us
    ppermute x7, waiting for transfers between devices, shards(): lax.ppermute(packed[step], 'z', [(i, (i + step) % NZ) for i in range(NZ)])  14.4 us
    all_to_all x1, waiting for transfers between devices, shards(): lax.all_to_all(cuts, ('col', 'x', 'core'), split_axis=0, concat_axis=0, t...  9.97 us
    ppermute x7, starting transfers between devices, shards(): far.append(lax.ppermute(packed[1 + number], ('x', 'core'), pairs))  9.88 us
    ppermute x3, waiting for transfers between devices, shards(): cuts.append(lax.ppermute(result[step], 'col', pairs))  9.69 us
    all_to_all x1, starting transfers between devices, shards(): lax.all_to_all(cuts, ('col', 'x', 'core'), split_axis=0, concat_axis=0, t...  8.73 us
    pallas_call x1, Pallas kernels, far_sums(): pl.pallas_call(far_kernel, out_shape=[jax.ShapeDtypeStruct((HEIGHT * QUAR...  5.3 us
    ppermute x3, starting transfers between devices, shards(): cuts.append(lax.ppermute(result[step], 'col', pairs))  4.34 us
  transfers between devices with their start and end apart: 19, of which 8 were waited for; matrix products, arithmetic and copies ran while one was open for 2% of the time, Pallas kernels for 10%

profile of v10, /device:TPU:1, one launch (start us, length us, event | category | flops | bytes accessed | tf_op | source)
XLA Modules:
  0.0 116.9 jit_solution(3578592625642474756)
XLA Ops:
  6.5 0.1 pad_add_fusion.position_ref
  6.6 2.9 %prepare.1 = bf16[32,32,512]{2,1,0:T(8,128)(2,1)} custom-call(s32[4]{0:T(128)S(1)} %pad_add_fusion.position_ref, s32[4,7]{1,0:T(4,128)} %keep_ref.3, bf16[4,7,128,128]{3,2,1,0:T(8,128)(2,1)} %blocks_ref.2), custom_call_target="tpu_custom_call" | custom-call | tf_op jit(solution)/shard_map/prepare/pallas_call | solution.py:87
  9.5 0.0 copy-start.4
  9.5 0.0 copy-start.5
  9.5 0.0 copy-start.6
  9.5 8.7 %all-to-all-start.1 = ((bf16[32,32,512]{2,1,0:T(8,128)(2,1)}), bf16[32,32,512]{2,1,0:T(8,128)(2,1)S(1)}, u32[]{:S(2)}, u32[]{:S(2)}) async-start(bf16[32,32,512]{2,1,0:T(8,128)(2,1)} %prepare.1), calls=%async_computation.2 | async-start | bytes 2097152 | tf_op jit(solution)/shard_map/all_to_all | solution.py:645
  18.3 0.0 all-gather.6.cloned.1.call-start
  18.3 0.9 copy.101
  19.2 0.3 reshape.211
  19.5 0.1 reshape.212
  19.6 0.1 reshape.213.entries_ref
  19.7 0.9 copy.103.columns_ref
  20.6 2.4 %turn.1 = bf16[4,7,128,128]{3,2,1,0:T(8,128)(2,1)} custom-call(s32[4,7]{1,0:T(4,128)} %keep_ref.3, bf16[4,7,128,128]{3,2,1,0:T(8,128)(2,1)} %blocks_ref.2), custom_call_target="tpu_custom_call" | custom-call | flops 117440512 | bytes 1835008 | tf_op jit(solution)/shard_map/turn/pallas_call | solution.py:108
  23.0 2.5 %pattern.1 = (s32[256,256]{1,0:T(8,128)S(1)}, f32[128,256]{1,0:T(8,128)S(1)}, f32[128,1024]{1,0:T(8,128)S(1)}, f32[8,1024]{1,0:T(8,128)S(1)}) custom-call(s32[4]{0:T(128)S(1)} %pad_add_fusion.position_ref, s32[256,28]{1,0:T(8,128)S(1)} %copy.103.columns_ref, s32[1,1024]{1,0:T(1,128)S(1)} %reshape.213.entries_ref), custom_call_target="tpu_custom_call" | custom-call | flops 234881024 | bytes 524288 | tf_op jit(solution)/shard_map/pattern/pallas_call | solution.py:355
  25.5 10.0 %all-to-all-done.1 = bf16[32,32,512]{2,1,0:T(8,128)(2,1)S(1)} async-done(((bf16[32,32,512]{2,1,0:T(8,128)(2,1)}), bf16[32,32,512]{2,1,0:T(8,128)(2,1)S(1)}, u32[]{:S(2)}, u32[]{:S(2)}) %all-to-all-start.1) | async-done | bytes 1048608 | tf_op jit(solution)/shard_map/all_to_all | solution.py:645
  35.4 0.0 all-gather.6.cloned.1.call-update
  35.5 3.1 %send.1 = (bf16[128,512]{1,0:T(8,128)(2,1)S(1)}, bf16[128,512]{1,0:T(8,128)(2,1)S(1)}, bf16[128,512]{1,0:T(8,128)(2,1)S(1)}, bf16[128,512]{1,0:T(8,128)(2,1)S(1)...) custom-call(s32[4]{0:T(128)S(1)} %pad_add_fusion.position_ref, ...), custom_call_target="tpu_custom_call" | custom-call | tf_op jit(solution)/shard_map/send/pallas_call | solution.py:414
  38.6 7.0 %collective-permute-start = (bf16[128,512]{1,0:T(8,128)(2,1)S(1)}, bf16[128,512]{1,0:T(8,128)(2,1)S(1)}, u32[]{:S(2)}, u32[]{:S(2)}) collective-permute-start(bf16[128,512]{1,0:T(8,128)(2,1)S(1)} %get-tuple-element.109), channel_id=1, source_target_pairs={{0,32},{8,40},{16,48},{24,56},{32,0},{40,8},{48,16},{56,24},{1,33}... | collective-permute-start | bytes 393224 | tf_op jit(solution)/shard_map/ppermute | solution.py:652
  45.6 1.6 %collective-permute-start.1 = (bf16[128,512]{1,0:T(8,128)(2,1)S(1)}, bf16[128,512]{1,0:T(8,128)(2,1)S(1)}, u32[]{:S(2)}, u32[]{:S(2)}) collective-permute-start(bf16[128,512]{1,0:T(8,128)(2,1)S(1)} %get-tuple-element.110), channel_id=1, source_target_pairs={{0,24},{8,32},{16,40},{24,48},{32,56},{40,0},{48,8},{56,16},{1,25}... | collective-permute-start | bytes 393224 | tf_op jit(solution)/shard_map/ppermute | solution.py:652
  47.2 2.8 %collective-permute-start.2 = (bf16[128,512]{1,0:T(8,128)(2,1)S(1)}, bf16[128,512]{1,0:T(8,128)(2,1)S(1)}, u32[]{:S(2)}, u32[]{:S(2)}) collective-permute-start(bf16[128,512]{1,0:T(8,128)(2,1)S(1)} %get-tuple-element.111), channel_id=1, source_target_pairs={{0,40},{8,48},{16,56},{24,0},{32,8},{40,16},{48,24},{56,32},{1,41}... | collective-permute-start | bytes 393224 | tf_op jit(solution)/shard_map/ppermute | solution.py:652
  50.1 1.2 %collective-permute-start.3 = (bf16[128,512]{1,0:T(8,128)(2,1)S(1)}, bf16[128,512]{1,0:T(8,128)(2,1)S(1)}, u32[]{:S(2)}, u32[]{:S(2)}) collective-permute-start(bf16[128,512]{1,0:T(8,128)(2,1)S(1)} %get-tuple-element.112), channel_id=1, source_target_pairs={{0,16},{8,24},{16,32},{24,40},{32,48},{40,56},{48,0},{56,8},{1,17}... | collective-permute-start | bytes 393224 | tf_op jit(solution)/shard_map/ppermute | solution.py:652
  51.3 2.4 %collective-permute-start.4 = (bf16[128,512]{1,0:T(8,128)(2,1)S(1)}, bf16[128,512]{1,0:T(8,128)(2,1)S(1)}, u32[]{:S(2)}, u32[]{:S(2)}) collective-permute-start(bf16[128,512]{1,0:T(8,128)(2,1)S(1)} %get-tuple-element.113), channel_id=1, source_target_pairs={{0,48},{8,56},{16,0},{24,8},{32,16},{40,24},{48,32},{56,40},{1,49}... | collective-permute-start | bytes 393224 | tf_op jit(solution)/shard_map/ppermute | solution.py:652
  53.6 0.0 collective-permute-done.refs_1_
  53.6 0.7 collective-permute-start.5
  54.4 7.4 %collective-permute-done.1.refs_2_ = bf16[128,512]{1,0:T(8,128)(2,1)S(1)} collective-permute-done((bf16[128,512]{1,0:T(8,128)(2,1)S(1)}, bf16[128,512]{1,0:T(8,128)(2,1)S(1)}, u32[]{:S(2)}, u32[]{:S(2)}) %collective-permute-start.1) | collective-permute-done | bytes 131104 | tf_op jit(solution)/shard_map/ppermute | solution.py:652
  61.8 0.0 collective-permute-start.6
  61.8 0.8 own_plan.1.plan_ref.own_ref
  62.6 0.0 collective-permute-done.2.refs_3_
  62.6 0.0 collective-permute-done.3.refs_4_
  62.6 3.3 %collective-permute-done.4.refs_5_ = bf16[128,512]{1,0:T(8,128)(2,1)S(1)} collective-permute-done((bf16[128,512]{1,0:T(8,128)(2,1)S(1)}, bf16[128,512]{1,0:T(8,128)(2,1)S(1)}, u32[]{:S(2)}, u32[]{:S(2)}) %collective-permute-start.4) | collective-permute-done | bytes 131104 | tf_op jit(solution)/shard_map/ppermute | solution.py:652
  65.9 3.1 %collective-permute-done.5.refs_6_ = bf16[128,512]{1,0:T(8,128)(2,1)S(1)} collective-permute-done((bf16[128,512]{1,0:T(8,128)(2,1)S(1)}, bf16[128,512]{1,0:T(8,128)(2,1)S(1)}, u32[]{:S(2)}, u32[]{:S(2)}) %collective-permute-start.5) | collective-permute-done | bytes 131104 | tf_op jit(solution)/shard_map/ppermute | solution.py:652
  69.0 0.7 collective-permute-done.6.refs_7_
  69.6 1.9 %route.1 = (bf16[120,512]{1,0:T(8,128)(2,1)S(1)}, bf16[120,512]{1,0:T(8,128)(2,1)S(1)}, bf16[120,512]{1,0:T(8,128)(2,1)S(1)}, bf16[120,512]{1,0:T(8,128)(2,1)S(1...) custom-call(s32[4]{0:T(128)S(1)} %pad_add_fusion.position_ref, ...), custom_call_target="tpu_custom_call" | custom-call | tf_op jit(solution)/shard_map/route/pallas_call | solution.py:463
  71.6 1.2 %collective-permute-start.7 = (bf16[120,512]{1,0:T(8,128)(2,1)S(1)}, bf16[120,512]{1,0:T(8,128)(2,1)S(1)}, u32[]{:S(2)}, u32[]{:S(2)}) collective-permute-start(bf16[120,512]{1,0:T(8,128)(2,1)S(1)} %get-tuple-element.135), channel_id=1, source_target_pairs={{0,128},{4,132},{64,192},{68,196},{128,0},{132,4},{192,64},{196,68... | collective-permute-start | bytes 368648 | tf_op jit(solution)/shard_map/ppermute | solution.py:663
  72.8 3.0 %collective-permute-start.8 = (bf16[120,512]{1,0:T(8,128)(2,1)S(1)}, bf16[120,512]{1,0:T(8,128)(2,1)S(1)}, u32[]{:S(2)}, u32[]{:S(2)}) collective-permute-start(bf16[120,512]{1,0:T(8,128)(2,1)S(1)} %get-tuple-element.136), channel_id=1, source_target_pairs={{0,132},{4,128},{64,196},{68,192},{128,4},{132,0},{192,68},{196,64... | collective-permute-start | bytes 368648 | tf_op jit(solution)/shard_map/ppermute | solution.py:663
  75.8 0.4 collective-permute-start.9
  76.2 2.3 %collective-permute-start.10 = (bf16[120,512]{1,0:T(8,128)(2,1)S(1)}, bf16[120,512]{1,0:T(8,128)(2,1)S(1)}, u32[]{:S(2)}, u32[]{:S(2)}) collective-permute-start(bf16[120,512]{1,0:T(8,128)(2,1)S(1)} %get-tuple-element.138), channel_id=1, source_target_pairs={{0,192},{4,196},{64,0},{68,4},{128,64},{132,68},{192,128},{196,132... | collective-permute-start | bytes 368648 | tf_op jit(solution)/shard_map/ppermute | solution.py:663
  78.5 0.0 collective-permute-start.11
  78.5 0.0 collective-permute-done.7.refs_1_
  78.5 3.0 %collective-permute-start.12 = (bf16[120,512]{1,0:T(8,128)(2,1)S(1)}, bf16[120,512]{1,0:T(8,128)(2,1)S(1)}, u32[]{:S(2)}, u32[]{:S(2)}) collective-permute-start(bf16[120,512]{1,0:T(8,128)(2,1)S(1)} %get-tuple-element.140), channel_id=1, source_target_pairs={{0,196},{4,192},{64,4},{68,0},{128,68},{132,64},{192,132},{196,128... | collective-permute-start | bytes 368648 | tf_op jit(solution)/shard_map/ppermute | solution.py:663
  81.4 0.3 collective-permute-done.8.refs_2_
  81.8 0.0 collective-permute-start.13
  81.8 1.6 %far_plan.1.plan_ref = s32[16,128]{1,0:T(8,128)S(1)} custom-call(s32[4]{0:T(128)S(1)} %pad_add_fusion.position_ref, s32[256,256]{1,0:T(8,128)S(1)} %get-tuple-element.116.slots_ref, f32[128,256]{1,0:T(8,128)S(1)} %get-tuple-element.117.union_ref, bf16[128,512]{1,0:T(8,128)(2,1)S(1)} %get-tuple-element.142.refs_0_, ...), custom_call_target="tpu_custom_call" | custom-call | flops 671088640 | bytes 524288 | tf_op jit(solution)/shard_map/far_plan/pallas_call | solution.py:581
  83.3 0.6 slice.68
  84.6 0.0 all-gather.6.cloned.1.call-done
  84.6 0.0 copy-start
  84.7 2.0 %copy-done = bf16[16,7,128,128]{3,2,1,0:T(8,128)(2,1)S(1)} copy-done((bf16[16,7,128,128]{3,2,1,0:T(8,128)(2,1)S(1)}, bf16[16,7,128,128]{3,2,1,0:T(8,128)(2,1)}, u32[]{:S(2)}) %copy-start) | copy-done | bytes 3670040
  86.7 2.2 %own_sums.1.near_ref = f32[112,32,128]{2,1,0:T(8,128)S(1)} custom-call(s32[16,128]{1,0:T(8,128)S(1)} %own_plan.1.plan_ref.own_ref, bf16[112,128,128]{2,1,0:T(8,128)(2,1)S(1)} %bitcast.150), custom_call_target="tpu_custom_call" | custom-call | flops 536870912 | bytes 5505024 | tf_op jit(solution)/shard_map/own_sums/pallas_call | solution.py:162
  88.9 0.0 collective-permute-done.9.refs_3_
  88.9 0.0 collective-permute-done.10.refs_4_
  88.9 0.0 collective-permute-done.11.refs_5_
  88.9 0.0 collective-permute-done.12.refs_6_
  88.9 0.0 collective-permute-done.13.refs_7_
  88.9 5.3 %far_sums.1 = (bf16[28,32,128]{2,1,0:T(8,128)(2,1)S(1)}, bf16[28,32,128]{2,1,0:T(8,128)(2,1)S(1)}, bf16[28,32,128]{2,1,0:T(8,128)(2,1)S(1)}, bf16[28,32,128]{2,1,0:T(8,128)(2,1)S(1)}) custom-call(s32[16,128]{1,0:T(8,128)S(1)} %own_plan.1.plan_ref.own_ref, s32[16,128]{1,0:T(8,128)S(1)} %far_plan.1.plan_ref, bf16[112,128,128]{2,1,0:T(8,128)(2,1)} %bitcast.149, ...), custom_call_target="tpu_custom_call" | custom-call | tf_op jit(solution)/shard_map/far_sums/pallas_call | solution.py:244
  94.3 1.7 %collective-permute-start.14 = (bf16[28,32,128]{2,1,0:T(8,128)(2,1)S(1)}, bf16[28,32,128]{2,1,0:T(8,128)(2,1)S(1)}, u32[]{:S(2)}, u32[]{:S(2)}) collective-permute-start(bf16[28,32,128]{2,1,0:T(8,128)(2,1)S(1)} %get-tuple-element.163), channel_id=1, source_target_pairs={{0,2},{1,3},{2,0},{3,1},{4,6},{5,7},{6,4},{7,5},{8,10},{9,11},{10,... | collective-permute-start | bytes 688136 | tf_op jit(solution)/shard_map/ppermute | solution.py:671
  95.9 0.0 collective-permute-start.15
  95.9 2.7 %collective-permute-start.16 = (bf16[28,32,128]{2,1,0:T(8,128)(2,1)S(1)}, bf16[28,32,128]{2,1,0:T(8,128)(2,1)S(1)}, u32[]{:S(2)}, u32[]{:S(2)}) collective-permute-start(bf16[28,32,128]{2,1,0:T(8,128)(2,1)S(1)} %get-tuple-element.165), channel_id=1, source_target_pairs={{0,3},{1,0},{2,1},{3,2},{4,7},{5,4},{6,5},{7,6},{8,11},{9,8},{10,9... | collective-permute-start | bytes 688136 | tf_op jit(solution)/shard_map/ppermute | solution.py:671
  98.6 3.9 %collective-permute-done.14.refs_1_ = bf16[28,32,128]{2,1,0:T(8,128)(2,1)S(1)} collective-permute-done((bf16[28,32,128]{2,1,0:T(8,128)(2,1)S(1)}, bf16[28,32,128]{2,1,0:T(8,128)(2,1)S(1)}, u32[]{:S(2)}, u32[]{:S(2)}) %collective-permute-start.14) | collective-permute-done | bytes 229408 | tf_op jit(solution)/shard_map/ppermute | solution.py:671
  102.5 5.8 %collective-permute-done.15.refs_2_ = bf16[28,32,128]{2,1,0:T(8,128)(2,1)S(1)} collective-permute-done((bf16[28,32,128]{2,1,0:T(8,128)(2,1)S(1)}, bf16[28,32,128]{2,1,0:T(8,128)(2,1)S(1)}, u32[]{:S(2)}, u32[]{:S(2)}) %collective-permute-start.15) | collective-permute-done | bytes 229408 | tf_op jit(solution)/shard_map/ppermute | solution.py:671
  108.3 0.0 collective-permute-done.16.refs_3_
  108.3 0.0 copy-done.4
  108.3 0.0 copy-done.5
  108.3 0.0 copy-done.6
  108.3 1.8 %finish.1 = bf16[4,7,128,128]{3,2,1,0:T(8,128)(2,1)} custom-call(s32[4]{0:T(128)S(1)} %pad_add_fusion.position_ref, bf16[28,32,128]{2,1,0:T(8,128)(2,1)S(1)} %get-tuple-element.162.refs_0_, bf16[28,32,128]{2,1,0:T(8,128)(2,1)S(1)} %collective-permute-done.14.refs_1_, bf16[28,32,128]{2,1,0:T(8,128)(2,1)S(1)} %collective-permute-done.15.refs_2_, ...), custom_call_target="tpu_custom_call" | custom-call | tf_op jit(solution)/shard_map/finish/pallas_call | solution.py:274
  (4 shorter events, 0.0 us)
Async XLA Ops:
  9.5 98.8 %copy-start.4 = (bf16[4,7,128,128]{3,2,1,0:T(8,128)(2,1)S(1)}, bf16[4,7,128,128]{3,2,1,0:T(8,128)(2,1)}, u32[]{:S(2)}) copy-start(bf16[4,7,128,128]{3,2,1,0:T(8,128)(2,1)} %blocks_ref.2) | copy-start | bytes 2752516
  9.5 98.8 %copy-start.5 = (s32[256,28]{0,1:T(8,128)S(1)}, s32[256,28]{0,1:T(8,128)}, u32[]{:S(2)}) copy-start(s32[256,28]{0,1:T(8,128)} %param.7) | copy-start | bytes 86020
  9.5 98.8 %copy-start.6 = (s32[4,7]{1,0:T(4,128)S(1)}, s32[4,7]{1,0:T(4,128)}, u32[]{:S(2)}) copy-start(s32[4,7]{1,0:T(4,128)} %keep_ref.3) | copy-start | bytes 340
  9.5 25.9 %all-to-all-start.1 = ((bf16[32,32,512]{2,1,0:T(8,128)(2,1)}), bf16[32,32,512]{2,1,0:T(8,128)(2,1)S(1)}, u32[]{:S(2)}, u32[]{:S(2)}) async-start(bf16[32,32,512]{2,1,0:T(8,128)(2,1)} %prepare.1), calls=%async_computation.2 | async-start | bytes 2097152 | tf_op jit(solution)/shard_map/all_to_all | solution.py:645
  18.3 66.4 %all-gather.6.cloned.1.call-start = ((), (), s32[]{:S(2)}) async-start(), calls=%async_computation.5 | async-start | bytes 4587520 | tf_op jit(solution)/shard_map/all_gather | solution.py:647
  38.6 15.0 %collective-permute-start = (bf16[128,512]{1,0:T(8,128)(2,1)S(1)}, bf16[128,512]{1,0:T(8,128)(2,1)S(1)}, u32[]{:S(2)}, u32[]{:S(2)}) collective-permute-start(bf16[128,512]{1,0:T(8,128)(2,1)S(1)} %get-tuple-element.109), channel_id=1, source_target_pairs={{0,32},{8,40},{16,48},{24,56},{32,0},{40,8},{48,16},{56,24},{1,33}... | collective-permute-start | bytes 393224 | tf_op jit(solution)/shard_map/ppermute | solution.py:652
  45.6 16.2 %collective-permute-start.1 = (bf16[128,512]{1,0:T(8,128)(2,1)S(1)}, bf16[128,512]{1,0:T(8,128)(2,1)S(1)}, u32[]{:S(2)}, u32[]{:S(2)}) collective-permute-start(bf16[128,512]{1,0:T(8,128)(2,1)S(1)} %get-tuple-element.110), channel_id=1, source_target_pairs={{0,24},{8,32},{16,40},{24,48},{32,56},{40,0},{48,8},{56,16},{1,25}... | collective-permute-start | bytes 393224 | tf_op jit(solution)/shard_map/ppermute | solution.py:652
  47.2 15.4 %collective-permute-start.2 = (bf16[128,512]{1,0:T(8,128)(2,1)S(1)}, bf16[128,512]{1,0:T(8,128)(2,1)S(1)}, u32[]{:S(2)}, u32[]{:S(2)}) collective-permute-start(bf16[128,512]{1,0:T(8,128)(2,1)S(1)} %get-tuple-element.111), channel_id=1, source_target_pairs={{0,40},{8,48},{16,56},{24,0},{32,8},{40,16},{48,24},{56,32},{1,41}... | collective-permute-start | bytes 393224 | tf_op jit(solution)/shard_map/ppermute | solution.py:652
  50.1 12.6 %collective-permute-start.3 = (bf16[128,512]{1,0:T(8,128)(2,1)S(1)}, bf16[128,512]{1,0:T(8,128)(2,1)S(1)}, u32[]{:S(2)}, u32[]{:S(2)}) collective-permute-start(bf16[128,512]{1,0:T(8,128)(2,1)S(1)} %get-tuple-element.112), channel_id=1, source_target_pairs={{0,16},{8,24},{16,32},{24,40},{32,48},{40,56},{48,0},{56,8},{1,17}... | collective-permute-start | bytes 393224 | tf_op jit(solution)/shard_map/ppermute | solution.py:652
  51.3 14.6 %collective-permute-start.4 = (bf16[128,512]{1,0:T(8,128)(2,1)S(1)}, bf16[128,512]{1,0:T(8,128)(2,1)S(1)}, u32[]{:S(2)}, u32[]{:S(2)}) collective-permute-start(bf16[128,512]{1,0:T(8,128)(2,1)S(1)} %get-tuple-element.113), channel_id=1, source_target_pairs={{0,48},{8,56},{16,0},{24,8},{32,16},{40,24},{48,32},{56,40},{1,49}... | collective-permute-start | bytes 393224 | tf_op jit(solution)/shard_map/ppermute | solution.py:652
  53.6 15.3 %collective-permute-start.5 = (bf16[128,512]{1,0:T(8,128)(2,1)S(1)}, bf16[128,512]{1,0:T(8,128)(2,1)S(1)}, u32[]{:S(2)}, u32[]{:S(2)}) collective-permute-start(bf16[128,512]{1,0:T(8,128)(2,1)S(1)} %get-tuple-element.114), channel_id=1, source_target_pairs={{0,8},{8,16},{16,24},{24,32},{32,40},{40,48},{48,56},{56,0},{1,9},... | collective-permute-start | bytes 393224 | tf_op jit(solution)/shard_map/ppermute | solution.py:652
  61.8 7.9 %collective-permute-start.6 = (bf16[128,512]{1,0:T(8,128)(2,1)S(1)}, bf16[128,512]{1,0:T(8,128)(2,1)S(1)}, u32[]{:S(2)}, u32[]{:S(2)}) collective-permute-start(bf16[128,512]{1,0:T(8,128)(2,1)S(1)} %get-tuple-element.115), channel_id=1, source_target_pairs={{0,56},{8,0},{16,8},{24,16},{32,24},{40,32},{48,40},{56,48},{1,57}... | collective-permute-start | bytes 393224 | tf_op jit(solution)/shard_map/ppermute | solution.py:652
  71.6 6.9 %collective-permute-start.7 = (bf16[120,512]{1,0:T(8,128)(2,1)S(1)}, bf16[120,512]{1,0:T(8,128)(2,1)S(1)}, u32[]{:S(2)}, u32[]{:S(2)}) collective-permute-start(bf16[120,512]{1,0:T(8,128)(2,1)S(1)} %get-tuple-element.135), channel_id=1, source_target_pairs={{0,128},{4,132},{64,192},{68,196},{128,0},{132,4},{192,64},{196,68... | collective-permute-start | bytes 368648 | tf_op jit(solution)/shard_map/ppermute | solution.py:663
  72.8 9.0 %collective-permute-start.8 = (bf16[120,512]{1,0:T(8,128)(2,1)S(1)}, bf16[120,512]{1,0:T(8,128)(2,1)S(1)}, u32[]{:S(2)}, u32[]{:S(2)}) collective-permute-start(bf16[120,512]{1,0:T(8,128)(2,1)S(1)} %get-tuple-element.136), channel_id=1, source_target_pairs={{0,132},{4,128},{64,196},{68,192},{128,4},{132,0},{192,68},{196,64... | collective-permute-start | bytes 368648 | tf_op jit(solution)/shard_map/ppermute | solution.py:663
  75.8 13.1 %collective-permute-start.9 = (bf16[120,512]{1,0:T(8,128)(2,1)S(1)}, bf16[120,512]{1,0:T(8,128)(2,1)S(1)}, u32[]{:S(2)}, u32[]{:S(2)}) collective-permute-start(bf16[120,512]{1,0:T(8,128)(2,1)S(1)} %get-tuple-element.137), channel_id=1, source_target_pairs={{0,64},{4,68},{64,128},{68,132},{128,192},{132,196},{192,0},{196,4... | collective-permute-start | bytes 368648 | tf_op jit(solution)/shard_map/ppermute | solution.py:663
  76.2 12.7 %collective-permute-start.10 = (bf16[120,512]{1,0:T(8,128)(2,1)S(1)}, bf16[120,512]{1,0:T(8,128)(2,1)S(1)}, u32[]{:S(2)}, u32[]{:S(2)}) collective-permute-start(bf16[120,512]{1,0:T(8,128)(2,1)S(1)} %get-tuple-element.138), channel_id=1, source_target_pairs={{0,192},{4,196},{64,0},{68,4},{128,64},{132,68},{192,128},{196,132... | collective-permute-start | bytes 368648 | tf_op jit(solution)/shard_map/ppermute | solution.py:663
  78.5 10.4 %collective-permute-start.11 = (bf16[120,512]{1,0:T(8,128)(2,1)S(1)}, bf16[120,512]{1,0:T(8,128)(2,1)S(1)}, u32[]{:S(2)}, u32[]{:S(2)}) collective-permute-start(bf16[120,512]{1,0:T(8,128)(2,1)S(1)} %get-tuple-element.139), channel_id=1, source_target_pairs={{0,68},{4,64},{64,132},{68,128},{128,196},{132,192},{192,4},{196,0... | collective-permute-start | bytes 368648 | tf_op jit(solution)/shard_map/ppermute | solution.py:663
  78.5 10.4 %collective-permute-start.12 = (bf16[120,512]{1,0:T(8,128)(2,1)S(1)}, bf16[120,512]{1,0:T(8,128)(2,1)S(1)}, u32[]{:S(2)}, u32[]{:S(2)}) collective-permute-start(bf16[120,512]{1,0:T(8,128)(2,1)S(1)} %get-tuple-element.140), channel_id=1, source_target_pairs={{0,196},{4,192},{64,4},{68,0},{128,68},{132,64},{192,132},{196,128... | collective-permute-start | bytes 368648 | tf_op jit(solution)/shard_map/ppermute | solution.py:663
  81.8 7.2 %collective-permute-start.13 = (bf16[120,512]{1,0:T(8,128)(2,1)S(1)}, bf16[120,512]{1,0:T(8,128)(2,1)S(1)}, u32[]{:S(2)}, u32[]{:S(2)}) collective-permute-start(bf16[120,512]{1,0:T(8,128)(2,1)S(1)} %get-tuple-element.141), channel_id=1, source_target_pairs={{0,4},{4,0},{64,68},{68,64},{128,132},{132,128},{192,196},{196,192... | collective-permute-start | bytes 368648 | tf_op jit(solution)/shard_map/ppermute | solution.py:663
  84.6 2.0 %copy-start = (bf16[16,7,128,128]{3,2,1,0:T(8,128)(2,1)S(1)}, bf16[16,7,128,128]{3,2,1,0:T(8,128)(2,1)}, u32[]{:S(2)}) copy-start(bf16[16,7,128,128]{3,2,1,0:T(8,128)(2,1)} %all-gather.6.cloned.1.call-done) | copy-start | bytes 11010052
  94.3 8.3 %collective-permute-start.14 = (bf16[28,32,128]{2,1,0:T(8,128)(2,1)S(1)}, bf16[28,32,128]{2,1,0:T(8,128)(2,1)S(1)}, u32[]{:S(2)}, u32[]{:S(2)}) collective-permute-start(bf16[28,32,128]{2,1,0:T(8,128)(2,1)S(1)} %get-tuple-element.163), channel_id=1, source_target_pairs={{0,2},{1,3},{2,0},{3,1},{4,6},{5,7},{6,4},{7,5},{8,10},{9,11},{10,... | collective-permute-start | bytes 688136 | tf_op jit(solution)/shard_map/ppermute | solution.py:671
  95.9 12.4 %collective-permute-start.15 = (bf16[28,32,128]{2,1,0:T(8,128)(2,1)S(1)}, bf16[28,32,128]{2,1,0:T(8,128)(2,1)S(1)}, u32[]{:S(2)}, u32[]{:S(2)}) collective-permute-start(bf16[28,32,128]{2,1,0:T(8,128)(2,1)S(1)} %get-tuple-element.164), channel_id=1, source_target_pairs={{0,1},{1,2},{2,3},{3,0},{4,5},{5,6},{6,7},{7,4},{8,9},{9,10},{10,1... | collective-permute-start | bytes 688136 | tf_op jit(solution)/shard_map/ppermute | solution.py:671
  95.9 12.4 %collective-permute-start.16 = (bf16[28,32,128]{2,1,0:T(8,128)(2,1)S(1)}, bf16[28,32,128]{2,1,0:T(8,128)(2,1)S(1)}, u32[]{:S(2)}, u32[]{:S(2)}) collective-permute-start(bf16[28,32,128]{2,1,0:T(8,128)(2,1)S(1)} %get-tuple-element.165), channel_id=1, source_target_pairs={{0,3},{1,0},{2,1},{3,2},{4,7},{5,4},{6,5},{7,6},{8,11},{9,8},{10,9... | collective-permute-start | bytes 688136 | tf_op jit(solution)/shard_map/ppermute | solution.py:671
Sparse Core Ops, SparseCore 0:
  35.6 45.4 all-gather.5

commit v11 on v10

--- a/solution.py
+++ b/solution.py
@@ -643,7 +643,7 @@
     turned = turn(nonzero, same)
     slots, union, need, kq = pattern(position, names, plane_columns(columns))
     near = lax.all_to_all(cuts, ("col", "x", "core"), split_axis=0, concat_axis=0, tiled=True)
-    near, turned, need = lax.optimization_barrier((near, turned, need))
+    turned, need = lax.optimization_barrier((turned, need))
     whole = lax.all_gather(turned, "col", axis=0, tiled=False)
     whole = whole.reshape(ZERO_BLOCK, SIDE, SIDE)
     packed = send(position, need, kq, near.reshape(ENTRIES, PIECE))
@@ -663,7 +663,7 @@
         far.append(lax.ppermute(packed[1 + number], ("x", "core"), pairs))
     far_lists = far_plan(position, slots, union, notes)
     own = own_sums(own_lists, whole)
-    far, fits, own = lax.optimization_barrier((far, far_lists[9, 0] != 0, own))
+    far, own = lax.optimization_barrier((far, own))
     result = far_sums(own_lists, far_lists, whole, own, position, far)
     cuts = [result[0]]
     for step in ORDER_Y:
@@ -671,7 +671,7 @@
         cuts.append(lax.ppermute(result[step], "col", pairs))
     square = finish(position, cuts)
     return lax.cond(
-        fits,
+        far_lists[9, 0] != 0,
         lambda value, *_: value,
         lambda _, *inputs: dense(*inputs),
         square,

time: 117 us -> 123 us (1.051)
  blocking collectives: 0 us -> 25.6 us
  waiting for transfers between devices: 34.4 us -> 23.2 us
  starting transfers between devices: 38.8 us -> 30.5 us
    all_to_all x0 -> x1, blocking collectives: none -> 25.6 us  [shards(): lax.all_to_all(cuts, ('col', 'x', 'core'), split_axis=0, concat_axis=0, t...]
    all_to_all x1 -> x0, waiting for transfers between devices: 9.97 us -> none  [shards(): lax.all_to_all(cuts, ('col', 'x', 'core'), split_axis=0, concat_axis=0, t...]
    all_to_all x1 -> x0, starting transfers between devices: 8.73 us -> none  [shards(): lax.all_to_all(cuts, ('col', 'x', 'core'), split_axis=0, concat_axis=0, t...]
  transfers between devices with their start and end apart: 19 -> 18, of which waited for: 8 -> 6; matrix products, arithmetic and copies ran while one was open for 2% -> 0% of each run, Pallas kernels for 10% -> 5%
where the time goes in v11:
time: 123 us; the launch traced here: 122 us
  starting transfers between devices  30.5 us (25%)
  blocking collectives  25.6 us (21%)
  Pallas kernels  23.5 us (19%)
  waiting for transfers between devices  23.2 us (19%)
  between operations  14.2 us (12%)
  local copies, waits for them, and re-layouts  4.85 us (4%)
    all_to_all x1, blocking collectives, shards(): lax.all_to_all(cuts, ('col', 'x', 'core'), split_axis=0, concat_axis=0, t...  25.6 us
    ppermute x7, starting transfers between devices, shards(): lax.ppermute(packed[step], 'z', [(i, (i + step) % NZ) for i in range(NZ)])  15.8 us
    ppermute x7, waiting for transfers between devices, shards(): lax.ppermute(packed[step], 'z', [(i, (i + step) % NZ) for i in range(NZ)])  14.3 us
    ppermute x7, starting transfers between devices, shards(): far.append(lax.ppermute(packed[1 + number], ('x', 'core'), pairs))  10.7 us
    ppermute x3, waiting for transfers between devices, shards(): cuts.append(lax.ppermute(result[step], 'col', pairs))  8.87 us
    pallas_call x1, Pallas kernels, far_sums(): pl.pallas_call(far_kernel, out_shape=[jax.ShapeDtypeStruct((HEIGHT * QUAR...  5.29 us
    ppermute x3, starting transfers between devices, shards(): cuts.append(lax.ppermute(result[step], 'col', pairs))  4 us
    pallas_call x1, Pallas kernels, send(): pl.pallas_call(send_kernel, out_shape=[jax.ShapeDtypeStruct((ROWS_Z, PIEC...  3.12 us
  transfers between devices with their start and end apart: 18, of which 6 were waited for; matrix products, arithmetic and copies ran while one was open for 0% of the time, Pallas kernels for 5%

profile of v11, /device:TPU:1, one launch (start us, length us, event | category | flops | bytes accessed | tf_op | source)
XLA Modules:
  0.0 122.2 jit_solution(5633879766096661801)
XLA Ops:
  6.5 0.0 all-gather.6.cloned.1.call-start
  6.5 0.9 copy.101
  7.4 0.3 reshape.213
  7.7 0.1 reshape.214
  7.8 0.1 reshape.215.entries_ref
  7.9 0.1 pad_add_fusion.position_ref
  8.0 1.9 %prepare.1 = bf16[32,32,512]{2,1,0:T(8,128)(2,1)S(1)} custom-call(s32[4]{0:T(128)S(1)} %pad_add_fusion.position_ref, s32[4,7]{1,0:T(4,128)} %keep_ref.3, bf16[4,7,128,128]{3,2,1,0:T(8,128)(2,1)} %blocks_ref.2), custom_call_target="tpu_custom_call" | custom-call | tf_op jit(solution)/shard_map/prepare/pallas_call | solution.py:87
  9.9 0.0 copy-start.4
  9.9 0.0 copy-start.5
  9.9 0.0 copy-start.6
  9.9 0.9 copy.103.columns_ref
  10.9 2.4 %turn.1 = bf16[4,7,128,128]{3,2,1,0:T(8,128)(2,1)} custom-call(s32[4,7]{1,0:T(4,128)} %keep_ref.3, bf16[4,7,128,128]{3,2,1,0:T(8,128)(2,1)} %blocks_ref.2), custom_call_target="tpu_custom_call" | custom-call | flops 117440512 | bytes 1835008 | tf_op jit(solution)/shard_map/turn/pallas_call | solution.py:108
  13.3 2.5 %pattern.1 = (s32[256,256]{1,0:T(8,128)S(1)}, f32[128,256]{1,0:T(8,128)S(1)}, f32[128,1024]{1,0:T(8,128)S(1)}, f32[8,1024]{1,0:T(8,128)S(1)}) custom-call(s32[4]{0:T(128)S(1)} %pad_add_fusion.position_ref, s32[256,28]{1,0:T(8,128)S(1)} %copy.103.columns_ref, s32[1,1024]{1,0:T(1,128)S(1)} %reshape.215.entries_ref), custom_call_target="tpu_custom_call" | custom-call | flops 234881024 | bytes 524288 | tf_op jit(solution)/shard_map/pattern/pallas_call | solution.py:355
  15.8 0.0 all-gather.6.cloned.1.call-update
  15.8 25.6 %all_to_all.9 = bf16[32,32,512]{2,1,0:T(8,128)(2,1)S(1)} all-to-all(bf16[32,32,512]{2,1,0:T(8,128)(2,1)S(1)} %prepare.1), channel_id=1, replica_groups=mesh['x'=4,'z'=8,'core'=2,'col'=4] {'col','x','core'}, dimensions={0} | all-to-all | bytes 2097152 | tf_op jit(solution)/shard_map/all_to_all | solution.py:645
  41.4 3.1 %send.1 = (bf16[128,512]{1,0:T(8,128)(2,1)S(1)}, bf16[128,512]{1,0:T(8,128)(2,1)S(1)}, bf16[128,512]{1,0:T(8,128)(2,1)S(1)}, bf16[128,512]{1,0:T(8,128)(2,1)S(1)...) custom-call(s32[4]{0:T(128)S(1)} %pad_add_fusion.position_ref, ...), custom_call_target="tpu_custom_call" | custom-call | tf_op jit(solution)/shard_map/send/pallas_call | solution.py:414
  44.5 7.0 %collective-permute-start = (bf16[128,512]{1,0:T(8,128)(2,1)S(1)}, bf16[128,512]{1,0:T(8,128)(2,1)S(1)}, u32[]{:S(2)}, u32[]{:S(2)}) collective-permute-start(bf16[128,512]{1,0:T(8,128)(2,1)S(1)} %get-tuple-element.108), channel_id=1, source_target_pairs={{0,32},{8,40},{16,48},{24,56},{32,0},{40,8},{48,16},{56,24},{1,33}... | collective-permute-start | bytes 393224 | tf_op jit(solution)/shard_map/ppermute | solution.py:652
  51.5 1.6 %collective-permute-start.1 = (bf16[128,512]{1,0:T(8,128)(2,1)S(1)}, bf16[128,512]{1,0:T(8,128)(2,1)S(1)}, u32[]{:S(2)}, u32[]{:S(2)}) collective-permute-start(bf16[128,512]{1,0:T(8,128)(2,1)S(1)} %get-tuple-element.109), channel_id=1, source_target_pairs={{0,24},{8,32},{16,40},{24,48},{32,56},{40,0},{48,8},{56,16},{1,25}... | collective-permute-start | bytes 393224 | tf_op jit(solution)/shard_map/ppermute | solution.py:652
  53.1 2.8 %collective-permute-start.2 = (bf16[128,512]{1,0:T(8,128)(2,1)S(1)}, bf16[128,512]{1,0:T(8,128)(2,1)S(1)}, u32[]{:S(2)}, u32[]{:S(2)}) collective-permute-start(bf16[128,512]{1,0:T(8,128)(2,1)S(1)} %get-tuple-element.110), channel_id=1, source_target_pairs={{0,40},{8,48},{16,56},{24,0},{32,8},{40,16},{48,24},{56,32},{1,41}... | collective-permute-start | bytes 393224 | tf_op jit(solution)/shard_map/ppermute | solution.py:652
  56.0 1.2 collective-permute-start.3
  57.2 2.4 %collective-permute-start.4 = (bf16[128,512]{1,0:T(8,128)(2,1)S(1)}, bf16[128,512]{1,0:T(8,128)(2,1)S(1)}, u32[]{:S(2)}, u32[]{:S(2)}) collective-permute-start(bf16[128,512]{1,0:T(8,128)(2,1)S(1)} %get-tuple-element.112), channel_id=1, source_target_pairs={{0,48},{8,56},{16,0},{24,8},{32,16},{40,24},{48,32},{56,40},{1,49}... | collective-permute-start | bytes 393224 | tf_op jit(solution)/shard_map/ppermute | solution.py:652
  59.5 0.0 collective-permute-done.refs_1_
  59.5 0.7 collective-permute-start.5
  60.3 7.4 %collective-permute-done.1.refs_2_ = bf16[128,512]{1,0:T(8,128)(2,1)S(1)} collective-permute-done((bf16[128,512]{1,0:T(8,128)(2,1)S(1)}, bf16[128,512]{1,0:T(8,128)(2,1)S(1)}, u32[]{:S(2)}, u32[]{:S(2)}) %collective-permute-start.1) | collective-permute-done | bytes 131104 | tf_op jit(solution)/shard_map/ppermute | solution.py:652
  67.7 0.0 collective-permute-start.6
  67.7 0.8 own_plan.1.plan_ref.own_ref
  68.5 0.0 collective-permute-done.2.refs_3_
  68.5 0.0 collective-permute-done.3.refs_4_
  68.5 3.2 %collective-permute-done.4.refs_5_ = bf16[128,512]{1,0:T(8,128)(2,1)S(1)} collective-permute-done((bf16[128,512]{1,0:T(8,128)(2,1)S(1)}, bf16[128,512]{1,0:T(8,128)(2,1)S(1)}, u32[]{:S(2)}, u32[]{:S(2)}) %collective-permute-start.4) | collective-permute-done | bytes 131104 | tf_op jit(solution)/shard_map/ppermute | solution.py:652
  71.7 3.1 %collective-permute-done.5.refs_6_ = bf16[128,512]{1,0:T(8,128)(2,1)S(1)} collective-permute-done((bf16[128,512]{1,0:T(8,128)(2,1)S(1)}, bf16[128,512]{1,0:T(8,128)(2,1)S(1)}, u32[]{:S(2)}, u32[]{:S(2)}) %collective-permute-start.5) | collective-permute-done | bytes 131104 | tf_op jit(solution)/shard_map/ppermute | solution.py:652
  74.8 0.7 collective-permute-done.6.refs_7_
  75.4 1.9 %route.1 = (bf16[120,512]{1,0:T(8,128)(2,1)S(1)}, bf16[120,512]{1,0:T(8,128)(2,1)S(1)}, bf16[120,512]{1,0:T(8,128)(2,1)S(1)}, bf16[120,512]{1,0:T(8,128)(2,1)S(1...) custom-call(s32[4]{0:T(128)S(1)} %pad_add_fusion.position_ref, ...), custom_call_target="tpu_custom_call" | custom-call | tf_op jit(solution)/shard_map/route/pallas_call | solution.py:463
  77.4 2.4 %collective-permute-start.7 = (bf16[120,512]{1,0:T(8,128)(2,1)S(1)}, bf16[120,512]{1,0:T(8,128)(2,1)S(1)}, u32[]{:S(2)}, u32[]{:S(2)}) collective-permute-start(bf16[120,512]{1,0:T(8,128)(2,1)S(1)} %get-tuple-element.142), channel_id=1, source_target_pairs={{0,128},{4,132},{64,192},{68,196},{128,0},{132,4},{192,64},{196,68... | collective-permute-start | bytes 368648 | tf_op jit(solution)/shard_map/ppermute | solution.py:663
  79.8 2.0 %collective-permute-start.8 = (bf16[120,512]{1,0:T(8,128)(2,1)S(1)}, bf16[120,512]{1,0:T(8,128)(2,1)S(1)}, u32[]{:S(2)}, u32[]{:S(2)}) collective-permute-start(bf16[120,512]{1,0:T(8,128)(2,1)S(1)} %get-tuple-element.143), channel_id=1, source_target_pairs={{0,132},{4,128},{64,196},{68,192},{128,4},{132,0},{192,68},{196,64... | collective-permute-start | bytes 368648 | tf_op jit(solution)/shard_map/ppermute | solution.py:663
  81.7 0.4 collective-permute-start.9
  82.1 2.3 %collective-permute-start.10 = (bf16[120,512]{1,0:T(8,128)(2,1)S(1)}, bf16[120,512]{1,0:T(8,128)(2,1)S(1)}, u32[]{:S(2)}, u32[]{:S(2)}) collective-permute-start(bf16[120,512]{1,0:T(8,128)(2,1)S(1)} %get-tuple-element.145), channel_id=1, source_target_pairs={{0,192},{4,196},{64,0},{68,4},{128,64},{132,68},{192,128},{196,132... | collective-permute-start | bytes 368648 | tf_op jit(solution)/shard_map/ppermute | solution.py:663
  84.4 0.0 collective-permute-start.11
  84.4 0.0 collective-permute-done.7.refs_1_
  84.4 3.0 %collective-permute-start.12 = (bf16[120,512]{1,0:T(8,128)(2,1)S(1)}, bf16[120,512]{1,0:T(8,128)(2,1)S(1)}, u32[]{:S(2)}, u32[]{:S(2)}) collective-permute-start(bf16[120,512]{1,0:T(8,128)(2,1)S(1)} %get-tuple-element.147), channel_id=1, source_target_pairs={{0,196},{4,192},{64,4},{68,0},{128,68},{132,64},{192,132},{196,128... | collective-permute-start | bytes 368648 | tf_op jit(solution)/shard_map/ppermute | solution.py:663
  87.4 0.0 collective-permute-done.8.refs_2_
  87.4 0.7 collective-permute-start.13
  88.1 1.6 %far_plan.1.plan_ref = s32[16,128]{1,0:T(8,128)S(1)} custom-call(s32[4]{0:T(128)S(1)} %pad_add_fusion.position_ref, s32[256,256]{1,0:T(8,128)S(1)} %get-tuple-element.105.slots_ref, f32[128,256]{1,0:T(8,128)S(1)} %get-tuple-element.106.union_ref, bf16[128,512]{1,0:T(8,128)(2,1)S(1)} %get-tuple-element.131.refs_0_, ...), custom_call_target="tpu_custom_call" | custom-call | flops 671088640 | bytes 524288 | tf_op jit(solution)/shard_map/far_plan/pallas_call | solution.py:581
  89.7 0.0 all-gather.6.cloned.1.call-done
  89.7 0.0 copy-start
  89.7 2.0 %copy-done = bf16[16,7,128,128]{3,2,1,0:T(8,128)(2,1)S(1)} copy-done((bf16[16,7,128,128]{3,2,1,0:T(8,128)(2,1)S(1)}, bf16[16,7,128,128]{3,2,1,0:T(8,128)(2,1)}, u32[]{:S(2)}) %copy-start) | copy-done | bytes 3670040
  91.7 2.2 %own_sums.1.near_ref = f32[112,32,128]{2,1,0:T(8,128)S(1)} custom-call(s32[16,128]{1,0:T(8,128)S(1)} %own_plan.1.plan_ref.own_ref, bf16[112,128,128]{2,1,0:T(8,128)(2,1)S(1)} %bitcast.150), custom_call_target="tpu_custom_call" | custom-call | flops 536870912 | bytes 5505024 | tf_op jit(solution)/shard_map/own_sums/pallas_call | solution.py:162
  93.9 0.0 collective-permute-done.9.refs_3_
  93.9 0.0 collective-permute-done.10.refs_4_
  93.9 0.0 collective-permute-done.11.refs_5_
  93.9 0.0 collective-permute-done.12.refs_6_
  94.0 0.0 collective-permute-done.13.refs_7_
  94.0 5.3 %far_sums.1 = (bf16[28,32,128]{2,1,0:T(8,128)(2,1)S(1)}, bf16[28,32,128]{2,1,0:T(8,128)(2,1)S(1)}, bf16[28,32,128]{2,1,0:T(8,128)(2,1)S(1)}, bf16[28,32,128]{2,1,0:T(8,128)(2,1)S(1)}) custom-call(s32[16,128]{1,0:T(8,128)S(1)} %own_plan.1.plan_ref.own_ref, s32[16,128]{1,0:T(8,128)S(1)} %far_plan.1.plan_ref, bf16[112,128,128]{2,1,0:T(8,128)(2,1)} %bitcast.149, ...), custom_call_target="tpu_custom_call" | custom-call | tf_op jit(solution)/shard_map/far_sums/pallas_call | solution.py:244
  99.3 1.3 %collective-permute-start.14 = (bf16[28,32,128]{2,1,0:T(8,128)(2,1)S(1)}, bf16[28,32,128]{2,1,0:T(8,128)(2,1)S(1)}, u32[]{:S(2)}, u32[]{:S(2)}) collective-permute-start(bf16[28,32,128]{2,1,0:T(8,128)(2,1)S(1)} %get-tuple-element.159), channel_id=1, source_target_pairs={{0,2},{1,3},{2,0},{3,1},{4,6},{5,7},{6,4},{7,5},{8,10},{9,11},{10,... | collective-permute-start | bytes 688136 | tf_op jit(solution)/shard_map/ppermute | solution.py:671
  100.6 0.0 collective-permute-start.15
  100.6 2.7 %collective-permute-start.16 = (bf16[28,32,128]{2,1,0:T(8,128)(2,1)S(1)}, bf16[28,32,128]{2,1,0:T(8,128)(2,1)S(1)}, u32[]{:S(2)}, u32[]{:S(2)}) collective-permute-start(bf16[28,32,128]{2,1,0:T(8,128)(2,1)S(1)} %get-tuple-element.161), channel_id=1, source_target_pairs={{0,3},{1,0},{2,1},{3,2},{4,7},{5,4},{6,5},{7,6},{8,11},{9,8},{10,9... | collective-permute-start | bytes 688136 | tf_op jit(solution)/shard_map/ppermute | solution.py:671
  103.3 0.5 slice.68
  104.4 3.1 %collective-permute-done.14.refs_1_ = bf16[28,32,128]{2,1,0:T(8,128)(2,1)S(1)} collective-permute-done((bf16[28,32,128]{2,1,0:T(8,128)(2,1)S(1)}, bf16[28,32,128]{2,1,0:T(8,128)(2,1)S(1)}, u32[]{:S(2)}, u32[]{:S(2)}) %collective-permute-start.14) | collective-permute-done | bytes 229408 | tf_op jit(solution)/shard_map/ppermute | solution.py:671
  107.5 5.8 %collective-permute-done.15.refs_2_ = bf16[28,32,128]{2,1,0:T(8,128)(2,1)S(1)} collective-permute-done((bf16[28,32,128]{2,1,0:T(8,128)(2,1)S(1)}, bf16[28,32,128]{2,1,0:T(8,128)(2,1)S(1)}, u32[]{:S(2)}, u32[]{:S(2)}) %collective-permute-start.15) | collective-permute-done | bytes 229408 | tf_op jit(solution)/shard_map/ppermute | solution.py:671
  113.3 0.0 collective-permute-done.16.refs_3_
  113.3 1.8 %finish.1 = bf16[4,7,128,128]{3,2,1,0:T(8,128)(2,1)} custom-call(s32[4]{0:T(128)S(1)} %pad_add_fusion.position_ref, bf16[28,32,128]{2,1,0:T(8,128)(2,1)S(1)} %get-tuple-element.158.refs_0_, bf16[28,32,128]{2,1,0:T(8,128)(2,1)S(1)} %collective-permute-done.14.refs_1_, bf16[28,32,128]{2,1,0:T(8,128)(2,1)S(1)} %collective-permute-done.15.refs_2_, ...), custom_call_target="tpu_custom_call" | custom-call | tf_op jit(solution)/shard_map/finish/pallas_call | solution.py:274
  115.1 0.0 copy-done.4
  115.1 0.0 copy-done.5
  115.1 0.0 copy-done.6
  115.1 0.3 conditional.1
  (3 shorter events, 0.0 us)
Async XLA Ops:
  6.5 83.1 %all-gather.6.cloned.1.call-start = ((), (), s32[]{:S(2)}) async-start(), calls=%async_computation.5 | async-start | bytes 4587520 | tf_op jit(solution)/shard_map/all_gather | solution.py:647
  9.9 105.2 %copy-start.4 = (bf16[4,7,128,128]{3,2,1,0:T(8,128)(2,1)S(1)}, bf16[4,7,128,128]{3,2,1,0:T(8,128)(2,1)}, u32[]{:S(2)}) copy-start(bf16[4,7,128,128]{3,2,1,0:T(8,128)(2,1)} %blocks_ref.2) | copy-start | bytes 2752516
  9.9 105.2 %copy-start.5 = (s32[256,28]{0,1:T(8,128)S(1)}, s32[256,28]{0,1:T(8,128)}, u32[]{:S(2)}) copy-start(s32[256,28]{0,1:T(8,128)} %param.7) | copy-start | bytes 86020
  9.9 105.2 %copy-start.6 = (s32[4,7]{1,0:T(4,128)S(1)}, s32[4,7]{1,0:T(4,128)}, u32[]{:S(2)}) copy-start(s32[4,7]{1,0:T(4,128)} %keep_ref.3) | copy-start | bytes 340
  44.5 15.0 %collective-permute-start = (bf16[128,512]{1,0:T(8,128)(2,1)S(1)}, bf16[128,512]{1,0:T(8,128)(2,1)S(1)}, u32[]{:S(2)}, u32[]{:S(2)}) collective-permute-start(bf16[128,512]{1,0:T(8,128)(2,1)S(1)} %get-tuple-element.108), channel_id=1, source_target_pairs={{0,32},{8,40},{16,48},{24,56},{32,0},{40,8},{48,16},{56,24},{1,33}... | collective-permute-start | bytes 393224 | tf_op jit(solution)/shard_map/ppermute | solution.py:652
  51.5 16.2 %collective-permute-start.1 = (bf16[128,512]{1,0:T(8,128)(2,1)S(1)}, bf16[128,512]{1,0:T(8,128)(2,1)S(1)}, u32[]{:S(2)}, u32[]{:S(2)}) collective-permute-start(bf16[128,512]{1,0:T(8,128)(2,1)S(1)} %get-tuple-element.109), channel_id=1, source_target_pairs={{0,24},{8,32},{16,40},{24,48},{32,56},{40,0},{48,8},{56,16},{1,25}... | collective-permute-start | bytes 393224 | tf_op jit(solution)/shard_map/ppermute | solution.py:652
  53.1 15.4 %collective-permute-start.2 = (bf16[128,512]{1,0:T(8,128)(2,1)S(1)}, bf16[128,512]{1,0:T(8,128)(2,1)S(1)}, u32[]{:S(2)}, u32[]{:S(2)}) collective-permute-start(bf16[128,512]{1,0:T(8,128)(2,1)S(1)} %get-tuple-element.110), channel_id=1, source_target_pairs={{0,40},{8,48},{16,56},{24,0},{32,8},{40,16},{48,24},{56,32},{1,41}... | collective-permute-start | bytes 393224 | tf_op jit(solution)/shard_map/ppermute | solution.py:652
  56.0 12.5 %collective-permute-start.3 = (bf16[128,512]{1,0:T(8,128)(2,1)S(1)}, bf16[128,512]{1,0:T(8,128)(2,1)S(1)}, u32[]{:S(2)}, u32[]{:S(2)}) collective-permute-start(bf16[128,512]{1,0:T(8,128)(2,1)S(1)} %get-tuple-element.111), channel_id=1, source_target_pairs={{0,16},{8,24},{16,32},{24,40},{32,48},{40,56},{48,0},{56,8},{1,17}... | collective-permute-start | bytes 393224 | tf_op jit(solution)/shard_map/ppermute | solution.py:652
  57.2 14.5 %collective-permute-start.4 = (bf16[128,512]{1,0:T(8,128)(2,1)S(1)}, bf16[128,512]{1,0:T(8,128)(2,1)S(1)}, u32[]{:S(2)}, u32[]{:S(2)}) collective-permute-start(bf16[128,512]{1,0:T(8,128)(2,1)S(1)} %get-tuple-element.112), channel_id=1, source_target_pairs={{0,48},{8,56},{16,0},{24,8},{32,16},{40,24},{48,32},{56,40},{1,49}... | collective-permute-start | bytes 393224 | tf_op jit(solution)/shard_map/ppermute | solution.py:652
  59.5 15.2 %collective-permute-start.5 = (bf16[128,512]{1,0:T(8,128)(2,1)S(1)}, bf16[128,512]{1,0:T(8,128)(2,1)S(1)}, u32[]{:S(2)}, u32[]{:S(2)}) collective-permute-start(bf16[128,512]{1,0:T(8,128)(2,1)S(1)} %get-tuple-element.113), channel_id=1, source_target_pairs={{0,8},{8,16},{16,24},{24,32},{32,40},{40,48},{48,56},{56,0},{1,9},... | collective-permute-start | bytes 393224 | tf_op jit(solution)/shard_map/ppermute | solution.py:652
  67.7 7.8 %collective-permute-start.6 = (bf16[128,512]{1,0:T(8,128)(2,1)S(1)}, bf16[128,512]{1,0:T(8,128)(2,1)S(1)}, u32[]{:S(2)}, u32[]{:S(2)}) collective-permute-start(bf16[128,512]{1,0:T(8,128)(2,1)S(1)} %get-tuple-element.114), channel_id=1, source_target_pairs={{0,56},{8,0},{16,8},{24,16},{32,24},{40,32},{48,40},{56,48},{1,57}... | collective-permute-start | bytes 393224 | tf_op jit(solution)/shard_map/ppermute | solution.py:652
  77.4 7.0 %collective-permute-start.7 = (bf16[120,512]{1,0:T(8,128)(2,1)S(1)}, bf16[120,512]{1,0:T(8,128)(2,1)S(1)}, u32[]{:S(2)}, u32[]{:S(2)}) collective-permute-start(bf16[120,512]{1,0:T(8,128)(2,1)S(1)} %get-tuple-element.142), channel_id=1, source_target_pairs={{0,128},{4,132},{64,192},{68,196},{128,0},{132,4},{192,64},{196,68... | collective-permute-start | bytes 368648 | tf_op jit(solution)/shard_map/ppermute | solution.py:663
  79.8 7.6 %collective-permute-start.8 = (bf16[120,512]{1,0:T(8,128)(2,1)S(1)}, bf16[120,512]{1,0:T(8,128)(2,1)S(1)}, u32[]{:S(2)}, u32[]{:S(2)}) collective-permute-start(bf16[120,512]{1,0:T(8,128)(2,1)S(1)} %get-tuple-element.143), channel_id=1, source_target_pairs={{0,132},{4,128},{64,196},{68,192},{128,4},{132,0},{192,68},{196,64... | collective-permute-start | bytes 368648 | tf_op jit(solution)/shard_map/ppermute | solution.py:663
  81.7 12.2 %collective-permute-start.9 = (bf16[120,512]{1,0:T(8,128)(2,1)S(1)}, bf16[120,512]{1,0:T(8,128)(2,1)S(1)}, u32[]{:S(2)}, u32[]{:S(2)}) collective-permute-start(bf16[120,512]{1,0:T(8,128)(2,1)S(1)} %get-tuple-element.144), channel_id=1, source_target_pairs={{0,64},{4,68},{64,128},{68,132},{128,192},{132,196},{192,0},{196,4... | collective-permute-start | bytes 368648 | tf_op jit(solution)/shard_map/ppermute | solution.py:663
  82.1 11.8 %collective-permute-start.10 = (bf16[120,512]{1,0:T(8,128)(2,1)S(1)}, bf16[120,512]{1,0:T(8,128)(2,1)S(1)}, u32[]{:S(2)}, u32[]{:S(2)}) collective-permute-start(bf16[120,512]{1,0:T(8,128)(2,1)S(1)} %get-tuple-element.145), channel_id=1, source_target_pairs={{0,192},{4,196},{64,0},{68,4},{128,64},{132,68},{192,128},{196,132... | collective-permute-start | bytes 368648 | tf_op jit(solution)/shard_map/ppermute | solution.py:663
  84.4 9.5 %collective-permute-start.11 = (bf16[120,512]{1,0:T(8,128)(2,1)S(1)}, bf16[120,512]{1,0:T(8,128)(2,1)S(1)}, u32[]{:S(2)}, u32[]{:S(2)}) collective-permute-start(bf16[120,512]{1,0:T(8,128)(2,1)S(1)} %get-tuple-element.146), channel_id=1, source_target_pairs={{0,68},{4,64},{64,132},{68,128},{128,196},{132,192},{192,4},{196,0... | collective-permute-start | bytes 368648 | tf_op jit(solution)/shard_map/ppermute | solution.py:663
  84.4 9.5 %collective-permute-start.12 = (bf16[120,512]{1,0:T(8,128)(2,1)S(1)}, bf16[120,512]{1,0:T(8,128)(2,1)S(1)}, u32[]{:S(2)}, u32[]{:S(2)}) collective-permute-start(bf16[120,512]{1,0:T(8,128)(2,1)S(1)} %get-tuple-element.147), channel_id=1, source_target_pairs={{0,196},{4,192},{64,4},{68,0},{128,68},{132,64},{192,132},{196,128... | collective-permute-start | bytes 368648 | tf_op jit(solution)/shard_map/ppermute | solution.py:663
  87.4 6.6 %collective-permute-start.13 = (bf16[120,512]{1,0:T(8,128)(2,1)S(1)}, bf16[120,512]{1,0:T(8,128)(2,1)S(1)}, u32[]{:S(2)}, u32[]{:S(2)}) collective-permute-start(bf16[120,512]{1,0:T(8,128)(2,1)S(1)} %get-tuple-element.148), channel_id=1, source_target_pairs={{0,4},{4,0},{64,68},{68,64},{128,132},{132,128},{192,196},{196,192... | collective-permute-start | bytes 368648 | tf_op jit(solution)/shard_map/ppermute | solution.py:663
  89.7 2.0 %copy-start = (bf16[16,7,128,128]{3,2,1,0:T(8,128)(2,1)S(1)}, bf16[16,7,128,128]{3,2,1,0:T(8,128)(2,1)}, u32[]{:S(2)}) copy-start(bf16[16,7,128,128]{3,2,1,0:T(8,128)(2,1)} %all-gather.6.cloned.1.call-done) | copy-start | bytes 11010052
  99.3 8.3 %collective-permute-start.14 = (bf16[28,32,128]{2,1,0:T(8,128)(2,1)S(1)}, bf16[28,32,128]{2,1,0:T(8,128)(2,1)S(1)}, u32[]{:S(2)}, u32[]{:S(2)}) collective-permute-start(bf16[28,32,128]{2,1,0:T(8,128)(2,1)S(1)} %get-tuple-element.159), channel_id=1, source_target_pairs={{0,2},{1,3},{2,0},{3,1},{4,6},{5,7},{6,4},{7,5},{8,10},{9,11},{10,... | collective-permute-start | bytes 688136 | tf_op jit(solution)/shard_map/ppermute | solution.py:671
  100.6 12.7 %collective-permute-start.15 = (bf16[28,32,128]{2,1,0:T(8,128)(2,1)S(1)}, bf16[28,32,128]{2,1,0:T(8,128)(2,1)S(1)}, u32[]{:S(2)}, u32[]{:S(2)}) collective-permute-start(bf16[28,32,128]{2,1,0:T(8,128)(2,1)S(1)} %get-tuple-element.160), channel_id=1, source_target_pairs={{0,1},{1,2},{2,3},{3,0},{4,5},{5,6},{6,7},{7,4},{8,9},{9,10},{10,1... | collective-permute-start | bytes 688136 | tf_op jit(solution)/shard_map/ppermute | solution.py:671
  100.6 12.7 %collective-permute-start.16 = (bf16[28,32,128]{2,1,0:T(8,128)(2,1)S(1)}, bf16[28,32,128]{2,1,0:T(8,128)(2,1)S(1)}, u32[]{:S(2)}, u32[]{:S(2)}) collective-permute-start(bf16[28,32,128]{2,1,0:T(8,128)(2,1)S(1)} %get-tuple-element.161), channel_id=1, source_target_pairs={{0,3},{1,0},{2,1},{3,2},{4,7},{5,4},{6,5},{7,6},{8,11},{9,8},{10,9... | collective-permute-start | bytes 688136 | tf_op jit(solution)/shard_map/ppermute | solution.py:671
Sparse Core Ops, SparseCore 0:
  15.9 53.6 all-gather.5

commit v12 on v11

--- a/solution.py
+++ b/solution.py
@@ -643,7 +643,7 @@
     turned = turn(nonzero, same)
     slots, union, need, kq = pattern(position, names, plane_columns(columns))
     near = lax.all_to_all(cuts, ("col", "x", "core"), split_axis=0, concat_axis=0, tiled=True)
-    turned, need = lax.optimization_barrier((turned, need))
+    near, turned, need = lax.optimization_barrier((near, turned, need))
     whole = lax.all_gather(turned, "col", axis=0, tiled=False)
     whole = whole.reshape(ZERO_BLOCK, SIDE, SIDE)
     packed = send(position, need, kq, near.reshape(ENTRIES, PIECE))
@@ -661,6 +661,7 @@
             (i, ((i // NC + along_x) % NX) * NC + (i + across) % NC) for i in range(TARGETS)
         ]
         far.append(lax.ppermute(packed[1 + number], ("x", "core"), pairs))
+    notes, whole = lax.optimization_barrier((notes, whole))
     far_lists = far_plan(position, slots, union, notes)
     own = own_sums(own_lists, whole)
     far, own = lax.optimization_barrier((far, own))

time: 123 us -> 117 us (0.951)
  blocking collectives: 25.6 us -> 0 us
  waiting for transfers between devices: 23.2 us -> 34 us
  starting transfers between devices: 30.5 us -> 38.5 us
    all_to_all x1 -> x0, blocking collectives: 25.6 us -> none  [shards(): lax.all_to_all(cuts, ('col', 'x', 'core'), split_axis=0, concat_axis=0, t...]
    all_to_all x0 -> x1, waiting for transfers between devices: none -> 9.97 us  [shards(): lax.all_to_all(cuts, ('col', 'x', 'core'), split_axis=0, concat_axis=0, t...]
    all_to_all x0 -> x1, starting transfers between devices: none -> 8.72 us  [shards(): lax.all_to_all(cuts, ('col', 'x', 'core'), split_axis=0, concat_axis=0, t...]
  transfers between devices with their start and end apart: 18 -> 19, of which waited for: 6 -> 9; matrix products, arithmetic and copies ran while one was open for 0% -> 2% of each run, Pallas kernels for 5% -> 8%
where the time goes in v12:
time: 117 us; the launch traced here: 116 us
  starting transfers between devices  38.5 us (33%)
  waiting for transfers between devices  34 us (29%)
  Pallas kernels  23.7 us (20%)
  between operations  14.2 us (12%)
  local copies, waits for them, and re-layouts  5.68 us (5%)
    ppermute x7, starting transfers between devices, shards(): lax.ppermute(packed[step], 'z', [(i, (i + step) % NZ) for i in range(NZ)])  15.8 us
    ppermute x7, waiting for transfers between devices, shards(): lax.ppermute(packed[step], 'z', [(i, (i + step) % NZ) for i in range(NZ)])  14.4 us
    all_to_all x1, waiting for transfers between devices, shards(): lax.all_to_all(cuts, ('col', 'x', 'core'), split_axis=0, concat_axis=0, t...  9.97 us
    ppermute x7, starting transfers between devices, shards(): far.append(lax.ppermute(packed[1 + number], ('x', 'core'), pairs))  9.88 us
    ppermute x3, waiting for transfers between devices, shards(): cuts.append(lax.ppermute(result[step], 'col', pairs))  8.8 us
    all_to_all x1, starting transfers between devices, shards(): lax.all_to_all(cuts, ('col', 'x', 'core'), split_axis=0, concat_axis=0, t...  8.72 us
    pallas_call x1, Pallas kernels, far_sums(): pl.pallas_call(far_kernel, out_shape=[jax.ShapeDtypeStruct((HEIGHT * QUAR...  5.31 us
    ppermute x3, starting transfers between devices, shards(): cuts.append(lax.ppermute(result[step], 'col', pairs))  4.07 us
  transfers between devices with their start and end apart: 19, of which 9 were waited for; matrix products, arithmetic and copies ran while one was open for 2% of the time, Pallas kernels for 8%

profile of v12, /device:TPU:1, one launch (start us, length us, event | category | flops | bytes accessed | tf_op | source)
XLA Modules:
  0.0 116.4 jit_solution(3582850329782419106)
XLA Ops:
  6.5 0.1 pad_add_fusion.position_ref
  6.6 2.9 %prepare.1 = bf16[32,32,512]{2,1,0:T(8,128)(2,1)} custom-call(s32[4]{0:T(128)S(1)} %pad_add_fusion.position_ref, s32[4,7]{1,0:T(4,128)} %keep_ref.3, bf16[4,7,128,128]{3,2,1,0:T(8,128)(2,1)} %blocks_ref.2), custom_call_target="tpu_custom_call" | custom-call | tf_op jit(solution)/shard_map/prepare/pallas_call | solution.py:87
  9.5 0.0 copy-start.5
  9.5 0.0 copy-start.6
  9.5 8.7 %all-to-all-start.1 = ((bf16[32,32,512]{2,1,0:T(8,128)(2,1)}), bf16[32,32,512]{2,1,0:T(8,128)(2,1)S(1)}, u32[]{:S(2)}, u32[]{:S(2)}) async-start(bf16[32,32,512]{2,1,0:T(8,128)(2,1)} %prepare.1), calls=%async_computation.2 | async-start | bytes 2097152 | tf_op jit(solution)/shard_map/all_to_all | solution.py:645
  18.3 0.0 all-gather.6.cloned.1.call-start
  18.3 0.9 copy.101
  19.2 0.3 reshape.213
  19.5 0.1 reshape.214
  19.6 0.1 reshape.215.entries_ref
  19.7 0.9 copy.103.columns_ref
  20.5 2.4 %turn.1 = bf16[4,7,128,128]{3,2,1,0:T(8,128)(2,1)} custom-call(s32[4,7]{1,0:T(4,128)} %keep_ref.3, bf16[4,7,128,128]{3,2,1,0:T(8,128)(2,1)} %blocks_ref.2), custom_call_target="tpu_custom_call" | custom-call | flops 117440512 | bytes 1835008 | tf_op jit(solution)/shard_map/turn/pallas_call | solution.py:108
  23.0 2.5 %pattern.1 = (s32[256,256]{1,0:T(8,128)S(1)}, f32[128,256]{1,0:T(8,128)S(1)}, f32[128,1024]{1,0:T(8,128)S(1)}, f32[8,1024]{1,0:T(8,128)S(1)}) custom-call(s32[4]{0:T(128)S(1)} %pad_add_fusion.position_ref, s32[256,28]{1,0:T(8,128)S(1)} %copy.103.columns_ref, s32[1,1024]{1,0:T(1,128)S(1)} %reshape.215.entries_ref), custom_call_target="tpu_custom_call" | custom-call | flops 234881024 | bytes 524288 | tf_op jit(solution)/shard_map/pattern/pallas_call | solution.py:355
  25.5 10.0 %all-to-all-done.1 = bf16[32,32,512]{2,1,0:T(8,128)(2,1)S(1)} async-done(((bf16[32,32,512]{2,1,0:T(8,128)(2,1)}), bf16[32,32,512]{2,1,0:T(8,128)(2,1)S(1)}, u32[]{:S(2)}, u32[]{:S(2)}) %all-to-all-start.1) | async-done | bytes 1048608 | tf_op jit(solution)/shard_map/all_to_all | solution.py:645
  35.4 0.0 all-gather.6.cloned.1.call-update
  35.5 3.1 %send.1 = (bf16[128,512]{1,0:T(8,128)(2,1)S(1)}, bf16[128,512]{1,0:T(8,128)(2,1)S(1)}, bf16[128,512]{1,0:T(8,128)(2,1)S(1)}, bf16[128,512]{1,0:T(8,128)(2,1)S(1)...) custom-call(s32[4]{0:T(128)S(1)} %pad_add_fusion.position_ref, ...), custom_call_target="tpu_custom_call" | custom-call | tf_op jit(solution)/shard_map/send/pallas_call | solution.py:414
  38.6 7.0 %collective-permute-start = (bf16[128,512]{1,0:T(8,128)(2,1)S(1)}, bf16[128,512]{1,0:T(8,128)(2,1)S(1)}, u32[]{:S(2)}, u32[]{:S(2)}) collective-permute-start(bf16[128,512]{1,0:T(8,128)(2,1)S(1)} %get-tuple-element.119), channel_id=1, source_target_pairs={{0,32},{8,40},{16,48},{24,56},{32,0},{40,8},{48,16},{56,24},{1,33}... | collective-permute-start | bytes 393224 | tf_op jit(solution)/shard_map/ppermute | solution.py:652
  45.6 1.6 %collective-permute-start.1 = (bf16[128,512]{1,0:T(8,128)(2,1)S(1)}, bf16[128,512]{1,0:T(8,128)(2,1)S(1)}, u32[]{:S(2)}, u32[]{:S(2)}) collective-permute-start(bf16[128,512]{1,0:T(8,128)(2,1)S(1)} %get-tuple-element.120), channel_id=1, source_target_pairs={{0,24},{8,32},{16,40},{24,48},{32,56},{40,0},{48,8},{56,16},{1,25}... | collective-permute-start | bytes 393224 | tf_op jit(solution)/shard_map/ppermute | solution.py:652
  47.2 2.8 %collective-permute-start.2 = (bf16[128,512]{1,0:T(8,128)(2,1)S(1)}, bf16[128,512]{1,0:T(8,128)(2,1)S(1)}, u32[]{:S(2)}, u32[]{:S(2)}) collective-permute-start(bf16[128,512]{1,0:T(8,128)(2,1)S(1)} %get-tuple-element.121), channel_id=1, source_target_pairs={{0,40},{8,48},{16,56},{24,0},{32,8},{40,16},{48,24},{56,32},{1,41}... | collective-permute-start | bytes 393224 | tf_op jit(solution)/shard_map/ppermute | solution.py:652
  50.1 1.2 %collective-permute-start.3 = (bf16[128,512]{1,0:T(8,128)(2,1)S(1)}, bf16[128,512]{1,0:T(8,128)(2,1)S(1)}, u32[]{:S(2)}, u32[]{:S(2)}) collective-permute-start(bf16[128,512]{1,0:T(8,128)(2,1)S(1)} %get-tuple-element.122), channel_id=1, source_target_pairs={{0,16},{8,24},{16,32},{24,40},{32,48},{40,56},{48,0},{56,8},{1,17}... | collective-permute-start | bytes 393224 | tf_op jit(solution)/shard_map/ppermute | solution.py:652
  51.2 2.4 %collective-permute-start.4 = (bf16[128,512]{1,0:T(8,128)(2,1)S(1)}, bf16[128,512]{1,0:T(8,128)(2,1)S(1)}, u32[]{:S(2)}, u32[]{:S(2)}) collective-permute-start(bf16[128,512]{1,0:T(8,128)(2,1)S(1)} %get-tuple-element.123), channel_id=1, source_target_pairs={{0,48},{8,56},{16,0},{24,8},{32,16},{40,24},{48,32},{56,40},{1,49}... | collective-permute-start | bytes 393224 | tf_op jit(solution)/shard_map/ppermute | solution.py:652
  53.6 0.0 collective-permute-done.refs_1_
  53.6 0.7 collective-permute-start.5
  54.4 7.4 %collective-permute-done.1.refs_2_ = bf16[128,512]{1,0:T(8,128)(2,1)S(1)} collective-permute-done((bf16[128,512]{1,0:T(8,128)(2,1)S(1)}, bf16[128,512]{1,0:T(8,128)(2,1)S(1)}, u32[]{:S(2)}, u32[]{:S(2)}) %collective-permute-start.1) | collective-permute-done | bytes 131104 | tf_op jit(solution)/shard_map/ppermute | solution.py:652
  61.8 0.0 collective-permute-start.6
  61.8 0.8 own_plan.1.plan_ref.own_ref
  62.6 0.0 collective-permute-done.2.refs_3_
  62.6 0.0 collective-permute-done.3.refs_4_
  62.6 3.3 %collective-permute-done.4.refs_5_ = bf16[128,512]{1,0:T(8,128)(2,1)S(1)} collective-permute-done((bf16[128,512]{1,0:T(8,128)(2,1)S(1)}, bf16[128,512]{1,0:T(8,128)(2,1)S(1)}, u32[]{:S(2)}, u32[]{:S(2)}) %collective-permute-start.4) | collective-permute-done | bytes 131104 | tf_op jit(solution)/shard_map/ppermute | solution.py:652
  65.9 3.1 %collective-permute-done.5.refs_6_ = bf16[128,512]{1,0:T(8,128)(2,1)S(1)} collective-permute-done((bf16[128,512]{1,0:T(8,128)(2,1)S(1)}, bf16[128,512]{1,0:T(8,128)(2,1)S(1)}, u32[]{:S(2)}, u32[]{:S(2)}) %collective-permute-start.5) | collective-permute-done | bytes 131104 | tf_op jit(solution)/shard_map/ppermute | solution.py:652
  68.9 0.7 collective-permute-done.6.refs_7_
  69.6 1.9 %route.1 = (bf16[120,512]{1,0:T(8,128)(2,1)S(1)}, bf16[120,512]{1,0:T(8,128)(2,1)S(1)}, bf16[120,512]{1,0:T(8,128)(2,1)S(1)}, bf16[120,512]{1,0:T(8,128)(2,1)S(1...) custom-call(s32[4]{0:T(128)S(1)} %pad_add_fusion.position_ref, ...), custom_call_target="tpu_custom_call" | custom-call | tf_op jit(solution)/shard_map/route/pallas_call | solution.py:463
  71.6 1.2 %collective-permute-start.7 = (bf16[120,512]{1,0:T(8,128)(2,1)S(1)}, bf16[120,512]{1,0:T(8,128)(2,1)S(1)}, u32[]{:S(2)}, u32[]{:S(2)}) collective-permute-start(bf16[120,512]{1,0:T(8,128)(2,1)S(1)} %get-tuple-element.162), channel_id=1, source_target_pairs={{0,128},{4,132},{64,192},{68,196},{128,0},{132,4},{192,64},{196,68... | collective-permute-start | bytes 368648 | tf_op jit(solution)/shard_map/ppermute | solution.py:663
  72.8 3.0 %collective-permute-start.8 = (bf16[120,512]{1,0:T(8,128)(2,1)S(1)}, bf16[120,512]{1,0:T(8,128)(2,1)S(1)}, u32[]{:S(2)}, u32[]{:S(2)}) collective-permute-start(bf16[120,512]{1,0:T(8,128)(2,1)S(1)} %get-tuple-element.163), channel_id=1, source_target_pairs={{0,132},{4,128},{64,196},{68,192},{128,4},{132,0},{192,68},{196,64... | collective-permute-start | bytes 368648 | tf_op jit(solution)/shard_map/ppermute | solution.py:663
  75.8 0.4 collective-permute-start.9
  76.2 2.3 %collective-permute-start.10 = (bf16[120,512]{1,0:T(8,128)(2,1)S(1)}, bf16[120,512]{1,0:T(8,128)(2,1)S(1)}, u32[]{:S(2)}, u32[]{:S(2)}) collective-permute-start(bf16[120,512]{1,0:T(8,128)(2,1)S(1)} %get-tuple-element.165), channel_id=1, source_target_pairs={{0,192},{4,196},{64,0},{68,4},{128,64},{132,68},{192,128},{196,132... | collective-permute-start | bytes 368648 | tf_op jit(solution)/shard_map/ppermute | solution.py:663
  78.5 0.0 collective-permute-start.11
  78.5 0.0 collective-permute-done.7.refs_1_
  78.5 3.0 %collective-permute-start.12 = (bf16[120,512]{1,0:T(8,128)(2,1)S(1)}, bf16[120,512]{1,0:T(8,128)(2,1)S(1)}, u32[]{:S(2)}, u32[]{:S(2)}) collective-permute-start(bf16[120,512]{1,0:T(8,128)(2,1)S(1)} %get-tuple-element.167), channel_id=1, source_target_pairs={{0,196},{4,192},{64,4},{68,0},{128,68},{132,64},{192,132},{196,128... | collective-permute-start | bytes 368648 | tf_op jit(solution)/shard_map/ppermute | solution.py:663
  81.4 0.3 collective-permute-done.8.refs_2_
  81.8 0.0 collective-permute-start.13
  81.8 0.0 all-gather.6.cloned.1.call-done
  81.8 2.0 %copy-done = bf16[16,7,128,128]{3,2,1,0:T(8,128)(2,1)S(1)} copy-done((bf16[16,7,128,128]{3,2,1,0:T(8,128)(2,1)S(1)}, bf16[16,7,128,128]{3,2,1,0:T(8,128)(2,1)}, u32[]{:S(2)}) %copy-start) | copy-done | bytes 3670040
  83.8 2.2 %own_sums.1.near_ref = f32[112,32,128]{2,1,0:T(8,128)S(1)} custom-call(s32[16,128]{1,0:T(8,128)S(1)} %own_plan.1.plan_ref.own_ref, bf16[112,128,128]{2,1,0:T(8,128)(2,1)S(1)} %bitcast.150), custom_call_target="tpu_custom_call" | custom-call | flops 536870912 | bytes 5505024 | tf_op jit(solution)/shard_map/own_sums/pallas_call | solution.py:162
  86.0 0.0 collective-permute-done.9.refs_3_
  86.0 0.0 collective-permute-done.10.refs_4_
  86.0 0.5 collective-permute-done.11.refs_5_
  86.6 0.0 collective-permute-done.12.refs_6_
  86.6 0.0 collective-permute-done.13.refs_7_
  86.6 1.6 %far_plan.1.plan_ref = s32[16,128]{1,0:T(8,128)S(1)} custom-call(s32[4]{0:T(128)S(1)} %pad_add_fusion.position_ref, s32[256,256]{1,0:T(8,128)S(1)} %get-tuple-element.116.slots_ref, f32[128,256]{1,0:T(8,128)S(1)} %get-tuple-element.117.union_ref, bf16[128,512]{1,0:T(8,128)(2,1)S(1)} %get-tuple-element.151.refs_0_, ...), custom_call_target="tpu_custom_call" | custom-call | flops 671088640 | bytes 524288 | tf_op jit(solution)/shard_map/far_plan/pallas_call | solution.py:581
  88.1 5.3 %far_sums.1 = (bf16[28,32,128]{2,1,0:T(8,128)(2,1)S(1)}, bf16[28,32,128]{2,1,0:T(8,128)(2,1)S(1)}, bf16[28,32,128]{2,1,0:T(8,128)(2,1)S(1)}, bf16[28,32,128]{2,1,0:T(8,128)(2,1)S(1)}) custom-call(s32[16,128]{1,0:T(8,128)S(1)} %own_plan.1.plan_ref.own_ref, s32[16,128]{1,0:T(8,128)S(1)} %far_plan.1.plan_ref, bf16[112,128,128]{2,1,0:T(8,128)(2,1)} %bitcast.149, ...), custom_call_target="tpu_custom_call" | custom-call | tf_op jit(solution)/shard_map/far_sums/pallas_call | solution.py:244
  93.4 1.4 %collective-permute-start.14 = (bf16[28,32,128]{2,1,0:T(8,128)(2,1)S(1)}, bf16[28,32,128]{2,1,0:T(8,128)(2,1)S(1)}, u32[]{:S(2)}, u32[]{:S(2)}) collective-permute-start(bf16[28,32,128]{2,1,0:T(8,128)(2,1)S(1)} %get-tuple-element.179), channel_id=1, source_target_pairs={{0,2},{1,3},{2,0},{3,1},{4,6},{5,7},{6,4},{7,5},{8,10},{9,11},{10,... | collective-permute-start | bytes 688136 | tf_op jit(solution)/shard_map/ppermute | solution.py:672
  94.8 0.0 collective-permute-start.15
  94.8 2.7 %collective-permute-start.16 = (bf16[28,32,128]{2,1,0:T(8,128)(2,1)S(1)}, bf16[28,32,128]{2,1,0:T(8,128)(2,1)S(1)}, u32[]{:S(2)}, u32[]{:S(2)}) collective-permute-start(bf16[28,32,128]{2,1,0:T(8,128)(2,1)S(1)} %get-tuple-element.181), channel_id=1, source_target_pairs={{0,3},{1,0},{2,1},{3,2},{4,7},{5,4},{6,5},{7,6},{8,11},{9,8},{10,9... | collective-permute-start | bytes 688136 | tf_op jit(solution)/shard_map/ppermute | solution.py:672
  97.5 0.5 slice.68
  98.7 3.2 %collective-permute-done.14.refs_1_ = bf16[28,32,128]{2,1,0:T(8,128)(2,1)S(1)} collective-permute-done((bf16[28,32,128]{2,1,0:T(8,128)(2,1)S(1)}, bf16[28,32,128]{2,1,0:T(8,128)(2,1)S(1)}, u32[]{:S(2)}, u32[]{:S(2)}) %collective-permute-start.14) | collective-permute-done | bytes 229408 | tf_op jit(solution)/shard_map/ppermute | solution.py:672
  101.9 5.6 %collective-permute-done.15.refs_2_ = bf16[28,32,128]{2,1,0:T(8,128)(2,1)S(1)} collective-permute-done((bf16[28,32,128]{2,1,0:T(8,128)(2,1)S(1)}, bf16[28,32,128]{2,1,0:T(8,128)(2,1)S(1)}, u32[]{:S(2)}, u32[]{:S(2)}) %collective-permute-start.15) | collective-permute-done | bytes 229408 | tf_op jit(solution)/shard_map/ppermute | solution.py:672
  107.5 0.0 collective-permute-done.16.refs_3_
  107.5 0.9 finish.1
  108.3 0.0 copy-done.5
  108.4 0.0 copy-done.6
  108.4 0.3 conditional.1
  108.6 0.0 copy-start.4
  108.7 0.9 copy-done.4
  (4 shorter events, 0.0 us)
Async XLA Ops:
  9.5 98.8 %copy-start.5 = (s32[256,28]{0,1:T(8,128)S(1)}, s32[256,28]{0,1:T(8,128)}, u32[]{:S(2)}) copy-start(s32[256,28]{0,1:T(8,128)} %param.7) | copy-start | bytes 86020
  9.5 98.8 %copy-start.6 = (s32[4,7]{1,0:T(4,128)S(1)}, s32[4,7]{1,0:T(4,128)}, u32[]{:S(2)}) copy-start(s32[4,7]{1,0:T(4,128)} %keep_ref.3) | copy-start | bytes 340
  9.5 25.9 %all-to-all-start.1 = ((bf16[32,32,512]{2,1,0:T(8,128)(2,1)}), bf16[32,32,512]{2,1,0:T(8,128)(2,1)S(1)}, u32[]{:S(2)}, u32[]{:S(2)}) async-start(bf16[32,32,512]{2,1,0:T(8,128)(2,1)} %prepare.1), calls=%async_computation.2 | async-start | bytes 2097152 | tf_op jit(solution)/shard_map/all_to_all | solution.py:645
  18.3 63.5 %all-gather.6.cloned.1.call-start = ((), (), s32[]{:S(2)}) async-start(), calls=%async_computation.5 | async-start | bytes 4587520 | tf_op jit(solution)/shard_map/all_gather | solution.py:647
  38.6 15.0 %collective-permute-start = (bf16[128,512]{1,0:T(8,128)(2,1)S(1)}, bf16[128,512]{1,0:T(8,128)(2,1)S(1)}, u32[]{:S(2)}, u32[]{:S(2)}) collective-permute-start(bf16[128,512]{1,0:T(8,128)(2,1)S(1)} %get-tuple-element.119), channel_id=1, source_target_pairs={{0,32},{8,40},{16,48},{24,56},{32,0},{40,8},{48,16},{56,24},{1,33}... | collective-permute-start | bytes 393224 | tf_op jit(solution)/shard_map/ppermute | solution.py:652
  45.6 16.2 %collective-permute-start.1 = (bf16[128,512]{1,0:T(8,128)(2,1)S(1)}, bf16[128,512]{1,0:T(8,128)(2,1)S(1)}, u32[]{:S(2)}, u32[]{:S(2)}) collective-permute-start(bf16[128,512]{1,0:T(8,128)(2,1)S(1)} %get-tuple-element.120), channel_id=1, source_target_pairs={{0,24},{8,32},{16,40},{24,48},{32,56},{40,0},{48,8},{56,16},{1,25}... | collective-permute-start | bytes 393224 | tf_op jit(solution)/shard_map/ppermute | solution.py:652
  47.2 15.4 %collective-permute-start.2 = (bf16[128,512]{1,0:T(8,128)(2,1)S(1)}, bf16[128,512]{1,0:T(8,128)(2,1)S(1)}, u32[]{:S(2)}, u32[]{:S(2)}) collective-permute-start(bf16[128,512]{1,0:T(8,128)(2,1)S(1)} %get-tuple-element.121), channel_id=1, source_target_pairs={{0,40},{8,48},{16,56},{24,0},{32,8},{40,16},{48,24},{56,32},{1,41}... | collective-permute-start | bytes 393224 | tf_op jit(solution)/shard_map/ppermute | solution.py:652
  50.1 12.6 %collective-permute-start.3 = (bf16[128,512]{1,0:T(8,128)(2,1)S(1)}, bf16[128,512]{1,0:T(8,128)(2,1)S(1)}, u32[]{:S(2)}, u32[]{:S(2)}) collective-permute-start(bf16[128,512]{1,0:T(8,128)(2,1)S(1)} %get-tuple-element.122), channel_id=1, source_target_pairs={{0,16},{8,24},{16,32},{24,40},{32,48},{40,56},{48,0},{56,8},{1,17}... | collective-permute-start | bytes 393224 | tf_op jit(solution)/shard_map/ppermute | solution.py:652
  51.2 14.6 %collective-permute-start.4 = (bf16[128,512]{1,0:T(8,128)(2,1)S(1)}, bf16[128,512]{1,0:T(8,128)(2,1)S(1)}, u32[]{:S(2)}, u32[]{:S(2)}) collective-permute-start(bf16[128,512]{1,0:T(8,128)(2,1)S(1)} %get-tuple-element.123), channel_id=1, source_target_pairs={{0,48},{8,56},{16,0},{24,8},{32,16},{40,24},{48,32},{56,40},{1,49}... | collective-permute-start | bytes 393224 | tf_op jit(solution)/shard_map/ppermute | solution.py:652
  53.6 15.3 %collective-permute-start.5 = (bf16[128,512]{1,0:T(8,128)(2,1)S(1)}, bf16[128,512]{1,0:T(8,128)(2,1)S(1)}, u32[]{:S(2)}, u32[]{:S(2)}) collective-permute-start(bf16[128,512]{1,0:T(8,128)(2,1)S(1)} %get-tuple-element.124), channel_id=1, source_target_pairs={{0,8},{8,16},{16,24},{24,32},{32,40},{40,48},{48,56},{56,0},{1,9},... | collective-permute-start | bytes 393224 | tf_op jit(solution)/shard_map/ppermute | solution.py:652
  61.8 7.9 %collective-permute-start.6 = (bf16[128,512]{1,0:T(8,128)(2,1)S(1)}, bf16[128,512]{1,0:T(8,128)(2,1)S(1)}, u32[]{:S(2)}, u32[]{:S(2)}) collective-permute-start(bf16[128,512]{1,0:T(8,128)(2,1)S(1)} %get-tuple-element.125), channel_id=1, source_target_pairs={{0,56},{8,0},{16,8},{24,16},{32,24},{40,32},{48,40},{56,48},{1,57}... | collective-permute-start | bytes 393224 | tf_op jit(solution)/shard_map/ppermute | solution.py:652
  71.6 6.9 %collective-permute-start.7 = (bf16[120,512]{1,0:T(8,128)(2,1)S(1)}, bf16[120,512]{1,0:T(8,128)(2,1)S(1)}, u32[]{:S(2)}, u32[]{:S(2)}) collective-permute-start(bf16[120,512]{1,0:T(8,128)(2,1)S(1)} %get-tuple-element.162), channel_id=1, source_target_pairs={{0,128},{4,132},{64,192},{68,196},{128,0},{132,4},{192,64},{196,68... | collective-permute-start | bytes 368648 | tf_op jit(solution)/shard_map/ppermute | solution.py:663
  72.8 9.0 %collective-permute-start.8 = (bf16[120,512]{1,0:T(8,128)(2,1)S(1)}, bf16[120,512]{1,0:T(8,128)(2,1)S(1)}, u32[]{:S(2)}, u32[]{:S(2)}) collective-permute-start(bf16[120,512]{1,0:T(8,128)(2,1)S(1)} %get-tuple-element.163), channel_id=1, source_target_pairs={{0,132},{4,128},{64,196},{68,192},{128,4},{132,0},{192,68},{196,64... | collective-permute-start | bytes 368648 | tf_op jit(solution)/shard_map/ppermute | solution.py:663
  75.8 10.2 %collective-permute-start.9 = (bf16[120,512]{1,0:T(8,128)(2,1)S(1)}, bf16[120,512]{1,0:T(8,128)(2,1)S(1)}, u32[]{:S(2)}, u32[]{:S(2)}) collective-permute-start(bf16[120,512]{1,0:T(8,128)(2,1)S(1)} %get-tuple-element.164), channel_id=1, source_target_pairs={{0,64},{4,68},{64,128},{68,132},{128,192},{132,196},{192,0},{196,4... | collective-permute-start | bytes 368648 | tf_op jit(solution)/shard_map/ppermute | solution.py:663
  76.2 9.9 %collective-permute-start.10 = (bf16[120,512]{1,0:T(8,128)(2,1)S(1)}, bf16[120,512]{1,0:T(8,128)(2,1)S(1)}, u32[]{:S(2)}, u32[]{:S(2)}) collective-permute-start(bf16[120,512]{1,0:T(8,128)(2,1)S(1)} %get-tuple-element.165), channel_id=1, source_target_pairs={{0,192},{4,196},{64,0},{68,4},{128,64},{132,68},{192,128},{196,132... | collective-permute-start | bytes 368648 | tf_op jit(solution)/shard_map/ppermute | solution.py:663
  78.5 8.1 %collective-permute-start.11 = (bf16[120,512]{1,0:T(8,128)(2,1)S(1)}, bf16[120,512]{1,0:T(8,128)(2,1)S(1)}, u32[]{:S(2)}, u32[]{:S(2)}) collective-permute-start(bf16[120,512]{1,0:T(8,128)(2,1)S(1)} %get-tuple-element.166), channel_id=1, source_target_pairs={{0,68},{4,64},{64,132},{68,128},{128,196},{132,192},{192,4},{196,0... | collective-permute-start | bytes 368648 | tf_op jit(solution)/shard_map/ppermute | solution.py:663
  78.5 8.1 %collective-permute-start.12 = (bf16[120,512]{1,0:T(8,128)(2,1)S(1)}, bf16[120,512]{1,0:T(8,128)(2,1)S(1)}, u32[]{:S(2)}, u32[]{:S(2)}) collective-permute-start(bf16[120,512]{1,0:T(8,128)(2,1)S(1)} %get-tuple-element.167), channel_id=1, source_target_pairs={{0,196},{4,192},{64,4},{68,0},{128,68},{132,64},{192,132},{196,128... | collective-permute-start | bytes 368648 | tf_op jit(solution)/shard_map/ppermute | solution.py:663
  81.8 4.8 %collective-permute-start.13 = (bf16[120,512]{1,0:T(8,128)(2,1)S(1)}, bf16[120,512]{1,0:T(8,128)(2,1)S(1)}, u32[]{:S(2)}, u32[]{:S(2)}) collective-permute-start(bf16[120,512]{1,0:T(8,128)(2,1)S(1)} %get-tuple-element.168), channel_id=1, source_target_pairs={{0,4},{4,0},{64,68},{68,64},{128,132},{132,128},{192,196},{196,192... | collective-permute-start | bytes 368648 | tf_op jit(solution)/shard_map/ppermute | solution.py:663
  81.8 2.0 %copy-start = (bf16[16,7,128,128]{3,2,1,0:T(8,128)(2,1)S(1)}, bf16[16,7,128,128]{3,2,1,0:T(8,128)(2,1)}, u32[]{:S(2)}) copy-start(bf16[16,7,128,128]{3,2,1,0:T(8,128)(2,1)} %all-gather.6.cloned.1.call-done) | copy-start | bytes 11010052
  93.4 8.4 %collective-permute-start.14 = (bf16[28,32,128]{2,1,0:T(8,128)(2,1)S(1)}, bf16[28,32,128]{2,1,0:T(8,128)(2,1)S(1)}, u32[]{:S(2)}, u32[]{:S(2)}) collective-permute-start(bf16[28,32,128]{2,1,0:T(8,128)(2,1)S(1)} %get-tuple-element.179), channel_id=1, source_target_pairs={{0,2},{1,3},{2,0},{3,1},{4,6},{5,7},{6,4},{7,5},{8,10},{9,11},{10,... | collective-permute-start | bytes 688136 | tf_op jit(solution)/shard_map/ppermute | solution.py:672
  94.8 12.6 %collective-permute-start.15 = (bf16[28,32,128]{2,1,0:T(8,128)(2,1)S(1)}, bf16[28,32,128]{2,1,0:T(8,128)(2,1)S(1)}, u32[]{:S(2)}, u32[]{:S(2)}) collective-permute-start(bf16[28,32,128]{2,1,0:T(8,128)(2,1)S(1)} %get-tuple-element.180), channel_id=1, source_target_pairs={{0,1},{1,2},{2,3},{3,0},{4,5},{5,6},{6,7},{7,4},{8,9},{9,10},{10,1... | collective-permute-start | bytes 688136 | tf_op jit(solution)/shard_map/ppermute | solution.py:672
  94.8 12.6 %collective-permute-start.16 = (bf16[28,32,128]{2,1,0:T(8,128)(2,1)S(1)}, bf16[28,32,128]{2,1,0:T(8,128)(2,1)S(1)}, u32[]{:S(2)}, u32[]{:S(2)}) collective-permute-start(bf16[28,32,128]{2,1,0:T(8,128)(2,1)S(1)} %get-tuple-element.181), channel_id=1, source_target_pairs={{0,3},{1,0},{2,1},{3,2},{4,7},{5,4},{6,5},{7,6},{8,11},{9,8},{10,9... | collective-permute-start | bytes 688136 | tf_op jit(solution)/shard_map/ppermute | solution.py:672
  108.6 0.9 copy-start.4
Sparse Core Ops, SparseCore 0:
  35.6 45.4 all-gather.5

commit v13 on v12

--- a/solution.py
+++ b/solution.py
@@ -663,6 +663,7 @@
         far.append(lax.ppermute(packed[1 + number], ("x", "core"), pairs))
     notes, whole = lax.optimization_barrier((notes, whole))
     far_lists = far_plan(position, slots, union, notes)
+    own_lists, far_lists = lax.optimization_barrier((own_lists, far_lists))
     own = own_sums(own_lists, whole)
     far, own = lax.optimization_barrier((far, own))
     result = far_sums(own_lists, far_lists, whole, own, position, far)

time: 117 us -> 116 us (level)
  transfers between devices with their start and end apart: 19 -> 19, of which waited for: 9 -> 8; matrix products, arithmetic and copies ran while one was open for 2% -> 2% of each run, Pallas kernels for 8% -> 10%
where the time goes in v13:
time: 116 us
  starting transfers between devices  38.7 us (33%)
  waiting for transfers between devices  33.3 us (29%)
  Pallas kernels  23.7 us (20%)
  between operations  14.2 us (12%)
  local copies, waits for them, and re-layouts  5.68 us (5%)
    ppermute x7, starting transfers between devices, shards(): lax.ppermute(packed[step], 'z', [(i, (i + step) % NZ) for i in range(NZ)])  15.8 us
    ppermute x7, waiting for transfers between devices, shards(): lax.ppermute(packed[step], 'z', [(i, (i + step) % NZ) for i in range(NZ)])  14.4 us
    all_to_all x1, waiting for transfers between devices, shards(): lax.all_to_all(cuts, ('col', 'x', 'core'), split_axis=0, concat_axis=0, t...  9.97 us
    ppermute x7, starting transfers between devices, shards(): far.append(lax.ppermute(packed[1 + number], ('x', 'core'), pairs))  9.88 us
    all_to_all x1, starting transfers between devices, shards(): lax.all_to_all(cuts, ('col', 'x', 'core'), split_axis=0, concat_axis=0, t...  8.72 us
    ppermute x3, waiting for transfers between devices, shards(): cuts.append(lax.ppermute(result[step], 'col', pairs))  8.58 us
    pallas_call x1, Pallas kernels, far_sums(): pl.pallas_call(far_kernel, out_shape=[jax.ShapeDtypeStruct((HEIGHT * QUAR...  5.32 us
    ppermute x3, starting transfers between devices, shards(): cuts.append(lax.ppermute(result[step], 'col', pairs))  4.32 us
  transfers between devices with their start and end apart: 19, of which 8 were waited for; matrix products, arithmetic and copies ran while one was open for 2% of the time, Pallas kernels for 10%

profile of v13, /device:TPU:1, one launch (start us, length us, event | category | flops | bytes accessed | tf_op | source)
XLA Modules:
  0.0 116.0 jit_solution(11020633665683283695)
XLA Ops:
  6.5 0.1 pad_add_fusion.position_ref
  6.6 2.9 %prepare.1 = bf16[32,32,512]{2,1,0:T(8,128)(2,1)} custom-call(s32[4]{0:T(128)S(1)} %pad_add_fusion.position_ref, s32[4,7]{1,0:T(4,128)} %keep_ref.3, bf16[4,7,128,128]{3,2,1,0:T(8,128)(2,1)} %blocks_ref.2), custom_call_target="tpu_custom_call" | custom-call | tf_op jit(solution)/shard_map/prepare/pallas_call | solution.py:87
  9.5 0.0 copy-start.6
  9.5 8.7 %all-to-all-start.1 = ((bf16[32,32,512]{2,1,0:T(8,128)(2,1)}), bf16[32,32,512]{2,1,0:T(8,128)(2,1)S(1)}, u32[]{:S(2)}, u32[]{:S(2)}) async-start(bf16[32,32,512]{2,1,0:T(8,128)(2,1)} %prepare.1), calls=%async_computation.2 | async-start | bytes 2097152 | tf_op jit(solution)/shard_map/all_to_all | solution.py:645
  18.3 0.0 all-gather.6.cloned.1.call-start
  18.3 0.9 copy.101
  19.2 0.3 reshape.213
  19.5 0.1 reshape.214
  19.6 0.1 reshape.215.entries_ref
  19.7 0.9 copy.103.columns_ref
  20.5 2.4 %turn.1 = bf16[4,7,128,128]{3,2,1,0:T(8,128)(2,1)} custom-call(s32[4,7]{1,0:T(4,128)} %keep_ref.3, bf16[4,7,128,128]{3,2,1,0:T(8,128)(2,1)} %blocks_ref.2), custom_call_target="tpu_custom_call" | custom-call | flops 117440512 | bytes 1835008 | tf_op jit(solution)/shard_map/turn/pallas_call | solution.py:108
  23.0 2.5 %pattern.1 = (s32[256,256]{1,0:T(8,128)S(1)}, f32[128,256]{1,0:T(8,128)S(1)}, f32[128,1024]{1,0:T(8,128)S(1)}, f32[8,1024]{1,0:T(8,128)S(1)}) custom-call(s32[4]{0:T(128)S(1)} %pad_add_fusion.position_ref, s32[256,28]{1,0:T(8,128)S(1)} %copy.103.columns_ref, s32[1,1024]{1,0:T(1,128)S(1)} %reshape.215.entries_ref), custom_call_target="tpu_custom_call" | custom-call | flops 234881024 | bytes 524288 | tf_op jit(solution)/shard_map/pattern/pallas_call | solution.py:355
  25.5 10.0 %all-to-all-done.1 = bf16[32,32,512]{2,1,0:T(8,128)(2,1)S(1)} async-done(((bf16[32,32,512]{2,1,0:T(8,128)(2,1)}), bf16[32,32,512]{2,1,0:T(8,128)(2,1)S(1)}, u32[]{:S(2)}, u32[]{:S(2)}) %all-to-all-start.1) | async-done | bytes 1048608 | tf_op jit(solution)/shard_map/all_to_all | solution.py:645
  35.4 0.0 all-gather.6.cloned.1.call-update
  35.5 3.1 %send.1 = (bf16[128,512]{1,0:T(8,128)(2,1)S(1)}, bf16[128,512]{1,0:T(8,128)(2,1)S(1)}, bf16[128,512]{1,0:T(8,128)(2,1)S(1)}, bf16[128,512]{1,0:T(8,128)(2,1)S(1)...) custom-call(s32[4]{0:T(128)S(1)} %pad_add_fusion.position_ref, ...), custom_call_target="tpu_custom_call" | custom-call | tf_op jit(solution)/shard_map/send/pallas_call | solution.py:414
  38.6 7.0 %collective-permute-start = (bf16[128,512]{1,0:T(8,128)(2,1)S(1)}, bf16[128,512]{1,0:T(8,128)(2,1)S(1)}, u32[]{:S(2)}, u32[]{:S(2)}) collective-permute-start(bf16[128,512]{1,0:T(8,128)(2,1)S(1)} %get-tuple-element.119), channel_id=1, source_target_pairs={{0,32},{8,40},{16,48},{24,56},{32,0},{40,8},{48,16},{56,24},{1,33}... | collective-permute-start | bytes 393224 | tf_op jit(solution)/shard_map/ppermute | solution.py:652
  45.6 1.6 %collective-permute-start.1 = (bf16[128,512]{1,0:T(8,128)(2,1)S(1)}, bf16[128,512]{1,0:T(8,128)(2,1)S(1)}, u32[]{:S(2)}, u32[]{:S(2)}) collective-permute-start(bf16[128,512]{1,0:T(8,128)(2,1)S(1)} %get-tuple-element.120), channel_id=1, source_target_pairs={{0,24},{8,32},{16,40},{24,48},{32,56},{40,0},{48,8},{56,16},{1,25}... | collective-permute-start | bytes 393224 | tf_op jit(solution)/shard_map/ppermute | solution.py:652
  47.2 2.8 %collective-permute-start.2 = (bf16[128,512]{1,0:T(8,128)(2,1)S(1)}, bf16[128,512]{1,0:T(8,128)(2,1)S(1)}, u32[]{:S(2)}, u32[]{:S(2)}) collective-permute-start(bf16[128,512]{1,0:T(8,128)(2,1)S(1)} %get-tuple-element.121), channel_id=1, source_target_pairs={{0,40},{8,48},{16,56},{24,0},{32,8},{40,16},{48,24},{56,32},{1,41}... | collective-permute-start | bytes 393224 | tf_op jit(solution)/shard_map/ppermute | solution.py:652
  50.1 1.2 %collective-permute-start.3 = (bf16[128,512]{1,0:T(8,128)(2,1)S(1)}, bf16[128,512]{1,0:T(8,128)(2,1)S(1)}, u32[]{:S(2)}, u32[]{:S(2)}) collective-permute-start(bf16[128,512]{1,0:T(8,128)(2,1)S(1)} %get-tuple-element.122), channel_id=1, source_target_pairs={{0,16},{8,24},{16,32},{24,40},{32,48},{40,56},{48,0},{56,8},{1,17}... | collective-permute-start | bytes 393224 | tf_op jit(solution)/shard_map/ppermute | solution.py:652
  51.2 2.4 %collective-permute-start.4 = (bf16[128,512]{1,0:T(8,128)(2,1)S(1)}, bf16[128,512]{1,0:T(8,128)(2,1)S(1)}, u32[]{:S(2)}, u32[]{:S(2)}) collective-permute-start(bf16[128,512]{1,0:T(8,128)(2,1)S(1)} %get-tuple-element.123), channel_id=1, source_target_pairs={{0,48},{8,56},{16,0},{24,8},{32,16},{40,24},{48,32},{56,40},{1,49}... | collective-permute-start | bytes 393224 | tf_op jit(solution)/shard_map/ppermute | solution.py:652
  53.6 0.0 collective-permute-done.refs_1_
  53.6 0.7 collective-permute-start.5
  54.4 7.4 %collective-permute-done.1.refs_2_ = bf16[128,512]{1,0:T(8,128)(2,1)S(1)} collective-permute-done((bf16[128,512]{1,0:T(8,128)(2,1)S(1)}, bf16[128,512]{1,0:T(8,128)(2,1)S(1)}, u32[]{:S(2)}, u32[]{:S(2)}) %collective-permute-start.1) | collective-permute-done | bytes 131104 | tf_op jit(solution)/shard_map/ppermute | solution.py:652
  61.8 0.0 collective-permute-start.6
  61.8 0.8 own_plan.1.plan_ref.own_ref
  62.6 0.0 collective-permute-done.2.refs_3_
  62.6 0.0 collective-permute-done.3.refs_4_
  62.6 3.3 %collective-permute-done.4.refs_5_ = bf16[128,512]{1,0:T(8,128)(2,1)S(1)} collective-permute-done((bf16[128,512]{1,0:T(8,128)(2,1)S(1)}, bf16[128,512]{1,0:T(8,128)(2,1)S(1)}, u32[]{:S(2)}, u32[]{:S(2)}) %collective-permute-start.4) | collective-permute-done | bytes 131104 | tf_op jit(solution)/shard_map/ppermute | solution.py:652
  65.9 3.1 %collective-permute-done.5.refs_6_ = bf16[128,512]{1,0:T(8,128)(2,1)S(1)} collective-permute-done((bf16[128,512]{1,0:T(8,128)(2,1)S(1)}, bf16[128,512]{1,0:T(8,128)(2,1)S(1)}, u32[]{:S(2)}, u32[]{:S(2)}) %collective-permute-start.5) | collective-permute-done | bytes 131104 | tf_op jit(solution)/shard_map/ppermute | solution.py:652
  68.9 0.7 collective-permute-done.6.refs_7_
  69.6 1.9 %route.1 = (bf16[120,512]{1,0:T(8,128)(2,1)S(1)}, bf16[120,512]{1,0:T(8,128)(2,1)S(1)}, bf16[120,512]{1,0:T(8,128)(2,1)S(1)}, bf16[120,512]{1,0:T(8,128)(2,1)S(1...) custom-call(s32[4]{0:T(128)S(1)} %pad_add_fusion.position_ref, ...), custom_call_target="tpu_custom_call" | custom-call | tf_op jit(solution)/shard_map/route/pallas_call | solution.py:463
  71.6 1.2 %collective-permute-start.7 = (bf16[120,512]{1,0:T(8,128)(2,1)S(1)}, bf16[120,512]{1,0:T(8,128)(2,1)S(1)}, u32[]{:S(2)}, u32[]{:S(2)}) collective-permute-start(bf16[120,512]{1,0:T(8,128)(2,1)S(1)} %get-tuple-element.166), channel_id=1, source_target_pairs={{0,128},{4,132},{64,192},{68,196},{128,0},{132,4},{192,64},{196,68... | collective-permute-start | bytes 368648 | tf_op jit(solution)/shard_map/ppermute | solution.py:663
  72.8 3.0 %collective-permute-start.8 = (bf16[120,512]{1,0:T(8,128)(2,1)S(1)}, bf16[120,512]{1,0:T(8,128)(2,1)S(1)}, u32[]{:S(2)}, u32[]{:S(2)}) collective-permute-start(bf16[120,512]{1,0:T(8,128)(2,1)S(1)} %get-tuple-element.167), channel_id=1, source_target_pairs={{0,132},{4,128},{64,196},{68,192},{128,4},{132,0},{192,68},{196,64... | collective-permute-start | bytes 368648 | tf_op jit(solution)/shard_map/ppermute | solution.py:663
  75.8 0.4 collective-permute-start.9
  76.2 2.3 %collective-permute-start.10 = (bf16[120,512]{1,0:T(8,128)(2,1)S(1)}, bf16[120,512]{1,0:T(8,128)(2,1)S(1)}, u32[]{:S(2)}, u32[]{:S(2)}) collective-permute-start(bf16[120,512]{1,0:T(8,128)(2,1)S(1)} %get-tuple-element.169), channel_id=1, source_target_pairs={{0,192},{4,196},{64,0},{68,4},{128,64},{132,68},{192,128},{196,132... | collective-permute-start | bytes 368648 | tf_op jit(solution)/shard_map/ppermute | solution.py:663
  78.5 0.0 collective-permute-start.11
  78.5 0.0 collective-permute-done.7.refs_1_
  78.5 3.0 %collective-permute-start.12 = (bf16[120,512]{1,0:T(8,128)(2,1)S(1)}, bf16[120,512]{1,0:T(8,128)(2,1)S(1)}, u32[]{:S(2)}, u32[]{:S(2)}) collective-permute-start(bf16[120,512]{1,0:T(8,128)(2,1)S(1)} %get-tuple-element.171), channel_id=1, source_target_pairs={{0,196},{4,192},{64,4},{68,0},{128,68},{132,64},{192,132},{196,128... | collective-permute-start | bytes 368648 | tf_op jit(solution)/shard_map/ppermute | solution.py:663
  81.4 0.3 collective-permute-done.8.refs_2_
  81.8 0.0 collective-permute-start.13
  81.8 0.0 all-gather.6.cloned.1.call-done
  81.8 1.6 %far_plan.1.plan_ref = s32[16,128]{1,0:T(8,128)S(1)} custom-call(s32[4]{0:T(128)S(1)} %pad_add_fusion.position_ref, s32[256,256]{1,0:T(8,128)S(1)} %get-tuple-element.126.slots_ref, f32[128,256]{1,0:T(8,128)S(1)} %get-tuple-element.127.union_ref, bf16[128,512]{1,0:T(8,128)(2,1)S(1)} %get-tuple-element.154.refs_0_, ...), custom_call_target="tpu_custom_call" | custom-call | flops 671088640 | bytes 524288 | tf_op jit(solution)/shard_map/far_plan/pallas_call | solution.py:581
  83.3 0.0 copy-start
  83.3 2.0 %copy-done = bf16[16,7,128,128]{3,2,1,0:T(8,128)(2,1)S(1)} copy-done((bf16[16,7,128,128]{3,2,1,0:T(8,128)(2,1)S(1)}, bf16[16,7,128,128]{3,2,1,0:T(8,128)(2,1)}, u32[]{:S(2)}) %copy-start) | copy-done | bytes 3670040
  85.4 2.2 %own_sums.1.near_ref = f32[112,32,128]{2,1,0:T(8,128)S(1)} custom-call(s32[16,128]{1,0:T(8,128)S(1)} %own_plan.1.plan_ref.own_ref, bf16[112,128,128]{2,1,0:T(8,128)(2,1)S(1)} %bitcast.150), custom_call_target="tpu_custom_call" | custom-call | flops 536870912 | bytes 5505024 | tf_op jit(solution)/shard_map/own_sums/pallas_call | solution.py:162
  87.6 0.0 collective-permute-done.9.refs_3_
  87.6 0.0 collective-permute-done.10.refs_4_
  87.6 0.0 collective-permute-done.11.refs_5_
  87.6 0.0 collective-permute-done.12.refs_6_
  87.6 0.0 collective-permute-done.13.refs_7_
  87.6 5.3 %far_sums.1 = (bf16[28,32,128]{2,1,0:T(8,128)(2,1)S(1)}, bf16[28,32,128]{2,1,0:T(8,128)(2,1)S(1)}, bf16[28,32,128]{2,1,0:T(8,128)(2,1)S(1)}, bf16[28,32,128]{2,1,0:T(8,128)(2,1)S(1)}) custom-call(s32[16,128]{1,0:T(8,128)S(1)} %own_plan.1.plan_ref.own_ref, s32[16,128]{1,0:T(8,128)S(1)} %far_plan.1.plan_ref, bf16[112,128,128]{2,1,0:T(8,128)(2,1)} %bitcast.149, ...), custom_call_target="tpu_custom_call" | custom-call | tf_op jit(solution)/shard_map/far_sums/pallas_call | solution.py:244
  93.0 1.6 %collective-permute-start.14 = (bf16[28,32,128]{2,1,0:T(8,128)(2,1)S(1)}, bf16[28,32,128]{2,1,0:T(8,128)(2,1)S(1)}, u32[]{:S(2)}, u32[]{:S(2)}) collective-permute-start(bf16[28,32,128]{2,1,0:T(8,128)(2,1)S(1)} %get-tuple-element.183), channel_id=1, source_target_pairs={{0,2},{1,3},{2,0},{3,1},{4,6},{5,7},{6,4},{7,5},{8,10},{9,11},{10,... | collective-permute-start | bytes 688136 | tf_op jit(solution)/shard_map/ppermute | solution.py:673
  94.6 0.0 collective-permute-start.15
  94.6 2.7 %collective-permute-start.16 = (bf16[28,32,128]{2,1,0:T(8,128)(2,1)S(1)}, bf16[28,32,128]{2,1,0:T(8,128)(2,1)S(1)}, u32[]{:S(2)}, u32[]{:S(2)}) collective-permute-start(bf16[28,32,128]{2,1,0:T(8,128)(2,1)S(1)} %get-tuple-element.185), channel_id=1, source_target_pairs={{0,3},{1,0},{2,1},{3,2},{4,7},{5,4},{6,5},{7,6},{8,11},{9,8},{10,9... | collective-permute-start | bytes 688136 | tf_op jit(solution)/shard_map/ppermute | solution.py:673
  97.3 0.5 slice.51
  98.4 3.4 %collective-permute-done.14.refs_1_ = bf16[28,32,128]{2,1,0:T(8,128)(2,1)S(1)} collective-permute-done((bf16[28,32,128]{2,1,0:T(8,128)(2,1)S(1)}, bf16[28,32,128]{2,1,0:T(8,128)(2,1)S(1)}, u32[]{:S(2)}, u32[]{:S(2)}) %collective-permute-start.14) | collective-permute-done | bytes 229408 | tf_op jit(solution)/shard_map/ppermute | solution.py:673
  101.9 5.2 %collective-permute-done.15.refs_2_ = bf16[28,32,128]{2,1,0:T(8,128)(2,1)S(1)} collective-permute-done((bf16[28,32,128]{2,1,0:T(8,128)(2,1)S(1)}, bf16[28,32,128]{2,1,0:T(8,128)(2,1)S(1)}, u32[]{:S(2)}, u32[]{:S(2)}) %collective-permute-start.15) | collective-permute-done | bytes 229408 | tf_op jit(solution)/shard_map/ppermute | solution.py:673
  107.0 0.0 collective-permute-done.16.refs_3_
  107.0 0.9 finish.1
  107.9 0.0 copy-done.5
  107.9 0.0 copy-done.6
  107.9 0.3 conditional.1
  108.2 0.0 copy-start.4
  108.2 0.9 copy-done.4
  (4 shorter events, 0.0 us)
Async XLA Ops:
  9.5 98.4 %copy-start.5 = (s32[256,28]{0,1:T(8,128)S(1)}, s32[256,28]{0,1:T(8,128)}, u32[]{:S(2)}) copy-start(s32[256,28]{0,1:T(8,128)} %param.7) | copy-start | bytes 86020
  9.5 98.4 %copy-start.6 = (s32[4,7]{1,0:T(4,128)S(1)}, s32[4,7]{1,0:T(4,128)}, u32[]{:S(2)}) copy-start(s32[4,7]{1,0:T(4,128)} %keep_ref.3) | copy-start | bytes 340
  9.5 25.9 %all-to-all-start.1 = ((bf16[32,32,512]{2,1,0:T(8,128)(2,1)}), bf16[32,32,512]{2,1,0:T(8,128)(2,1)S(1)}, u32[]{:S(2)}, u32[]{:S(2)}) async-start(bf16[32,32,512]{2,1,0:T(8,128)(2,1)} %prepare.1), calls=%async_computation.2 | async-start | bytes 2097152 | tf_op jit(solution)/shard_map/all_to_all | solution.py:645
  18.3 63.5 %all-gather.6.cloned.1.call-start = ((), (), s32[]{:S(2)}) async-start(), calls=%async_computation.5 | async-start | bytes 4587520 | tf_op jit(solution)/shard_map/all_gather | solution.py:647
  38.6 15.0 %collective-permute-start = (bf16[128,512]{1,0:T(8,128)(2,1)S(1)}, bf16[128,512]{1,0:T(8,128)(2,1)S(1)}, u32[]{:S(2)}, u32[]{:S(2)}) collective-permute-start(bf16[128,512]{1,0:T(8,128)(2,1)S(1)} %get-tuple-element.119), channel_id=1, source_target_pairs={{0,32},{8,40},{16,48},{24,56},{32,0},{40,8},{48,16},{56,24},{1,33}... | collective-permute-start | bytes 393224 | tf_op jit(solution)/shard_map/ppermute | solution.py:652
  45.6 16.2 %collective-permute-start.1 = (bf16[128,512]{1,0:T(8,128)(2,1)S(1)}, bf16[128,512]{1,0:T(8,128)(2,1)S(1)}, u32[]{:S(2)}, u32[]{:S(2)}) collective-permute-start(bf16[128,512]{1,0:T(8,128)(2,1)S(1)} %get-tuple-element.120), channel_id=1, source_target_pairs={{0,24},{8,32},{16,40},{24,48},{32,56},{40,0},{48,8},{56,16},{1,25}... | collective-permute-start | bytes 393224 | tf_op jit(solution)/shard_map/ppermute | solution.py:652
  47.2 15.4 %collective-permute-start.2 = (bf16[128,512]{1,0:T(8,128)(2,1)S(1)}, bf16[128,512]{1,0:T(8,128)(2,1)S(1)}, u32[]{:S(2)}, u32[]{:S(2)}) collective-permute-start(bf16[128,512]{1,0:T(8,128)(2,1)S(1)} %get-tuple-element.121), channel_id=1, source_target_pairs={{0,40},{8,48},{16,56},{24,0},{32,8},{40,16},{48,24},{56,32},{1,41}... | collective-permute-start | bytes 393224 | tf_op jit(solution)/shard_map/ppermute | solution.py:652
  50.1 12.6 %collective-permute-start.3 = (bf16[128,512]{1,0:T(8,128)(2,1)S(1)}, bf16[128,512]{1,0:T(8,128)(2,1)S(1)}, u32[]{:S(2)}, u32[]{:S(2)}) collective-permute-start(bf16[128,512]{1,0:T(8,128)(2,1)S(1)} %get-tuple-element.122), channel_id=1, source_target_pairs={{0,16},{8,24},{16,32},{24,40},{32,48},{40,56},{48,0},{56,8},{1,17}... | collective-permute-start | bytes 393224 | tf_op jit(solution)/shard_map/ppermute | solution.py:652
  51.2 14.6 %collective-permute-start.4 = (bf16[128,512]{1,0:T(8,128)(2,1)S(1)}, bf16[128,512]{1,0:T(8,128)(2,1)S(1)}, u32[]{:S(2)}, u32[]{:S(2)}) collective-permute-start(bf16[128,512]{1,0:T(8,128)(2,1)S(1)} %get-tuple-element.123), channel_id=1, source_target_pairs={{0,48},{8,56},{16,0},{24,8},{32,16},{40,24},{48,32},{56,40},{1,49}... | collective-permute-start | bytes 393224 | tf_op jit(solution)/shard_map/ppermute | solution.py:652
  53.6 15.3 %collective-permute-start.5 = (bf16[128,512]{1,0:T(8,128)(2,1)S(1)}, bf16[128,512]{1,0:T(8,128)(2,1)S(1)}, u32[]{:S(2)}, u32[]{:S(2)}) collective-permute-start(bf16[128,512]{1,0:T(8,128)(2,1)S(1)} %get-tuple-element.124), channel_id=1, source_target_pairs={{0,8},{8,16},{16,24},{24,32},{32,40},{40,48},{48,56},{56,0},{1,9},... | collective-permute-start | bytes 393224 | tf_op jit(solution)/shard_map/ppermute | solution.py:652
  61.8 7.9 %collective-permute-start.6 = (bf16[128,512]{1,0:T(8,128)(2,1)S(1)}, bf16[128,512]{1,0:T(8,128)(2,1)S(1)}, u32[]{:S(2)}, u32[]{:S(2)}) collective-permute-start(bf16[128,512]{1,0:T(8,128)(2,1)S(1)} %get-tuple-element.125), channel_id=1, source_target_pairs={{0,56},{8,0},{16,8},{24,16},{32,24},{40,32},{48,40},{56,48},{1,57}... | collective-permute-start | bytes 393224 | tf_op jit(solution)/shard_map/ppermute | solution.py:652
  71.6 6.9 %collective-permute-start.7 = (bf16[120,512]{1,0:T(8,128)(2,1)S(1)}, bf16[120,512]{1,0:T(8,128)(2,1)S(1)}, u32[]{:S(2)}, u32[]{:S(2)}) collective-permute-start(bf16[120,512]{1,0:T(8,128)(2,1)S(1)} %get-tuple-element.166), channel_id=1, source_target_pairs={{0,128},{4,132},{64,192},{68,196},{128,0},{132,4},{192,64},{196,68... | collective-permute-start | bytes 368648 | tf_op jit(solution)/shard_map/ppermute | solution.py:663
  72.8 9.0 %collective-permute-start.8 = (bf16[120,512]{1,0:T(8,128)(2,1)S(1)}, bf16[120,512]{1,0:T(8,128)(2,1)S(1)}, u32[]{:S(2)}, u32[]{:S(2)}) collective-permute-start(bf16[120,512]{1,0:T(8,128)(2,1)S(1)} %get-tuple-element.167), channel_id=1, source_target_pairs={{0,132},{4,128},{64,196},{68,192},{128,4},{132,0},{192,68},{196,64... | collective-permute-start | bytes 368648 | tf_op jit(solution)/shard_map/ppermute | solution.py:663
  75.8 11.8 %collective-permute-start.9 = (bf16[120,512]{1,0:T(8,128)(2,1)S(1)}, bf16[120,512]{1,0:T(8,128)(2,1)S(1)}, u32[]{:S(2)}, u32[]{:S(2)}) collective-permute-start(bf16[120,512]{1,0:T(8,128)(2,1)S(1)} %get-tuple-element.168), channel_id=1, source_target_pairs={{0,64},{4,68},{64,128},{68,132},{128,192},{132,196},{192,0},{196,4... | collective-permute-start | bytes 368648 | tf_op jit(solution)/shard_map/ppermute | solution.py:663
  76.2 11.4 %collective-permute-start.10 = (bf16[120,512]{1,0:T(8,128)(2,1)S(1)}, bf16[120,512]{1,0:T(8,128)(2,1)S(1)}, u32[]{:S(2)}, u32[]{:S(2)}) collective-permute-start(bf16[120,512]{1,0:T(8,128)(2,1)S(1)} %get-tuple-element.169), channel_id=1, source_target_pairs={{0,192},{4,196},{64,0},{68,4},{128,64},{132,68},{192,128},{196,132... | collective-permute-start | bytes 368648 | tf_op jit(solution)/shard_map/ppermute | solution.py:663
  78.5 9.1 %collective-permute-start.11 = (bf16[120,512]{1,0:T(8,128)(2,1)S(1)}, bf16[120,512]{1,0:T(8,128)(2,1)S(1)}, u32[]{:S(2)}, u32[]{:S(2)}) collective-permute-start(bf16[120,512]{1,0:T(8,128)(2,1)S(1)} %get-tuple-element.170), channel_id=1, source_target_pairs={{0,68},{4,64},{64,132},{68,128},{128,196},{132,192},{192,4},{196,0... | collective-permute-start | bytes 368648 | tf_op jit(solution)/shard_map/ppermute | solution.py:663
  78.5 9.1 %collective-permute-start.12 = (bf16[120,512]{1,0:T(8,128)(2,1)S(1)}, bf16[120,512]{1,0:T(8,128)(2,1)S(1)}, u32[]{:S(2)}, u32[]{:S(2)}) collective-permute-start(bf16[120,512]{1,0:T(8,128)(2,1)S(1)} %get-tuple-element.171), channel_id=1, source_target_pairs={{0,196},{4,192},{64,4},{68,0},{128,68},{132,64},{192,132},{196,128... | collective-permute-start | bytes 368648 | tf_op jit(solution)/shard_map/ppermute | solution.py:663
  81.8 5.9 %collective-permute-start.13 = (bf16[120,512]{1,0:T(8,128)(2,1)S(1)}, bf16[120,512]{1,0:T(8,128)(2,1)S(1)}, u32[]{:S(2)}, u32[]{:S(2)}) collective-permute-start(bf16[120,512]{1,0:T(8,128)(2,1)S(1)} %get-tuple-element.172), channel_id=1, source_target_pairs={{0,4},{4,0},{64,68},{68,64},{128,132},{132,128},{192,196},{196,192... | collective-permute-start | bytes 368648 | tf_op jit(solution)/shard_map/ppermute | solution.py:663
  83.3 2.0 %copy-start = (bf16[16,7,128,128]{3,2,1,0:T(8,128)(2,1)S(1)}, bf16[16,7,128,128]{3,2,1,0:T(8,128)(2,1)}, u32[]{:S(2)}) copy-start(bf16[16,7,128,128]{3,2,1,0:T(8,128)(2,1)} %all-gather.6.cloned.1.call-done) | copy-start | bytes 11010052
  93.0 8.9 %collective-permute-start.14 = (bf16[28,32,128]{2,1,0:T(8,128)(2,1)S(1)}, bf16[28,32,128]{2,1,0:T(8,128)(2,1)S(1)}, u32[]{:S(2)}, u32[]{:S(2)}) collective-permute-start(bf16[28,32,128]{2,1,0:T(8,128)(2,1)S(1)} %get-tuple-element.183), channel_id=1, source_target_pairs={{0,2},{1,3},{2,0},{3,1},{4,6},{5,7},{6,4},{7,5},{8,10},{9,11},{10,... | collective-permute-start | bytes 688136 | tf_op jit(solution)/shard_map/ppermute | solution.py:673
  94.6 12.4 %collective-permute-start.15 = (bf16[28,32,128]{2,1,0:T(8,128)(2,1)S(1)}, bf16[28,32,128]{2,1,0:T(8,128)(2,1)S(1)}, u32[]{:S(2)}, u32[]{:S(2)}) collective-permute-start(bf16[28,32,128]{2,1,0:T(8,128)(2,1)S(1)} %get-tuple-element.184), channel_id=1, source_target_pairs={{0,1},{1,2},{2,3},{3,0},{4,5},{5,6},{6,7},{7,4},{8,9},{9,10},{10,1... | collective-permute-start | bytes 688136 | tf_op jit(solution)/shard_map/ppermute | solution.py:673
  94.6 12.4 %collective-permute-start.16 = (bf16[28,32,128]{2,1,0:T(8,128)(2,1)S(1)}, bf16[28,32,128]{2,1,0:T(8,128)(2,1)S(1)}, u32[]{:S(2)}, u32[]{:S(2)}) collective-permute-start(bf16[28,32,128]{2,1,0:T(8,128)(2,1)S(1)} %get-tuple-element.185), channel_id=1, source_target_pairs={{0,3},{1,0},{2,1},{3,2},{4,7},{5,4},{6,5},{7,6},{8,11},{9,8},{10,9... | collective-permute-start | bytes 688136 | tf_op jit(solution)/shard_map/ppermute | solution.py:673
  108.2 0.9 copy-start.4
Sparse Core Ops, SparseCore 0:
  35.6 45.4 all-gather.5
